TPU v7x, 32 devices: a whole 2x2x4 slice. The times are simulated.
32 devices in a mesh: grp: 8 (over z, y), head: 4 (over x, core).
Axes of the slice: x: 2, y: 2, z: 4, core: 2. Of those that a mesh axis runs over, the one named last changes fastest.
Arguments:
- tokens: bfloat16 [4096, 1024], P(('grp', 'head')), may hold values from -6 to 6
- norm_gain: float32 [1024], replicated, may hold values from 0.5 to 1.5
- w_qkv: bfloat16 [1024, 3072], replicated, may hold values from -0.1875 to 0.1875
- w_gates: bfloat16 [1024, 16], replicated, may hold values from -0.1875 to 0.1875
- conv_weight: float32 [4, 3072], replicated, may hold values from -3 to 3
- conv_state: bfloat16 [8, 3, 3072], P('grp'), may hold values from -6 to 6
- decay_rate: float32 [8], replicated, may hold values from 0.0005 to 0.1
- ridge: float32 [8], P('head'), may hold values from 0.25 to 2
- w_out: bfloat16 [1024, 1024], replicated, may hold values from -0.1875 to 0.1875
- cache_keys: bfloat16 [512, 128, 8, 128], P('grp', None, 'head'), may hold values from -0.59765625 to 0.59765625
- cache_values: bfloat16 [512, 128, 8, 128], P('grp', None, 'head'), may hold values from -6 to 6
- page_table: int32 [8, 64], replicated, may hold values from 0 to 511, as said below
- cache_lengths: int32 [8], replicated, may hold values from 1 to 8192, 32768 in all
- group_prompt: int32 [8], replicated, may hold values from 0 to 7
- prompt_state: float32 [8, 8, 2, 128, 128], P('grp', 'head'), may hold values from -8 to 16
Outputs:
- layer_out: bfloat16 [4096, 1024], P(('grp', 'head'))
Inputs may be any that keep to these rules, and one draw needn't show every extreme that they name: `page_table`: every pool page is named exactly once in the table; each pool shard of 64 consecutive pages holds exactly 8 pages of every group's requests. `cache_lengths`: some request has exactly 8192 cached tokens.
All inputs are finite; a program needn't handle non-finite values.
Results may differ from a plain program's by a relative error of at most 0.0045.
Values may be sent and summed in bfloat16 or wider, within the bound.
No kernel may reach another device: no remote copies, remote signals or barrier semaphores. Data moves between devices by JAX's collectives and lax.ppermute only.
A program may use at most 128 MiB of HBM per device.

v0:
```python
import functools

import jax
import jax.numpy as jnp
from jax import lax
from jax.experimental import pallas as pl
from jax.experimental.pallas import tpu as pltpu
from jax.sharding import PartitionSpec as P

HEADS = 8
HDIM = 128
CONV = 4
CG_STEPS = 8
PAGE = 128
CHUNK = 128
PAIR = 2 * CHUNK
EPS_NORM = 1e-06
F32 = jnp.float32
BF16 = jnp.bfloat16


def swap(block, axis, distance):
    size = lax.axis_size(axis)
    return lax.ppermute(block, axis, [(i, i ^ distance) for i in range(size)])


def dot(a, b):
    return jnp.dot(a, b, preferred_element_type=F32)


def silu(a):
    return a * jax.nn.sigmoid(a)


def unit_rows(a):
    return a * lax.rsqrt(jnp.sum(a * a, axis=-1, keepdims=True) + EPS_NORM)


def block_diag(a):
    first = lax.broadcasted_iota(jnp.int32, a.shape, 1) < CHUNK
    zero = jnp.zeros_like(a)
    return jnp.concatenate([jnp.where(first, a, zero), jnp.where(first, zero, a)], axis=0)


def gram_kernel(heads, owners, code_ref, meta_ref, pick_ref, keys_ref, values_ref, prompt_ref,
                send_ref, keep_ref, acc_ref):
    step = pl.program_id(0)
    pages, rows = keys_ref.shape[0], keys_ref.shape[1]

    @pl.when(step == 0)
    def _():
        acc_ref[...] = jnp.zeros_like(acc_ref)

    lane = lax.broadcasted_iota(jnp.int32, (HDIM, rows), 1)
    for page in range(pages):
        code = code_ref[step * pages + page]
        owner, live = code // 256, code % 256
        keys = keys_ref[page]
        turned = keys.T
        zero = jnp.zeros_like(turned)
        left = jnp.concatenate(
            [
                jnp.where((lane % heads == head) & (lane < live * heads), turned, zero)
                for head in range(heads)
            ],
            axis=0,
        )
        right = jnp.concatenate([keys, values_ref[page]], axis=1)
        acc_ref[owner] += dot(left, right)

    @pl.when(step == pl.num_programs(0) - 1)
    def _():
        mine, bit = meta_ref[0], meta_ref[1]
        stored = prompt_ref.shape[0]

        def add_prompt(owner, carry):
            for slot in range(stored):

                @pl.when(pick_ref[owner] == mine * stored + slot)
                def _():
                    for head in range(heads):
                        rows_here = slice(head * HDIM, (head + 1) * HDIM)
                        acc_ref[owner, rows_here, :HDIM] += prompt_ref[slot, head, 0].T
                        acc_ref[owner, rows_here, HDIM:] += prompt_ref[slot, head, 1].T

            return carry

        lax.fori_loop(0, owners, add_prompt, 0)
        for pair in range(owners // 2):
            send_ref[pair] = acc_ref[2 * pair + 1 - bit].astype(BF16)
            keep_ref[pair] = acc_ref[2 * pair + bit].astype(BF16)


def page_sums(code, meta, group_prompt, keys, values, prompt_state, owners):
    pool, rows, _ = keys.shape
    heads = prompt_state.shape[1]
    pages = 8
    half = (owners // 2, heads * HDIM, 2 * HDIM)
    page_spec = pl.BlockSpec((pages, rows, HDIM), lambda i, *_: (i, 0, 0))
    out_spec = pl.BlockSpec(half, lambda i, *_: (0, 0, 0))
    return pl.pallas_call(
        functools.partial(gram_kernel, heads, owners),
        grid_spec=pltpu.PrefetchScalarGridSpec(
            num_scalar_prefetch=3,
            grid=(pool // pages,),
            in_specs=[
                page_spec,
                page_spec,
                pl.BlockSpec(prompt_state.shape, lambda i, *_: (0, 0, 0, 0, 0)),
            ],
            out_specs=[out_spec, out_spec],
            scratch_shapes=[pltpu.VMEM((owners, heads * HDIM, 2 * HDIM), F32)],
        ),
        out_shape=[jax.ShapeDtypeStruct(half, BF16)] * 2,
        compiler_params=pltpu.CompilerParams(vmem_limit_bytes=32 * 2**20),
        cost_estimate=pl.CostEstimate(
            flops=2 * pool * rows * heads * HDIM * 2 * HDIM,
            bytes_accessed=4 * pool * rows * HDIM,
            transcendentals=0,
        ),
        name="page_sums",
    )(code, meta, group_prompt, keys, values, prompt_state)


def halve_kernel(meta_ref, keep_ref, got_ref, *outs):
    for distance, out_ref in enumerate(outs):
        row = meta_ref[2] ^ distance
        total = keep_ref[row].astype(F32) + got_ref[row].astype(F32)
        out_ref[...] = total.astype(out_ref.dtype)


def halve_sums(meta, keep, got):
    count, rows, cols = keep.shape
    outs = [jax.ShapeDtypeStruct((rows, cols), F32 if i == 0 else BF16) for i in range(count)]
    whole = pl.BlockSpec(memory_space=pltpu.VMEM)
    return pl.pallas_call(
        halve_kernel,
        in_specs=[pl.BlockSpec(memory_space=pltpu.SMEM), whole, whole],
        out_specs=[whole] * count,
        out_shape=outs,
        compiler_params=pltpu.CompilerParams(vmem_limit_bytes=32 * 2**20),
        cost_estimate=pl.CostEstimate(
            flops=count * rows * cols, bytes_accessed=6 * count * rows * cols, transcendentals=0
        ),
        name="halve_sums",
    )(meta, keep, got)


def token_kernel(heads, place_ref, rate_ref, *refs):
    head_count = HEADS // heads
    blocks = refs[:head_count]
    (gain_ref, w_ref, wg_ref, taps_ref, state_ref) = refs[head_count : head_count + 5]
    (q_ref, k_ref, kt_ref, vt_ref, weight_ref, prefix_ref, rows_ref) = refs[head_count + 5 : -2]
    ext_ref, gate_ref = refs[-2:]
    me = place_ref[0]
    tok_rows = blocks[0].shape[0]
    length = tok_rows * head_count
    chunks = length // CHUNK
    base = 8
    ext_ref[base - (CONV - 1) : base, :] = state_ref[0].astype(F32)
    gate_ref[...] = jnp.zeros_like(gate_ref)
    for distance, block in enumerate(blocks):
        first = pl.multiple_of((me ^ distance) * tok_rows, tok_rows)
        wide = block[...].astype(F32)
        scale = lax.rsqrt(jnp.mean(wide * wide, axis=-1, keepdims=True) + EPS_NORM)
        normed = (wide * scale * gain_ref[...]).astype(BF16)
        mixed = dot(normed, w_ref[...]).astype(BF16)
        ext_ref[pl.ds(pl.multiple_of(base + first, 8), tok_rows), :] = mixed.astype(F32)
        gate_ref[pl.ds(first, tok_rows), : 2 * HEADS] = dot(normed, wg_ref[...])

    shift = lax.rem(HDIM - 2 * heads * me, HDIM)
    logits = pltpu.roll(gate_ref[...], shift, 1)
    lane = lax.broadcasted_iota(jnp.int32, (1, HDIM), 1)
    rate = jnp.zeros((1, HDIM), F32)
    for head in range(heads):
        rate = jnp.where(lane == 2 * head + 1, rate_ref[me * heads + head], rate)
    write = jax.nn.sigmoid(logits).astype(BF16).astype(F32)
    soft = jnp.maximum(logits, 0.0) + jnp.log1p(jnp.exp(-jnp.abs(logits)))
    decay = (-rate * soft).astype(BF16)
    here = lax.broadcasted_iota(jnp.int32, (CHUNK, CHUNK), 0)
    there = lax.broadcasted_iota(jnp.int32, (CHUNK, CHUNK), 1)
    lower = (here >= there).astype(F32).astype(BF16)
    cumul = [dot(lower, decay[c * CHUNK : (c + 1) * CHUNK]) for c in range(chunks)]
    turned = [block.T for block in cumul]

    for head in range(heads):
        parts = []
        for part in range(3):
            cols = slice((3 * head + part) * HDIM, (3 * head + part + 1) * HDIM)
            total = taps_ref[CONV - 1 : CONV, cols] * ext_ref[base : base + length, cols]
            for lag in range(1, CONV):
                total = total + taps_ref[CONV - 1 - lag : CONV - lag, cols] * (
                    ext_ref[base - lag : base - lag + length, cols]
                )
            parts.append(total)
        query = unit_rows(silu(parts[0])).astype(BF16)
        key = unit_rows(silu(parts[1])).astype(BF16)
        value = parts[2].astype(BF16)
        q_ref[head] = query.T
        k_ref[head] = key
        kt_ref[head] = key.T
        vt_ref[head] = value.T
        prefix = jnp.zeros((HDIM, 2 * HDIM), F32)
        so_far = jnp.zeros((1, 1), F32)
        for c in range(chunks):
            rows = slice(c * CHUNK, (c + 1) * CHUNK)
            col = cumul[c][:, 2 * head + 1 : 2 * head + 2]
            row = turned[c][2 * head + 1 : 2 * head + 2, :]
            gate = write[rows, 2 * head : 2 * head + 1]
            spread = jnp.exp(jnp.minimum(row - col, 0.0)) * gate
            half = slice((c % 2) * CHUNK, (c % 2 + 1) * CHUNK)
            weight_ref[head, c // 2, :, half] = jnp.where(here <= there, spread, 0.0)
            rows_ref[head, c // 2, 0:1, half] = jnp.exp(row)
            rows_ref[head, c // 2, 1:2, half] = jnp.broadcast_to(jnp.exp(so_far), (1, CHUNK))
            prefix_ref[head, c, :HDIM] = prefix[:, :HDIM]
            prefix_ref[head, c, HDIM:] = prefix[:, HDIM:].T
            if c + 1 < chunks:
                whole = cumul[c][CHUNK - 1 :, 2 * head + 1 : 2 * head + 2]
                carry = jnp.exp(whole - col) * gate
                both = jnp.concatenate([key[rows], value[rows]], axis=1).astype(F32)
                prefix = prefix * jnp.exp(whole) + dot(
                    kt_ref[head, :, rows], (both * carry).astype(BF16)
                )
                so_far = so_far + whole


def token_vectors(place, decay_rate, blocks, norm_gain, w_qkv, w_gates, conv_weight, conv_state):
    head_count = len(blocks)
    heads = HEADS // head_count
    width = heads * 3 * HDIM
    tok_rows, model = blocks[0].shape
    length = head_count * tok_rows
    chunks = length // CHUNK

    def full(shape):
        return pl.BlockSpec(shape, lambda i, *_: (0,) * len(shape))

    outs = [
        jax.ShapeDtypeStruct((heads, HDIM, length), BF16),
        jax.ShapeDtypeStruct((heads, length, HDIM), BF16),
        jax.ShapeDtypeStruct((heads, HDIM, length), BF16),
        jax.ShapeDtypeStruct((heads, HDIM, length), BF16),
        jax.ShapeDtypeStruct((heads, chunks // 2, CHUNK, PAIR), F32),
        jax.ShapeDtypeStruct((heads, chunks, 2 * HDIM, HDIM), F32),
        jax.ShapeDtypeStruct((heads, chunks // 2, 8, PAIR), F32),
    ]
    return pl.pallas_call(
        functools.partial(token_kernel, heads),
        grid_spec=pltpu.PrefetchScalarGridSpec(
            num_scalar_prefetch=2,
            grid=(1,),
            in_specs=[full(b.shape) for b in blocks]
            + [
                full((1, model)),
                pl.BlockSpec((model, width), lambda i, place, rate: (0, place[0])),
                full(w_gates.shape),
                pl.BlockSpec((CONV, width), lambda i, place, rate: (0, place[0])),
                pl.BlockSpec((1, CONV - 1, width), lambda i, place, rate: (0, 0, place[0])),
            ],
            out_specs=[full(o.shape) for o in outs],
            scratch_shapes=[pltpu.VMEM((8 + length, width), F32), pltpu.VMEM((length, HDIM), F32)],
        ),
        out_shape=outs,
        compiler_params=pltpu.CompilerParams(vmem_limit_bytes=40 * 2**20),
        cost_estimate=pl.CostEstimate(
            flops=2 * length * model * width,
            bytes_accessed=2 * model * (length + width) + 4 * 2**20,
            transcendentals=length * width,
        ),
        name="token_vectors",
    )(place, decay_rate, *blocks, norm_gain.reshape(1, model), w_qkv, w_gates, conv_weight, conv_state)


def read_kernel(heads, terms, place_ref, ridge_ref, *refs):
    head_count = HEADS // heads
    sums = refs[:terms]
    (q_ref, k_ref, kt_ref, vt_ref, weight_ref, prefix_ref, rows_ref) = refs[terms : terms + 7]
    outs = refs[terms + 7 : terms + 7 + head_count]
    left_ref, cross_ref, x_ref, r_ref, d_ref, o_ref = refs[terms + 7 + head_count :]
    me = place_ref[0]
    pairs = q_ref.shape[2] // PAIR
    groups = [(head, pair) for head in range(heads) for pair in range(pairs)]
    norms = []
    for head in range(heads):
        rows = slice(head * HDIM, (head + 1) * HDIM)
        total = sums[0][rows, :].astype(F32)
        for term in sums[1:]:
            total = total + term[rows, :].astype(F32)
        gram, cross = total[:, :HDIM].T, total[:, HDIM:].T
        for pair in range(pairs):
            for side in range(2):
                c = 2 * pair + side
                half = slice(side * CHUNK, (side + 1) * CHUNK)
                scale = rows_ref[head, pair, 1:2, half]
                left_ref[head, pair, :HDIM, half] = (
                    gram * scale + prefix_ref[head, c, :HDIM]
                ).astype(BF16)
                left_ref[head, pair, HDIM:, half] = k_ref[head, c * CHUNK : (c + 1) * CHUNK]
                cross_ref[head, pair, :, half] = (
                    cross * scale + prefix_ref[head, c, HDIM:]
                ).astype(BF16)
            query = q_ref[head, :, pair * PAIR : (pair + 1) * PAIR].astype(F32)
            x_ref[head, pair] = jnp.zeros_like(query)
            r_ref[head, pair] = query
            d_ref[head, pair] = query
            norms.append(jnp.sum(query * query, axis=0, keepdims=True))

    def one_step(_, norms):
        firsts = [dot(left_ref[g], block_diag(d_ref[g].astype(BF16))) for g in groups]
        seconds = []
        for (head, pair), first in zip(groups, firsts):
            scores = (first[HDIM:] * weight_ref[head, pair]).astype(BF16)
            seconds.append(
                dot(kt_ref[head, :, pair * PAIR : (pair + 1) * PAIR], block_diag(scores))
            )
        later = []
        for (head, pair), first, second, norm in zip(groups, firsts, seconds, norms):
            direction = d_ref[head, pair]
            image = (
                rows_ref[head, pair, 0:1] * first[:HDIM] + ridge_ref[head] * direction + second
            )
            alpha = norm / jnp.sum(direction * image, axis=0, keepdims=True)
            x_ref[head, pair] += alpha * direction
            residue = r_ref[head, pair] - alpha * image
            r_ref[head, pair] = residue
            norm_next = jnp.sum(residue * residue, axis=0, keepdims=True)
            d_ref[head, pair] = residue + norm_next / norm * direction
            later.append(norm_next)
        return tuple(later)

    lax.fori_loop(0, CG_STEPS, one_step, tuple(norms))
    for head, pair in groups:
        left_ref[head, pair, :HDIM] = cross_ref[head, pair]
        first = dot(left_ref[head, pair], block_diag(x_ref[head, pair].astype(BF16)))
        scores = (first[HDIM:] * weight_ref[head, pair]).astype(BF16)
        span = slice(pair * PAIR, (pair + 1) * PAIR)
        read = rows_ref[head, pair, 0:1] * first[:HDIM] + dot(
            vt_ref[head, :, span], block_diag(scores)
        )
        o_ref[span, head * HDIM : (head + 1) * HDIM] = read.T.astype(BF16)
    tok_rows = outs[0].shape[0]
    for distance, out_ref in enumerate(outs):
        first_row = pl.multiple_of((me ^ distance) * tok_rows, tok_rows)
        out_ref[...] = o_ref[pl.ds(first_row, tok_rows), :]


def ridge_reads(place, ridge, sums, vectors, head_count):
    heads = HEADS // head_count
    length = vectors[0].shape[2]
    pairs = length // PAIR
    tok_rows = length // head_count
    whole = pl.BlockSpec(memory_space=pltpu.VMEM)
    small = pl.BlockSpec(memory_space=pltpu.SMEM)
    state = pltpu.VMEM((heads, pairs, HDIM, PAIR), F32)
    return pl.pallas_call(
        functools.partial(read_kernel, heads, len(sums)),
        in_specs=[small, small] + [whole] * (len(sums) + len(vectors)),
        out_specs=[whole] * head_count,
        out_shape=[jax.ShapeDtypeStruct((tok_rows, heads * HDIM), BF16)] * head_count,
        scratch_shapes=[
            pltpu.VMEM((heads, pairs, 2 * HDIM, PAIR), BF16),
            pltpu.VMEM((heads, pairs, HDIM, PAIR), BF16),
            state,
            state,
            state,
            pltpu.VMEM((length, heads * HDIM), BF16),
        ],
        compiler_params=pltpu.CompilerParams(vmem_limit_bytes=32 * 2**20),
        cost_estimate=pl.CostEstimate(
            flops=CG_STEPS * heads * pairs * 6 * CHUNK**3 * 4,
            bytes_accessed=4 * 2**20,
            transcendentals=0,
        ),
        name="ridge_reads",
    )(place, ridge, *sums, *vectors)


def output_kernel(place_ref, tokens_ref, w_ref, *refs):
    out_ref = refs[-1]
    me = place_ref[0]
    total = tokens_ref[...].astype(F32)
    for distance, part in enumerate(refs[:-1]):
        width = part.shape[1]
        first = pl.multiple_of((me ^ distance) * width, width)
        total = total + dot(part[...], w_ref[pl.ds(first, width), :])
    out_ref[...] = total.astype(BF16)


def output_rows(place, tokens, w_out, reads):
    whole = pl.BlockSpec(memory_space=pltpu.VMEM)
    return pl.pallas_call(
        output_kernel,
        in_specs=[pl.BlockSpec(memory_space=pltpu.SMEM)] + [whole] * (2 + len(reads)),
        out_specs=whole,
        out_shape=jax.ShapeDtypeStruct(tokens.shape, BF16),
        compiler_params=pltpu.CompilerParams(vmem_limit_bytes=24 * 2**20),
        cost_estimate=pl.CostEstimate(
            flops=2 * tokens.shape[0] * w_out.shape[0] * w_out.shape[1],
            bytes_accessed=2 * w_out.size + 6 * tokens.size,
            transcendentals=0,
        ),
        name="output_rows",
    )(place, tokens, w_out, *reads)


def shards(
    tokens,
    norm_gain,
    w_qkv,
    w_gates,
    conv_weight,
    conv_state,
    decay_rate,
    ridge,
    w_out,
    cache_keys,
    cache_values,
    page_table,
    cache_lengths,
    group_prompt,
    prompt_state,
):
    head_count = lax.axis_size("head")
    owners = lax.axis_size("grp")
    me = lax.axis_index("head").astype(jnp.int32)
    group = lax.axis_index("grp").astype(jnp.int32)
    place = me.reshape(1)
    meta = jnp.stack([group, group % 2, group // 2])

    blocks = {0: tokens}
    bit = head_count // 2
    while bit:
        for held in list(blocks):
            blocks[held ^ bit] = swap(blocks[held], "head", bit)
        bit //= 2
    blocks = [blocks[i] for i in range(head_count)]

    pool, page, heads, _ = cache_keys.shape
    ids = group * pool + jnp.arange(pool, dtype=jnp.int32)
    slots = page_table.shape[1]
    live = jnp.clip(cache_lengths[:, None] - jnp.arange(slots, dtype=jnp.int32) * PAGE, 0, PAGE)
    tag = jnp.arange(owners, dtype=jnp.int32)[:, None] * 256 + live
    code = jnp.sum(
        jnp.where(page_table[:, :, None] == ids, tag[:, :, None], 0), axis=(0, 1), dtype=jnp.int32
    )
    send, keep = page_sums(
        code,
        meta,
        group_prompt,
        cache_keys.reshape(pool, page * heads, HDIM),
        cache_values.reshape(pool, page * heads, HDIM),
        prompt_state,
        owners,
    )
    got = swap(send, "grp", 1)
    vectors = token_vectors(
        place, decay_rate, blocks, norm_gain, w_qkv, w_gates, conv_weight, conv_state
    )
    sums = halve_sums(meta, keep, got)
    sums = [sums[0]] + [swap(sums[i], "grp", 2 * i) for i in range(1, owners // 2)]
    reads = ridge_reads(place, ridge, sums, vectors, head_count)
    reads = [reads[0]] + [swap(reads[i], "head", i) for i in range(1, head_count)]
    return output_rows(place, tokens, w_out, reads)


def solution(mesh):
    placed = (
        P(("grp", "head"), None),
        P(),
        P(),
        P(),
        P(),
        P("grp", None, None),
        P(),
        P("head"),
        P(),
        P("grp", None, "head", None),
        P("grp", None, "head", None),
        P(),
        P(),
        P(),
        P("grp", "head", None, None, None),
    )
    return jax.shard_map(
        shards, mesh=mesh, in_specs=placed, out_specs=P(("grp", "head"), None), check_vma=False
    )
```

profile of v0, /device:TPU:0, one launch (start us, length us, event | category | flops | bytes accessed | tf_op | source)
XLA Modules:
  0.0 57.1 jit_solution(313147454901689755)
XLA Ops:
  0.0 0.1 pad_add_fusion.meta_ref
  0.1 0.7 %clamp_add_fusion = s32[8,64]{1,0:T(8,128)S(1)} fusion(s32[64]{0:T(128)S(1)} %iota_multiply_fusion, s32[8]{0:T(128)} %param.27, s32[8]{0:T(128)S(1)} %iota_multiply_fusion.1), kind=kLoop, calls=%fused_computation.1 | loop fusion | flops 1536 | bytes 2368 | tf_op jit(solution)/shard_map/add | solution.py:442
  0.8 0.9 %select_reduce_fusion.code_ref = s32[64]{0:T(128)S(1)} fusion(s32[8,64]{1,0:T(8,128)S(1)} %clamp_add_fusion, s32[64]{0:T(128)S(1)} %iota_add_fusion, s32[8,64]{1,0:T(8,128)} %param.26), kind=kLoop, calls=%fused_computation | loop fusion | flops 98240 | bytes 4608 | tf_op jit(solution)/shard_map/reduce_sum | solution.py:443
  1.7 0.0 copy-start.1
  1.7 2.2 %copy-done.1 = bf16[64,128,2,128]{3,2,1,0:T(2,128)(2,1)S(1)} copy-done((bf16[64,128,2,128]{3,2,1,0:T(2,128)(2,1)S(1)}, bf16[64,128,2,128]{3,2,1,0:T(2,128)(2,1)}, u32[]{:S(2)}) %copy-start.1) | copy-done | bytes 4194328
  3.9 0.0 copy-start.2
  3.9 2.2 %copy-done.2 = bf16[64,128,2,128]{3,2,1,0:T(2,128)(2,1)S(1)} copy-done((bf16[64,128,2,128]{3,2,1,0:T(2,128)(2,1)S(1)}, bf16[64,128,2,128]{3,2,1,0:T(2,128)(2,1)}, u32[]{:S(2)}) %copy-start.2) | copy-done | bytes 4194328
  6.1 0.0 copy-start.5
  6.1 0.9 %copy-done.5 = f32[1,2,2,128,128]{4,3,2,1,0:T(8,128)S(1)} copy-done((f32[1,2,2,128,128]{4,3,2,1,0:T(8,128)S(1)}, f32[1,2,2,128,128]{4,3,2,1,0:T(8,128)}, u32[]{:S(2)}) %copy-start.5) | copy-done | bytes 262168
  7.0 0.0 copy-start.9
  7.1 0.7 %copy-done.9 = s32[8]{0:T(128)S(1)} copy-done((s32[8]{0:T(128)S(1)}, s32[8]{0:T(128)}, u32[]{:S(2)}) %copy-start.9) | copy-done | bytes 56
  7.7 0.0 copy-start.4
  7.7 0.0 copy-start.12
  7.7 0.0 copy-start.6
  7.7 0.0 copy-start.7
  7.7 0.0 copy-start.8
  7.7 0.0 copy-start.10
  7.7 5.4 %page_sums.1 = (bf16[4,256,256]{2,1,0:T(8,128)(2,1)S(1)}, bf16[4,256,256]{2,1,0:T(8,128)(2,1)S(1)}) custom-call(s32[64]{0:T(128)S(1)} %select_reduce_fusion.code_ref, s32[3]{0:T(128)S(1)} %pad_add_fusion.meta_ref, s32[8]{0:T(128)S(1)} %copy-done.9, bf16[64,256,128]{2,1,0:T(8,128)(2,1)S(1)} %bitcast.7, bf16[64,256,128]{2,1,0:T(8,128)(2,1)S(1)} %bitcast.8, ...), custom_call_target="tpu_custom_call" | custom-call | flops 2147483648 | bytes 8388608 | tf_op jit(solution)/shard_map/page_sums/pallas_call | solution.py:101
  13.2 2.9 %collective-permute-start = (bf16[4,256,256]{2,1,0:T(8,128)(2,1)S(1)}, bf16[4,256,256]{2,1,0:T(8,128)(2,1)S(1)}, u32[]{:S(2)}, u32[]{:S(2)}) collective-permute-start(bf16[4,256,256]{2,1,0:T(8,128)(2,1)S(1)} %get-tuple-element.23), channel_id=1, source_target_pairs={{0,4},{4,0},{8,12},{12,8},{16,20},{20,16},{24,28},{28,24},{1,5},{5... | collective-permute-start | bytes 1572872 | tf_op jit(solution)/shard_map/ppermute | solution.py:24
  16.1 0.0 copy-done.4
  16.1 1.5 %collective-permute-start.5 = (bf16[128,1024]{1,0:T(8,128)(2,1)S(1)}, bf16[128,1024]{1,0:T(8,128)(2,1)S(1)}, u32[]{:S(2)}, u32[]{:S(2)}) collective-permute-start(bf16[128,1024]{1,0:T(8,128)(2,1)S(1)} %copy-done.4), channel_id=1, source_target_pairs={{0,2},{1,3},{2,0},{3,1},{4,6},{5,7},{6,4},{7,5},{8,10},{9,11},{10,... | collective-permute-start | bytes 786440 | tf_op jit(solution)/shard_map/ppermute | solution.py:24
  17.6 0.0 collective-permute-start.4
  17.6 6.3 %collective-permute-done.5.refs_2_ = bf16[128,1024]{1,0:T(8,128)(2,1)S(1)} collective-permute-done((bf16[128,1024]{1,0:T(8,128)(2,1)S(1)}, bf16[128,1024]{1,0:T(8,128)(2,1)S(1)}, u32[]{:S(2)}, u32[]{:S(2)}) %collective-permute-start.5) | collective-permute-done | bytes 262176 | tf_op jit(solution)/shard_map/ppermute | solution.py:24
  23.9 0.0 collective-permute-start.6
  23.9 4.2 %collective-permute-done.got_ref = bf16[4,256,256]{2,1,0:T(8,128)(2,1)S(1)} collective-permute-done((bf16[4,256,256]{2,1,0:T(8,128)(2,1)S(1)}, bf16[4,256,256]{2,1,0:T(8,128)(2,1)S(1)}, u32[]{:S(2)}, u32[]{:S(2)}) %collective-permute-start) | collective-permute-done | bytes 524320 | tf_op jit(solution)/shard_map/ppermute | solution.py:24
  28.0 0.7 %halve_sums.1 = (f32[256,256]{1,0:T(8,128)S(1)}, bf16[256,256]{1,0:T(8,128)(2,1)S(1)}, bf16[256,256]{1,0:T(8,128)(2,1)S(1)}, bf16[256,256]{1,0:T(8,128)(2,1)S(1)}) custom-call(s32[3]{0:T(128)S(1)} %pad_add_fusion.meta_ref, bf16[4,256,256]{2,1,0:T(8,128)(2,1)S(1)} %get-tuple-element.22.keep_ref, bf16[4,256,256]{2,1,0:T(8,128)(2,1)S(1)} %collective-permute-done.got_ref), custom_call_target="tpu_custom_call" | custom-call | flops 262144 | bytes 1572864 | tf_op jit(solution)/shard_map/halve_sums/pallas_call | solution.py:136
  28.7 0.0 copy-start.11
  28.7 1.7 %collective-permute-start.1 = (bf16[256,256]{1,0:T(8,128)(2,1)S(1)}, bf16[256,256]{1,0:T(8,128)(2,1)S(1)}, u32[]{:S(2)}, u32[]{:S(2)}) collective-permute-start(bf16[256,256]{1,0:T(8,128)(2,1)S(1)} %get-tuple-element.25), channel_id=1, source_target_pairs={{0,8},{4,12},{8,0},{12,4},{16,24},{20,28},{24,16},{28,20},{1,9},{5... | collective-permute-start | bytes 393224 | tf_op jit(solution)/shard_map/ppermute | solution.py:24
  30.4 2.6 %collective-permute-start.2 = (bf16[256,256]{1,0:T(8,128)(2,1)S(1)}, bf16[256,256]{1,0:T(8,128)(2,1)S(1)}, u32[]{:S(2)}, u32[]{:S(2)}) collective-permute-start(bf16[256,256]{1,0:T(8,128)(2,1)S(1)} %get-tuple-element.26), channel_id=1, source_target_pairs={{0,16},{4,20},{8,24},{12,28},{16,0},{20,4},{24,8},{28,12},{1,17},{... | collective-permute-start | bytes 393224 | tf_op jit(solution)/shard_map/ppermute | solution.py:24
  33.0 0.1 collective-permute-start.3
  33.1 0.0 copy-done.12
  33.1 0.2 copy.17.refs_6_
  33.3 0.0 collective-permute-done.4.refs_1_
  33.3 0.0 collective-permute-done.6.refs_3_
  33.3 0.0 copy-done.6
  33.3 0.0 copy-done.7
  33.4 0.0 copy-done.8
  33.4 0.0 copy-done.10
  33.4 0.0 copy-start
  33.4 2.8 %copy-done = bf16[1024,3072]{1,0:T(8,128)(2,1)S(1)} copy-done((bf16[1024,3072]{1,0:T(8,128)(2,1)S(1)}, bf16[1024,3072]{1,0:T(8,128)(2,1)}, u32[]{:S(2)}) %copy-start) | copy-done | bytes 6291480
  36.2 4.1 %token_vectors.1 = (bf16[2,128,512]{2,1,0:T(8,128)(2,1)S(1)}, bf16[2,512,128]{2,1,0:T(8,128)(2,1)S(1)}, bf16[2,128,512]{2,1,0:T(8,128)(2,1)S(1)}, bf16[2,128,512...) custom-call(s32[1]{0:T(128)} %bitcast.place_ref, ...), custom_call_target="tpu_custom_call" | custom-call | flops 805306368 | bytes 6815744 | tf_op jit(solution)/shard_map/token_vectors/pallas_call | solution.py:247
  40.2 0.0 copy-start.3
  40.2 0.0 collective-permute-done.1.refs_1_
  40.2 2.2 %collective-permute-done.2.refs_2_ = bf16[256,256]{1,0:T(8,128)(2,1)S(1)} collective-permute-done((bf16[256,256]{1,0:T(8,128)(2,1)S(1)}, bf16[256,256]{1,0:T(8,128)(2,1)S(1)}, u32[]{:S(2)}, u32[]{:S(2)}) %collective-permute-start.2) | collective-permute-done | bytes 131104 | tf_op jit(solution)/shard_map/ppermute | solution.py:24
  42.5 0.0 collective-permute-done.3.refs_3_
  42.5 0.0 copy-done.11
  42.5 7.8 %ridge_reads.1 = (bf16[128,256]{1,0:T(8,128)(2,1)S(1)}, bf16[128,256]{1,0:T(8,128)(2,1)S(1)}, bf16[128,256]{1,0:T(8,128)(2,1)S(1)}, bf16[128,256]{1,0:T(8,128)(2,1)S(1)}) custom-call(s32[1]{0:T(128)} %bitcast.place_ref, f32[2]{0:T(128)S(1)} %copy-done.11, f32[256,256]{1,0:T(8,128)S(1)} %get-tuple-element.24.refs_0_, ...), custom_call_target="tpu_custom_call" | custom-call | flops 1610612736 | bytes 4194304 | tf_op jit(solution)/shard_map/ridge_reads/pallas_call | solution.py:355
  50.3 0.1 collective-permute-start.7
  50.4 1.5 %collective-permute-start.8 = (bf16[128,256]{1,0:T(8,128)(2,1)S(1)}, bf16[128,256]{1,0:T(8,128)(2,1)S(1)}, u32[]{:S(2)}, u32[]{:S(2)}) collective-permute-start(bf16[128,256]{1,0:T(8,128)(2,1)S(1)} %get-tuple-element.37), channel_id=1, source_target_pairs={{0,2},{1,3},{2,0},{3,1},{4,6},{5,7},{6,4},{7,5},{8,10},{9,11},{10,... | collective-permute-start | bytes 196616 | tf_op jit(solution)/shard_map/ppermute | solution.py:24
  51.9 0.4 collective-permute-start.9
  52.3 0.0 collective-permute-done.7.refs_1_
  52.3 2.7 %collective-permute-done.8.refs_2_ = bf16[128,256]{1,0:T(8,128)(2,1)S(1)} collective-permute-done((bf16[128,256]{1,0:T(8,128)(2,1)S(1)}, bf16[128,256]{1,0:T(8,128)(2,1)S(1)}, u32[]{:S(2)}, u32[]{:S(2)}) %collective-permute-start.8) | collective-permute-done | bytes 65568 | tf_op jit(solution)/shard_map/ppermute | solution.py:24
  54.9 1.0 %collective-permute-done.9.refs_3_ = bf16[128,256]{1,0:T(8,128)(2,1)S(1)} collective-permute-done((bf16[128,256]{1,0:T(8,128)(2,1)S(1)}, bf16[128,256]{1,0:T(8,128)(2,1)S(1)}, u32[]{:S(2)}, u32[]{:S(2)}) %collective-permute-start.9) | collective-permute-done | bytes 65568 | tf_op jit(solution)/shard_map/ppermute | solution.py:24
  56.0 0.0 copy-done.3
  56.0 1.2 %output_rows.1 = bf16[128,1024]{1,0:T(8,128)(2,1)} custom-call(s32[1]{0:T(128)} %bitcast.place_ref, bf16[128,1024]{1,0:T(8,128)(2,1)S(1)} %copy-done.4, bf16[1024,1024]{1,0:T(8,128)(2,1)S(1)} %copy-done.3, bf16[128,256]{1,0:T(8,128)(2,1)S(1)} %get-tuple-element.35.refs_0_, bf16[128,256]{1,0:T(8,128)(2,1)S(1)} %collective-permute-done.7.refs_1_, ...), custom_call_target="tpu_custom_call" | custom-call | flops 268435456 | bytes 2883584 | tf_op jit(solution)/shard_map/output_rows/pallas_call | solution.py:391
  (3 shorter events, 0.0 us)
Async XLA Ops:
  1.7 2.2 %copy-start.1 = (bf16[64,128,2,128]{3,2,1,0:T(2,128)(2,1)S(1)}, bf16[64,128,2,128]{3,2,1,0:T(2,128)(2,1)}, u32[]{:S(2)}) copy-start(bf16[64,128,2,128]{3,2,1,0:T(2,128)(2,1)} %param.24) | copy-start | bytes 12582916
  3.9 2.2 %copy-start.2 = (bf16[64,128,2,128]{3,2,1,0:T(2,128)(2,1)S(1)}, bf16[64,128,2,128]{3,2,1,0:T(2,128)(2,1)}, u32[]{:S(2)}) copy-start(bf16[64,128,2,128]{3,2,1,0:T(2,128)(2,1)} %param.25) | copy-start | bytes 12582916
  6.1 0.9 %copy-start.5 = (f32[1,2,2,128,128]{4,3,2,1,0:T(8,128)S(1)}, f32[1,2,2,128,128]{4,3,2,1,0:T(8,128)}, u32[]{:S(2)}) copy-start(f32[1,2,2,128,128]{4,3,2,1,0:T(8,128)} %prompt_ref.1) | copy-start | bytes 786436
  7.0 0.7 %copy-start.9 = (s32[8]{0:T(128)S(1)}, s32[8]{0:T(128)}, u32[]{:S(2)}) copy-start(s32[8]{0:T(128)} %pick_ref.1) | copy-start | bytes 100
  7.7 8.4 %copy-start.4 = (bf16[128,1024]{1,0:T(8,128)(2,1)S(1)}, bf16[128,1024]{1,0:T(8,128)(2,1)}, u32[]{:S(2)}) copy-start(bf16[128,1024]{1,0:T(8,128)(2,1)} %tokens_ref.1) | copy-start | bytes 786436
  7.7 25.4 %copy-start.12 = (bf16[1024,16]{0,1:T(8,128)(2,1)S(1)}, bf16[1024,16]{0,1:T(8,128)(2,1)}, u32[]{:S(2)}) copy-start(bf16[1024,16]{0,1:T(8,128)(2,1)} %param.18) | copy-start | bytes 98308
  7.7 25.6 %copy-start.6 = (f32[4,3072]{1,0:T(4,128)S(1)}, f32[4,3072]{1,0:T(4,128)}, u32[]{:S(2)}) copy-start(f32[4,3072]{1,0:T(4,128)} %refs_7_.1) | copy-start | bytes 147460
  7.7 25.6 %copy-start.7 = (bf16[1,3,3072]{2,1,0:T(4,128)(2,1)S(1)}, bf16[1,3,3072]{2,1,0:T(4,128)(2,1)}, u32[]{:S(2)}) copy-start(bf16[1,3,3072]{2,1,0:T(4,128)(2,1)} %refs_8_.1) | copy-start | bytes 55300
  7.7 25.6 %copy-start.8 = (f32[1024]{0:T(1024)S(1)}, f32[1024]{0:T(1024)}, u32[]{:S(2)}) copy-start(f32[1024]{0:T(1024)} %param.16) | copy-start | bytes 12292
  7.7 25.6 %copy-start.10 = (f32[8]{0:T(128)S(1)}, f32[8]{0:T(128)}, u32[]{:S(2)}) copy-start(f32[8]{0:T(128)} %rate_ref.1) | copy-start | bytes 100
  13.2 14.8 %collective-permute-start = (bf16[4,256,256]{2,1,0:T(8,128)(2,1)S(1)}, bf16[4,256,256]{2,1,0:T(8,128)(2,1)S(1)}, u32[]{:S(2)}, u32[]{:S(2)}) collective-permute-start(bf16[4,256,256]{2,1,0:T(8,128)(2,1)S(1)} %get-tuple-element.23), channel_id=1, source_target_pairs={{0,4},{4,0},{8,12},{12,8},{16,20},{20,16},{24,28},{28,24},{1,5},{5... | collective-permute-start | bytes 1572872 | tf_op jit(solution)/shard_map/ppermute | solution.py:24
  16.1 7.8 %collective-permute-start.5 = (bf16[128,1024]{1,0:T(8,128)(2,1)S(1)}, bf16[128,1024]{1,0:T(8,128)(2,1)S(1)}, u32[]{:S(2)}, u32[]{:S(2)}) collective-permute-start(bf16[128,1024]{1,0:T(8,128)(2,1)S(1)} %copy-done.4), channel_id=1, source_target_pairs={{0,2},{1,3},{2,0},{3,1},{4,6},{5,7},{6,4},{7,5},{8,10},{9,11},{10,... | collective-permute-start | bytes 786440 | tf_op jit(solution)/shard_map/ppermute | solution.py:24
  17.6 15.7 %collective-permute-start.4 = (bf16[128,1024]{1,0:T(8,128)(2,1)S(1)}, bf16[128,1024]{1,0:T(8,128)(2,1)S(1)}, u32[]{:S(2)}, u32[]{:S(2)}) collective-permute-start(bf16[128,1024]{1,0:T(8,128)(2,1)S(1)} %copy-done.4), channel_id=1, source_target_pairs={{0,1},{1,0},{2,3},{3,2},{4,5},{5,4},{6,7},{7,6},{8,9},{9,8},{10,11... | collective-permute-start | bytes 786440 | tf_op jit(solution)/shard_map/ppermute | solution.py:24
  23.9 9.5 %collective-permute-start.6 = (bf16[128,1024]{1,0:T(8,128)(2,1)S(1)}, bf16[128,1024]{1,0:T(8,128)(2,1)S(1)}, u32[]{:S(2)}, u32[]{:S(2)}) collective-permute-start(bf16[128,1024]{1,0:T(8,128)(2,1)S(1)} %collective-permute-done.5.refs_2_), channel_id=1, source_target_pairs={{0,1},{1,0},{2,3},{3,2},{4,5},{5,4},{6,7},{7,6},{8,9},{9,8},{10,11... | collective-permute-start | bytes 786440 | tf_op jit(solution)/shard_map/ppermute | solution.py:24
  28.7 13.8 %copy-start.11 = (f32[2]{0:T(128)S(1)}, f32[2]{0:T(128)}, u32[]{:S(2)}) copy-start(f32[2]{0:T(128)} %ridge_ref.1) | copy-start | bytes 28
  28.7 11.6 %collective-permute-start.1 = (bf16[256,256]{1,0:T(8,128)(2,1)S(1)}, bf16[256,256]{1,0:T(8,128)(2,1)S(1)}, u32[]{:S(2)}, u32[]{:S(2)}) collective-permute-start(bf16[256,256]{1,0:T(8,128)(2,1)S(1)} %get-tuple-element.25), channel_id=1, source_target_pairs={{0,8},{4,12},{8,0},{12,4},{16,24},{20,28},{24,16},{28,20},{1,9},{5... | collective-permute-start | bytes 393224 | tf_op jit(solution)/shard_map/ppermute | solution.py:24
  30.4 12.1 %collective-permute-start.2 = (bf16[256,256]{1,0:T(8,128)(2,1)S(1)}, bf16[256,256]{1,0:T(8,128)(2,1)S(1)}, u32[]{:S(2)}, u32[]{:S(2)}) collective-permute-start(bf16[256,256]{1,0:T(8,128)(2,1)S(1)} %get-tuple-element.26), channel_id=1, source_target_pairs={{0,16},{4,20},{8,24},{12,28},{16,0},{20,4},{24,8},{28,12},{1,17},{... | collective-permute-start | bytes 393224 | tf_op jit(solution)/shard_map/ppermute | solution.py:24
  33.0 9.5 %collective-permute-start.3 = (bf16[256,256]{1,0:T(8,128)(2,1)S(1)}, bf16[256,256]{1,0:T(8,128)(2,1)S(1)}, u32[]{:S(2)}, u32[]{:S(2)}) collective-permute-start(bf16[256,256]{1,0:T(8,128)(2,1)S(1)} %get-tuple-element.27), channel_id=1, source_target_pairs={{0,24},{4,28},{8,16},{12,20},{16,8},{20,12},{24,0},{28,4},{1,25},{... | collective-permute-start | bytes 393224 | tf_op jit(solution)/shard_map/ppermute | solution.py:24
  33.4 2.8 %copy-start = (bf16[1024,3072]{1,0:T(8,128)(2,1)S(1)}, bf16[1024,3072]{1,0:T(8,128)(2,1)}, u32[]{:S(2)}) copy-start(bf16[1024,3072]{1,0:T(8,128)(2,1)} %refs_5_.1) | copy-start | bytes 18874372
  40.2 15.7 %copy-start.3 = (bf16[1024,1024]{1,0:T(8,128)(2,1)S(1)}, bf16[1024,1024]{1,0:T(8,128)(2,1)}, u32[]{:S(2)}) copy-start(bf16[1024,1024]{1,0:T(8,128)(2,1)} %w_ref.1) | copy-start | bytes 6291460
  50.3 1.9 %collective-permute-start.7 = (bf16[128,256]{1,0:T(8,128)(2,1)S(1)}, bf16[128,256]{1,0:T(8,128)(2,1)S(1)}, u32[]{:S(2)}, u32[]{:S(2)}) collective-permute-start(bf16[128,256]{1,0:T(8,128)(2,1)S(1)} %get-tuple-element.36), channel_id=1, source_target_pairs={{0,1},{1,0},{2,3},{3,2},{4,5},{5,4},{6,7},{7,6},{8,9},{9,8},{10,11... | collective-permute-start | bytes 196616 | tf_op jit(solution)/shard_map/ppermute | solution.py:24
  50.4 4.5 %collective-permute-start.8 = (bf16[128,256]{1,0:T(8,128)(2,1)S(1)}, bf16[128,256]{1,0:T(8,128)(2,1)S(1)}, u32[]{:S(2)}, u32[]{:S(2)}) collective-permute-start(bf16[128,256]{1,0:T(8,128)(2,1)S(1)} %get-tuple-element.37), channel_id=1, source_target_pairs={{0,2},{1,3},{2,0},{3,1},{4,6},{5,7},{6,4},{7,5},{8,10},{9,11},{10,... | collective-permute-start | bytes 196616 | tf_op jit(solution)/shard_map/ppermute | solution.py:24
  51.9 4.1 %collective-permute-start.9 = (bf16[128,256]{1,0:T(8,128)(2,1)S(1)}, bf16[128,256]{1,0:T(8,128)(2,1)S(1)}, u32[]{:S(2)}, u32[]{:S(2)}) collective-permute-start(bf16[128,256]{1,0:T(8,128)(2,1)S(1)} %get-tuple-element.38), channel_id=1, source_target_pairs={{0,3},{1,2},{2,1},{3,0},{4,7},{5,6},{6,5},{7,4},{8,11},{9,10},{10,... | collective-permute-start | bytes 196616 | tf_op jit(solution)/shard_map/ppermute | solution.py:24
where the time goes:
time: 57.4 us; the launch traced here: 57.1 us
  Pallas kernels  19.1 us (33%)
  waiting for transfers between devices  16.4 us (29%)
  starting transfers between devices  10.8 us (19%)
  local copies, waits for them, and re-layouts  8.96 us (16%)
  other arithmetic  1.71 us (3%)
    ppermute x10, waiting for transfers between devices, swap(): return lax.ppermute(block, axis, [(i, i ^ distance) for i in range(size)])  16.4 us
    ppermute x10, starting transfers between devices, swap(): return lax.ppermute(block, axis, [(i, i ^ distance) for i in range(size)])  10.8 us
    unnamed x27, local copies, waits for them, and re-layouts  8.96 us
    pallas_call x1, Pallas kernels, ridge_reads(): pl.pallas_call(functools.partial(read_kernel, heads, len(sums)), in_specs...  7.84 us
    pallas_call x1, Pallas kernels, page_sums(): pl.pallas_call(functools.partial(gram_kernel, heads, owners), grid_spec=p...  5.41 us
    pallas_call x1, Pallas kernels, token_vectors(): pl.pallas_call(functools.partial(token_kernel, heads), grid_spec=pltpu.Pr...  4.07 us
    pallas_call x1, Pallas kernels, output_rows(): pl.pallas_call(output_kernel, in_specs=[pl.BlockSpec(memory_space=pltpu.S...  1.16 us
  transfers between devices with their start and end apart: 10, of which 5 were waited for; matrix products, arithmetic and copies ran while one was open for 0% of the time, Pallas kernels for 8%

commit v1 on v0

--- a/solution.py
+++ b/solution.py
@@ -15,6 +15,8 @@
 CHUNK = 128
 PAIR = 2 * CHUNK
 EPS_NORM = 1e-06
+PAGE_VMEM = 50
+TOKEN_VMEM = 48
 F32 = jnp.float32
 BF16 = jnp.bfloat16
 
@@ -37,13 +39,19 @@
 
 
 def block_diag(a):
-    first = lax.broadcasted_iota(jnp.int32, a.shape, 1) < CHUNK
-    zero = jnp.zeros_like(a)
-    return jnp.concatenate([jnp.where(first, a, zero), jnp.where(first, zero, a)], axis=0)
-
-
-def gram_kernel(heads, owners, code_ref, meta_ref, pick_ref, keys_ref, values_ref, prompt_ref,
-                send_ref, keep_ref, acc_ref):
+    zero = jnp.zeros((a.shape[0], CHUNK), a.dtype)
+    return jnp.concatenate(
+        [
+            jnp.concatenate([a[:, :CHUNK], zero], axis=1),
+            jnp.concatenate([zero, a[:, CHUNK:]], axis=1),
+        ],
+        axis=0,
+    )
+
+
+def sums_kernel(heads, owners, slots, cross, code_ref, meta_ref, *refs):
+    keys_ref, right_ref, prompt_ref = refs[0], refs[1 if cross else 0], refs[2 if cross else 1]
+    send_ref, keep_ref, acc_ref = refs[-3:]
     step = pl.program_id(0)
     pages, rows = keys_ref.shape[0], keys_ref.shape[1]
 
@@ -51,22 +59,17 @@
     def _():
         acc_ref[...] = jnp.zeros_like(acc_ref)
 
-    lane = lax.broadcasted_iota(jnp.int32, (HDIM, rows), 1)
+    lane = lax.broadcasted_iota(jnp.int32, (1, rows), 1)
     for page in range(pages):
         code = code_ref[step * pages + page]
-        owner, live = code // 256, code % 256
-        keys = keys_ref[page]
-        turned = keys.T
-        zero = jnp.zeros_like(turned)
-        left = jnp.concatenate(
-            [
-                jnp.where((lane % heads == head) & (lane < live * heads), turned, zero)
-                for head in range(heads)
-            ],
-            axis=0,
-        )
-        right = jnp.concatenate([keys, values_ref[page]], axis=1)
-        acc_ref[owner] += dot(left, right)
+        owner, slot = code // slots, code % slots
+        live = jnp.clip(meta_ref[3 + owners + owner] - slot * PAGE, 0, PAGE)
+        turned = keys_ref[page].T
+        left = []
+        for head in range(heads):
+            mask = (lane % heads == head) & (lane < live * heads)
+            left.append(turned * mask.astype(F32).astype(BF16))
+        acc_ref[owner] += dot(jnp.concatenate(left, axis=0), right_ref[page])
 
     @pl.when(step == pl.num_programs(0) - 1)
     def _():
@@ -76,12 +79,13 @@
         def add_prompt(owner, carry):
             for slot in range(stored):
 
-                @pl.when(pick_ref[owner] == mine * stored + slot)
+                @pl.when(meta_ref[3 + owner] == mine * stored + slot)
                 def _():
                     for head in range(heads):
-                        rows_here = slice(head * HDIM, (head + 1) * HDIM)
-                        acc_ref[owner, rows_here, :HDIM] += prompt_ref[slot, head, 0].T
-                        acc_ref[owner, rows_here, HDIM:] += prompt_ref[slot, head, 1].T
+                        block = prompt_ref[slot, head, 0]
+                        acc_ref[owner, head * HDIM : (head + 1) * HDIM, :] += (
+                            block.T if cross else block
+                        )
 
             return carry
 
@@ -91,35 +95,40 @@
             keep_ref[pair] = acc_ref[2 * pair + bit].astype(BF16)
 
 
-def page_sums(code, meta, group_prompt, keys, values, prompt_state, owners):
+def page_sums(code, meta, keys, values, prompt_state, owners, slots, after=()):
+    cross = values is not None
     pool, rows, _ = keys.shape
-    heads = prompt_state.shape[1]
+    stored, heads = prompt_state.shape[:2]
     pages = 8
-    half = (owners // 2, heads * HDIM, 2 * HDIM)
+    half = (owners // 2, heads * HDIM, HDIM)
     page_spec = pl.BlockSpec((pages, rows, HDIM), lambda i, *_: (i, 0, 0))
     out_spec = pl.BlockSpec(half, lambda i, *_: (0, 0, 0))
+    blocks = [keys, values] if cross else [keys]
+    touch = pl.BlockSpec((16, HDIM), lambda i, *_: (0, 0))
     return pl.pallas_call(
-        functools.partial(gram_kernel, heads, owners),
+        functools.partial(sums_kernel, heads, owners, slots, cross),
         grid_spec=pltpu.PrefetchScalarGridSpec(
-            num_scalar_prefetch=3,
+            num_scalar_prefetch=2,
             grid=(pool // pages,),
-            in_specs=[
-                page_spec,
-                page_spec,
-                pl.BlockSpec(prompt_state.shape, lambda i, *_: (0, 0, 0, 0, 0)),
-            ],
+            in_specs=[page_spec] * len(blocks)
+            + [
+                pl.BlockSpec(
+                    (stored, heads, 1, HDIM, HDIM), lambda i, *_: (0, 0, int(cross), 0, 0)
+                )
+            ]
+            + [touch] * len(after),
             out_specs=[out_spec, out_spec],
-            scratch_shapes=[pltpu.VMEM((owners, heads * HDIM, 2 * HDIM), F32)],
+            scratch_shapes=[pltpu.VMEM((owners, heads * HDIM, HDIM), F32)],
         ),
         out_shape=[jax.ShapeDtypeStruct(half, BF16)] * 2,
-        compiler_params=pltpu.CompilerParams(vmem_limit_bytes=32 * 2**20),
+        compiler_params=pltpu.CompilerParams(vmem_limit_bytes=PAGE_VMEM * 2**20),
         cost_estimate=pl.CostEstimate(
-            flops=2 * pool * rows * heads * HDIM * 2 * HDIM,
-            bytes_accessed=4 * pool * rows * HDIM,
+            flops=4 * pool * rows * heads * HDIM * HDIM,
+            bytes_accessed=2 * len(blocks) * pool * rows * HDIM,
             transcendentals=0,
         ),
-        name="page_sums",
-    )(code, meta, group_prompt, keys, values, prompt_state)
+        name="cross_sums" if cross else "gram_sums",
+    )(code, meta, *blocks, prompt_state, *after)
 
 
 def halve_kernel(meta_ref, keep_ref, got_ref, *outs):
@@ -150,7 +159,7 @@
     head_count = HEADS // heads
     blocks = refs[:head_count]
     (gain_ref, w_ref, wg_ref, taps_ref, state_ref) = refs[head_count : head_count + 5]
-    (q_ref, k_ref, kt_ref, vt_ref, weight_ref, prefix_ref, rows_ref) = refs[head_count + 5 : -2]
+    (q_ref, k_ref, kt_ref, vt_ref, weight_ref, prefix_ref, rows_ref) = refs[-9:-2]
     ext_ref, gate_ref = refs[-2:]
     me = place_ref[0]
     tok_rows = blocks[0].shape[0]
@@ -224,13 +233,17 @@
                 so_far = so_far + whole
 
 
-def token_vectors(place, decay_rate, blocks, norm_gain, w_qkv, w_gates, conv_weight, conv_state):
+def token_vectors(
+    place, decay_rate, blocks, norm_gain, w_qkv, w_gates, conv_weight, conv_state, after=()
+):
     head_count = len(blocks)
     heads = HEADS // head_count
     width = heads * 3 * HDIM
     tok_rows, model = blocks[0].shape
     length = head_count * tok_rows
     chunks = length // CHUNK
+
+    touch = pl.BlockSpec((16, HDIM), lambda i, *_: (0, 0))
 
     def full(shape):
         return pl.BlockSpec(shape, lambda i, *_: (0,) * len(shape))
@@ -256,37 +269,44 @@
                 full(w_gates.shape),
                 pl.BlockSpec((CONV, width), lambda i, place, rate: (0, place[0])),
                 pl.BlockSpec((1, CONV - 1, width), lambda i, place, rate: (0, 0, place[0])),
-            ],
+            ]
+            + [touch] * len(after),
             out_specs=[full(o.shape) for o in outs],
             scratch_shapes=[pltpu.VMEM((8 + length, width), F32), pltpu.VMEM((length, HDIM), F32)],
         ),
         out_shape=outs,
-        compiler_params=pltpu.CompilerParams(vmem_limit_bytes=40 * 2**20),
+        compiler_params=pltpu.CompilerParams(vmem_limit_bytes=TOKEN_VMEM * 2**20),
         cost_estimate=pl.CostEstimate(
             flops=2 * length * model * width,
             bytes_accessed=2 * model * (length + width) + 4 * 2**20,
             transcendentals=length * width,
         ),
         name="token_vectors",
-    )(place, decay_rate, *blocks, norm_gain.reshape(1, model), w_qkv, w_gates, conv_weight, conv_state)
-
-
-def read_kernel(heads, terms, place_ref, ridge_ref, *refs):
-    head_count = HEADS // heads
-    sums = refs[:terms]
+    )(
+        place,
+        decay_rate,
+        *blocks,
+        norm_gain.reshape(1, model),
+        w_qkv,
+        w_gates,
+        conv_weight,
+        conv_state,
+        *after,
+    )
+
+
+def read_kernel(heads, terms, ridge_ref, *refs):
+    grams = refs[:terms]
     (q_ref, k_ref, kt_ref, vt_ref, weight_ref, prefix_ref, rows_ref) = refs[terms : terms + 7]
-    outs = refs[terms + 7 : terms + 7 + head_count]
-    left_ref, cross_ref, x_ref, r_ref, d_ref, o_ref = refs[terms + 7 + head_count :]
-    me = place_ref[0]
+    base_ref, solved_ref, left_ref, x_ref, r_ref, d_ref = refs[-6:]
     pairs = q_ref.shape[2] // PAIR
     groups = [(head, pair) for head in range(heads) for pair in range(pairs)]
     norms = []
     for head in range(heads):
         rows = slice(head * HDIM, (head + 1) * HDIM)
-        total = sums[0][rows, :].astype(F32)
-        for term in sums[1:]:
-            total = total + term[rows, :].astype(F32)
-        gram, cross = total[:, :HDIM].T, total[:, HDIM:].T
+        gram = grams[0][rows, :].astype(F32)
+        for term in grams[1:]:
+            gram = gram + term[rows, :].astype(F32)
         for pair in range(pairs):
             for side in range(2):
                 c = 2 * pair + side
@@ -296,9 +316,6 @@
                     gram * scale + prefix_ref[head, c, :HDIM]
                 ).astype(BF16)
                 left_ref[head, pair, HDIM:, half] = k_ref[head, c * CHUNK : (c + 1) * CHUNK]
-                cross_ref[head, pair, :, half] = (
-                    cross * scale + prefix_ref[head, c, HDIM:]
-                ).astype(BF16)
             query = q_ref[head, :, pair * PAIR : (pair + 1) * PAIR].astype(F32)
             x_ref[head, pair] = jnp.zeros_like(query)
             r_ref[head, pair] = query
@@ -330,49 +347,78 @@
 
     lax.fori_loop(0, CG_STEPS, one_step, tuple(norms))
     for head, pair in groups:
-        left_ref[head, pair, :HDIM] = cross_ref[head, pair]
-        first = dot(left_ref[head, pair], block_diag(x_ref[head, pair].astype(BF16)))
+        cols = slice(head * HDIM, (head + 1) * HDIM)
+        span = slice(pair * PAIR, (pair + 1) * PAIR)
+        for side in range(2):
+            half = slice(side * CHUNK, (side + 1) * CHUNK)
+            left_ref[head, pair, :HDIM, half] = prefix_ref[head, 2 * pair + side, HDIM:].astype(BF16)
+        solved = x_ref[head, pair]
+        first = dot(left_ref[head, pair], block_diag(solved.astype(BF16)))
         scores = (first[HDIM:] * weight_ref[head, pair]).astype(BF16)
-        span = slice(pair * PAIR, (pair + 1) * PAIR)
-        read = rows_ref[head, pair, 0:1] * first[:HDIM] + dot(
-            vt_ref[head, :, span], block_diag(scores)
-        )
-        o_ref[span, head * HDIM : (head + 1) * HDIM] = read.T.astype(BF16)
+        carry = rows_ref[head, pair, 0:1]
+        read = carry * first[:HDIM] + dot(vt_ref[head, :, span], block_diag(scores))
+        base_ref[span, cols] = read.T
+        solved_ref[span, cols] = (solved * (carry * rows_ref[head, pair, 1:2])).T.astype(BF16)
+
+
+def ridge_reads(ridge, grams, vectors, after=()):
+    heads, _, length = vectors[0].shape
+    pairs = length // PAIR
+    whole = pl.BlockSpec(memory_space=pltpu.VMEM)
+    state = pltpu.VMEM((heads, pairs, HDIM, PAIR), F32)
+    return pl.pallas_call(
+        functools.partial(read_kernel, heads, len(grams)),
+        in_specs=[pl.BlockSpec(memory_space=pltpu.SMEM)]
+        + [whole] * (len(grams) + len(vectors))
+        + [whole] * len(after),
+        out_specs=[whole] * 2,
+        out_shape=[
+            jax.ShapeDtypeStruct((length, heads * HDIM), F32),
+            jax.ShapeDtypeStruct((length, heads * HDIM), BF16),
+        ],
+        scratch_shapes=[pltpu.VMEM((heads, pairs, 2 * HDIM, PAIR), BF16), state, state, state],
+        compiler_params=pltpu.CompilerParams(vmem_limit_bytes=32 * 2**20),
+        cost_estimate=pl.CostEstimate(
+            flops=CG_STEPS * heads * pairs * 6 * CHUNK**3 * 16,
+            bytes_accessed=8 * 2**20,
+            transcendentals=0,
+        ),
+        name="ridge_reads",
+    )(ridge, *grams, *vectors, *after)
+
+
+def cross_kernel(heads, terms, place_ref, *refs):
+    crosses, (base_ref, solved_ref) = refs[:terms], refs[terms : terms + 2]
+    outs, o_ref = refs[terms + 2 : -1], refs[-1]
+    me = place_ref[0]
+    for head in range(heads):
+        cols = slice(head * HDIM, (head + 1) * HDIM)
+        cross = crosses[0][cols, :].astype(F32)
+        for term in crosses[1:]:
+            cross = cross + term[cols, :].astype(F32)
+        read = base_ref[:, cols] + dot(solved_ref[:, cols], cross.astype(BF16))
+        o_ref[:, cols] = read.astype(BF16)
     tok_rows = outs[0].shape[0]
     for distance, out_ref in enumerate(outs):
         first_row = pl.multiple_of((me ^ distance) * tok_rows, tok_rows)
         out_ref[...] = o_ref[pl.ds(first_row, tok_rows), :]
 
 
-def ridge_reads(place, ridge, sums, vectors, head_count):
-    heads = HEADS // head_count
-    length = vectors[0].shape[2]
-    pairs = length // PAIR
-    tok_rows = length // head_count
+def cross_reads(place, crosses, base, solved, head_count):
+    length, width = base.shape
     whole = pl.BlockSpec(memory_space=pltpu.VMEM)
-    small = pl.BlockSpec(memory_space=pltpu.SMEM)
-    state = pltpu.VMEM((heads, pairs, HDIM, PAIR), F32)
     return pl.pallas_call(
-        functools.partial(read_kernel, heads, len(sums)),
-        in_specs=[small, small] + [whole] * (len(sums) + len(vectors)),
+        functools.partial(cross_kernel, width // HDIM, len(crosses)),
+        in_specs=[pl.BlockSpec(memory_space=pltpu.SMEM)] + [whole] * (len(crosses) + 2),
         out_specs=[whole] * head_count,
-        out_shape=[jax.ShapeDtypeStruct((tok_rows, heads * HDIM), BF16)] * head_count,
-        scratch_shapes=[
-            pltpu.VMEM((heads, pairs, 2 * HDIM, PAIR), BF16),
-            pltpu.VMEM((heads, pairs, HDIM, PAIR), BF16),
-            state,
-            state,
-            state,
-            pltpu.VMEM((length, heads * HDIM), BF16),
-        ],
-        compiler_params=pltpu.CompilerParams(vmem_limit_bytes=32 * 2**20),
+        out_shape=[jax.ShapeDtypeStruct((length // head_count, width), BF16)] * head_count,
+        scratch_shapes=[pltpu.VMEM((length, width), BF16)],
+        compiler_params=pltpu.CompilerParams(vmem_limit_bytes=24 * 2**20),
         cost_estimate=pl.CostEstimate(
-            flops=CG_STEPS * heads * pairs * 6 * CHUNK**3 * 4,
-            bytes_accessed=4 * 2**20,
-            transcendentals=0,
-        ),
-        name="ridge_reads",
-    )(place, ridge, *sums, *vectors)
+            flops=2 * length * width * HDIM, bytes_accessed=8 * length * width, transcendentals=0
+        ),
+        name="cross_reads",
+    )(place, *crosses, base, solved)
 
 
 def output_kernel(place_ref, tokens_ref, w_ref, *refs):
@@ -425,7 +471,9 @@
     me = lax.axis_index("head").astype(jnp.int32)
     group = lax.axis_index("grp").astype(jnp.int32)
     place = me.reshape(1)
-    meta = jnp.stack([group, group % 2, group // 2])
+    meta = jnp.concatenate(
+        [jnp.stack([group, group & 1, group >> 1]), group_prompt, cache_lengths]
+    )
 
     blocks = {0: tokens}
     bit = head_count // 2
@@ -436,29 +484,29 @@
     blocks = [blocks[i] for i in range(head_count)]
 
     pool, page, heads, _ = cache_keys.shape
+    slots = page_table.shape[1]
     ids = group * pool + jnp.arange(pool, dtype=jnp.int32)
-    slots = page_table.shape[1]
-    live = jnp.clip(cache_lengths[:, None] - jnp.arange(slots, dtype=jnp.int32) * PAGE, 0, PAGE)
-    tag = jnp.arange(owners, dtype=jnp.int32)[:, None] * 256 + live
+    tag = jnp.arange(owners * slots, dtype=jnp.int32).reshape(owners, slots, 1)
     code = jnp.sum(
-        jnp.where(page_table[:, :, None] == ids, tag[:, :, None], 0), axis=(0, 1), dtype=jnp.int32
-    )
-    send, keep = page_sums(
-        code,
-        meta,
-        group_prompt,
-        cache_keys.reshape(pool, page * heads, HDIM),
-        cache_values.reshape(pool, page * heads, HDIM),
-        prompt_state,
-        owners,
-    )
-    got = swap(send, "grp", 1)
+        jnp.where(page_table[:, :, None] == ids, tag, 0), axis=(0, 1), dtype=jnp.int32
+    )
+    keys = cache_keys.reshape(pool, page * heads, HDIM)
+    values = cache_values.reshape(pool, page * heads, HDIM)
+
+    def halved(parts):
+        return halve_sums(meta, parts[1], swap(parts[0], "grp", 1))
+
+    def scattered(parts):
+        return [parts[0]] + [swap(parts[i], "grp", 2 * i) for i in range(1, owners // 2)]
+
+    grams = halved(page_sums(code, meta, keys, None, prompt_state, owners, slots))
+    early = [blocks[head_count // 2], blocks[1]]
+    crosses = halved(page_sums(code, meta, keys, values, prompt_state, owners, slots, early))
     vectors = token_vectors(
-        place, decay_rate, blocks, norm_gain, w_qkv, w_gates, conv_weight, conv_state
-    )
-    sums = halve_sums(meta, keep, got)
-    sums = [sums[0]] + [swap(sums[i], "grp", 2 * i) for i in range(1, owners // 2)]
-    reads = ridge_reads(place, ridge, sums, vectors, head_count)
+        place, decay_rate, blocks, norm_gain, w_qkv, w_gates, conv_weight, conv_state, [grams[0]]
+    )
+    base, solved = ridge_reads(ridge, scattered(grams), vectors, [crosses[0]])
+    reads = cross_reads(place, scattered(crosses), base, solved, head_count)
     reads = [reads[0]] + [swap(reads[i], "head", i) for i in range(1, head_count)]
     return output_rows(place, tokens, w_out, reads)
 

time: 57.4 us -> 57.6 us (level)
  Pallas kernels: 19.1 us -> 31.9 us
  waiting for transfers between devices: 16.4 us -> 6.46 us
  local copies, waits for them, and re-layouts: 8.96 us -> 1.91 us
  starting transfers between devices: 10.8 us -> 15.8 us
  other arithmetic: 1.71 us -> 0.91 us
    pallas_call x2 -> x4, Pallas kernels: 13.2 us -> 24.1 us  [the longest x2 16.2 us: page_sums(): pl.pallas_call(functools.partial(sums_kernel, heads, owners, slots, cross...]
    ppermute x10 -> x14, waiting for transfers between devices: 16.4 us -> 6.46 us  [swap(): return lax.ppermute(block, axis, [(i, i ^ distance) for i in range(size)])]
    unnamed x27 -> x19, local copies, waits for them, and re-layouts: 8.96 us -> 1.16 us
    ppermute x10 -> x14, starting transfers between devices: 10.8 us -> 15.8 us  [swap(): return lax.ppermute(block, axis, [(i, i ^ distance) for i in range(size)])]
    pallas_call x1, Pallas kernels: 4.07 us -> 5.44 us  [token_vectors(): pl.pallas_call(functools.partial(token_kernel, heads), grid_spec=pltpu.Pr...]
    concatenate x0 -> x1, local copies, waits for them, and re-layouts: none -> 0.75 us  [shards(): jnp.concatenate([jnp.stack([group, group & 1, group >> 1]), group_prompt,...]
    add x1 -> x0, other arithmetic: 0.73 us -> none  [shards(): tag = jnp.arange(owners, dtype=jnp.int32)[:, None] * 256 + live]
    pallas_call x1 -> x2, Pallas kernels: 0.66 us -> 1.21 us  [halve_sums(): pl.pallas_call(halve_kernel, in_specs=[pl.BlockSpec(memory_space=pltpu.SM...]
  transfers between devices with their start and end apart: 10 -> 14, of which waited for: 5 -> 3; matrix products, arithmetic and copies ran while one was open for 0% -> 3% of each run, Pallas kernels for 8% -> 53%
where the time goes in v1:
time: 57.6 us; the launch traced here: 57.2 us
  Pallas kernels  31.9 us (55%)
  starting transfers between devices  15.8 us (27%)
  waiting for transfers between devices  6.46 us (11%)
  local copies, waits for them, and re-layouts  1.91 us (3%)
  other arithmetic  0.91 us (2%)
    pallas_call x2, Pallas kernels, page_sums(): pl.pallas_call(functools.partial(sums_kernel, heads, owners, slots, cross...  16.2 us
    ppermute x14, starting transfers between devices, swap(): return lax.ppermute(block, axis, [(i, i ^ distance) for i in range(size)])  15.8 us
    pallas_call x1, Pallas kernels, ridge_reads(): pl.pallas_call(functools.partial(read_kernel, heads, len(grams)), in_spec...  7.67 us
    ppermute x14, waiting for transfers between devices, swap(): return lax.ppermute(block, axis, [(i, i ^ distance) for i in range(size)])  6.46 us
    pallas_call x1, Pallas kernels, token_vectors(): pl.pallas_call(functools.partial(token_kernel, heads), grid_spec=pltpu.Pr...  5.44 us
    pallas_call x2, Pallas kernels, halve_sums(): pl.pallas_call(halve_kernel, in_specs=[pl.BlockSpec(memory_space=pltpu.SM...  1.21 us
    pallas_call x1, Pallas kernels, output_rows(): pl.pallas_call(output_kernel, in_specs=[pl.BlockSpec(memory_space=pltpu.S...  1.16 us
    unnamed x19, local copies, waits for them, and re-layouts  1.16 us
  transfers between devices with their start and end apart: 14, of which 3 were waited for; matrix products, arithmetic and copies ran while one was open for 3% of the time, Pallas kernels for 53%

profile of v1, /device:TPU:0, one launch (start us, length us, event | category | flops | bytes accessed | tf_op | source)
XLA Modules:
  0.0 57.2 jit_solution(9695458856671381819)
XLA Ops:
  0.0 2.9 %collective-permute-start = (bf16[128,1024]{1,0:T(8,128)(2,1)}, bf16[128,1024]{1,0:T(8,128)(2,1)S(1)}, u32[]{:S(2)}, u32[]{:S(2)}) collective-permute-start(bf16[128,1024]{1,0:T(8,128)(2,1)} %tokens_ref.1), channel_id=1, source_target_pairs={{0,2},{1,3},{2,0},{3,1},{4,6},{5,7},{6,4},{7,5},{8,10},{9,11},{10,... | collective-permute-start | bytes 786440 | tf_op jit(solution)/shard_map/ppermute | solution.py:26
  2.9 0.0 collective-permute-start.1
  3.0 0.8 %concatenate.3.meta_ref = s32[19]{0:T(128)S(1)} concatenate(s32[1]{0:T(128)} %bitcast.1, s32[1]{0:T(128)} %bitcast.2, s32[1]{0:T(128)} %bitcast.3, s32[8]{0:T(128)} %param.28, s32[8]{0:T(128)} %param.27), dimensions={0} | concatenate | bytes 152 | tf_op jit(solution)/shard_map/concatenate | solution.py:474
  3.7 0.9 %select_reduce_fusion.code_ref = s32[64]{0:T(128)S(1)} fusion(s32[8,64]{1,0:T(8,128)S(1)} %multiply_add_fusion, s32[64]{0:T(128)S(1)} %iota_add_fusion, s32[8,64]{1,0:T(8,128)} %param.26), kind=kLoop, calls=%fused_computation | loop fusion | flops 98240 | bytes 4608 | tf_op jit(solution)/shard_map/reduce_sum | solution.py:490
  4.6 0.0 copy-start.2
  4.6 0.9 %copy-done.2 = f32[1,2,2,128,128]{4,3,2,1,0:T(8,128)S(1)} copy-done((f32[1,2,2,128,128]{4,3,2,1,0:T(8,128)S(1)}, f32[1,2,2,128,128]{4,3,2,1,0:T(8,128)}, u32[]{:S(2)}) %copy-start.2) | copy-done | bytes 262168
  5.6 7.6 %gram_sums.1 = (bf16[4,256,128]{2,1,0:T(8,128)(2,1)S(1)}, bf16[4,256,128]{2,1,0:T(8,128)(2,1)S(1)}) custom-call(s32[64]{0:T(128)S(1)} %select_reduce_fusion.code_ref, s32[19]{0:T(128)S(1)} %concatenate.3.meta_ref, bf16[64,256,128]{2,1,0:T(8,128)(2,1)} %bitcast.8, f32[1,2,2,128,128]{4,3,2,1,0:T(8,128)S(1)} %copy-done.2), custom_call_target="tpu_custom_call" | custom-call | flops 2147483648 | bytes 4194304 | tf_op jit(solution)/shard_map/gram_sums/pallas_call | solution.py:108
  13.2 1.6 %collective-permute-start.6 = (bf16[4,256,128]{2,1,0:T(8,128)(2,1)S(1)}, bf16[4,256,128]{2,1,0:T(8,128)(2,1)S(1)}, u32[]{:S(2)}, u32[]{:S(2)}) collective-permute-start(bf16[4,256,128]{2,1,0:T(8,128)(2,1)S(1)} %get-tuple-element.37), channel_id=1, source_target_pairs={{0,4},{4,0},{8,12},{12,8},{16,20},{20,16},{24,28},{28,24},{1,5},{5... | collective-permute-start | bytes 786440 | tf_op jit(solution)/shard_map/ppermute | solution.py:26
  14.8 0.0 collective-permute-done.refs_3_.refs_2_
  14.8 0.0 collective-permute-done.1.refs_4_.refs_1_
  14.8 0.0 copy-start.8
  14.8 0.0 copy-start.1
  14.8 0.0 copy-start.3
  14.8 0.0 copy-start.4
  14.8 0.0 copy-start.5
  14.8 0.0 copy-start.6
  14.9 8.6 %cross_sums.1 = (bf16[4,256,128]{2,1,0:T(8,128)(2,1)S(1)}, bf16[4,256,128]{2,1,0:T(8,128)(2,1)S(1)}) custom-call(s32[64]{0:T(128)S(1)} %select_reduce_fusion.code_ref, s32[19]{0:T(128)S(1)} %concatenate.3.meta_ref, bf16[64,256,128]{2,1,0:T(8,128)(2,1)} %bitcast.9, bf16[64,256,128]{2,1,0:T(8,128)(2,1)} %bitcast.10, f32[1,2,2,128,128]{4,3,2,1,0:T(8,128)S(1)} %copy-done.2, ...), custom_call_target="tpu_custom_call" | custom-call | flops 2147483648 | bytes 8388608 | tf_op jit(solution)/shard_map/cross_sums/pallas_call | solution.py:108
  23.4 0.4 collective-permute-start.2
  23.8 0.0 collective-permute-start.10
  23.8 0.0 copy-done.8
  23.8 0.2 copy.17.refs_6_
  24.0 0.0 collective-permute-done.6.got_ref
  24.0 0.6 %halve_sums.3 = (f32[256,128]{1,0:T(8,128)S(1)}, bf16[256,128]{1,0:T(8,128)(2,1)S(1)}, bf16[256,128]{1,0:T(8,128)(2,1)S(1)}, bf16[256,128]{1,0:T(8,128)(2,1)S(1)}) custom-call(s32[19]{0:T(128)S(1)} %concatenate.3.meta_ref, bf16[4,256,128]{2,1,0:T(8,128)(2,1)S(1)} %get-tuple-element.36.keep_ref, bf16[4,256,128]{2,1,0:T(8,128)(2,1)S(1)} %collective-permute-done.6.got_ref), custom_call_target="tpu_custom_call" | custom-call | flops 131072 | bytes 786432 | tf_op jit(solution)/shard_map/halve_sums/pallas_call | solution.py:145
  24.6 0.0 copy-start.7
  24.6 1.7 %collective-permute-start.7 = (bf16[256,128]{1,0:T(8,128)(2,1)S(1)}, bf16[256,128]{1,0:T(8,128)(2,1)S(1)}, u32[]{:S(2)}, u32[]{:S(2)}) collective-permute-start(bf16[256,128]{1,0:T(8,128)(2,1)S(1)} %get-tuple-element.39), channel_id=1, source_target_pairs={{0,8},{4,12},{8,0},{12,4},{16,24},{20,28},{24,16},{28,20},{1,9},{5... | collective-permute-start | bytes 196616 | tf_op jit(solution)/shard_map/ppermute | solution.py:26
  26.3 2.6 %collective-permute-start.8 = (bf16[256,128]{1,0:T(8,128)(2,1)S(1)}, bf16[256,128]{1,0:T(8,128)(2,1)S(1)}, u32[]{:S(2)}, u32[]{:S(2)}) collective-permute-start(bf16[256,128]{1,0:T(8,128)(2,1)S(1)} %get-tuple-element.40), channel_id=1, source_target_pairs={{0,16},{4,20},{8,24},{12,28},{16,0},{20,4},{24,8},{28,12},{1,17},{... | collective-permute-start | bytes 196616 | tf_op jit(solution)/shard_map/ppermute | solution.py:26
  28.9 0.2 collective-permute-start.9
  29.1 2.8 %collective-permute-done.2.got_ref = bf16[4,256,128]{2,1,0:T(8,128)(2,1)S(1)} collective-permute-done((bf16[4,256,128]{2,1,0:T(8,128)(2,1)S(1)}, bf16[4,256,128]{2,1,0:T(8,128)(2,1)S(1)}, u32[]{:S(2)}, u32[]{:S(2)}) %collective-permute-start.2) | collective-permute-done | bytes 262176 | tf_op jit(solution)/shard_map/ppermute | solution.py:26
  31.9 0.6 %halve_sums.2 = (f32[256,128]{1,0:T(8,128)S(1)}, bf16[256,128]{1,0:T(8,128)(2,1)S(1)}, bf16[256,128]{1,0:T(8,128)(2,1)S(1)}, bf16[256,128]{1,0:T(8,128)(2,1)S(1)}) custom-call(s32[19]{0:T(128)S(1)} %concatenate.3.meta_ref, bf16[4,256,128]{2,1,0:T(8,128)(2,1)S(1)} %get-tuple-element.30.keep_ref, bf16[4,256,128]{2,1,0:T(8,128)(2,1)S(1)} %collective-permute-done.2.got_ref), custom_call_target="tpu_custom_call" | custom-call | flops 131072 | bytes 786432 | tf_op jit(solution)/shard_map/halve_sums/pallas_call | solution.py:145
  32.5 1.6 %collective-permute-start.3 = (bf16[256,128]{1,0:T(8,128)(2,1)S(1)}, bf16[256,128]{1,0:T(8,128)(2,1)S(1)}, u32[]{:S(2)}, u32[]{:S(2)}) collective-permute-start(bf16[256,128]{1,0:T(8,128)(2,1)S(1)} %get-tuple-element.33), channel_id=1, source_target_pairs={{0,8},{4,12},{8,0},{12,4},{16,24},{20,28},{24,16},{28,20},{1,9},{5... | collective-permute-start | bytes 196616 | tf_op jit(solution)/shard_map/ppermute | solution.py:26
  34.2 0.0 collective-permute-done.10.refs_3_
  34.2 2.6 %collective-permute-start.4 = (bf16[256,128]{1,0:T(8,128)(2,1)S(1)}, bf16[256,128]{1,0:T(8,128)(2,1)S(1)}, u32[]{:S(2)}, u32[]{:S(2)}) collective-permute-start(bf16[256,128]{1,0:T(8,128)(2,1)S(1)} %get-tuple-element.34), channel_id=1, source_target_pairs={{0,16},{4,20},{8,24},{12,28},{16,0},{20,4},{24,8},{28,12},{1,17},{... | collective-permute-start | bytes 196616 | tf_op jit(solution)/shard_map/ppermute | solution.py:26
  36.8 0.0 copy-done.1
  36.8 0.0 copy-done.3
  36.8 0.0 copy-done.4
  36.8 0.0 copy-done.5
  36.8 0.0 copy-done.6
  36.8 5.4 %token_vectors.1 = (bf16[2,128,512]{2,1,0:T(8,128)(2,1)S(1)}, bf16[2,512,128]{2,1,0:T(8,128)(2,1)S(1)}, bf16[2,128,512]{2,1,0:T(8,128)(2,1)S(1)}, bf16[2,128,512...) custom-call(s32[1]{0:T(128)} %bitcast.place_ref, ...), custom_call_target="tpu_custom_call" | custom-call | flops 805306368 | bytes 6815744 | tf_op jit(solution)/shard_map/token_vectors/pallas_call | solution.py:260
  42.2 0.0 collective-permute-done.7.refs_1_
  42.2 0.3 collective-permute-start.5
  42.5 0.0 collective-permute-done.8.refs_2_
  42.5 0.0 collective-permute-done.9.refs_3_
  42.5 0.0 copy-done.7
  42.5 0.0 copy-start
  42.5 7.7 %ridge_reads.1 = (f32[512,256]{1,0:T(8,128)S(1)}, bf16[512,256]{1,0:T(8,128)(2,1)S(1)}) custom-call(f32[2]{0:T(128)S(1)} %copy-done.7, f32[256,128]{1,0:T(8,128)S(1)} %get-tuple-element.38.refs_9_.refs_0_, bf16[256,128]{1,0:T(8,128)(2,1)S(1)} %collective-permute-done.7.refs_1_, bf16[256,128]{1,0:T(8,128)(2,1)S(1)} %collective-permute-done.8.refs_2_, ...), custom_call_target="tpu_custom_call" | custom-call | flops 6442450944 | bytes 8388608 | tf_op jit(solution)/shard_map/ridge_reads/pallas_call | solution.py:369
  50.2 0.0 collective-permute-done.3.refs_1_
  50.2 0.0 collective-permute-done.4.refs_2_
  50.2 0.0 collective-permute-done.5.refs_3_
  50.2 0.3 cross_reads.1
  50.5 0.1 collective-permute-start.11
  50.6 0.6 %collective-permute-start.12 = (bf16[128,256]{1,0:T(8,128)(2,1)S(1)}, bf16[128,256]{1,0:T(8,128)(2,1)S(1)}, u32[]{:S(2)}, u32[]{:S(2)}) collective-permute-start(bf16[128,256]{1,0:T(8,128)(2,1)S(1)} %get-tuple-element.53), channel_id=1, source_target_pairs={{0,2},{1,3},{2,0},{3,1},{4,6},{5,7},{6,4},{7,5},{8,10},{9,11},{10,... | collective-permute-start | bytes 196616 | tf_op jit(solution)/shard_map/ppermute | solution.py:26
  51.2 1.3 %collective-permute-start.13 = (bf16[128,256]{1,0:T(8,128)(2,1)S(1)}, bf16[128,256]{1,0:T(8,128)(2,1)S(1)}, u32[]{:S(2)}, u32[]{:S(2)}) collective-permute-start(bf16[128,256]{1,0:T(8,128)(2,1)S(1)} %get-tuple-element.54), channel_id=1, source_target_pairs={{0,3},{1,2},{2,1},{3,0},{4,7},{5,6},{6,5},{7,4},{8,11},{9,10},{10,... | collective-permute-start | bytes 196616 | tf_op jit(solution)/shard_map/ppermute | solution.py:26
  52.4 0.0 collective-permute-done.11.refs_1_
  52.4 3.1 %collective-permute-done.12.refs_2_ = bf16[128,256]{1,0:T(8,128)(2,1)S(1)} collective-permute-done((bf16[128,256]{1,0:T(8,128)(2,1)S(1)}, bf16[128,256]{1,0:T(8,128)(2,1)S(1)}, u32[]{:S(2)}, u32[]{:S(2)}) %collective-permute-start.12) | collective-permute-done | bytes 65568 | tf_op jit(solution)/shard_map/ppermute | solution.py:26
  55.5 0.5 collective-permute-done.13.refs_3_
  56.0 0.0 copy-done
  56.0 1.2 %output_rows.1 = bf16[128,1024]{1,0:T(8,128)(2,1)} custom-call(s32[1]{0:T(128)} %bitcast.place_ref, bf16[128,1024]{1,0:T(8,128)(2,1)S(1)} %copy-done.1, bf16[1024,1024]{1,0:T(8,128)(2,1)S(1)} %copy-done, bf16[128,256]{1,0:T(8,128)(2,1)S(1)} %get-tuple-element.51.refs_0_, bf16[128,256]{1,0:T(8,128)(2,1)S(1)} %collective-permute-done.11.refs_1_, ...), custom_call_target="tpu_custom_call" | custom-call | flops 268435456 | bytes 2883584 | tf_op jit(solution)/shard_map/output_rows/pallas_call | solution.py:437
  (2 shorter events, 0.0 us)
Async XLA Ops:
  0.0 14.8 %collective-permute-start = (bf16[128,1024]{1,0:T(8,128)(2,1)}, bf16[128,1024]{1,0:T(8,128)(2,1)S(1)}, u32[]{:S(2)}, u32[]{:S(2)}) collective-permute-start(bf16[128,1024]{1,0:T(8,128)(2,1)} %tokens_ref.1), channel_id=1, source_target_pairs={{0,2},{1,3},{2,0},{3,1},{4,6},{5,7},{6,4},{7,5},{8,10},{9,11},{10,... | collective-permute-start | bytes 786440 | tf_op jit(solution)/shard_map/ppermute | solution.py:26
  2.9 11.8 %collective-permute-start.1 = (bf16[128,1024]{1,0:T(8,128)(2,1)}, bf16[128,1024]{1,0:T(8,128)(2,1)S(1)}, u32[]{:S(2)}, u32[]{:S(2)}) collective-permute-start(bf16[128,1024]{1,0:T(8,128)(2,1)} %tokens_ref.1), channel_id=1, source_target_pairs={{0,1},{1,0},{2,3},{3,2},{4,5},{5,4},{6,7},{7,6},{8,9},{9,8},{10,11... | collective-permute-start | bytes 786440 | tf_op jit(solution)/shard_map/ppermute | solution.py:26
  4.6 1.0 %copy-start.2 = (f32[1,2,2,128,128]{4,3,2,1,0:T(8,128)S(1)}, f32[1,2,2,128,128]{4,3,2,1,0:T(8,128)}, u32[]{:S(2)}) copy-start(f32[1,2,2,128,128]{4,3,2,1,0:T(8,128)} %refs_1_.1) | copy-start | bytes 786436
  13.2 10.8 %collective-permute-start.6 = (bf16[4,256,128]{2,1,0:T(8,128)(2,1)S(1)}, bf16[4,256,128]{2,1,0:T(8,128)(2,1)S(1)}, u32[]{:S(2)}, u32[]{:S(2)}) collective-permute-start(bf16[4,256,128]{2,1,0:T(8,128)(2,1)S(1)} %get-tuple-element.37), channel_id=1, source_target_pairs={{0,4},{4,0},{8,12},{12,8},{16,20},{20,16},{24,28},{28,24},{1,5},{5... | collective-permute-start | bytes 786440 | tf_op jit(solution)/shard_map/ppermute | solution.py:26
  14.8 9.0 %copy-start.8 = (bf16[1024,16]{0,1:T(8,128)(2,1)S(1)}, bf16[1024,16]{0,1:T(8,128)(2,1)}, u32[]{:S(2)}) copy-start(bf16[1024,16]{0,1:T(8,128)(2,1)} %param.18) | copy-start | bytes 98308
  14.8 22.0 %copy-start.1 = (bf16[128,1024]{1,0:T(8,128)(2,1)S(1)}, bf16[128,1024]{1,0:T(8,128)(2,1)}, u32[]{:S(2)}) copy-start(bf16[128,1024]{1,0:T(8,128)(2,1)} %tokens_ref.1) | copy-start | bytes 786436
  14.8 22.0 %copy-start.3 = (f32[4,3072]{1,0:T(4,128)S(1)}, f32[4,3072]{1,0:T(4,128)}, u32[]{:S(2)}) copy-start(f32[4,3072]{1,0:T(4,128)} %refs_7_.1) | copy-start | bytes 147460
  14.8 21.9 %copy-start.4 = (bf16[1,3,3072]{2,1,0:T(4,128)(2,1)S(1)}, bf16[1,3,3072]{2,1,0:T(4,128)(2,1)}, u32[]{:S(2)}) copy-start(bf16[1,3,3072]{2,1,0:T(4,128)(2,1)} %refs_8_.1) | copy-start | bytes 55300
  14.8 21.9 %copy-start.5 = (f32[1024]{0:T(1024)S(1)}, f32[1024]{0:T(1024)}, u32[]{:S(2)}) copy-start(f32[1024]{0:T(1024)} %param.16) | copy-start | bytes 12292
  14.8 21.9 %copy-start.6 = (f32[8]{0:T(128)S(1)}, f32[8]{0:T(128)}, u32[]{:S(2)}) copy-start(f32[8]{0:T(128)} %rate_ref.1) | copy-start | bytes 100
  23.4 8.5 %collective-permute-start.2 = (bf16[4,256,128]{2,1,0:T(8,128)(2,1)S(1)}, bf16[4,256,128]{2,1,0:T(8,128)(2,1)S(1)}, u32[]{:S(2)}, u32[]{:S(2)}) collective-permute-start(bf16[4,256,128]{2,1,0:T(8,128)(2,1)S(1)} %get-tuple-element.31), channel_id=1, source_target_pairs={{0,4},{4,0},{8,12},{12,8},{16,20},{20,16},{24,28},{28,24},{1,5},{5... | collective-permute-start | bytes 786440 | tf_op jit(solution)/shard_map/ppermute | solution.py:26
  23.8 10.4 %collective-permute-start.10 = (bf16[128,1024]{1,0:T(8,128)(2,1)S(1)}, bf16[128,1024]{1,0:T(8,128)(2,1)S(1)}, u32[]{:S(2)}, u32[]{:S(2)}) collective-permute-start(bf16[128,1024]{1,0:T(8,128)(2,1)S(1)} %collective-permute-done.refs_3_.refs_2_), channel_id=1, source_target_pairs={{0,1},{1,0},{2,3},{3,2},{4,5},{5,4},{6,7},{7,6},{8,9},{9,8},{10,11... | collective-permute-start | bytes 786440 | tf_op jit(solution)/shard_map/ppermute | solution.py:26
  24.6 17.9 %copy-start.7 = (f32[2]{0:T(128)S(1)}, f32[2]{0:T(128)}, u32[]{:S(2)}) copy-start(f32[2]{0:T(128)} %ridge_ref.1) | copy-start | bytes 28
  24.6 17.6 %collective-permute-start.7 = (bf16[256,128]{1,0:T(8,128)(2,1)S(1)}, bf16[256,128]{1,0:T(8,128)(2,1)S(1)}, u32[]{:S(2)}, u32[]{:S(2)}) collective-permute-start(bf16[256,128]{1,0:T(8,128)(2,1)S(1)} %get-tuple-element.39), channel_id=1, source_target_pairs={{0,8},{4,12},{8,0},{12,4},{16,24},{20,28},{24,16},{28,20},{1,9},{5... | collective-permute-start | bytes 196616 | tf_op jit(solution)/shard_map/ppermute | solution.py:26
  26.3 16.2 %collective-permute-start.8 = (bf16[256,128]{1,0:T(8,128)(2,1)S(1)}, bf16[256,128]{1,0:T(8,128)(2,1)S(1)}, u32[]{:S(2)}, u32[]{:S(2)}) collective-permute-start(bf16[256,128]{1,0:T(8,128)(2,1)S(1)} %get-tuple-element.40), channel_id=1, source_target_pairs={{0,16},{4,20},{8,24},{12,28},{16,0},{20,4},{24,8},{28,12},{1,17},{... | collective-permute-start | bytes 196616 | tf_op jit(solution)/shard_map/ppermute | solution.py:26
  28.9 13.6 %collective-permute-start.9 = (bf16[256,128]{1,0:T(8,128)(2,1)S(1)}, bf16[256,128]{1,0:T(8,128)(2,1)S(1)}, u32[]{:S(2)}, u32[]{:S(2)}) collective-permute-start(bf16[256,128]{1,0:T(8,128)(2,1)S(1)} %get-tuple-element.41), channel_id=1, source_target_pairs={{0,24},{4,28},{8,16},{12,20},{16,8},{20,12},{24,0},{28,4},{1,25},{... | collective-permute-start | bytes 196616 | tf_op jit(solution)/shard_map/ppermute | solution.py:26
  32.5 17.7 %collective-permute-start.3 = (bf16[256,128]{1,0:T(8,128)(2,1)S(1)}, bf16[256,128]{1,0:T(8,128)(2,1)S(1)}, u32[]{:S(2)}, u32[]{:S(2)}) collective-permute-start(bf16[256,128]{1,0:T(8,128)(2,1)S(1)} %get-tuple-element.33), channel_id=1, source_target_pairs={{0,8},{4,12},{8,0},{12,4},{16,24},{20,28},{24,16},{28,20},{1,9},{5... | collective-permute-start | bytes 196616 | tf_op jit(solution)/shard_map/ppermute | solution.py:26
  34.2 16.0 %collective-permute-start.4 = (bf16[256,128]{1,0:T(8,128)(2,1)S(1)}, bf16[256,128]{1,0:T(8,128)(2,1)S(1)}, u32[]{:S(2)}, u32[]{:S(2)}) collective-permute-start(bf16[256,128]{1,0:T(8,128)(2,1)S(1)} %get-tuple-element.34), channel_id=1, source_target_pairs={{0,16},{4,20},{8,24},{12,28},{16,0},{20,4},{24,8},{28,12},{1,17},{... | collective-permute-start | bytes 196616 | tf_op jit(solution)/shard_map/ppermute | solution.py:26
  42.2 8.0 %collective-permute-start.5 = (bf16[256,128]{1,0:T(8,128)(2,1)S(1)}, bf16[256,128]{1,0:T(8,128)(2,1)S(1)}, u32[]{:S(2)}, u32[]{:S(2)}) collective-permute-start(bf16[256,128]{1,0:T(8,128)(2,1)S(1)} %get-tuple-element.35), channel_id=1, source_target_pairs={{0,24},{4,28},{8,16},{12,20},{16,8},{20,12},{24,0},{28,4},{1,25},{... | collective-permute-start | bytes 196616 | tf_op jit(solution)/shard_map/ppermute | solution.py:26
  42.5 13.5 %copy-start = (bf16[1024,1024]{1,0:T(8,128)(2,1)S(1)}, bf16[1024,1024]{1,0:T(8,128)(2,1)}, u32[]{:S(2)}) copy-start(bf16[1024,1024]{1,0:T(8,128)(2,1)} %w_ref.1) | copy-start | bytes 6291460
  50.5 1.9 %collective-permute-start.11 = (bf16[128,256]{1,0:T(8,128)(2,1)S(1)}, bf16[128,256]{1,0:T(8,128)(2,1)S(1)}, u32[]{:S(2)}, u32[]{:S(2)}) collective-permute-start(bf16[128,256]{1,0:T(8,128)(2,1)S(1)} %get-tuple-element.52), channel_id=1, source_target_pairs={{0,1},{1,0},{2,3},{3,2},{4,5},{5,4},{6,7},{7,6},{8,9},{9,8},{10,11... | collective-permute-start | bytes 196616 | tf_op jit(solution)/shard_map/ppermute | solution.py:26
  50.6 5.0 %collective-permute-start.12 = (bf16[128,256]{1,0:T(8,128)(2,1)S(1)}, bf16[128,256]{1,0:T(8,128)(2,1)S(1)}, u32[]{:S(2)}, u32[]{:S(2)}) collective-permute-start(bf16[128,256]{1,0:T(8,128)(2,1)S(1)} %get-tuple-element.53), channel_id=1, source_target_pairs={{0,2},{1,3},{2,0},{3,1},{4,6},{5,7},{6,4},{7,5},{8,10},{9,11},{10,... | collective-permute-start | bytes 196616 | tf_op jit(solution)/shard_map/ppermute | solution.py:26
  51.2 4.9 %collective-permute-start.13 = (bf16[128,256]{1,0:T(8,128)(2,1)S(1)}, bf16[128,256]{1,0:T(8,128)(2,1)S(1)}, u32[]{:S(2)}, u32[]{:S(2)}) collective-permute-start(bf16[128,256]{1,0:T(8,128)(2,1)S(1)} %get-tuple-element.54), channel_id=1, source_target_pairs={{0,3},{1,2},{2,1},{3,0},{4,7},{5,6},{6,5},{7,4},{8,11},{9,10},{10,... | collective-permute-start | bytes 196616 | tf_op jit(solution)/shard_map/ppermute | solution.py:26

commit v2 on v1

--- a/solution.py
+++ b/solution.py
@@ -15,7 +15,7 @@
 CHUNK = 128
 PAIR = 2 * CHUNK
 EPS_NORM = 1e-06
-PAGE_VMEM = 50
+PAGE_VMEM = 53
 TOKEN_VMEM = 48
 F32 = jnp.float32
 BF16 = jnp.bfloat16
@@ -24,6 +24,18 @@
 def swap(block, axis, distance):
     size = lax.axis_size(axis)
     return lax.ppermute(block, axis, [(i, i ^ distance) for i in range(size)])
+
+
+def hold(block, other):
+    anywhere = pl.BlockSpec(memory_space=pl.ANY)
+    return pl.pallas_call(
+        lambda *refs: None,
+        in_specs=[anywhere, anywhere],
+        out_specs=anywhere,
+        out_shape=jax.ShapeDtypeStruct(block.shape, block.dtype),
+        input_output_aliases={0: 0},
+        name="hold",
+    )(block, other)
 
 
 def dot(a, b):
@@ -49,91 +61,114 @@
     )
 
 
-def sums_kernel(heads, owners, slots, cross, code_ref, meta_ref, *refs):
-    keys_ref, right_ref, prompt_ref = refs[0], refs[1 if cross else 0], refs[2 if cross else 1]
-    send_ref, keep_ref, acc_ref = refs[-3:]
+def sums_kernel(heads, owners, slots, code_ref, meta_ref, keys_ref, values_ref, prompt_ref,
+                send_gram, send_cross, keep_gram, keep_cross, acc_ref, parity_ref, stored_ref, sem):
     step = pl.program_id(0)
     pages, rows = keys_ref.shape[0], keys_ref.shape[1]
+    load_prompt = pltpu.make_async_copy(prompt_ref, stored_ref, sem)
+    lane = lax.broadcasted_iota(jnp.int32, (HDIM, rows), 1)
 
     @pl.when(step == 0)
     def _():
+        load_prompt.start()
         acc_ref[...] = jnp.zeros_like(acc_ref)
-
-    lane = lax.broadcasted_iota(jnp.int32, (1, rows), 1)
-    for page in range(pages):
+        for head in range(heads):
+            parity_ref[head] = (lane % heads == head).astype(F32).astype(BF16)
+
+    def place(page):
         code = code_ref[step * pages + page]
         owner, slot = code // slots, code % slots
-        live = jnp.clip(meta_ref[3 + owners + owner] - slot * PAGE, 0, PAGE)
-        turned = keys_ref[page].T
-        left = []
-        for head in range(heads):
-            mask = (lane % heads == head) & (lane < live * heads)
-            left.append(turned * mask.astype(F32).astype(BF16))
-        acc_ref[owner] += dot(jnp.concatenate(left, axis=0), right_ref[page])
+        return owner, jnp.clip(meta_ref[owners + owner] - slot * PAGE, 0, PAGE)
+
+    def add(page, owner, turned):
+        left = turned
+        if heads > 1:
+            left = jnp.concatenate([turned * parity_ref[head] for head in range(heads)], axis=0)
+        right = jnp.concatenate([keys_ref[page], values_ref[page]], axis=1)
+        acc_ref[owner] += dot(left, right)
+
+    partial = jnp.int32(0)
+    for page in range(pages):
+        owner, live = place(page)
+        add(page, jnp.where(live == PAGE, owner, owners), keys_ref[page].T)
+        partial = partial | ((live > 0) & (live < PAGE)).astype(jnp.int32)
+
+    @pl.when(partial > 0)
+    def _():
+        def one_page(page, carry):
+            owner, live = place(page)
+
+            @pl.when((live > 0) & (live < PAGE))
+            def _():
+                turned = keys_ref[page].T
+                add(page, owner, jnp.where(lane < live * heads, turned, jnp.zeros_like(turned)))
+
+            return carry
+
+        lax.fori_loop(0, pages, one_page, 0)
 
     @pl.when(step == pl.num_programs(0) - 1)
     def _():
-        mine, bit = meta_ref[0], meta_ref[1]
-        stored = prompt_ref.shape[0]
+        load_prompt.wait()
+        mine, bit = meta_ref[2 * owners], meta_ref[2 * owners + 1]
+        stored = stored_ref.shape[0]
 
         def add_prompt(owner, carry):
             for slot in range(stored):
 
-                @pl.when(meta_ref[3 + owner] == mine * stored + slot)
+                @pl.when(meta_ref[owner] == mine * stored + slot)
                 def _():
                     for head in range(heads):
-                        block = prompt_ref[slot, head, 0]
-                        acc_ref[owner, head * HDIM : (head + 1) * HDIM, :] += (
-                            block.T if cross else block
-                        )
+                        at = slice(head * HDIM, (head + 1) * HDIM)
+                        acc_ref[owner, at, :HDIM] += stored_ref[slot, head, 0]
+                        acc_ref[owner, at, HDIM:] += stored_ref[slot, head, 1].T
 
             return carry
 
         lax.fori_loop(0, owners, add_prompt, 0)
         for pair in range(owners // 2):
-            send_ref[pair] = acc_ref[2 * pair + 1 - bit].astype(BF16)
-            keep_ref[pair] = acc_ref[2 * pair + bit].astype(BF16)
-
-
-def page_sums(code, meta, keys, values, prompt_state, owners, slots, after=()):
-    cross = values is not None
+            there, here = 2 * pair + 1 - bit, 2 * pair + bit
+            send_gram[pair] = acc_ref[there, :, :HDIM].astype(BF16)
+            send_cross[pair] = acc_ref[there, :, HDIM:].astype(BF16)
+            keep_gram[pair] = acc_ref[here, :, :HDIM].astype(BF16)
+            keep_cross[pair] = acc_ref[here, :, HDIM:].astype(BF16)
+
+
+def page_sums(code, meta, keys, values, prompt_state, owners, slots):
     pool, rows, _ = keys.shape
-    stored, heads = prompt_state.shape[:2]
+    heads = prompt_state.shape[1]
     pages = 8
     half = (owners // 2, heads * HDIM, HDIM)
     page_spec = pl.BlockSpec((pages, rows, HDIM), lambda i, *_: (i, 0, 0))
     out_spec = pl.BlockSpec(half, lambda i, *_: (0, 0, 0))
-    blocks = [keys, values] if cross else [keys]
-    touch = pl.BlockSpec((16, HDIM), lambda i, *_: (0, 0))
-    return pl.pallas_call(
-        functools.partial(sums_kernel, heads, owners, slots, cross),
+    return pl.pallas_call(
+        functools.partial(sums_kernel, heads, owners, slots),
         grid_spec=pltpu.PrefetchScalarGridSpec(
             num_scalar_prefetch=2,
             grid=(pool // pages,),
-            in_specs=[page_spec] * len(blocks)
-            + [
-                pl.BlockSpec(
-                    (stored, heads, 1, HDIM, HDIM), lambda i, *_: (0, 0, int(cross), 0, 0)
-                )
-            ]
-            + [touch] * len(after),
-            out_specs=[out_spec, out_spec],
-            scratch_shapes=[pltpu.VMEM((owners, heads * HDIM, HDIM), F32)],
-        ),
-        out_shape=[jax.ShapeDtypeStruct(half, BF16)] * 2,
+            in_specs=[page_spec, page_spec, pl.BlockSpec(memory_space=pl.ANY)],
+            out_specs=[out_spec] * 4,
+            scratch_shapes=[
+                pltpu.VMEM((owners + 1, heads * HDIM, 2 * HDIM), F32),
+                pltpu.VMEM((heads, HDIM, rows), BF16),
+                pltpu.VMEM(prompt_state.shape, F32),
+                pltpu.SemaphoreType.DMA,
+            ],
+        ),
+        out_shape=[jax.ShapeDtypeStruct(half, BF16)] * 4,
         compiler_params=pltpu.CompilerParams(vmem_limit_bytes=PAGE_VMEM * 2**20),
         cost_estimate=pl.CostEstimate(
-            flops=4 * pool * rows * heads * HDIM * HDIM,
-            bytes_accessed=2 * len(blocks) * pool * rows * HDIM,
+            flops=8 * pool * rows * heads * HDIM * HDIM,
+            bytes_accessed=4 * pool * rows * HDIM,
             transcendentals=0,
         ),
-        name="cross_sums" if cross else "gram_sums",
-    )(code, meta, *blocks, prompt_state, *after)
-
-
-def halve_kernel(meta_ref, keep_ref, got_ref, *outs):
+        name="page_sums",
+    )(code, meta, keys, values, prompt_state)
+
+
+def halve_kernel(owners, meta_ref, keep_ref, got_ref, *outs):
     for distance, out_ref in enumerate(outs):
-        row = meta_ref[2] ^ distance
+        row = meta_ref[2 * owners + 2] ^ distance
         total = keep_ref[row].astype(F32) + got_ref[row].astype(F32)
         out_ref[...] = total.astype(out_ref.dtype)
 
@@ -143,7 +178,7 @@
     outs = [jax.ShapeDtypeStruct((rows, cols), F32 if i == 0 else BF16) for i in range(count)]
     whole = pl.BlockSpec(memory_space=pltpu.VMEM)
     return pl.pallas_call(
-        halve_kernel,
+        functools.partial(halve_kernel, 2 * count),
         in_specs=[pl.BlockSpec(memory_space=pltpu.SMEM), whole, whole],
         out_specs=[whole] * count,
         out_shape=outs,
@@ -234,7 +269,7 @@
 
 
 def token_vectors(
-    place, decay_rate, blocks, norm_gain, w_qkv, w_gates, conv_weight, conv_state, after=()
+    place, decay_rate, blocks, norm_gain, w_qkv, w_gates, conv_weight, conv_state, held
 ):
     head_count = len(blocks)
     heads = HEADS // head_count
@@ -243,7 +278,7 @@
     length = head_count * tok_rows
     chunks = length // CHUNK
 
-    touch = pl.BlockSpec((16, HDIM), lambda i, *_: (0, 0))
+    anywhere = pl.BlockSpec(memory_space=pl.ANY)
 
     def full(shape):
         return pl.BlockSpec(shape, lambda i, *_: (0,) * len(shape))
@@ -270,11 +305,12 @@
                 pl.BlockSpec((CONV, width), lambda i, place, rate: (0, place[0])),
                 pl.BlockSpec((1, CONV - 1, width), lambda i, place, rate: (0, 0, place[0])),
             ]
-            + [touch] * len(after),
-            out_specs=[full(o.shape) for o in outs],
+            + [anywhere],
+            out_specs=[anywhere] + [full(o.shape) for o in outs],
             scratch_shapes=[pltpu.VMEM((8 + length, width), F32), pltpu.VMEM((length, HDIM), F32)],
         ),
-        out_shape=outs,
+        out_shape=[jax.ShapeDtypeStruct(held.shape, held.dtype)] + outs,
+        input_output_aliases={2 + len(blocks) + 5: 0},
         compiler_params=pltpu.CompilerParams(vmem_limit_bytes=TOKEN_VMEM * 2**20),
         cost_estimate=pl.CostEstimate(
             flops=2 * length * model * width,
@@ -291,7 +327,7 @@
         w_gates,
         conv_weight,
         conv_state,
-        *after,
+        held,
     )
 
 
@@ -471,17 +507,18 @@
     me = lax.axis_index("head").astype(jnp.int32)
     group = lax.axis_index("grp").astype(jnp.int32)
     place = me.reshape(1)
-    meta = jnp.concatenate(
-        [jnp.stack([group, group & 1, group >> 1]), group_prompt, cache_lengths]
-    )
-
+    extra = jnp.arange(3, dtype=jnp.int32)
+    own = jnp.where(extra == 0, group, jnp.where(extra == 1, group & 1, group >> 1))
+    meta = (
+        jnp.pad(group_prompt, (0, owners + 3))
+        + jnp.pad(cache_lengths, (owners, 3))
+        + jnp.pad(own, (2 * owners, 0))
+    )
+
+    bits = [head_count >> i for i in range(1, head_count.bit_length())]
     blocks = {0: tokens}
-    bit = head_count // 2
-    while bit:
-        for held in list(blocks):
-            blocks[held ^ bit] = swap(blocks[held], "head", bit)
-        bit //= 2
-    blocks = [blocks[i] for i in range(head_count)]
+    for bit in bits:
+        blocks[bit] = swap(tokens, "head", bit)
 
     pool, page, heads, _ = cache_keys.shape
     slots = page_table.shape[1]
@@ -493,18 +530,24 @@
     keys = cache_keys.reshape(pool, page * heads, HDIM)
     values = cache_values.reshape(pool, page * heads, HDIM)
 
-    def halved(parts):
-        return halve_sums(meta, parts[1], swap(parts[0], "grp", 1))
-
     def scattered(parts):
         return [parts[0]] + [swap(parts[i], "grp", 2 * i) for i in range(1, owners // 2)]
 
-    grams = halved(page_sums(code, meta, keys, None, prompt_state, owners, slots))
-    early = [blocks[head_count // 2], blocks[1]]
-    crosses = halved(page_sums(code, meta, keys, values, prompt_state, owners, slots, early))
-    vectors = token_vectors(
-        place, decay_rate, blocks, norm_gain, w_qkv, w_gates, conv_weight, conv_state, [grams[0]]
-    )
+    send_gram, send_cross, keep_gram, keep_cross = page_sums(
+        code, meta, keys, values, prompt_state, owners, slots
+    )
+    got_gram = swap(send_gram, "grp", 1)
+    for bit in bits[1:]:
+        for distance in list(blocks):
+            if distance and not distance & bit and distance ^ bit not in blocks:
+                blocks[distance] = hold(blocks[distance], keep_gram)
+                blocks[distance ^ bit] = swap(blocks[distance], "head", bit)
+    blocks = [blocks[i] for i in range(head_count)]
+    send_cross, *vectors = token_vectors(
+        place, decay_rate, blocks, norm_gain, w_qkv, w_gates, conv_weight, conv_state, send_cross
+    )
+    grams = halve_sums(meta, keep_gram, got_gram)
+    crosses = halve_sums(meta, keep_cross, swap(send_cross, "grp", 1))
     base, solved = ridge_reads(ridge, scattered(grams), vectors, [crosses[0]])
     reads = cross_reads(place, scattered(crosses), base, solved, head_count)
     reads = [reads[0]] + [swap(reads[i], "head", i) for i in range(1, head_count)]

time: 57.6 us -> 52.9 us (0.918)
  Pallas kernels: 31.9 us -> 25.6 us
  starting transfers between devices: 15.8 us -> 16.9 us
  waiting for transfers between devices: 6.46 us -> 5.68 us
  other arithmetic: 0.91 us -> 1.67 us
  local copies, waits for them, and re-layouts: 1.91 us -> 2.58 us
    pallas_call x4, Pallas kernels: 17.4 us -> 11.1 us  [the longest x1 9.9 us: page_sums(): pl.pallas_call(functools.partial(sums_kernel, heads, owners, slots), grid...]
    unnamed x19 -> x27, local copies, waits for them, and re-layouts: 1.16 us -> 2.58 us
    ppermute x14, starting transfers between devices: 15.8 us -> 16.9 us  [swap(): return lax.ppermute(block, axis, [(i, i ^ distance) for i in range(size)])]
    ppermute x14, waiting for transfers between devices: 6.46 us -> 5.68 us  [swap(): return lax.ppermute(block, axis, [(i, i ^ distance) for i in range(size)])]
    concatenate x1 -> x0, local copies, waits for them, and re-layouts: 0.75 us -> none  [shards(): jnp.concatenate([jnp.stack([group, group & 1, group >> 1]), group_prompt,...]
    add x0 -> x1, other arithmetic: none -> 0.75 us  [shards(): jnp.pad(group_prompt, (0, owners + 3)) + jnp.pad(cache_lengths, (owners, 3))]
  transfers between devices with their start and end apart: 14 -> 14, of which waited for: 3 -> 3; matrix products, arithmetic and copies ran while one was open for 3% -> 3% of each run, Pallas kernels for 53% -> 46%
where the time goes in v2:
time: 52.9 us; the launch traced here: 52.7 us
  Pallas kernels  25.6 us (48%)
  starting transfers between devices  16.9 us (32%)
  waiting for transfers between devices  5.68 us (11%)
  local copies, waits for them, and re-layouts  2.58 us (5%)
  other arithmetic  1.67 us (3%)
    ppermute x14, starting transfers between devices, swap(): return lax.ppermute(block, axis, [(i, i ^ distance) for i in range(size)])  16.9 us
    pallas_call x1, Pallas kernels, page_sums(): pl.pallas_call(functools.partial(sums_kernel, heads, owners, slots), grid...  9.9 us
    pallas_call x1, Pallas kernels, ridge_reads(): pl.pallas_call(functools.partial(read_kernel, heads, len(grams)), in_spec...  7.63 us
    ppermute x14, waiting for transfers between devices, swap(): return lax.ppermute(block, axis, [(i, i ^ distance) for i in range(size)])  5.68 us
    pallas_call x1, Pallas kernels, token_vectors(): pl.pallas_call(functools.partial(token_kernel, heads), grid_spec=pltpu.Pr...  5.4 us
    unnamed x27, local copies, waits for them, and re-layouts  2.58 us
    pallas_call x2, Pallas kernels, halve_sums(): pl.pallas_call(functools.partial(halve_kernel, 2 * count), in_specs=[pl.B...  1.21 us
    pallas_call x1, Pallas kernels, output_rows(): pl.pallas_call(output_kernel, in_specs=[pl.BlockSpec(memory_space=pltpu.S...  1.18 us
  transfers between devices with their start and end apart: 14, of which 3 were waited for; matrix products, arithmetic and copies ran while one was open for 3% of the time, Pallas kernels for 46%

profile of v2, /device:TPU:0, one launch (start us, length us, event | category | flops | bytes accessed | tf_op | source)
XLA Modules:
  0.0 52.7 jit_solution(7393977498516363610)
XLA Ops:
  0.0 2.9 %collective-permute-start.1 = (bf16[128,1024]{1,0:T(8,128)(2,1)}, bf16[128,1024]{1,0:T(8,128)(2,1)S(1)}, u32[]{:S(2)}, u32[]{:S(2)}) collective-permute-start(bf16[128,1024]{1,0:T(8,128)(2,1)} %tokens_ref.1), channel_id=1, source_target_pairs={{0,2},{1,3},{2,0},{3,1},{4,6},{5,7},{6,4},{7,5},{8,10},{9,11},{10,... | collective-permute-start | bytes 786440 | tf_op jit(solution)/shard_map/ppermute | solution.py:26
  2.9 0.0 collective-permute-start
  3.0 0.8 %pad_add_fusion.meta_ref = s32[19]{0:T(128)S(1)} fusion(s32[3]{0:T(128)S(1)} %compare_select_fusion.1, s32[8]{0:T(128)} %param.27, s32[8]{0:T(128)} %param.28), kind=kLoop, calls=%fused_computation.5 | loop fusion | flops 38 | bytes 152 | tf_op jit(solution)/shard_map/add | solution.py:513
  3.7 0.9 %select_reduce_fusion.code_ref = s32[64]{0:T(128)S(1)} fusion(s32[8,64]{1,0:T(8,128)S(1)} %multiply_add_fusion, s32[64]{0:T(128)S(1)} %iota_add_fusion, s32[8,64]{1,0:T(8,128)} %param.26), kind=kLoop, calls=%fused_computation | loop fusion | flops 98240 | bytes 4608 | tf_op jit(solution)/shard_map/reduce_sum | solution.py:527
  4.6 0.0 copy-start.12
  4.6 0.0 copy-start.1
  4.6 0.0 copy-start.7
  4.7 0.0 copy-start.8
  4.7 0.0 copy-start.9
  4.7 0.0 copy-start.10
  4.7 9.9 %page_sums.1 = (bf16[4,256,128]{2,1,0:T(8,128)(2,1)S(1)}, bf16[4,256,128]{2,1,0:T(8,128)(2,1)S(1)}, bf16[4,256,128]{2,1,0:T(8,128)(2,1)S(1)}, bf16[4,256,128]{2,1,0:T(8,128)(2,1)}) custom-call(s32[64]{0:T(128)S(1)} %select_reduce_fusion.code_ref, s32[19]{0:T(128)S(1)} %pad_add_fusion.meta_ref, bf16[64,256,128]{2,1,0:T(8,128)(2,1)} %bitcast.5, ...), custom_call_target="tpu_custom_call" | custom-call | flops 4294967296 | bytes 8388608 | tf_op jit(solution)/shard_map/page_sums/pallas_call | solution.py:144
  14.6 0.0 copy-start.4
  14.6 0.7 %copy-done.4 = bf16[4,256,128]{2,1,0:T(8,128)(2,1)} copy-done((bf16[4,256,128]{2,1,0:T(8,128)(2,1)}, bf16[4,256,128]{2,1,0:T(8,128)(2,1)S(1)}, u32[]{:S(2)}) %copy-start.4) | copy-done | bytes 262168
  15.3 0.0 collective-permute-done.1.refs_0_
  15.3 0.0 copy-start.2
  15.3 0.7 %copy-done.2 = bf16[128,1024]{1,0:T(8,128)(2,1)} copy-done((bf16[128,1024]{1,0:T(8,128)(2,1)}, bf16[128,1024]{1,0:T(8,128)(2,1)S(1)}, u32[]{:S(2)}) %copy-start.2) | copy-done | bytes 262168
  16.0 0.0 copy-start.5
  16.0 0.5 collective-permute-start.2
  16.5 1.4 %collective-permute-start.7 = (bf16[4,256,128]{2,1,0:T(8,128)(2,1)S(1)}, bf16[4,256,128]{2,1,0:T(8,128)(2,1)S(1)}, u32[]{:S(2)}, u32[]{:S(2)}) collective-permute-start(bf16[4,256,128]{2,1,0:T(8,128)(2,1)S(1)} %get-tuple-element.39), channel_id=1, source_target_pairs={{0,4},{4,0},{8,12},{12,8},{16,20},{20,16},{24,28},{28,24},{1,5},{5... | collective-permute-start | bytes 786440 | tf_op jit(solution)/shard_map/ppermute | solution.py:26
  18.0 0.0 copy-done.12
  18.0 0.2 copy.19.refs_6_
  18.1 0.0 collective-permute-done.refs_1_
  18.2 0.0 collective-permute-done.2.refs_3_
  18.2 0.0 copy-done.1
  18.2 0.0 copy-done.7
  18.2 0.0 copy-done.8
  18.2 0.0 copy-done.9
  18.2 0.0 copy-done.10
  18.2 0.0 copy-start.3
  18.2 0.9 %copy-done.3 = bf16[128,1024]{1,0:T(8,128)(2,1)S(1)} copy-done((bf16[128,1024]{1,0:T(8,128)(2,1)S(1)}, bf16[128,1024]{1,0:T(8,128)(2,1)}, u32[]{:S(2)}) %copy-start.3) | copy-done | bytes 262168
  19.2 0.0 copy-start.6
  19.2 0.0 copy-start.11
  19.2 5.4 %token_vectors.1 = (bf16[4,256,128]{2,1,0:T(8,128)(2,1)S(1)}, bf16[2,128,512]{2,1,0:T(8,128)(2,1)S(1)}, bf16[2,512,128]{2,1,0:T(8,128)(2,1)S(1)}, bf16[2,128,512...) custom-call(s32[1]{0:T(128)} %bitcast.place_ref, ...), custom_call_target="tpu_custom_call", output_to_operand_aliasing={{0}: (11, {})} | custom-call | flops 805306368 | bytes 6815744 | tf_op jit(solution)/shard_map/token_vectors/pallas_call | solution.py:295
  24.6 1.2 %collective-permute-start.3 = (bf16[4,256,128]{2,1,0:T(8,128)(2,1)S(1)}, bf16[4,256,128]{2,1,0:T(8,128)(2,1)S(1)}, u32[]{:S(2)}, u32[]{:S(2)}) collective-permute-start(bf16[4,256,128]{2,1,0:T(8,128)(2,1)S(1)} %get-tuple-element.34), channel_id=1, source_target_pairs={{0,4},{4,0},{8,12},{12,8},{16,20},{20,16},{24,28},{28,24},{1,5},{5... | collective-permute-start | bytes 786440 | tf_op jit(solution)/shard_map/ppermute | solution.py:26
  25.8 0.0 collective-permute-done.7.got_ref
  25.8 0.0 copy-done.5
  25.8 0.6 %halve_sums.3 = (f32[256,128]{1,0:T(8,128)S(1)}, bf16[256,128]{1,0:T(8,128)(2,1)S(1)}, bf16[256,128]{1,0:T(8,128)(2,1)S(1)}, bf16[256,128]{1,0:T(8,128)(2,1)S(1)}) custom-call(s32[19]{0:T(128)S(1)} %pad_add_fusion.meta_ref, bf16[4,256,128]{2,1,0:T(8,128)(2,1)S(1)} %copy-done.5, bf16[4,256,128]{2,1,0:T(8,128)(2,1)S(1)} %collective-permute-done.7.got_ref), custom_call_target="tpu_custom_call" | custom-call | flops 131072 | bytes 786432 | tf_op jit(solution)/shard_map/halve_sums/pallas_call | solution.py:180
  26.4 1.5 %collective-permute-start.8 = (bf16[256,128]{1,0:T(8,128)(2,1)S(1)}, bf16[256,128]{1,0:T(8,128)(2,1)S(1)}, u32[]{:S(2)}, u32[]{:S(2)}) collective-permute-start(bf16[256,128]{1,0:T(8,128)(2,1)S(1)} %get-tuple-element.41), channel_id=1, source_target_pairs={{0,8},{4,12},{8,0},{12,4},{16,24},{20,28},{24,16},{28,20},{1,9},{5... | collective-permute-start | bytes 196616 | tf_op jit(solution)/shard_map/ppermute | solution.py:26
  27.9 2.6 %collective-permute-start.9 = (bf16[256,128]{1,0:T(8,128)(2,1)S(1)}, bf16[256,128]{1,0:T(8,128)(2,1)S(1)}, u32[]{:S(2)}, u32[]{:S(2)}) collective-permute-start(bf16[256,128]{1,0:T(8,128)(2,1)S(1)} %get-tuple-element.42), channel_id=1, source_target_pairs={{0,16},{4,20},{8,24},{12,28},{16,0},{20,4},{24,8},{28,12},{1,17},{... | collective-permute-start | bytes 196616 | tf_op jit(solution)/shard_map/ppermute | solution.py:26
  30.5 0.4 collective-permute-start.10
  30.9 2.1 %collective-permute-done.3.got_ref = bf16[4,256,128]{2,1,0:T(8,128)(2,1)S(1)} collective-permute-done((bf16[4,256,128]{2,1,0:T(8,128)(2,1)S(1)}, bf16[4,256,128]{2,1,0:T(8,128)(2,1)S(1)}, u32[]{:S(2)}, u32[]{:S(2)}) %collective-permute-start.3) | collective-permute-done | bytes 262176 | tf_op jit(solution)/shard_map/ppermute | solution.py:26
  32.9 0.0 copy-done.6
  32.9 0.6 %halve_sums.2 = (f32[256,128]{1,0:T(8,128)S(1)}, bf16[256,128]{1,0:T(8,128)(2,1)S(1)}, bf16[256,128]{1,0:T(8,128)(2,1)S(1)}, bf16[256,128]{1,0:T(8,128)(2,1)S(1)}) custom-call(s32[19]{0:T(128)S(1)} %pad_add_fusion.meta_ref, bf16[4,256,128]{2,1,0:T(8,128)(2,1)S(1)} %copy-done.6, bf16[4,256,128]{2,1,0:T(8,128)(2,1)S(1)} %collective-permute-done.3.got_ref), custom_call_target="tpu_custom_call" | custom-call | flops 131072 | bytes 786432 | tf_op jit(solution)/shard_map/halve_sums/pallas_call | solution.py:180
  33.6 1.4 %collective-permute-start.4 = (bf16[256,128]{1,0:T(8,128)(2,1)S(1)}, bf16[256,128]{1,0:T(8,128)(2,1)S(1)}, u32[]{:S(2)}, u32[]{:S(2)}) collective-permute-start(bf16[256,128]{1,0:T(8,128)(2,1)S(1)} %get-tuple-element.36), channel_id=1, source_target_pairs={{0,8},{4,12},{8,0},{12,4},{16,24},{20,28},{24,16},{28,20},{1,9},{5... | collective-permute-start | bytes 196616 | tf_op jit(solution)/shard_map/ppermute | solution.py:26
  34.9 2.7 %collective-permute-start.5 = (bf16[256,128]{1,0:T(8,128)(2,1)S(1)}, bf16[256,128]{1,0:T(8,128)(2,1)S(1)}, u32[]{:S(2)}, u32[]{:S(2)}) collective-permute-start(bf16[256,128]{1,0:T(8,128)(2,1)S(1)} %get-tuple-element.37), channel_id=1, source_target_pairs={{0,16},{4,20},{8,24},{12,28},{16,0},{20,4},{24,8},{28,12},{1,17},{... | collective-permute-start | bytes 196616 | tf_op jit(solution)/shard_map/ppermute | solution.py:26
  37.6 0.0 collective-permute-done.8.refs_1_
  37.6 0.4 collective-permute-start.6
  38.0 0.0 collective-permute-done.9.refs_2_
  38.0 0.0 collective-permute-done.10.refs_3_
  38.0 0.0 copy-done.11
  38.0 0.0 copy-start
  38.0 7.6 %ridge_reads.1 = (f32[512,256]{1,0:T(8,128)S(1)}, bf16[512,256]{1,0:T(8,128)(2,1)S(1)}) custom-call(f32[2]{0:T(128)S(1)} %copy-done.11, f32[256,128]{1,0:T(8,128)S(1)} %get-tuple-element.40.refs_0_, bf16[256,128]{1,0:T(8,128)(2,1)S(1)} %collective-permute-done.8.refs_1_, bf16[256,128]{1,0:T(8,128)(2,1)S(1)} %collective-permute-done.9.refs_2_, ...), custom_call_target="tpu_custom_call" | custom-call | flops 6442450944 | bytes 8388608 | tf_op jit(solution)/shard_map/ridge_reads/pallas_call | solution.py:405
  45.7 0.0 collective-permute-done.4.refs_1_
  45.7 0.0 collective-permute-done.5.refs_2_
  45.7 0.0 collective-permute-done.6.refs_3_
  45.7 0.3 cross_reads.1
  46.0 0.1 collective-permute-start.11
  46.0 0.3 collective-permute-start.12
  46.3 1.6 %collective-permute-start.13 = (bf16[128,256]{1,0:T(8,128)(2,1)S(1)}, bf16[128,256]{1,0:T(8,128)(2,1)S(1)}, u32[]{:S(2)}, u32[]{:S(2)}) collective-permute-start(bf16[128,256]{1,0:T(8,128)(2,1)S(1)} %get-tuple-element.56), channel_id=1, source_target_pairs={{0,3},{1,2},{2,1},{3,0},{4,7},{5,6},{6,5},{7,4},{8,11},{9,10},{10,... | collective-permute-start | bytes 196616 | tf_op jit(solution)/shard_map/ppermute | solution.py:26
  47.9 0.0 collective-permute-done.11.refs_1_
  47.9 3.1 %collective-permute-done.12.refs_2_ = bf16[128,256]{1,0:T(8,128)(2,1)S(1)} collective-permute-done((bf16[128,256]{1,0:T(8,128)(2,1)S(1)}, bf16[128,256]{1,0:T(8,128)(2,1)S(1)}, u32[]{:S(2)}, u32[]{:S(2)}) %collective-permute-start.12) | collective-permute-done | bytes 65568 | tf_op jit(solution)/shard_map/ppermute | solution.py:26
  51.0 0.5 collective-permute-done.13.refs_3_
  51.5 0.0 copy-done
  51.5 1.2 %output_rows.1 = bf16[128,1024]{1,0:T(8,128)(2,1)} custom-call(s32[1]{0:T(128)} %bitcast.place_ref, bf16[128,1024]{1,0:T(8,128)(2,1)S(1)} %copy-done.1, bf16[1024,1024]{1,0:T(8,128)(2,1)S(1)} %copy-done, bf16[128,256]{1,0:T(8,128)(2,1)S(1)} %get-tuple-element.53.refs_0_, bf16[128,256]{1,0:T(8,128)(2,1)S(1)} %collective-permute-done.11.refs_1_, ...), custom_call_target="tpu_custom_call" | custom-call | flops 268435456 | bytes 2883584 | tf_op jit(solution)/shard_map/output_rows/pallas_call | solution.py:473
  (4 shorter events, 0.0 us)
Async XLA Ops:
  0.0 15.3 %collective-permute-start.1 = (bf16[128,1024]{1,0:T(8,128)(2,1)}, bf16[128,1024]{1,0:T(8,128)(2,1)S(1)}, u32[]{:S(2)}, u32[]{:S(2)}) collective-permute-start(bf16[128,1024]{1,0:T(8,128)(2,1)} %tokens_ref.1), channel_id=1, source_target_pairs={{0,2},{1,3},{2,0},{3,1},{4,6},{5,7},{6,4},{7,5},{8,10},{9,11},{10,... | collective-permute-start | bytes 786440 | tf_op jit(solution)/shard_map/ppermute | solution.py:26
  2.9 15.2 %collective-permute-start = (bf16[128,1024]{1,0:T(8,128)(2,1)}, bf16[128,1024]{1,0:T(8,128)(2,1)S(1)}, u32[]{:S(2)}, u32[]{:S(2)}) collective-permute-start(bf16[128,1024]{1,0:T(8,128)(2,1)} %tokens_ref.1), channel_id=1, source_target_pairs={{0,1},{1,0},{2,3},{3,2},{4,5},{5,4},{6,7},{7,6},{8,9},{9,8},{10,11... | collective-permute-start | bytes 786440 | tf_op jit(solution)/shard_map/ppermute | solution.py:26
  4.6 13.4 %copy-start.12 = (bf16[1024,16]{0,1:T(8,128)(2,1)S(1)}, bf16[1024,16]{0,1:T(8,128)(2,1)}, u32[]{:S(2)}) copy-start(bf16[1024,16]{0,1:T(8,128)(2,1)} %param.18) | copy-start | bytes 98308
  4.6 13.5 %copy-start.1 = (bf16[128,1024]{1,0:T(8,128)(2,1)S(1)}, bf16[128,1024]{1,0:T(8,128)(2,1)}, u32[]{:S(2)}) copy-start(bf16[128,1024]{1,0:T(8,128)(2,1)} %tokens_ref.1) | copy-start | bytes 786436
  4.6 13.5 %copy-start.7 = (f32[4,3072]{1,0:T(4,128)S(1)}, f32[4,3072]{1,0:T(4,128)}, u32[]{:S(2)}) copy-start(f32[4,3072]{1,0:T(4,128)} %refs_7_.1) | copy-start | bytes 147460
  4.7 13.5 %copy-start.8 = (bf16[1,3,3072]{2,1,0:T(4,128)(2,1)S(1)}, bf16[1,3,3072]{2,1,0:T(4,128)(2,1)}, u32[]{:S(2)}) copy-start(bf16[1,3,3072]{2,1,0:T(4,128)(2,1)} %refs_8_.1) | copy-start | bytes 55300
  4.7 13.5 %copy-start.9 = (f32[1024]{0:T(1024)S(1)}, f32[1024]{0:T(1024)}, u32[]{:S(2)}) copy-start(f32[1024]{0:T(1024)} %param.16) | copy-start | bytes 12292
  4.7 13.5 %copy-start.10 = (f32[8]{0:T(128)S(1)}, f32[8]{0:T(128)}, u32[]{:S(2)}) copy-start(f32[8]{0:T(128)} %rate_ref.1) | copy-start | bytes 100
  14.6 0.7 %copy-start.4 = (bf16[4,256,128]{2,1,0:T(8,128)(2,1)}, bf16[4,256,128]{2,1,0:T(8,128)(2,1)S(1)}, u32[]{:S(2)}) copy-start(bf16[4,256,128]{2,1,0:T(8,128)(2,1)S(1)} %get-tuple-element.32.refs_1_.keep_ref) | copy-start | bytes 786436
  15.3 0.7 %copy-start.2 = (bf16[128,1024]{1,0:T(8,128)(2,1)}, bf16[128,1024]{1,0:T(8,128)(2,1)S(1)}, u32[]{:S(2)}) copy-start(bf16[128,1024]{1,0:T(8,128)(2,1)S(1)} %collective-permute-done.1.refs_0_) | copy-start | bytes 786436
  16.0 9.8 %copy-start.5 = (bf16[4,256,128]{2,1,0:T(8,128)(2,1)S(1)}, bf16[4,256,128]{2,1,0:T(8,128)(2,1)}, u32[]{:S(2)}) copy-start(bf16[4,256,128]{2,1,0:T(8,128)(2,1)} %copy-done.4) | copy-start | bytes 786436
  16.0 2.1 %collective-permute-start.2 = (bf16[128,1024]{1,0:T(8,128)(2,1)}, bf16[128,1024]{1,0:T(8,128)(2,1)S(1)}, u32[]{:S(2)}, u32[]{:S(2)}) collective-permute-start(bf16[128,1024]{1,0:T(8,128)(2,1)} %hold.1.refs_2_), channel_id=1, source_target_pairs={{0,1},{1,0},{2,3},{3,2},{4,5},{5,4},{6,7},{7,6},{8,9},{9,8},{10,11... | collective-permute-start | bytes 786440 | tf_op jit(solution)/shard_map/ppermute | solution.py:26
  16.5 9.3 %collective-permute-start.7 = (bf16[4,256,128]{2,1,0:T(8,128)(2,1)S(1)}, bf16[4,256,128]{2,1,0:T(8,128)(2,1)S(1)}, u32[]{:S(2)}, u32[]{:S(2)}) collective-permute-start(bf16[4,256,128]{2,1,0:T(8,128)(2,1)S(1)} %get-tuple-element.39), channel_id=1, source_target_pairs={{0,4},{4,0},{8,12},{12,8},{16,20},{20,16},{24,28},{28,24},{1,5},{5... | collective-permute-start | bytes 786440 | tf_op jit(solution)/shard_map/ppermute | solution.py:26
  18.2 1.0 %copy-start.3 = (bf16[128,1024]{1,0:T(8,128)(2,1)S(1)}, bf16[128,1024]{1,0:T(8,128)(2,1)}, u32[]{:S(2)}) copy-start(bf16[128,1024]{1,0:T(8,128)(2,1)} %hold.1.refs_2_) | copy-start | bytes 786436
  19.2 13.8 %copy-start.6 = (bf16[4,256,128]{2,1,0:T(8,128)(2,1)S(1)}, bf16[4,256,128]{2,1,0:T(8,128)(2,1)}, u32[]{:S(2)}) copy-start(bf16[4,256,128]{2,1,0:T(8,128)(2,1)} %get-tuple-element.31.keep_ref) | copy-start | bytes 786436
  19.2 18.8 %copy-start.11 = (f32[2]{0:T(128)S(1)}, f32[2]{0:T(128)}, u32[]{:S(2)}) copy-start(f32[2]{0:T(128)} %ridge_ref.1) | copy-start | bytes 28
  24.6 8.4 %collective-permute-start.3 = (bf16[4,256,128]{2,1,0:T(8,128)(2,1)S(1)}, bf16[4,256,128]{2,1,0:T(8,128)(2,1)S(1)}, u32[]{:S(2)}, u32[]{:S(2)}) collective-permute-start(bf16[4,256,128]{2,1,0:T(8,128)(2,1)S(1)} %get-tuple-element.34), channel_id=1, source_target_pairs={{0,4},{4,0},{8,12},{12,8},{16,20},{20,16},{24,28},{28,24},{1,5},{5... | collective-permute-start | bytes 786440 | tf_op jit(solution)/shard_map/ppermute | solution.py:26
  26.4 11.2 %collective-permute-start.8 = (bf16[256,128]{1,0:T(8,128)(2,1)S(1)}, bf16[256,128]{1,0:T(8,128)(2,1)S(1)}, u32[]{:S(2)}, u32[]{:S(2)}) collective-permute-start(bf16[256,128]{1,0:T(8,128)(2,1)S(1)} %get-tuple-element.41), channel_id=1, source_target_pairs={{0,8},{4,12},{8,0},{12,4},{16,24},{20,28},{24,16},{28,20},{1,9},{5... | collective-permute-start | bytes 196616 | tf_op jit(solution)/shard_map/ppermute | solution.py:26
  27.9 10.1 %collective-permute-start.9 = (bf16[256,128]{1,0:T(8,128)(2,1)S(1)}, bf16[256,128]{1,0:T(8,128)(2,1)S(1)}, u32[]{:S(2)}, u32[]{:S(2)}) collective-permute-start(bf16[256,128]{1,0:T(8,128)(2,1)S(1)} %get-tuple-element.42), channel_id=1, source_target_pairs={{0,16},{4,20},{8,24},{12,28},{16,0},{20,4},{24,8},{28,12},{1,17},{... | collective-permute-start | bytes 196616 | tf_op jit(solution)/shard_map/ppermute | solution.py:26
  30.5 7.5 %collective-permute-start.10 = (bf16[256,128]{1,0:T(8,128)(2,1)S(1)}, bf16[256,128]{1,0:T(8,128)(2,1)S(1)}, u32[]{:S(2)}, u32[]{:S(2)}) collective-permute-start(bf16[256,128]{1,0:T(8,128)(2,1)S(1)} %get-tuple-element.43), channel_id=1, source_target_pairs={{0,24},{4,28},{8,16},{12,20},{16,8},{20,12},{24,0},{28,4},{1,25},{... | collective-permute-start | bytes 196616 | tf_op jit(solution)/shard_map/ppermute | solution.py:26
  33.6 12.1 %collective-permute-start.4 = (bf16[256,128]{1,0:T(8,128)(2,1)S(1)}, bf16[256,128]{1,0:T(8,128)(2,1)S(1)}, u32[]{:S(2)}, u32[]{:S(2)}) collective-permute-start(bf16[256,128]{1,0:T(8,128)(2,1)S(1)} %get-tuple-element.36), channel_id=1, source_target_pairs={{0,8},{4,12},{8,0},{12,4},{16,24},{20,28},{24,16},{28,20},{1,9},{5... | collective-permute-start | bytes 196616 | tf_op jit(solution)/shard_map/ppermute | solution.py:26
  34.9 10.8 %collective-permute-start.5 = (bf16[256,128]{1,0:T(8,128)(2,1)S(1)}, bf16[256,128]{1,0:T(8,128)(2,1)S(1)}, u32[]{:S(2)}, u32[]{:S(2)}) collective-permute-start(bf16[256,128]{1,0:T(8,128)(2,1)S(1)} %get-tuple-element.37), channel_id=1, source_target_pairs={{0,16},{4,20},{8,24},{12,28},{16,0},{20,4},{24,8},{28,12},{1,17},{... | collective-permute-start | bytes 196616 | tf_op jit(solution)/shard_map/ppermute | solution.py:26
  37.6 8.1 %collective-permute-start.6 = (bf16[256,128]{1,0:T(8,128)(2,1)S(1)}, bf16[256,128]{1,0:T(8,128)(2,1)S(1)}, u32[]{:S(2)}, u32[]{:S(2)}) collective-permute-start(bf16[256,128]{1,0:T(8,128)(2,1)S(1)} %get-tuple-element.38), channel_id=1, source_target_pairs={{0,24},{4,28},{8,16},{12,20},{16,8},{20,12},{24,0},{28,4},{1,25},{... | collective-permute-start | bytes 196616 | tf_op jit(solution)/shard_map/ppermute | solution.py:26
  38.0 13.5 %copy-start = (bf16[1024,1024]{1,0:T(8,128)(2,1)S(1)}, bf16[1024,1024]{1,0:T(8,128)(2,1)}, u32[]{:S(2)}) copy-start(bf16[1024,1024]{1,0:T(8,128)(2,1)} %w_ref.1) | copy-start | bytes 6291460
  46.0 1.9 %collective-permute-start.11 = (bf16[128,256]{1,0:T(8,128)(2,1)S(1)}, bf16[128,256]{1,0:T(8,128)(2,1)S(1)}, u32[]{:S(2)}, u32[]{:S(2)}) collective-permute-start(bf16[128,256]{1,0:T(8,128)(2,1)S(1)} %get-tuple-element.54), channel_id=1, source_target_pairs={{0,1},{1,0},{2,3},{3,2},{4,5},{5,4},{6,7},{7,6},{8,9},{9,8},{10,11... | collective-permute-start | bytes 196616 | tf_op jit(solution)/shard_map/ppermute | solution.py:26
  46.0 5.0 %collective-permute-start.12 = (bf16[128,256]{1,0:T(8,128)(2,1)S(1)}, bf16[128,256]{1,0:T(8,128)(2,1)S(1)}, u32[]{:S(2)}, u32[]{:S(2)}) collective-permute-start(bf16[128,256]{1,0:T(8,128)(2,1)S(1)} %get-tuple-element.55), channel_id=1, source_target_pairs={{0,2},{1,3},{2,0},{3,1},{4,6},{5,7},{6,4},{7,5},{8,10},{9,11},{10,... | collective-permute-start | bytes 196616 | tf_op jit(solution)/shard_map/ppermute | solution.py:26
  46.3 5.2 %collective-permute-start.13 = (bf16[128,256]{1,0:T(8,128)(2,1)S(1)}, bf16[128,256]{1,0:T(8,128)(2,1)S(1)}, u32[]{:S(2)}, u32[]{:S(2)}) collective-permute-start(bf16[128,256]{1,0:T(8,128)(2,1)S(1)} %get-tuple-element.56), channel_id=1, source_target_pairs={{0,3},{1,2},{2,1},{3,0},{4,7},{5,6},{6,5},{7,4},{8,11},{9,10},{10,... | collective-permute-start | bytes 196616 | tf_op jit(solution)/shard_map/ppermute | solution.py:26

commit v3 on v2

--- a/solution.py
+++ b/solution.py
@@ -34,6 +34,7 @@
         out_specs=anywhere,
         out_shape=jax.ShapeDtypeStruct(block.shape, block.dtype),
         input_output_aliases={0: 0},
+        compiler_params=pltpu.CompilerParams(vmem_limit_bytes=2**20),
         name="hold",
     )(block, other)
 
@@ -62,7 +63,7 @@
 
 
 def sums_kernel(heads, owners, slots, code_ref, meta_ref, keys_ref, values_ref, prompt_ref,
-                send_gram, send_cross, keep_gram, keep_cross, acc_ref, parity_ref, stored_ref, sem):
+                send_gram, send_cross, keep_gram, keep_cross, acc_ref, stored_ref, sem):
     step = pl.program_id(0)
     pages, rows = keys_ref.shape[0], keys_ref.shape[1]
     load_prompt = pltpu.make_async_copy(prompt_ref, stored_ref, sem)
@@ -72,8 +73,6 @@
     def _():
         load_prompt.start()
         acc_ref[...] = jnp.zeros_like(acc_ref)
-        for head in range(heads):
-            parity_ref[head] = (lane % heads == head).astype(F32).astype(BF16)
 
     def place(page):
         code = code_ref[step * pages + page]
@@ -81,9 +80,12 @@
         return owner, jnp.clip(meta_ref[owners + owner] - slot * PAGE, 0, PAGE)
 
     def add(page, owner, turned):
+        zero = jnp.zeros_like(turned)
         left = turned
         if heads > 1:
-            left = jnp.concatenate([turned * parity_ref[head] for head in range(heads)], axis=0)
+            left = jnp.concatenate(
+                [jnp.where(lane % heads == head, turned, zero) for head in range(heads)], axis=0
+            )
         right = jnp.concatenate([keys_ref[page], values_ref[page]], axis=1)
         acc_ref[owner] += dot(left, right)
 
@@ -150,7 +152,6 @@
             out_specs=[out_spec] * 4,
             scratch_shapes=[
                 pltpu.VMEM((owners + 1, heads * HDIM, 2 * HDIM), F32),
-                pltpu.VMEM((heads, HDIM, rows), BF16),
                 pltpu.VMEM(prompt_state.shape, F32),
                 pltpu.SemaphoreType.DMA,
             ],
@@ -381,7 +382,7 @@
             later.append(norm_next)
         return tuple(later)
 
-    lax.fori_loop(0, CG_STEPS, one_step, tuple(norms))
+    lax.fori_loop(0, CG_STEPS, one_step, tuple(norms), unroll=2)
     for head, pair in groups:
         cols = slice(head * HDIM, (head + 1) * HDIM)
         span = slice(pair * PAIR, (pair + 1) * PAIR)

time: 52.9 us -> 50.2 us (0.949)
  local copies, waits for them, and re-layouts: 2.58 us -> 0.22 us
  Pallas kernels: 25.6 us -> 24.7 us
  starting transfers between devices: 16.9 us -> 17.6 us
    unnamed x27 -> x19, local copies, waits for them, and re-layouts: 2.58 us -> 0.22 us
    ppermute x14, starting transfers between devices: 16.9 us -> 17.6 us  [swap(): return lax.ppermute(block, axis, [(i, i ^ distance) for i in range(size)])]
  transfers between devices with their start and end apart: 14 -> 14, of which waited for: 3 -> 3; matrix products, arithmetic and copies ran while one was open for 3% -> 4% of each run, Pallas kernels for 46% -> 47%
where the time goes in v3:
time: 50.2 us; the launch traced here: 50.1 us
  Pallas kernels  24.7 us (49%)
  starting transfers between devices  17.6 us (35%)
  waiting for transfers between devices  5.61 us (11%)
  other arithmetic  1.67 us (3%)
    ppermute x14, starting transfers between devices, swap(): return lax.ppermute(block, axis, [(i, i ^ distance) for i in range(size)])  17.6 us
    pallas_call x1, Pallas kernels, page_sums(): pl.pallas_call(functools.partial(sums_kernel, heads, owners, slots), grid...  9.41 us
    pallas_call x1, Pallas kernels, ridge_reads(): pl.pallas_call(functools.partial(read_kernel, heads, len(grams)), in_spec...  7.26 us
    ppermute x14, waiting for transfers between devices, swap(): return lax.ppermute(block, axis, [(i, i ^ distance) for i in range(size)])  5.61 us
    pallas_call x1, Pallas kernels, token_vectors(): pl.pallas_call(functools.partial(token_kernel, heads), grid_spec=pltpu.Pr...  5.44 us
    pallas_call x2, Pallas kernels, halve_sums(): pl.pallas_call(functools.partial(halve_kernel, 2 * count), in_specs=[pl.B...  1.21 us
    pallas_call x1, Pallas kernels, output_rows(): pl.pallas_call(output_kernel, in_specs=[pl.BlockSpec(memory_space=pltpu.S...  1.17 us
  transfers between devices with their start and end apart: 14, of which 3 were waited for; matrix products, arithmetic and copies ran while one was open for 4% of the time, Pallas kernels for 47%

profile of v3, /device:TPU:0, one launch (start us, length us, event | category | flops | bytes accessed | tf_op | source)
XLA Modules:
  0.0 50.1 jit_solution(15318838083180012588)
XLA Ops:
  0.0 2.9 %collective-permute-start.1 = (bf16[128,1024]{1,0:T(8,128)(2,1)}, bf16[128,1024]{1,0:T(8,128)(2,1)S(1)}, u32[]{:S(2)}, u32[]{:S(2)}) collective-permute-start(bf16[128,1024]{1,0:T(8,128)(2,1)} %tokens_ref.1), channel_id=1, source_target_pairs={{0,2},{1,3},{2,0},{3,1},{4,6},{5,7},{6,4},{7,5},{8,10},{9,11},{10,... | collective-permute-start | bytes 786440 | tf_op jit(solution)/shard_map/ppermute | solution.py:26
  2.9 0.0 collective-permute-start
  3.0 0.8 %pad_add_fusion.meta_ref = s32[19]{0:T(128)S(1)} fusion(s32[3]{0:T(128)S(1)} %compare_select_fusion.1, s32[8]{0:T(128)} %param.27, s32[8]{0:T(128)} %param.28), kind=kLoop, calls=%fused_computation.5 | loop fusion | flops 38 | bytes 152 | tf_op jit(solution)/shard_map/add | solution.py:514
  3.7 0.9 %select_reduce_fusion.code_ref = s32[64]{0:T(128)S(1)} fusion(s32[8,64]{1,0:T(8,128)S(1)} %multiply_add_fusion, s32[64]{0:T(128)S(1)} %iota_add_fusion, s32[8,64]{1,0:T(8,128)} %param.26), kind=kLoop, calls=%fused_computation | loop fusion | flops 98240 | bytes 4608 | tf_op jit(solution)/shard_map/reduce_sum | solution.py:528
  4.6 0.0 copy-start.8
  4.6 0.0 copy-start.1
  4.6 0.0 copy-start.3
  4.7 0.0 copy-start.4
  4.7 0.0 copy-start.5
  4.7 0.0 copy-start.6
  4.7 9.4 %page_sums.1 = (bf16[4,256,128]{2,1,0:T(8,128)(2,1)S(1)}, bf16[4,256,128]{2,1,0:T(8,128)(2,1)S(1)}, bf16[4,256,128]{2,1,0:T(8,128)(2,1)S(1)}, bf16[4,256,128]{2,1,0:T(8,128)(2,1)}) custom-call(s32[64]{0:T(128)S(1)} %select_reduce_fusion.code_ref, s32[19]{0:T(128)S(1)} %pad_add_fusion.meta_ref, bf16[64,256,128]{2,1,0:T(8,128)(2,1)} %bitcast.5, ...), custom_call_target="tpu_custom_call" | custom-call | flops 4294967296 | bytes 8388608 | tf_op jit(solution)/shard_map/page_sums/pallas_call | solution.py:146
  14.1 0.0 collective-permute-done.1.refs_0_
  14.1 0.6 %collective-permute-start.2 = (bf16[128,1024]{1,0:T(8,128)(2,1)S(1)}, bf16[128,1024]{1,0:T(8,128)(2,1)S(1)}, u32[]{:S(2)}, u32[]{:S(2)}) collective-permute-start(bf16[128,1024]{1,0:T(8,128)(2,1)S(1)} %hold.1.refs_2_), channel_id=1, source_target_pairs={{0,1},{1,0},{2,3},{3,2},{4,5},{5,4},{6,7},{7,6},{8,9},{9,8},{10,11... | collective-permute-start | bytes 786440 | tf_op jit(solution)/shard_map/ppermute | solution.py:26
  14.7 2.2 %collective-permute-start.7 = (bf16[4,256,128]{2,1,0:T(8,128)(2,1)S(1)}, bf16[4,256,128]{2,1,0:T(8,128)(2,1)S(1)}, u32[]{:S(2)}, u32[]{:S(2)}) collective-permute-start(bf16[4,256,128]{2,1,0:T(8,128)(2,1)S(1)} %get-tuple-element.39), channel_id=1, source_target_pairs={{0,4},{4,0},{8,12},{12,8},{16,20},{20,16},{24,28},{28,24},{1,5},{5... | collective-permute-start | bytes 786440 | tf_op jit(solution)/shard_map/ppermute | solution.py:26
  16.9 0.0 copy-done.8
  16.9 0.2 copy.19.refs_6_
  17.1 0.0 collective-permute-done.refs_1_
  17.1 0.0 collective-permute-done.2.refs_3_
  17.1 0.0 copy-done.1
  17.1 0.0 copy-done.3
  17.1 0.0 copy-done.4
  17.1 0.0 copy-done.5
  17.2 0.0 copy-done.6
  17.2 0.0 copy-start.2
  17.2 0.0 copy-start.7
  17.2 5.4 %token_vectors.1 = (bf16[4,256,128]{2,1,0:T(8,128)(2,1)S(1)}, bf16[2,128,512]{2,1,0:T(8,128)(2,1)S(1)}, bf16[2,512,128]{2,1,0:T(8,128)(2,1)S(1)}, bf16[2,128,512...) custom-call(s32[1]{0:T(128)} %bitcast.place_ref, ...), custom_call_target="tpu_custom_call", output_to_operand_aliasing={{0}: (11, {})} | custom-call | flops 805306368 | bytes 6815744 | tf_op jit(solution)/shard_map/token_vectors/pallas_call | solution.py:296
  22.6 1.0 %collective-permute-start.3 = (bf16[4,256,128]{2,1,0:T(8,128)(2,1)S(1)}, bf16[4,256,128]{2,1,0:T(8,128)(2,1)S(1)}, u32[]{:S(2)}, u32[]{:S(2)}) collective-permute-start(bf16[4,256,128]{2,1,0:T(8,128)(2,1)S(1)} %get-tuple-element.34), channel_id=1, source_target_pairs={{0,4},{4,0},{8,12},{12,8},{16,20},{20,16},{24,28},{28,24},{1,5},{5... | collective-permute-start | bytes 786440 | tf_op jit(solution)/shard_map/ppermute | solution.py:26
  23.6 0.0 collective-permute-done.7.got_ref
  23.6 0.6 %halve_sums.3 = (f32[256,128]{1,0:T(8,128)S(1)}, bf16[256,128]{1,0:T(8,128)(2,1)S(1)}, bf16[256,128]{1,0:T(8,128)(2,1)S(1)}, bf16[256,128]{1,0:T(8,128)(2,1)S(1)}) custom-call(s32[19]{0:T(128)S(1)} %pad_add_fusion.meta_ref, bf16[4,256,128]{2,1,0:T(8,128)(2,1)S(1)} %get-tuple-element.32.refs_1_.keep_ref, bf16[4,256,128]{2,1,0:T(8,128)(2,1)S(1)} %collective-permute-done.7.got_ref), custom_call_target="tpu_custom_call" | custom-call | flops 131072 | bytes 786432 | tf_op jit(solution)/shard_map/halve_sums/pallas_call | solution.py:181
  24.3 1.1 %collective-permute-start.8 = (bf16[256,128]{1,0:T(8,128)(2,1)S(1)}, bf16[256,128]{1,0:T(8,128)(2,1)S(1)}, u32[]{:S(2)}, u32[]{:S(2)}) collective-permute-start(bf16[256,128]{1,0:T(8,128)(2,1)S(1)} %get-tuple-element.41), channel_id=1, source_target_pairs={{0,8},{4,12},{8,0},{12,4},{16,24},{20,28},{24,16},{28,20},{1,9},{5... | collective-permute-start | bytes 196616 | tf_op jit(solution)/shard_map/ppermute | solution.py:26
  25.4 2.7 %collective-permute-start.9 = (bf16[256,128]{1,0:T(8,128)(2,1)S(1)}, bf16[256,128]{1,0:T(8,128)(2,1)S(1)}, u32[]{:S(2)}, u32[]{:S(2)}) collective-permute-start(bf16[256,128]{1,0:T(8,128)(2,1)S(1)} %get-tuple-element.42), channel_id=1, source_target_pairs={{0,16},{4,20},{8,24},{12,28},{16,0},{20,4},{24,8},{28,12},{1,17},{... | collective-permute-start | bytes 196616 | tf_op jit(solution)/shard_map/ppermute | solution.py:26
  28.1 0.6 %collective-permute-start.10 = (bf16[256,128]{1,0:T(8,128)(2,1)S(1)}, bf16[256,128]{1,0:T(8,128)(2,1)S(1)}, u32[]{:S(2)}, u32[]{:S(2)}) collective-permute-start(bf16[256,128]{1,0:T(8,128)(2,1)S(1)} %get-tuple-element.43), channel_id=1, source_target_pairs={{0,24},{4,28},{8,16},{12,20},{16,8},{20,12},{24,0},{28,4},{1,25},{... | collective-permute-start | bytes 196616 | tf_op jit(solution)/shard_map/ppermute | solution.py:26
  28.7 2.0 %collective-permute-done.3.got_ref = bf16[4,256,128]{2,1,0:T(8,128)(2,1)S(1)} collective-permute-done((bf16[4,256,128]{2,1,0:T(8,128)(2,1)S(1)}, bf16[4,256,128]{2,1,0:T(8,128)(2,1)S(1)}, u32[]{:S(2)}, u32[]{:S(2)}) %collective-permute-start.3) | collective-permute-done | bytes 262176 | tf_op jit(solution)/shard_map/ppermute | solution.py:26
  30.7 0.0 copy-done.2
  30.7 0.6 %halve_sums.2 = (f32[256,128]{1,0:T(8,128)S(1)}, bf16[256,128]{1,0:T(8,128)(2,1)S(1)}, bf16[256,128]{1,0:T(8,128)(2,1)S(1)}, bf16[256,128]{1,0:T(8,128)(2,1)S(1)}) custom-call(s32[19]{0:T(128)S(1)} %pad_add_fusion.meta_ref, bf16[4,256,128]{2,1,0:T(8,128)(2,1)S(1)} %copy-done.2, bf16[4,256,128]{2,1,0:T(8,128)(2,1)S(1)} %collective-permute-done.3.got_ref), custom_call_target="tpu_custom_call" | custom-call | flops 131072 | bytes 786432 | tf_op jit(solution)/shard_map/halve_sums/pallas_call | solution.py:181
  31.3 1.1 %collective-permute-start.4 = (bf16[256,128]{1,0:T(8,128)(2,1)S(1)}, bf16[256,128]{1,0:T(8,128)(2,1)S(1)}, u32[]{:S(2)}, u32[]{:S(2)}) collective-permute-start(bf16[256,128]{1,0:T(8,128)(2,1)S(1)} %get-tuple-element.36), channel_id=1, source_target_pairs={{0,8},{4,12},{8,0},{12,4},{16,24},{20,28},{24,16},{28,20},{1,9},{5... | collective-permute-start | bytes 196616 | tf_op jit(solution)/shard_map/ppermute | solution.py:26
  32.5 2.7 %collective-permute-start.5 = (bf16[256,128]{1,0:T(8,128)(2,1)S(1)}, bf16[256,128]{1,0:T(8,128)(2,1)S(1)}, u32[]{:S(2)}, u32[]{:S(2)}) collective-permute-start(bf16[256,128]{1,0:T(8,128)(2,1)S(1)} %get-tuple-element.37), channel_id=1, source_target_pairs={{0,16},{4,20},{8,24},{12,28},{16,0},{20,4},{24,8},{28,12},{1,17},{... | collective-permute-start | bytes 196616 | tf_op jit(solution)/shard_map/ppermute | solution.py:26
  35.1 0.0 collective-permute-done.8.refs_1_
  35.1 0.6 %collective-permute-start.6 = (bf16[256,128]{1,0:T(8,128)(2,1)S(1)}, bf16[256,128]{1,0:T(8,128)(2,1)S(1)}, u32[]{:S(2)}, u32[]{:S(2)}) collective-permute-start(bf16[256,128]{1,0:T(8,128)(2,1)S(1)} %get-tuple-element.38), channel_id=1, source_target_pairs={{0,24},{4,28},{8,16},{12,20},{16,8},{20,12},{24,0},{28,4},{1,25},{... | collective-permute-start | bytes 196616 | tf_op jit(solution)/shard_map/ppermute | solution.py:26
  35.8 0.0 collective-permute-done.9.refs_2_
  35.8 0.0 collective-permute-done.10.refs_3_
  35.8 0.0 copy-done.7
  35.8 0.0 copy-start
  35.8 7.3 %ridge_reads.1 = (f32[512,256]{1,0:T(8,128)S(1)}, bf16[512,256]{1,0:T(8,128)(2,1)S(1)}) custom-call(f32[2]{0:T(128)S(1)} %copy-done.7, f32[256,128]{1,0:T(8,128)S(1)} %get-tuple-element.40.refs_0_, bf16[256,128]{1,0:T(8,128)(2,1)S(1)} %collective-permute-done.8.refs_1_, bf16[256,128]{1,0:T(8,128)(2,1)S(1)} %collective-permute-done.9.refs_2_, ...), custom_call_target="tpu_custom_call" | custom-call | flops 6442450944 | bytes 8388608 | tf_op jit(solution)/shard_map/ridge_reads/pallas_call | solution.py:406
  43.1 0.0 collective-permute-done.4.refs_1_
  43.1 0.0 collective-permute-done.5.refs_2_
  43.1 0.0 collective-permute-done.6.refs_3_
  43.1 0.3 cross_reads.1
  43.4 0.1 collective-permute-start.11
  43.4 0.6 %collective-permute-start.12 = (bf16[128,256]{1,0:T(8,128)(2,1)S(1)}, bf16[128,256]{1,0:T(8,128)(2,1)S(1)}, u32[]{:S(2)}, u32[]{:S(2)}) collective-permute-start(bf16[128,256]{1,0:T(8,128)(2,1)S(1)} %get-tuple-element.55), channel_id=1, source_target_pairs={{0,2},{1,3},{2,0},{3,1},{4,6},{5,7},{6,4},{7,5},{8,10},{9,11},{10,... | collective-permute-start | bytes 196616 | tf_op jit(solution)/shard_map/ppermute | solution.py:26
  44.0 1.3 %collective-permute-start.13 = (bf16[128,256]{1,0:T(8,128)(2,1)S(1)}, bf16[128,256]{1,0:T(8,128)(2,1)S(1)}, u32[]{:S(2)}, u32[]{:S(2)}) collective-permute-start(bf16[128,256]{1,0:T(8,128)(2,1)S(1)} %get-tuple-element.56), channel_id=1, source_target_pairs={{0,3},{1,2},{2,1},{3,0},{4,7},{5,6},{6,5},{7,4},{8,11},{9,10},{10,... | collective-permute-start | bytes 196616 | tf_op jit(solution)/shard_map/ppermute | solution.py:26
  45.3 0.0 collective-permute-done.11.refs_1_
  45.3 3.1 %collective-permute-done.12.refs_2_ = bf16[128,256]{1,0:T(8,128)(2,1)S(1)} collective-permute-done((bf16[128,256]{1,0:T(8,128)(2,1)S(1)}, bf16[128,256]{1,0:T(8,128)(2,1)S(1)}, u32[]{:S(2)}, u32[]{:S(2)}) %collective-permute-start.12) | collective-permute-done | bytes 65568 | tf_op jit(solution)/shard_map/ppermute | solution.py:26
  48.4 0.5 collective-permute-done.13.refs_3_
  48.9 0.0 copy-done
  48.9 1.2 %output_rows.1 = bf16[128,1024]{1,0:T(8,128)(2,1)} custom-call(s32[1]{0:T(128)} %bitcast.place_ref, bf16[128,1024]{1,0:T(8,128)(2,1)S(1)} %copy-done.1, bf16[1024,1024]{1,0:T(8,128)(2,1)S(1)} %copy-done, bf16[128,256]{1,0:T(8,128)(2,1)S(1)} %get-tuple-element.53.refs_0_, bf16[128,256]{1,0:T(8,128)(2,1)S(1)} %collective-permute-done.11.refs_1_, ...), custom_call_target="tpu_custom_call" | custom-call | flops 268435456 | bytes 2883584 | tf_op jit(solution)/shard_map/output_rows/pallas_call | solution.py:474
  (4 shorter events, 0.0 us)
Async XLA Ops:
  0.0 14.1 %collective-permute-start.1 = (bf16[128,1024]{1,0:T(8,128)(2,1)}, bf16[128,1024]{1,0:T(8,128)(2,1)S(1)}, u32[]{:S(2)}, u32[]{:S(2)}) collective-permute-start(bf16[128,1024]{1,0:T(8,128)(2,1)} %tokens_ref.1), channel_id=1, source_target_pairs={{0,2},{1,3},{2,0},{3,1},{4,6},{5,7},{6,4},{7,5},{8,10},{9,11},{10,... | collective-permute-start | bytes 786440 | tf_op jit(solution)/shard_map/ppermute | solution.py:26
  2.9 14.2 %collective-permute-start = (bf16[128,1024]{1,0:T(8,128)(2,1)}, bf16[128,1024]{1,0:T(8,128)(2,1)S(1)}, u32[]{:S(2)}, u32[]{:S(2)}) collective-permute-start(bf16[128,1024]{1,0:T(8,128)(2,1)} %tokens_ref.1), channel_id=1, source_target_pairs={{0,1},{1,0},{2,3},{3,2},{4,5},{5,4},{6,7},{7,6},{8,9},{9,8},{10,11... | collective-permute-start | bytes 786440 | tf_op jit(solution)/shard_map/ppermute | solution.py:26
  4.6 12.3 %copy-start.8 = (bf16[1024,16]{0,1:T(8,128)(2,1)S(1)}, bf16[1024,16]{0,1:T(8,128)(2,1)}, u32[]{:S(2)}) copy-start(bf16[1024,16]{0,1:T(8,128)(2,1)} %param.18) | copy-start | bytes 98308
  4.6 12.5 %copy-start.1 = (bf16[128,1024]{1,0:T(8,128)(2,1)S(1)}, bf16[128,1024]{1,0:T(8,128)(2,1)}, u32[]{:S(2)}) copy-start(bf16[128,1024]{1,0:T(8,128)(2,1)} %tokens_ref.1) | copy-start | bytes 786436
  4.6 12.5 %copy-start.3 = (f32[4,3072]{1,0:T(4,128)S(1)}, f32[4,3072]{1,0:T(4,128)}, u32[]{:S(2)}) copy-start(f32[4,3072]{1,0:T(4,128)} %refs_7_.1) | copy-start | bytes 147460
  4.7 12.5 %copy-start.4 = (bf16[1,3,3072]{2,1,0:T(4,128)(2,1)S(1)}, bf16[1,3,3072]{2,1,0:T(4,128)(2,1)}, u32[]{:S(2)}) copy-start(bf16[1,3,3072]{2,1,0:T(4,128)(2,1)} %refs_8_.1) | copy-start | bytes 55300
  4.7 12.5 %copy-start.5 = (f32[1024]{0:T(1024)S(1)}, f32[1024]{0:T(1024)}, u32[]{:S(2)}) copy-start(f32[1024]{0:T(1024)} %param.16) | copy-start | bytes 12292
  4.7 12.5 %copy-start.6 = (f32[8]{0:T(128)S(1)}, f32[8]{0:T(128)}, u32[]{:S(2)}) copy-start(f32[8]{0:T(128)} %rate_ref.1) | copy-start | bytes 100
  14.1 3.0 %collective-permute-start.2 = (bf16[128,1024]{1,0:T(8,128)(2,1)S(1)}, bf16[128,1024]{1,0:T(8,128)(2,1)S(1)}, u32[]{:S(2)}, u32[]{:S(2)}) collective-permute-start(bf16[128,1024]{1,0:T(8,128)(2,1)S(1)} %hold.1.refs_2_), channel_id=1, source_target_pairs={{0,1},{1,0},{2,3},{3,2},{4,5},{5,4},{6,7},{7,6},{8,9},{9,8},{10,11... | collective-permute-start | bytes 786440 | tf_op jit(solution)/shard_map/ppermute | solution.py:26
  14.7 9.0 %collective-permute-start.7 = (bf16[4,256,128]{2,1,0:T(8,128)(2,1)S(1)}, bf16[4,256,128]{2,1,0:T(8,128)(2,1)S(1)}, u32[]{:S(2)}, u32[]{:S(2)}) collective-permute-start(bf16[4,256,128]{2,1,0:T(8,128)(2,1)S(1)} %get-tuple-element.39), channel_id=1, source_target_pairs={{0,4},{4,0},{8,12},{12,8},{16,20},{20,16},{24,28},{28,24},{1,5},{5... | collective-permute-start | bytes 786440 | tf_op jit(solution)/shard_map/ppermute | solution.py:26
  17.2 13.5 %copy-start.2 = (bf16[4,256,128]{2,1,0:T(8,128)(2,1)S(1)}, bf16[4,256,128]{2,1,0:T(8,128)(2,1)}, u32[]{:S(2)}) copy-start(bf16[4,256,128]{2,1,0:T(8,128)(2,1)} %get-tuple-element.31.keep_ref) | copy-start | bytes 786436
  17.2 18.6 %copy-start.7 = (f32[2]{0:T(128)S(1)}, f32[2]{0:T(128)}, u32[]{:S(2)}) copy-start(f32[2]{0:T(128)} %ridge_ref.1) | copy-start | bytes 28
  22.6 8.1 %collective-permute-start.3 = (bf16[4,256,128]{2,1,0:T(8,128)(2,1)S(1)}, bf16[4,256,128]{2,1,0:T(8,128)(2,1)S(1)}, u32[]{:S(2)}, u32[]{:S(2)}) collective-permute-start(bf16[4,256,128]{2,1,0:T(8,128)(2,1)S(1)} %get-tuple-element.34), channel_id=1, source_target_pairs={{0,4},{4,0},{8,12},{12,8},{16,20},{20,16},{24,28},{28,24},{1,5},{5... | collective-permute-start | bytes 786440 | tf_op jit(solution)/shard_map/ppermute | solution.py:26
  24.3 10.9 %collective-permute-start.8 = (bf16[256,128]{1,0:T(8,128)(2,1)S(1)}, bf16[256,128]{1,0:T(8,128)(2,1)S(1)}, u32[]{:S(2)}, u32[]{:S(2)}) collective-permute-start(bf16[256,128]{1,0:T(8,128)(2,1)S(1)} %get-tuple-element.41), channel_id=1, source_target_pairs={{0,8},{4,12},{8,0},{12,4},{16,24},{20,28},{24,16},{28,20},{1,9},{5... | collective-permute-start | bytes 196616 | tf_op jit(solution)/shard_map/ppermute | solution.py:26
  25.4 10.4 %collective-permute-start.9 = (bf16[256,128]{1,0:T(8,128)(2,1)S(1)}, bf16[256,128]{1,0:T(8,128)(2,1)S(1)}, u32[]{:S(2)}, u32[]{:S(2)}) collective-permute-start(bf16[256,128]{1,0:T(8,128)(2,1)S(1)} %get-tuple-element.42), channel_id=1, source_target_pairs={{0,16},{4,20},{8,24},{12,28},{16,0},{20,4},{24,8},{28,12},{1,17},{... | collective-permute-start | bytes 196616 | tf_op jit(solution)/shard_map/ppermute | solution.py:26
  28.1 7.6 %collective-permute-start.10 = (bf16[256,128]{1,0:T(8,128)(2,1)S(1)}, bf16[256,128]{1,0:T(8,128)(2,1)S(1)}, u32[]{:S(2)}, u32[]{:S(2)}) collective-permute-start(bf16[256,128]{1,0:T(8,128)(2,1)S(1)} %get-tuple-element.43), channel_id=1, source_target_pairs={{0,24},{4,28},{8,16},{12,20},{16,8},{20,12},{24,0},{28,4},{1,25},{... | collective-permute-start | bytes 196616 | tf_op jit(solution)/shard_map/ppermute | solution.py:26
  31.3 11.8 %collective-permute-start.4 = (bf16[256,128]{1,0:T(8,128)(2,1)S(1)}, bf16[256,128]{1,0:T(8,128)(2,1)S(1)}, u32[]{:S(2)}, u32[]{:S(2)}) collective-permute-start(bf16[256,128]{1,0:T(8,128)(2,1)S(1)} %get-tuple-element.36), channel_id=1, source_target_pairs={{0,8},{4,12},{8,0},{12,4},{16,24},{20,28},{24,16},{28,20},{1,9},{5... | collective-permute-start | bytes 196616 | tf_op jit(solution)/shard_map/ppermute | solution.py:26
  32.5 10.6 %collective-permute-start.5 = (bf16[256,128]{1,0:T(8,128)(2,1)S(1)}, bf16[256,128]{1,0:T(8,128)(2,1)S(1)}, u32[]{:S(2)}, u32[]{:S(2)}) collective-permute-start(bf16[256,128]{1,0:T(8,128)(2,1)S(1)} %get-tuple-element.37), channel_id=1, source_target_pairs={{0,16},{4,20},{8,24},{12,28},{16,0},{20,4},{24,8},{28,12},{1,17},{... | collective-permute-start | bytes 196616 | tf_op jit(solution)/shard_map/ppermute | solution.py:26
  35.1 7.9 %collective-permute-start.6 = (bf16[256,128]{1,0:T(8,128)(2,1)S(1)}, bf16[256,128]{1,0:T(8,128)(2,1)S(1)}, u32[]{:S(2)}, u32[]{:S(2)}) collective-permute-start(bf16[256,128]{1,0:T(8,128)(2,1)S(1)} %get-tuple-element.38), channel_id=1, source_target_pairs={{0,24},{4,28},{8,16},{12,20},{16,8},{20,12},{24,0},{28,4},{1,25},{... | collective-permute-start | bytes 196616 | tf_op jit(solution)/shard_map/ppermute | solution.py:26
  35.8 13.1 %copy-start = (bf16[1024,1024]{1,0:T(8,128)(2,1)S(1)}, bf16[1024,1024]{1,0:T(8,128)(2,1)}, u32[]{:S(2)}) copy-start(bf16[1024,1024]{1,0:T(8,128)(2,1)} %w_ref.1) | copy-start | bytes 6291460
  43.4 1.9 %collective-permute-start.11 = (bf16[128,256]{1,0:T(8,128)(2,1)S(1)}, bf16[128,256]{1,0:T(8,128)(2,1)S(1)}, u32[]{:S(2)}, u32[]{:S(2)}) collective-permute-start(bf16[128,256]{1,0:T(8,128)(2,1)S(1)} %get-tuple-element.54), channel_id=1, source_target_pairs={{0,1},{1,0},{2,3},{3,2},{4,5},{5,4},{6,7},{7,6},{8,9},{9,8},{10,11... | collective-permute-start | bytes 196616 | tf_op jit(solution)/shard_map/ppermute | solution.py:26
  43.4 5.0 %collective-permute-start.12 = (bf16[128,256]{1,0:T(8,128)(2,1)S(1)}, bf16[128,256]{1,0:T(8,128)(2,1)S(1)}, u32[]{:S(2)}, u32[]{:S(2)}) collective-permute-start(bf16[128,256]{1,0:T(8,128)(2,1)S(1)} %get-tuple-element.55), channel_id=1, source_target_pairs={{0,2},{1,3},{2,0},{3,1},{4,6},{5,7},{6,4},{7,5},{8,10},{9,11},{10,... | collective-permute-start | bytes 196616 | tf_op jit(solution)/shard_map/ppermute | solution.py:26
  44.0 4.9 %collective-permute-start.13 = (bf16[128,256]{1,0:T(8,128)(2,1)S(1)}, bf16[128,256]{1,0:T(8,128)(2,1)S(1)}, u32[]{:S(2)}, u32[]{:S(2)}) collective-permute-start(bf16[128,256]{1,0:T(8,128)(2,1)S(1)} %get-tuple-element.56), channel_id=1, source_target_pairs={{0,3},{1,2},{2,1},{3,0},{4,7},{5,6},{6,5},{7,4},{8,11},{9,10},{10,... | collective-permute-start | bytes 196616 | tf_op jit(solution)/shard_map/ppermute | solution.py:26

commit v4 on v3

--- a/solution.py
+++ b/solution.py
@@ -62,22 +62,49 @@
     )
 
 
-def sums_kernel(heads, owners, slots, code_ref, meta_ref, keys_ref, values_ref, prompt_ref,
-                send_gram, send_cross, keep_gram, keep_cross, acc_ref, stored_ref, sem):
-    step = pl.program_id(0)
-    pages, rows = keys_ref.shape[0], keys_ref.shape[1]
-    load_prompt = pltpu.make_async_copy(prompt_ref, stored_ref, sem)
+def sums_kernel(heads, owners, pages, table_ref, keys_hbm, values_hbm,
+                prompt_hbm, send_gram, send_cross, keep_gram, keep_cross,
+                acc_ref, keys_ref, values_ref, stored_ref, code_ref, key_sem, value_sem, sem):
+    pool, rows = keys_ref.shape[0], keys_ref.shape[1]
+    blocks = pool // pages
+    slots = table_ref.shape[1]
+    mine = lax.axis_index("grp")
+
+    def load(block):
+        at = pl.ds(block * pages, pages)
+        return (
+            pltpu.make_async_copy(keys_hbm.at[at], keys_ref.at[at], key_sem.at[block]),
+            pltpu.make_async_copy(values_hbm.at[at], values_ref.at[at], value_sem.at[block]),
+        )
+
+    for block in range(blocks):
+        for copy in load(block):
+            copy.start()
+    load_prompt = pltpu.make_async_copy(prompt_hbm, stored_ref, sem)
+    load_prompt.start()
+    acc_ref[...] = jnp.zeros_like(acc_ref)
+
+    first = mine * pool
+    wide = 16
+    for owner in range(owners):
+
+        def note(chunk, carry):
+            for i in range(wide):
+                slot = chunk * wide + i
+                page = table_ref[owner, slot] - first
+                inside = (page >= 0) & (page < pool)
+                code_ref[jnp.where(inside, page, pool)] = owner * slots + slot
+            return carry
+
+        lax.fori_loop(0, slots // wide, note, 0)
+
     lane = lax.broadcasted_iota(jnp.int32, (HDIM, rows), 1)
 
-    @pl.when(step == 0)
-    def _():
-        load_prompt.start()
-        acc_ref[...] = jnp.zeros_like(acc_ref)
-
     def place(page):
-        code = code_ref[step * pages + page]
-        owner, slot = code // slots, code % slots
-        return owner, jnp.clip(meta_ref[owners + owner] - slot * PAGE, 0, PAGE)
+        code = code_ref[page]
+        owner = lax.div(code, jnp.int32(slots))
+        slot = code - owner * slots
+        return owner, jnp.clip(table_ref[owners, owner] - slot * PAGE, 0, PAGE)
 
     def add(page, owner, turned):
         zero = jnp.zeros_like(turned)
@@ -89,73 +116,79 @@
         right = jnp.concatenate([keys_ref[page], values_ref[page]], axis=1)
         acc_ref[owner] += dot(left, right)
 
-    partial = jnp.int32(0)
-    for page in range(pages):
-        owner, live = place(page)
-        add(page, jnp.where(live == PAGE, owner, owners), keys_ref[page].T)
-        partial = partial | ((live > 0) & (live < PAGE)).astype(jnp.int32)
-
-    @pl.when(partial > 0)
-    def _():
-        def one_page(page, carry):
+    def one_block(block, carry):
+        for copy in load(block):
+            copy.wait()
+        partial = jnp.int32(0)
+        for i in range(pages):
+            page = block * pages + i
             owner, live = place(page)
-
-            @pl.when((live > 0) & (live < PAGE))
+            add(page, jnp.where(live == PAGE, owner, owners), keys_ref[page].T)
+            partial = partial | ((live > 0) & (live < PAGE)).astype(jnp.int32)
+
+        @pl.when(partial > 0)
+        def _():
+            def one_page(page, inner):
+                owner, live = place(page)
+
+                @pl.when((live > 0) & (live < PAGE))
+                def _():
+                    turned = keys_ref[page].T
+                    add(page, owner, jnp.where(lane < live * heads, turned, jnp.zeros_like(turned)))
+
+                return inner
+
+            lax.fori_loop(block * pages, (block + 1) * pages, one_page, 0)
+
+        return carry
+
+    lax.fori_loop(0, blocks, one_block, 0)
+    load_prompt.wait()
+    stored = stored_ref.shape[0]
+
+    def add_prompt(owner, carry):
+        for slot in range(stored):
+
+            @pl.when(table_ref[owners + 1, owner] == mine * stored + slot)
             def _():
-                turned = keys_ref[page].T
-                add(page, owner, jnp.where(lane < live * heads, turned, jnp.zeros_like(turned)))
-
-            return carry
-
-        lax.fori_loop(0, pages, one_page, 0)
-
-    @pl.when(step == pl.num_programs(0) - 1)
-    def _():
-        load_prompt.wait()
-        mine, bit = meta_ref[2 * owners], meta_ref[2 * owners + 1]
-        stored = stored_ref.shape[0]
-
-        def add_prompt(owner, carry):
-            for slot in range(stored):
-
-                @pl.when(meta_ref[owner] == mine * stored + slot)
-                def _():
-                    for head in range(heads):
-                        at = slice(head * HDIM, (head + 1) * HDIM)
-                        acc_ref[owner, at, :HDIM] += stored_ref[slot, head, 0]
-                        acc_ref[owner, at, HDIM:] += stored_ref[slot, head, 1].T
-
-            return carry
-
-        lax.fori_loop(0, owners, add_prompt, 0)
-        for pair in range(owners // 2):
-            there, here = 2 * pair + 1 - bit, 2 * pair + bit
-            send_gram[pair] = acc_ref[there, :, :HDIM].astype(BF16)
-            send_cross[pair] = acc_ref[there, :, HDIM:].astype(BF16)
-            keep_gram[pair] = acc_ref[here, :, :HDIM].astype(BF16)
-            keep_cross[pair] = acc_ref[here, :, HDIM:].astype(BF16)
-
-
-def page_sums(code, meta, keys, values, prompt_state, owners, slots):
+                for head in range(heads):
+                    at = slice(head * HDIM, (head + 1) * HDIM)
+                    acc_ref[owner, at, :HDIM] += stored_ref[slot, head, 0]
+                    acc_ref[owner, at, HDIM:] += stored_ref[slot, head, 1].T
+
+        return carry
+
+    lax.fori_loop(0, owners, add_prompt, 0)
+    bit = mine & 1
+    for pair in range(owners // 2):
+        there, here = 2 * pair + 1 - bit, 2 * pair + bit
+        send_gram[pair] = acc_ref[there, :, :HDIM].astype(BF16)
+        send_cross[pair] = acc_ref[there, :, HDIM:].astype(BF16)
+        keep_gram[pair] = acc_ref[here, :, :HDIM].astype(BF16)
+        keep_cross[pair] = acc_ref[here, :, HDIM:].astype(BF16)
+
+
+def page_sums(table, keys, values, prompt_state, owners):
     pool, rows, _ = keys.shape
     heads = prompt_state.shape[1]
     pages = 8
     half = (owners // 2, heads * HDIM, HDIM)
-    page_spec = pl.BlockSpec((pages, rows, HDIM), lambda i, *_: (i, 0, 0))
-    out_spec = pl.BlockSpec(half, lambda i, *_: (0, 0, 0))
-    return pl.pallas_call(
-        functools.partial(sums_kernel, heads, owners, slots),
-        grid_spec=pltpu.PrefetchScalarGridSpec(
-            num_scalar_prefetch=2,
-            grid=(pool // pages,),
-            in_specs=[page_spec, page_spec, pl.BlockSpec(memory_space=pl.ANY)],
-            out_specs=[out_spec] * 4,
-            scratch_shapes=[
-                pltpu.VMEM((owners + 1, heads * HDIM, 2 * HDIM), F32),
-                pltpu.VMEM(prompt_state.shape, F32),
-                pltpu.SemaphoreType.DMA,
-            ],
-        ),
+    small = pl.BlockSpec(memory_space=pltpu.SMEM)
+    anywhere = pl.BlockSpec(memory_space=pl.ANY)
+    return pl.pallas_call(
+        functools.partial(sums_kernel, heads, owners, pages),
+        in_specs=[small] + [anywhere] * 3,
+        out_specs=[pl.BlockSpec(memory_space=pltpu.VMEM)] * 4,
+        scratch_shapes=[
+            pltpu.VMEM((owners + 1, heads * HDIM, 2 * HDIM), F32),
+            pltpu.VMEM(keys.shape, BF16),
+            pltpu.VMEM(values.shape, BF16),
+            pltpu.VMEM(prompt_state.shape, F32),
+            pltpu.SMEM((pool + 1,), jnp.int32),
+            pltpu.SemaphoreType.DMA((pool // pages,)),
+            pltpu.SemaphoreType.DMA((pool // pages,)),
+            pltpu.SemaphoreType.DMA,
+        ],
         out_shape=[jax.ShapeDtypeStruct(half, BF16)] * 4,
         compiler_params=pltpu.CompilerParams(vmem_limit_bytes=PAGE_VMEM * 2**20),
         cost_estimate=pl.CostEstimate(
@@ -164,23 +197,23 @@
             transcendentals=0,
         ),
         name="page_sums",
-    )(code, meta, keys, values, prompt_state)
-
-
-def halve_kernel(owners, meta_ref, keep_ref, got_ref, *outs):
+    )(table, keys, values, prompt_state)
+
+
+def halve_kernel(keep_ref, got_ref, *outs):
     for distance, out_ref in enumerate(outs):
-        row = meta_ref[2 * owners + 2] ^ distance
+        row = (lax.axis_index("grp") >> 1) ^ distance
         total = keep_ref[row].astype(F32) + got_ref[row].astype(F32)
         out_ref[...] = total.astype(out_ref.dtype)
 
 
-def halve_sums(meta, keep, got):
+def halve_sums(keep, got):
     count, rows, cols = keep.shape
     outs = [jax.ShapeDtypeStruct((rows, cols), F32 if i == 0 else BF16) for i in range(count)]
     whole = pl.BlockSpec(memory_space=pltpu.VMEM)
     return pl.pallas_call(
-        functools.partial(halve_kernel, 2 * count),
-        in_specs=[pl.BlockSpec(memory_space=pltpu.SMEM), whole, whole],
+        halve_kernel,
+        in_specs=[whole, whole],
         out_specs=[whole] * count,
         out_shape=outs,
         compiler_params=pltpu.CompilerParams(vmem_limit_bytes=32 * 2**20),
@@ -188,7 +221,7 @@
             flops=count * rows * cols, bytes_accessed=6 * count * rows * cols, transcendentals=0
         ),
         name="halve_sums",
-    )(meta, keep, got)
+    )(keep, got)
 
 
 def token_kernel(heads, place_ref, rate_ref, *refs):
@@ -506,28 +539,16 @@
     head_count = lax.axis_size("head")
     owners = lax.axis_size("grp")
     me = lax.axis_index("head").astype(jnp.int32)
-    group = lax.axis_index("grp").astype(jnp.int32)
     place = me.reshape(1)
-    extra = jnp.arange(3, dtype=jnp.int32)
-    own = jnp.where(extra == 0, group, jnp.where(extra == 1, group & 1, group >> 1))
-    meta = (
-        jnp.pad(group_prompt, (0, owners + 3))
-        + jnp.pad(cache_lengths, (owners, 3))
-        + jnp.pad(own, (2 * owners, 0))
-    )
-
     bits = [head_count >> i for i in range(1, head_count.bit_length())]
     blocks = {0: tokens}
     for bit in bits:
         blocks[bit] = swap(tokens, "head", bit)
 
     pool, page, heads, _ = cache_keys.shape
-    slots = page_table.shape[1]
-    ids = group * pool + jnp.arange(pool, dtype=jnp.int32)
-    tag = jnp.arange(owners * slots, dtype=jnp.int32).reshape(owners, slots, 1)
-    code = jnp.sum(
-        jnp.where(page_table[:, :, None] == ids, tag, 0), axis=(0, 1), dtype=jnp.int32
-    )
+    spare = (0, page_table.shape[1] - owners)
+    rows = [jnp.pad(row, spare)[None] for row in (cache_lengths, group_prompt)]
+    table = jnp.concatenate([page_table] + rows, axis=0)
     keys = cache_keys.reshape(pool, page * heads, HDIM)
     values = cache_values.reshape(pool, page * heads, HDIM)
 
@@ -535,7 +556,7 @@
         return [parts[0]] + [swap(parts[i], "grp", 2 * i) for i in range(1, owners // 2)]
 
     send_gram, send_cross, keep_gram, keep_cross = page_sums(
-        code, meta, keys, values, prompt_state, owners, slots
+        table, keys, values, prompt_state, owners
     )
     got_gram = swap(send_gram, "grp", 1)
     for bit in bits[1:]:
@@ -547,8 +568,8 @@
     send_cross, *vectors = token_vectors(
         place, decay_rate, blocks, norm_gain, w_qkv, w_gates, conv_weight, conv_state, send_cross
     )
-    grams = halve_sums(meta, keep_gram, got_gram)
-    crosses = halve_sums(meta, keep_cross, swap(send_cross, "grp", 1))
+    grams = halve_sums(keep_gram, got_gram)
+    crosses = halve_sums(keep_cross, swap(send_cross, "grp", 1))
     base, solved = ridge_reads(ridge, scattered(grams), vectors, [crosses[0]])
     reads = cross_reads(place, scattered(crosses), base, solved, head_count)
     reads = [reads[0]] + [swap(reads[i], "head", i) for i in range(1, head_count)]

time: 50.2 us -> 48.5 us (0.966)
  Pallas kernels: 24.7 us -> 23.2 us
  other arithmetic: 1.67 us -> 0.69 us
  local copies, waits for them, and re-layouts: 0.22 us -> 0.89 us
  waiting for transfers between devices: 5.61 us -> 6.27 us
    pallas_call x3, Pallas kernels: 10.6 us -> 9.13 us  [the longest x1 9 us: page_sums(): pl.pallas_call(functools.partial(sums_kernel, heads, owners, pages), in_s...]
    reduce_sum x1 -> x0, other arithmetic: 0.9 us -> none  [shards(): jnp.sum(jnp.where(page_table[:, :, None] == ids, tag, 0), axis=(0, 1), dt...]
    add x2 -> x0, other arithmetic: 0.75 us -> none  [the longest x1 0.75 us: shards(): jnp.pad(group_prompt, (0, owners + 3)) + jnp.pad(cache_lengths, (owners, 3))]
    concatenate x0 -> x1, other arithmetic: none -> 0.69 us  [shards(): table = jnp.concatenate([page_table] + rows, axis=0)]
    broadcast_in_dim x0 -> x1, local copies, waits for them, and re-layouts: none -> 0.67 us  [shards(): rows = [jnp.pad(row, spare)[None] for row in (cache_lengths, group_prompt)]]
    ppermute x14, waiting for transfers between devices: 5.61 us -> 6.27 us  [swap(): return lax.ppermute(block, axis, [(i, i ^ distance) for i in range(size)])]
  transfers between devices with their start and end apart: 14 -> 14, of which waited for: 3 -> 4; matrix products, arithmetic and copies ran while one was open for 4% -> 3% of each run, Pallas kernels for 47% -> 45%
where the time goes in v4:
time: 48.5 us
  Pallas kernels  23.2 us (48%)
  starting transfers between devices  17.2 us (35%)
  waiting for transfers between devices  6.27 us (13%)
  local copies, waits for them, and re-layouts  0.89 us (2%)
  other arithmetic  0.69 us (1%)
    ppermute x14, starting transfers between devices, swap(): return lax.ppermute(block, axis, [(i, i ^ distance) for i in range(size)])  17.2 us
    pallas_call x1, Pallas kernels, page_sums(): pl.pallas_call(functools.partial(sums_kernel, heads, owners, pages), in_s...  9 us
    pallas_call x1, Pallas kernels, ridge_reads(): pl.pallas_call(functools.partial(read_kernel, heads, len(grams)), in_spec...  7.25 us
    ppermute x14, waiting for transfers between devices, swap(): return lax.ppermute(block, axis, [(i, i ^ distance) for i in range(size)])  6.27 us
    pallas_call x1, Pallas kernels, token_vectors(): pl.pallas_call(functools.partial(token_kernel, heads), grid_spec=pltpu.Pr...  5.44 us
    pallas_call x1, Pallas kernels, output_rows(): pl.pallas_call(output_kernel, in_specs=[pl.BlockSpec(memory_space=pltpu.S...  1.17 us
  transfers between devices with their start and end apart: 14, of which 4 were waited for; matrix products, arithmetic and copies ran while one was open for 3% of the time, Pallas kernels for 45%

profile of v4, /device:TPU:0, one launch (start us, length us, event | category | flops | bytes accessed | tf_op | source)
XLA Modules:
  0.0 48.5 jit_solution(6241481209635830296)
XLA Ops:
  0.0 2.9 %collective-permute-start.1 = (bf16[128,1024]{1,0:T(8,128)(2,1)}, bf16[128,1024]{1,0:T(8,128)(2,1)S(1)}, u32[]{:S(2)}, u32[]{:S(2)}) collective-permute-start(bf16[128,1024]{1,0:T(8,128)(2,1)} %tokens_ref.1), channel_id=1, source_target_pairs={{0,2},{1,3},{2,0},{3,1},{4,6},{5,7},{6,4},{7,5},{8,10},{9,11},{10,... | collective-permute-start | bytes 786440 | tf_op jit(solution)/shard_map/ppermute | solution.py:26
  2.9 0.0 collective-permute-start
  2.9 0.7 %pad_bitcast_fusion = (s32[1,64]{1,0:T(1,128)S(1)}, s32[1,64]{1,0:T(1,128)S(1)}) fusion(s32[8]{0:T(128)} %param.28, s32[8]{0:T(128)} %param.27), kind=kLoop, calls=%fused_computation.1 | loop fusion | bytes 576 | tf_op jit(solution)/shard_map/broadcast_in_dim | solution.py:550
  3.6 0.7 %pad_add_fusion.table_ref = s32[10,64]{1,0:T(8,128)S(1)} fusion(s32[1,64]{1,0:T(1,128)S(1)} %get-tuple-element.57, s32[1,64]{1,0:T(1,128)S(1)} %get-tuple-element.58, s32[8,64]{1,0:T(8,128)} %param.26), kind=kLoop, calls=%fused_computation | loop fusion | flops 1280 | bytes 5120 | tf_op jit(solution)/shard_map/concatenate | solution.py:551
  4.3 0.0 copy-start.8
  4.3 0.0 copy-start.1
  4.3 0.0 copy-start.3
  4.3 0.0 copy-start.4
  4.3 0.0 copy-start.5
  4.4 0.0 copy-start.6
  4.4 9.0 %page_sums.1 = (bf16[4,256,128]{2,1,0:T(8,128)(2,1)S(1)}, bf16[4,256,128]{2,1,0:T(8,128)(2,1)S(1)}, bf16[4,256,128]{2,1,0:T(8,128)(2,1)S(1)}, bf16[4,256,128]{2,1,0:T(8,128)(2,1)}) custom-call(s32[10,64]{1,0:T(8,128)S(1)} %pad_add_fusion.table_ref, bf16[64,256,128]{2,1,0:T(8,128)(2,1)} %bitcast.9, bf16[64,256,128]{2,1,0:T(8,128)(2,1)} %bitcast.10, ...), custom_call_target="tpu_custom_call" | custom-call | flops 4294967296 | bytes 8388608 | tf_op jit(solution)/shard_map/page_sums/pallas_call | solution.py:178
  13.4 0.0 collective-permute-done.1.refs_0_
  13.4 0.6 %collective-permute-start.2 = (bf16[128,1024]{1,0:T(8,128)(2,1)S(1)}, bf16[128,1024]{1,0:T(8,128)(2,1)S(1)}, u32[]{:S(2)}, u32[]{:S(2)}) collective-permute-start(bf16[128,1024]{1,0:T(8,128)(2,1)S(1)} %hold.1.refs_2_), channel_id=1, source_target_pairs={{0,1},{1,0},{2,3},{3,2},{4,5},{5,4},{6,7},{7,6},{8,9},{9,8},{10,11... | collective-permute-start | bytes 786440 | tf_op jit(solution)/shard_map/ppermute | solution.py:26
  14.0 0.9 %collective-permute-start.7 = (bf16[4,256,128]{2,1,0:T(8,128)(2,1)S(1)}, bf16[4,256,128]{2,1,0:T(8,128)(2,1)S(1)}, u32[]{:S(2)}, u32[]{:S(2)}) collective-permute-start(bf16[4,256,128]{2,1,0:T(8,128)(2,1)S(1)} %get-tuple-element.39), channel_id=1, source_target_pairs={{0,4},{4,0},{8,12},{12,8},{16,20},{20,16},{24,28},{28,24},{1,5},{5... | collective-permute-start | bytes 786440 | tf_op jit(solution)/shard_map/ppermute | solution.py:26
  14.9 0.0 copy-done.8
  14.9 0.2 copy.18.refs_6_
  15.1 0.0 collective-permute-done.refs_1_
  15.1 0.0 collective-permute-done.2.refs_3_
  15.1 0.0 copy-done.1
  15.1 0.0 copy-done.3
  15.1 0.0 copy-done.4
  15.1 0.0 copy-done.5
  15.1 0.0 copy-done.6
  15.2 0.0 copy-start.2
  15.2 0.0 copy-start.7
  15.2 5.4 %token_vectors.1 = (bf16[4,256,128]{2,1,0:T(8,128)(2,1)S(1)}, bf16[2,128,512]{2,1,0:T(8,128)(2,1)S(1)}, bf16[2,512,128]{2,1,0:T(8,128)(2,1)S(1)}, bf16[2,128,512...) custom-call(s32[1]{0:T(128)} %bitcast.place_ref, ...), custom_call_target="tpu_custom_call", output_to_operand_aliasing={{0}: (11, {})} | custom-call | flops 805306368 | bytes 6815744 | tf_op jit(solution)/shard_map/token_vectors/pallas_call | solution.py:329
  20.6 1.1 %collective-permute-start.3 = (bf16[4,256,128]{2,1,0:T(8,128)(2,1)S(1)}, bf16[4,256,128]{2,1,0:T(8,128)(2,1)S(1)}, u32[]{:S(2)}, u32[]{:S(2)}) collective-permute-start(bf16[4,256,128]{2,1,0:T(8,128)(2,1)S(1)} %get-tuple-element.34), channel_id=1, source_target_pairs={{0,4},{4,0},{8,12},{12,8},{16,20},{20,16},{24,28},{28,24},{1,5},{5... | collective-permute-start | bytes 786440 | tf_op jit(solution)/shard_map/ppermute | solution.py:26
  21.8 0.5 %collective-permute-done.7.got_ref = bf16[4,256,128]{2,1,0:T(8,128)(2,1)S(1)} collective-permute-done((bf16[4,256,128]{2,1,0:T(8,128)(2,1)S(1)}, bf16[4,256,128]{2,1,0:T(8,128)(2,1)S(1)}, u32[]{:S(2)}, u32[]{:S(2)}) %collective-permute-start.7) | collective-permute-done | bytes 262176 | tf_op jit(solution)/shard_map/ppermute | solution.py:26
  22.3 0.1 halve_sums.3
  22.3 1.5 %collective-permute-start.8 = (bf16[256,128]{1,0:T(8,128)(2,1)S(1)}, bf16[256,128]{1,0:T(8,128)(2,1)S(1)}, u32[]{:S(2)}, u32[]{:S(2)}) collective-permute-start(bf16[256,128]{1,0:T(8,128)(2,1)S(1)} %get-tuple-element.41), channel_id=1, source_target_pairs={{0,8},{4,12},{8,0},{12,4},{16,24},{20,28},{24,16},{28,20},{1,9},{5... | collective-permute-start | bytes 196616 | tf_op jit(solution)/shard_map/ppermute | solution.py:26
  23.9 3.0 %collective-permute-start.9 = (bf16[256,128]{1,0:T(8,128)(2,1)S(1)}, bf16[256,128]{1,0:T(8,128)(2,1)S(1)}, u32[]{:S(2)}, u32[]{:S(2)}) collective-permute-start(bf16[256,128]{1,0:T(8,128)(2,1)S(1)} %get-tuple-element.42), channel_id=1, source_target_pairs={{0,16},{4,20},{8,24},{12,28},{16,0},{20,4},{24,8},{28,12},{1,17},{... | collective-permute-start | bytes 196616 | tf_op jit(solution)/shard_map/ppermute | solution.py:26
  26.9 0.3 collective-permute-start.10
  27.2 2.1 %collective-permute-done.3.got_ref = bf16[4,256,128]{2,1,0:T(8,128)(2,1)S(1)} collective-permute-done((bf16[4,256,128]{2,1,0:T(8,128)(2,1)S(1)}, bf16[4,256,128]{2,1,0:T(8,128)(2,1)S(1)}, u32[]{:S(2)}, u32[]{:S(2)}) %collective-permute-start.3) | collective-permute-done | bytes 262176 | tf_op jit(solution)/shard_map/ppermute | solution.py:26
  29.3 0.0 copy-done.2
  29.3 0.1 halve_sums.2
  29.3 1.5 %collective-permute-start.4 = (bf16[256,128]{1,0:T(8,128)(2,1)S(1)}, bf16[256,128]{1,0:T(8,128)(2,1)S(1)}, u32[]{:S(2)}, u32[]{:S(2)}) collective-permute-start(bf16[256,128]{1,0:T(8,128)(2,1)S(1)} %get-tuple-element.36), channel_id=1, source_target_pairs={{0,8},{4,12},{8,0},{12,4},{16,24},{20,28},{24,16},{28,20},{1,9},{5... | collective-permute-start | bytes 196616 | tf_op jit(solution)/shard_map/ppermute | solution.py:26
  30.9 3.0 %collective-permute-start.5 = (bf16[256,128]{1,0:T(8,128)(2,1)S(1)}, bf16[256,128]{1,0:T(8,128)(2,1)S(1)}, u32[]{:S(2)}, u32[]{:S(2)}) collective-permute-start(bf16[256,128]{1,0:T(8,128)(2,1)S(1)} %get-tuple-element.37), channel_id=1, source_target_pairs={{0,16},{4,20},{8,24},{12,28},{16,0},{20,4},{24,8},{28,12},{1,17},{... | collective-permute-start | bytes 196616 | tf_op jit(solution)/shard_map/ppermute | solution.py:26
  33.9 0.0 collective-permute-done.8.refs_1_
  33.9 0.3 collective-permute-start.6
  34.2 0.0 collective-permute-done.9.refs_2_
  34.2 0.0 collective-permute-done.10.refs_3_
  34.2 0.0 copy-done.7
  34.2 0.0 copy-start
  34.2 7.3 %ridge_reads.1 = (f32[512,256]{1,0:T(8,128)S(1)}, bf16[512,256]{1,0:T(8,128)(2,1)S(1)}) custom-call(f32[2]{0:T(128)S(1)} %copy-done.7, f32[256,128]{1,0:T(8,128)S(1)} %get-tuple-element.40.refs_0_, bf16[256,128]{1,0:T(8,128)(2,1)S(1)} %collective-permute-done.8.refs_1_, bf16[256,128]{1,0:T(8,128)(2,1)S(1)} %collective-permute-done.9.refs_2_, ...), custom_call_target="tpu_custom_call" | custom-call | flops 6442450944 | bytes 8388608 | tf_op jit(solution)/shard_map/ridge_reads/pallas_call | solution.py:439
  41.5 0.0 collective-permute-done.4.refs_1_
  41.5 0.0 collective-permute-done.5.refs_2_
  41.5 0.0 collective-permute-done.6.refs_3_
  41.5 0.3 cross_reads.1
  41.8 0.1 collective-permute-start.11
  41.8 0.6 %collective-permute-start.12 = (bf16[128,256]{1,0:T(8,128)(2,1)S(1)}, bf16[128,256]{1,0:T(8,128)(2,1)S(1)}, u32[]{:S(2)}, u32[]{:S(2)}) collective-permute-start(bf16[128,256]{1,0:T(8,128)(2,1)S(1)} %get-tuple-element.55), channel_id=1, source_target_pairs={{0,2},{1,3},{2,0},{3,1},{4,6},{5,7},{6,4},{7,5},{8,10},{9,11},{10,... | collective-permute-start | bytes 196616 | tf_op jit(solution)/shard_map/ppermute | solution.py:26
  42.4 1.3 %collective-permute-start.13 = (bf16[128,256]{1,0:T(8,128)(2,1)S(1)}, bf16[128,256]{1,0:T(8,128)(2,1)S(1)}, u32[]{:S(2)}, u32[]{:S(2)}) collective-permute-start(bf16[128,256]{1,0:T(8,128)(2,1)S(1)} %get-tuple-element.56), channel_id=1, source_target_pairs={{0,3},{1,2},{2,1},{3,0},{4,7},{5,6},{6,5},{7,4},{8,11},{9,10},{10,... | collective-permute-start | bytes 196616 | tf_op jit(solution)/shard_map/ppermute | solution.py:26
  43.7 0.0 collective-permute-done.11.refs_1_
  43.7 3.1 %collective-permute-done.12.refs_2_ = bf16[128,256]{1,0:T(8,128)(2,1)S(1)} collective-permute-done((bf16[128,256]{1,0:T(8,128)(2,1)S(1)}, bf16[128,256]{1,0:T(8,128)(2,1)S(1)}, u32[]{:S(2)}, u32[]{:S(2)}) %collective-permute-start.12) | collective-permute-done | bytes 65568 | tf_op jit(solution)/shard_map/ppermute | solution.py:26
  46.8 0.5 %collective-permute-done.13.refs_3_ = bf16[128,256]{1,0:T(8,128)(2,1)S(1)} collective-permute-done((bf16[128,256]{1,0:T(8,128)(2,1)S(1)}, bf16[128,256]{1,0:T(8,128)(2,1)S(1)}, u32[]{:S(2)}, u32[]{:S(2)}) %collective-permute-start.13) | collective-permute-done | bytes 65568 | tf_op jit(solution)/shard_map/ppermute | solution.py:26
  47.3 0.0 copy-done
  47.3 1.2 %output_rows.1 = bf16[128,1024]{1,0:T(8,128)(2,1)} custom-call(s32[1]{0:T(128)} %bitcast.place_ref, bf16[128,1024]{1,0:T(8,128)(2,1)S(1)} %copy-done.1, bf16[1024,1024]{1,0:T(8,128)(2,1)S(1)} %copy-done, bf16[128,256]{1,0:T(8,128)(2,1)S(1)} %get-tuple-element.53.refs_0_, bf16[128,256]{1,0:T(8,128)(2,1)S(1)} %collective-permute-done.11.refs_1_, ...), custom_call_target="tpu_custom_call" | custom-call | flops 268435456 | bytes 2883584 | tf_op jit(solution)/shard_map/output_rows/pallas_call | solution.py:507
  (1 shorter events, 0.0 us)
Async XLA Ops:
  0.0 13.4 %collective-permute-start.1 = (bf16[128,1024]{1,0:T(8,128)(2,1)}, bf16[128,1024]{1,0:T(8,128)(2,1)S(1)}, u32[]{:S(2)}, u32[]{:S(2)}) collective-permute-start(bf16[128,1024]{1,0:T(8,128)(2,1)} %tokens_ref.1), channel_id=1, source_target_pairs={{0,2},{1,3},{2,0},{3,1},{4,6},{5,7},{6,4},{7,5},{8,10},{9,11},{10,... | collective-permute-start | bytes 786440 | tf_op jit(solution)/shard_map/ppermute | solution.py:26
  2.9 12.1 %collective-permute-start = (bf16[128,1024]{1,0:T(8,128)(2,1)}, bf16[128,1024]{1,0:T(8,128)(2,1)S(1)}, u32[]{:S(2)}, u32[]{:S(2)}) collective-permute-start(bf16[128,1024]{1,0:T(8,128)(2,1)} %tokens_ref.1), channel_id=1, source_target_pairs={{0,1},{1,0},{2,3},{3,2},{4,5},{5,4},{6,7},{7,6},{8,9},{9,8},{10,11... | collective-permute-start | bytes 786440 | tf_op jit(solution)/shard_map/ppermute | solution.py:26
  4.3 10.6 %copy-start.8 = (bf16[1024,16]{0,1:T(8,128)(2,1)S(1)}, bf16[1024,16]{0,1:T(8,128)(2,1)}, u32[]{:S(2)}) copy-start(bf16[1024,16]{0,1:T(8,128)(2,1)} %param.18) | copy-start | bytes 98308
  4.3 10.8 %copy-start.1 = (bf16[128,1024]{1,0:T(8,128)(2,1)S(1)}, bf16[128,1024]{1,0:T(8,128)(2,1)}, u32[]{:S(2)}) copy-start(bf16[128,1024]{1,0:T(8,128)(2,1)} %tokens_ref.1) | copy-start | bytes 786436
  4.3 10.8 %copy-start.3 = (f32[4,3072]{1,0:T(4,128)S(1)}, f32[4,3072]{1,0:T(4,128)}, u32[]{:S(2)}) copy-start(f32[4,3072]{1,0:T(4,128)} %refs_7_.1) | copy-start | bytes 147460
  4.3 10.8 %copy-start.4 = (bf16[1,3,3072]{2,1,0:T(4,128)(2,1)S(1)}, bf16[1,3,3072]{2,1,0:T(4,128)(2,1)}, u32[]{:S(2)}) copy-start(bf16[1,3,3072]{2,1,0:T(4,128)(2,1)} %refs_8_.1) | copy-start | bytes 55300
  4.3 10.8 %copy-start.5 = (f32[1024]{0:T(1024)S(1)}, f32[1024]{0:T(1024)}, u32[]{:S(2)}) copy-start(f32[1024]{0:T(1024)} %param.16) | copy-start | bytes 12292
  4.4 10.8 %copy-start.6 = (f32[8]{0:T(128)S(1)}, f32[8]{0:T(128)}, u32[]{:S(2)}) copy-start(f32[8]{0:T(128)} %rate_ref.1) | copy-start | bytes 100
  13.4 1.7 %collective-permute-start.2 = (bf16[128,1024]{1,0:T(8,128)(2,1)S(1)}, bf16[128,1024]{1,0:T(8,128)(2,1)S(1)}, u32[]{:S(2)}, u32[]{:S(2)}) collective-permute-start(bf16[128,1024]{1,0:T(8,128)(2,1)S(1)} %hold.1.refs_2_), channel_id=1, source_target_pairs={{0,1},{1,0},{2,3},{3,2},{4,5},{5,4},{6,7},{7,6},{8,9},{9,8},{10,11... | collective-permute-start | bytes 786440 | tf_op jit(solution)/shard_map/ppermute | solution.py:26
  14.0 8.3 %collective-permute-start.7 = (bf16[4,256,128]{2,1,0:T(8,128)(2,1)S(1)}, bf16[4,256,128]{2,1,0:T(8,128)(2,1)S(1)}, u32[]{:S(2)}, u32[]{:S(2)}) collective-permute-start(bf16[4,256,128]{2,1,0:T(8,128)(2,1)S(1)} %get-tuple-element.39), channel_id=1, source_target_pairs={{0,4},{4,0},{8,12},{12,8},{16,20},{20,16},{24,28},{28,24},{1,5},{5... | collective-permute-start | bytes 786440 | tf_op jit(solution)/shard_map/ppermute | solution.py:26
  15.2 14.1 %copy-start.2 = (bf16[4,256,128]{2,1,0:T(8,128)(2,1)S(1)}, bf16[4,256,128]{2,1,0:T(8,128)(2,1)}, u32[]{:S(2)}) copy-start(bf16[4,256,128]{2,1,0:T(8,128)(2,1)} %get-tuple-element.31.keep_ref) | copy-start | bytes 786436
  15.2 19.0 %copy-start.7 = (f32[2]{0:T(128)S(1)}, f32[2]{0:T(128)}, u32[]{:S(2)}) copy-start(f32[2]{0:T(128)} %ridge_ref.1) | copy-start | bytes 28
  20.6 8.7 %collective-permute-start.3 = (bf16[4,256,128]{2,1,0:T(8,128)(2,1)S(1)}, bf16[4,256,128]{2,1,0:T(8,128)(2,1)S(1)}, u32[]{:S(2)}, u32[]{:S(2)}) collective-permute-start(bf16[4,256,128]{2,1,0:T(8,128)(2,1)S(1)} %get-tuple-element.34), channel_id=1, source_target_pairs={{0,4},{4,0},{8,12},{12,8},{16,20},{20,16},{24,28},{28,24},{1,5},{5... | collective-permute-start | bytes 786440 | tf_op jit(solution)/shard_map/ppermute | solution.py:26
  22.3 11.6 %collective-permute-start.8 = (bf16[256,128]{1,0:T(8,128)(2,1)S(1)}, bf16[256,128]{1,0:T(8,128)(2,1)S(1)}, u32[]{:S(2)}, u32[]{:S(2)}) collective-permute-start(bf16[256,128]{1,0:T(8,128)(2,1)S(1)} %get-tuple-element.41), channel_id=1, source_target_pairs={{0,8},{4,12},{8,0},{12,4},{16,24},{20,28},{24,16},{28,20},{1,9},{5... | collective-permute-start | bytes 196616 | tf_op jit(solution)/shard_map/ppermute | solution.py:26
  23.9 10.3 %collective-permute-start.9 = (bf16[256,128]{1,0:T(8,128)(2,1)S(1)}, bf16[256,128]{1,0:T(8,128)(2,1)S(1)}, u32[]{:S(2)}, u32[]{:S(2)}) collective-permute-start(bf16[256,128]{1,0:T(8,128)(2,1)S(1)} %get-tuple-element.42), channel_id=1, source_target_pairs={{0,16},{4,20},{8,24},{12,28},{16,0},{20,4},{24,8},{28,12},{1,17},{... | collective-permute-start | bytes 196616 | tf_op jit(solution)/shard_map/ppermute | solution.py:26
  26.9 7.3 %collective-permute-start.10 = (bf16[256,128]{1,0:T(8,128)(2,1)S(1)}, bf16[256,128]{1,0:T(8,128)(2,1)S(1)}, u32[]{:S(2)}, u32[]{:S(2)}) collective-permute-start(bf16[256,128]{1,0:T(8,128)(2,1)S(1)} %get-tuple-element.43), channel_id=1, source_target_pairs={{0,24},{4,28},{8,16},{12,20},{16,8},{20,12},{24,0},{28,4},{1,25},{... | collective-permute-start | bytes 196616 | tf_op jit(solution)/shard_map/ppermute | solution.py:26
  29.3 12.1 %collective-permute-start.4 = (bf16[256,128]{1,0:T(8,128)(2,1)S(1)}, bf16[256,128]{1,0:T(8,128)(2,1)S(1)}, u32[]{:S(2)}, u32[]{:S(2)}) collective-permute-start(bf16[256,128]{1,0:T(8,128)(2,1)S(1)} %get-tuple-element.36), channel_id=1, source_target_pairs={{0,8},{4,12},{8,0},{12,4},{16,24},{20,28},{24,16},{28,20},{1,9},{5... | collective-permute-start | bytes 196616 | tf_op jit(solution)/shard_map/ppermute | solution.py:26
  30.9 10.6 %collective-permute-start.5 = (bf16[256,128]{1,0:T(8,128)(2,1)S(1)}, bf16[256,128]{1,0:T(8,128)(2,1)S(1)}, u32[]{:S(2)}, u32[]{:S(2)}) collective-permute-start(bf16[256,128]{1,0:T(8,128)(2,1)S(1)} %get-tuple-element.37), channel_id=1, source_target_pairs={{0,16},{4,20},{8,24},{12,28},{16,0},{20,4},{24,8},{28,12},{1,17},{... | collective-permute-start | bytes 196616 | tf_op jit(solution)/shard_map/ppermute | solution.py:26
  33.9 7.6 %collective-permute-start.6 = (bf16[256,128]{1,0:T(8,128)(2,1)S(1)}, bf16[256,128]{1,0:T(8,128)(2,1)S(1)}, u32[]{:S(2)}, u32[]{:S(2)}) collective-permute-start(bf16[256,128]{1,0:T(8,128)(2,1)S(1)} %get-tuple-element.38), channel_id=1, source_target_pairs={{0,24},{4,28},{8,16},{12,20},{16,8},{20,12},{24,0},{28,4},{1,25},{... | collective-permute-start | bytes 196616 | tf_op jit(solution)/shard_map/ppermute | solution.py:26
  34.2 13.1 %copy-start = (bf16[1024,1024]{1,0:T(8,128)(2,1)S(1)}, bf16[1024,1024]{1,0:T(8,128)(2,1)}, u32[]{:S(2)}) copy-start(bf16[1024,1024]{1,0:T(8,128)(2,1)} %w_ref.1) | copy-start | bytes 6291460
  41.8 1.9 %collective-permute-start.11 = (bf16[128,256]{1,0:T(8,128)(2,1)S(1)}, bf16[128,256]{1,0:T(8,128)(2,1)S(1)}, u32[]{:S(2)}, u32[]{:S(2)}) collective-permute-start(bf16[128,256]{1,0:T(8,128)(2,1)S(1)} %get-tuple-element.54), channel_id=1, source_target_pairs={{0,1},{1,0},{2,3},{3,2},{4,5},{5,4},{6,7},{7,6},{8,9},{9,8},{10,11... | collective-permute-start | bytes 196616 | tf_op jit(solution)/shard_map/ppermute | solution.py:26
  41.8 5.0 %collective-permute-start.12 = (bf16[128,256]{1,0:T(8,128)(2,1)S(1)}, bf16[128,256]{1,0:T(8,128)(2,1)S(1)}, u32[]{:S(2)}, u32[]{:S(2)}) collective-permute-start(bf16[128,256]{1,0:T(8,128)(2,1)S(1)} %get-tuple-element.55), channel_id=1, source_target_pairs={{0,2},{1,3},{2,0},{3,1},{4,6},{5,7},{6,4},{7,5},{8,10},{9,11},{10,... | collective-permute-start | bytes 196616 | tf_op jit(solution)/shard_map/ppermute | solution.py:26
  42.4 4.9 %collective-permute-start.13 = (bf16[128,256]{1,0:T(8,128)(2,1)S(1)}, bf16[128,256]{1,0:T(8,128)(2,1)S(1)}, u32[]{:S(2)}, u32[]{:S(2)}) collective-permute-start(bf16[128,256]{1,0:T(8,128)(2,1)S(1)} %get-tuple-element.56), channel_id=1, source_target_pairs={{0,3},{1,2},{2,1},{3,0},{4,7},{5,6},{6,5},{7,4},{8,11},{9,10},{10,... | collective-permute-start | bytes 196616 | tf_op jit(solution)/shard_map/ppermute | solution.py:26

commit v5 on v4

--- a/solution.py
+++ b/solution.py
@@ -62,94 +62,94 @@
     )
 
 
-def sums_kernel(heads, owners, pages, table_ref, keys_hbm, values_hbm,
-                prompt_hbm, send_gram, send_cross, keep_gram, keep_cross,
-                acc_ref, keys_ref, values_ref, stored_ref, code_ref, key_sem, value_sem, sem):
-    pool, rows = keys_ref.shape[0], keys_ref.shape[1]
-    blocks = pool // pages
-    slots = table_ref.shape[1]
+def sums_kernel(heads, owners, table_hbm, keys_hbm, values_hbm, prompt_hbm,
+                send_gram, send_cross, keep_gram, keep_cross,
+                acc_ref, keys_ref, values_ref, stored_ref, table_ref, list_ref,
+                key_sem, value_sem, small_sem):
+    pool, rows = keys_hbm.shape[0], keys_hbm.shape[1]
+    slots = table_hbm.shape[1]
     mine = lax.axis_index("grp")
-
-    def load(block):
-        at = pl.ds(block * pages, pages)
-        return (
-            pltpu.make_async_copy(keys_hbm.at[at], keys_ref.at[at], key_sem.at[block]),
-            pltpu.make_async_copy(values_hbm.at[at], values_ref.at[at], value_sem.at[block]),
-        )
-
-    for block in range(blocks):
-        for copy in load(block):
-            copy.start()
-    load_prompt = pltpu.make_async_copy(prompt_hbm, stored_ref, sem)
+    load_table = pltpu.make_async_copy(table_hbm, table_ref, small_sem.at[0])
+    load_prompt = pltpu.make_async_copy(prompt_hbm, stored_ref, small_sem.at[1])
+    load_table.start()
     load_prompt.start()
     acc_ref[...] = jnp.zeros_like(acc_ref)
+    load_table.wait()
+
+    def load(item):
+        page = list_ref[item] & 0xFFFF
+        return (
+            pltpu.make_async_copy(keys_hbm.at[page], keys_ref.at[item], key_sem.at[item]),
+            pltpu.make_async_copy(values_hbm.at[page], values_ref.at[item], value_sem.at[item]),
+        )
+
+    def start(item, carry):
+        for copy in load(item):
+            copy.start()
+        return carry
 
     first = mine * pool
-    wide = 16
+    wide = 8
+    count = jnp.int32(0)
     for owner in range(owners):
 
-        def note(chunk, carry):
+        def note(chunk, count):
             for i in range(wide):
-                slot = chunk * wide + i
-                page = table_ref[owner, slot] - first
-                inside = (page >= 0) & (page < pool)
-                code_ref[jnp.where(inside, page, pool)] = owner * slots + slot
-            return carry
-
-        lax.fori_loop(0, slots // wide, note, 0)
+                entry = table_ref[owner, chunk * wide + i]
+                page = (entry & 0xFFFF) - first
+                live = entry & 0xFF0000
+                list_ref[count] = (owner << 24) | live | (page & 0xFFFF)
+                inside = (page >= 0) & (page < pool) & (live > 0)
+                count = count + inside.astype(jnp.int32)
+            return count
+
+        chunks = jnp.int32(0)
+        for slot in range(0, slots, wide):
+            chunks = chunks + ((table_ref[owner, slot] & 0xFF0000) > 0).astype(jnp.int32)
+        before = count
+        count = lax.fori_loop(0, chunks, note, before)
+        lax.fori_loop(before, count, start, 0)
+
+    turn = 4
+    turns = (count + (turn - 1)) >> 2
+
+    def fill(item, carry):
+        list_ref[item] = jnp.int32(owners << 24)
+        return start(item, carry)
+
+    lax.fori_loop(count, turns * turn, fill, 0)
 
     lane = lax.broadcasted_iota(jnp.int32, (HDIM, rows), 1)
 
-    def place(page):
-        code = code_ref[page]
-        owner = lax.div(code, jnp.int32(slots))
-        slot = code - owner * slots
-        return owner, jnp.clip(table_ref[owners, owner] - slot * PAGE, 0, PAGE)
-
-    def add(page, owner, turned):
-        zero = jnp.zeros_like(turned)
-        left = turned
-        if heads > 1:
+    def one_turn(step, carry):
+        for i in range(turn):
+            for copy in load(step * turn + i):
+                copy.wait()
+        for i in range(turn):
+            item = step * turn + i
+            code = list_ref[item]
+            owner, live = code >> 24, (code >> 16) & 0xFF
+            keys = keys_ref[item]
+            turned = keys.T
+            zero = jnp.zeros_like(turned)
             left = jnp.concatenate(
-                [jnp.where(lane % heads == head, turned, zero) for head in range(heads)], axis=0
+                [
+                    jnp.where((lane % heads == head) & (lane < live * heads), turned, zero)
+                    for head in range(heads)
+                ],
+                axis=0,
             )
-        right = jnp.concatenate([keys_ref[page], values_ref[page]], axis=1)
-        acc_ref[owner] += dot(left, right)
-
-    def one_block(block, carry):
-        for copy in load(block):
-            copy.wait()
-        partial = jnp.int32(0)
-        for i in range(pages):
-            page = block * pages + i
-            owner, live = place(page)
-            add(page, jnp.where(live == PAGE, owner, owners), keys_ref[page].T)
-            partial = partial | ((live > 0) & (live < PAGE)).astype(jnp.int32)
-
-        @pl.when(partial > 0)
-        def _():
-            def one_page(page, inner):
-                owner, live = place(page)
-
-                @pl.when((live > 0) & (live < PAGE))
-                def _():
-                    turned = keys_ref[page].T
-                    add(page, owner, jnp.where(lane < live * heads, turned, jnp.zeros_like(turned)))
-
-                return inner
-
-            lax.fori_loop(block * pages, (block + 1) * pages, one_page, 0)
-
+            acc_ref[owner] += dot(left, jnp.concatenate([keys, values_ref[item]], axis=1))
         return carry
 
-    lax.fori_loop(0, blocks, one_block, 0)
+    lax.fori_loop(0, turns, one_turn, 0)
     load_prompt.wait()
     stored = stored_ref.shape[0]
 
     def add_prompt(owner, carry):
         for slot in range(stored):
 
-            @pl.when(table_ref[owners + 1, owner] == mine * stored + slot)
+            @pl.when((table_ref[owner, 0] >> 24) == mine * stored + slot)
             def _():
                 for head in range(heads):
                     at = slice(head * HDIM, (head + 1) * HDIM)
@@ -171,23 +171,22 @@
 def page_sums(table, keys, values, prompt_state, owners):
     pool, rows, _ = keys.shape
     heads = prompt_state.shape[1]
-    pages = 8
     half = (owners // 2, heads * HDIM, HDIM)
-    small = pl.BlockSpec(memory_space=pltpu.SMEM)
-    anywhere = pl.BlockSpec(memory_space=pl.ANY)
-    return pl.pallas_call(
-        functools.partial(sums_kernel, heads, owners, pages),
-        in_specs=[small] + [anywhere] * 3,
+    items = pool + 4
+    return pl.pallas_call(
+        functools.partial(sums_kernel, heads, owners),
+        in_specs=[pl.BlockSpec(memory_space=pl.ANY)] * 4,
         out_specs=[pl.BlockSpec(memory_space=pltpu.VMEM)] * 4,
         scratch_shapes=[
             pltpu.VMEM((owners + 1, heads * HDIM, 2 * HDIM), F32),
-            pltpu.VMEM(keys.shape, BF16),
-            pltpu.VMEM(values.shape, BF16),
+            pltpu.VMEM((items, rows, HDIM), BF16),
+            pltpu.VMEM((items, rows, HDIM), BF16),
             pltpu.VMEM(prompt_state.shape, F32),
-            pltpu.SMEM((pool + 1,), jnp.int32),
-            pltpu.SemaphoreType.DMA((pool // pages,)),
-            pltpu.SemaphoreType.DMA((pool // pages,)),
-            pltpu.SemaphoreType.DMA,
+            pltpu.SMEM(table.shape, jnp.int32),
+            pltpu.SMEM((items,), jnp.int32),
+            pltpu.SemaphoreType.DMA((items,)),
+            pltpu.SemaphoreType.DMA((items,)),
+            pltpu.SemaphoreType.DMA((2,)),
         ],
         out_shape=[jax.ShapeDtypeStruct(half, BF16)] * 4,
         compiler_params=pltpu.CompilerParams(vmem_limit_bytes=PAGE_VMEM * 2**20),
@@ -224,34 +223,45 @@
     )(keep, got)
 
 
-def token_kernel(heads, place_ref, rate_ref, *refs):
+def token_kernel(heads, *refs):
     head_count = HEADS // heads
     blocks = refs[:head_count]
-    (gain_ref, w_ref, wg_ref, taps_ref, state_ref) = refs[head_count : head_count + 5]
-    (q_ref, k_ref, kt_ref, vt_ref, weight_ref, prefix_ref, rows_ref) = refs[-9:-2]
-    ext_ref, gate_ref = refs[-2:]
-    me = place_ref[0]
+    (gain_ref, w_hbm, wg_ref, taps_all, state_ref, rate_ref) = refs[head_count : head_count + 6]
+    (q_ref, k_ref, kt_ref, vt_ref, weight_ref, prefix_ref, rows_ref) = refs[-12:-5]
+    ext_ref, gate_ref, normed_ref, w_ref, w_sem = refs[-5:]
+    me = lax.axis_index("head")
     tok_rows = blocks[0].shape[0]
+    width = w_ref.shape[1]
+    columns = pl.ds(pl.multiple_of(me * width, HDIM), width)
+    load = pltpu.make_async_copy(w_hbm.at[:, columns], w_ref, w_sem)
+    load.start()
     length = tok_rows * head_count
     chunks = length // CHUNK
     base = 8
-    ext_ref[base - (CONV - 1) : base, :] = state_ref[0].astype(F32)
+    taps_ref = taps_all[:, columns]
+    ext_ref[base - (CONV - 1) : base, :] = state_ref[0, :, columns].astype(F32)
     gate_ref[...] = jnp.zeros_like(gate_ref)
     for distance, block in enumerate(blocks):
         first = pl.multiple_of((me ^ distance) * tok_rows, tok_rows)
         wide = block[...].astype(F32)
         scale = lax.rsqrt(jnp.mean(wide * wide, axis=-1, keepdims=True) + EPS_NORM)
         normed = (wide * scale * gain_ref[...]).astype(BF16)
-        mixed = dot(normed, w_ref[...]).astype(BF16)
-        ext_ref[pl.ds(pl.multiple_of(base + first, 8), tok_rows), :] = mixed.astype(F32)
+        normed_ref[pl.ds(first, tok_rows), :] = normed
         gate_ref[pl.ds(first, tok_rows), : 2 * HEADS] = dot(normed, wg_ref[...])
+    load.wait()
+    for c in range(chunks):
+        rows = slice(c * CHUNK, (c + 1) * CHUNK)
+        mixed = dot(normed_ref[rows, :], w_ref[...]).astype(BF16)
+        ext_ref[base + c * CHUNK : base + (c + 1) * CHUNK, :] = mixed.astype(F32)
 
     shift = lax.rem(HDIM - 2 * heads * me, HDIM)
     logits = pltpu.roll(gate_ref[...], shift, 1)
     lane = lax.broadcasted_iota(jnp.int32, (1, HDIM), 1)
     rate = jnp.zeros((1, HDIM), F32)
     for head in range(heads):
-        rate = jnp.where(lane == 2 * head + 1, rate_ref[me * heads + head], rate)
+        here = lax.broadcasted_iota(jnp.int32, (1, HEADS), 1) == me * heads + head
+        own = jnp.sum(jnp.where(here, rate_ref[...], 0.0), axis=1, keepdims=True)
+        rate = jnp.where(lane == 2 * head + 1, own, rate)
     write = jax.nn.sigmoid(logits).astype(BF16).astype(F32)
     soft = jnp.maximum(logits, 0.0) + jnp.log1p(jnp.exp(-jnp.abs(logits)))
     decay = (-rate * soft).astype(BF16)
@@ -303,7 +313,7 @@
 
 
 def token_vectors(
-    place, decay_rate, blocks, norm_gain, w_qkv, w_gates, conv_weight, conv_state, held
+    decay_rate, blocks, norm_gain, w_qkv, w_gates, conv_weight, conv_state, held
 ):
     head_count = len(blocks)
     heads = HEADS // head_count
@@ -311,12 +321,8 @@
     tok_rows, model = blocks[0].shape
     length = head_count * tok_rows
     chunks = length // CHUNK
-
+    whole = pl.BlockSpec(memory_space=pltpu.VMEM)
     anywhere = pl.BlockSpec(memory_space=pl.ANY)
-
-    def full(shape):
-        return pl.BlockSpec(shape, lambda i, *_: (0,) * len(shape))
-
     outs = [
         jax.ShapeDtypeStruct((heads, HDIM, length), BF16),
         jax.ShapeDtypeStruct((heads, length, HDIM), BF16),
@@ -328,23 +334,17 @@
     ]
     return pl.pallas_call(
         functools.partial(token_kernel, heads),
-        grid_spec=pltpu.PrefetchScalarGridSpec(
-            num_scalar_prefetch=2,
-            grid=(1,),
-            in_specs=[full(b.shape) for b in blocks]
-            + [
-                full((1, model)),
-                pl.BlockSpec((model, width), lambda i, place, rate: (0, place[0])),
-                full(w_gates.shape),
-                pl.BlockSpec((CONV, width), lambda i, place, rate: (0, place[0])),
-                pl.BlockSpec((1, CONV - 1, width), lambda i, place, rate: (0, 0, place[0])),
-            ]
-            + [anywhere],
-            out_specs=[anywhere] + [full(o.shape) for o in outs],
-            scratch_shapes=[pltpu.VMEM((8 + length, width), F32), pltpu.VMEM((length, HDIM), F32)],
-        ),
+        in_specs=[whole] * head_count + [whole, anywhere] + [whole] * 4 + [anywhere],
+        out_specs=[anywhere] + [whole] * len(outs),
+        scratch_shapes=[
+            pltpu.VMEM((8 + length, width), F32),
+            pltpu.VMEM((length, HDIM), F32),
+            pltpu.VMEM((length, model), BF16),
+            pltpu.VMEM((model, width), BF16),
+            pltpu.SemaphoreType.DMA,
+        ],
         out_shape=[jax.ShapeDtypeStruct(held.shape, held.dtype)] + outs,
-        input_output_aliases={2 + len(blocks) + 5: 0},
+        input_output_aliases={head_count + 6: 0},
         compiler_params=pltpu.CompilerParams(vmem_limit_bytes=TOKEN_VMEM * 2**20),
         cost_estimate=pl.CostEstimate(
             flops=2 * length * model * width,
@@ -353,14 +353,13 @@
         ),
         name="token_vectors",
     )(
-        place,
-        decay_rate,
         *blocks,
         norm_gain.reshape(1, model),
         w_qkv,
         w_gates,
         conv_weight,
         conv_state,
+        decay_rate.reshape(1, HEADS),
         held,
     )
 
@@ -404,7 +403,7 @@
         for (head, pair), first, second, norm in zip(groups, firsts, seconds, norms):
             direction = d_ref[head, pair]
             image = (
-                rows_ref[head, pair, 0:1] * first[:HDIM] + ridge_ref[head] * direction + second
+                rows_ref[head, pair, 0:1] * first[:HDIM] + ridge_ref[:, head : head + 1] * direction + second
             )
             alpha = norm / jnp.sum(direction * image, axis=0, keepdims=True)
             x_ref[head, pair] += alpha * direction
@@ -438,8 +437,7 @@
     state = pltpu.VMEM((heads, pairs, HDIM, PAIR), F32)
     return pl.pallas_call(
         functools.partial(read_kernel, heads, len(grams)),
-        in_specs=[pl.BlockSpec(memory_space=pltpu.SMEM)]
-        + [whole] * (len(grams) + len(vectors))
+        in_specs=[whole] * (1 + len(grams) + len(vectors))
         + [whole] * len(after),
         out_specs=[whole] * 2,
         out_shape=[
@@ -454,13 +452,13 @@
             transcendentals=0,
         ),
         name="ridge_reads",
-    )(ridge, *grams, *vectors, *after)
-
-
-def cross_kernel(heads, terms, place_ref, *refs):
+    )(ridge.reshape(1, heads), *grams, *vectors, *after)
+
+
+def cross_kernel(heads, terms, *refs):
     crosses, (base_ref, solved_ref) = refs[:terms], refs[terms : terms + 2]
     outs, o_ref = refs[terms + 2 : -1], refs[-1]
-    me = place_ref[0]
+    me = lax.axis_index("head")
     for head in range(heads):
         cols = slice(head * HDIM, (head + 1) * HDIM)
         cross = crosses[0][cols, :].astype(F32)
@@ -474,12 +472,12 @@
         out_ref[...] = o_ref[pl.ds(first_row, tok_rows), :]
 
 
-def cross_reads(place, crosses, base, solved, head_count):
+def cross_reads(crosses, base, solved, head_count):
     length, width = base.shape
     whole = pl.BlockSpec(memory_space=pltpu.VMEM)
     return pl.pallas_call(
         functools.partial(cross_kernel, width // HDIM, len(crosses)),
-        in_specs=[pl.BlockSpec(memory_space=pltpu.SMEM)] + [whole] * (len(crosses) + 2),
+        in_specs=[whole] * (len(crosses) + 2),
         out_specs=[whole] * head_count,
         out_shape=[jax.ShapeDtypeStruct((length // head_count, width), BF16)] * head_count,
         scratch_shapes=[pltpu.VMEM((length, width), BF16)],
@@ -488,12 +486,12 @@
             flops=2 * length * width * HDIM, bytes_accessed=8 * length * width, transcendentals=0
         ),
         name="cross_reads",
-    )(place, *crosses, base, solved)
-
-
-def output_kernel(place_ref, tokens_ref, w_ref, *refs):
+    )(*crosses, base, solved)
+
+
+def output_kernel(tokens_ref, w_ref, *refs):
     out_ref = refs[-1]
-    me = place_ref[0]
+    me = lax.axis_index("head")
     total = tokens_ref[...].astype(F32)
     for distance, part in enumerate(refs[:-1]):
         width = part.shape[1]
@@ -502,11 +500,11 @@
     out_ref[...] = total.astype(BF16)
 
 
-def output_rows(place, tokens, w_out, reads):
+def output_rows(tokens, w_out, reads):
     whole = pl.BlockSpec(memory_space=pltpu.VMEM)
     return pl.pallas_call(
         output_kernel,
-        in_specs=[pl.BlockSpec(memory_space=pltpu.SMEM)] + [whole] * (2 + len(reads)),
+        in_specs=[whole] * (2 + len(reads)),
         out_specs=whole,
         out_shape=jax.ShapeDtypeStruct(tokens.shape, BF16),
         compiler_params=pltpu.CompilerParams(vmem_limit_bytes=24 * 2**20),
@@ -516,7 +514,7 @@
             transcendentals=0,
         ),
         name="output_rows",
-    )(place, tokens, w_out, *reads)
+    )(tokens, w_out, *reads)
 
 
 def shards(
@@ -538,17 +536,15 @@
 ):
     head_count = lax.axis_size("head")
     owners = lax.axis_size("grp")
-    me = lax.axis_index("head").astype(jnp.int32)
-    place = me.reshape(1)
     bits = [head_count >> i for i in range(1, head_count.bit_length())]
     blocks = {0: tokens}
     for bit in bits:
         blocks[bit] = swap(tokens, "head", bit)
 
     pool, page, heads, _ = cache_keys.shape
-    spare = (0, page_table.shape[1] - owners)
-    rows = [jnp.pad(row, spare)[None] for row in (cache_lengths, group_prompt)]
-    table = jnp.concatenate([page_table] + rows, axis=0)
+    starts = jnp.arange(page_table.shape[1], dtype=jnp.int32) * PAGE
+    live = jnp.clip(cache_lengths[:, None] - starts, 0, PAGE)
+    table = page_table | (live << 16) | (group_prompt[:, None] << 24)
     keys = cache_keys.reshape(pool, page * heads, HDIM)
     values = cache_values.reshape(pool, page * heads, HDIM)
 
@@ -566,14 +562,14 @@
                 blocks[distance ^ bit] = swap(blocks[distance], "head", bit)
     blocks = [blocks[i] for i in range(head_count)]
     send_cross, *vectors = token_vectors(
-        place, decay_rate, blocks, norm_gain, w_qkv, w_gates, conv_weight, conv_state, send_cross
+        decay_rate, blocks, norm_gain, w_qkv, w_gates, conv_weight, conv_state, send_cross
     )
     grams = halve_sums(keep_gram, got_gram)
     crosses = halve_sums(keep_cross, swap(send_cross, "grp", 1))
     base, solved = ridge_reads(ridge, scattered(grams), vectors, [crosses[0]])
-    reads = cross_reads(place, scattered(crosses), base, solved, head_count)
+    reads = cross_reads(scattered(crosses), base, solved, head_count)
     reads = [reads[0]] + [swap(reads[i], "head", i) for i in range(1, head_count)]
-    return output_rows(place, tokens, w_out, reads)
+    return output_rows(tokens, w_out, reads)
 
 
 def solution(mesh):

time: 48.5 us -> 46.6 us (0.961)
  Pallas kernels: 23.2 us -> 21.6 us
  other arithmetic: 0.69 us -> 1.42 us
  local copies, waits for them, and re-layouts: 0.89 us -> 0.22 us
  starting transfers between devices: 17.2 us -> 16.7 us
    pallas_call x3, Pallas kernels: 15.6 us -> 14.5 us  [the longest x1 8.54 us: page_sums(): pl.pallas_call(functools.partial(sums_kernel, heads, owners), in_specs=[p...]
    or x0 -> x1, other arithmetic: none -> 0.76 us  [shards(): table = page_table | live << 16 | group_prompt[:, None] << 24]
    concatenate x1 -> x0, other arithmetic: 0.69 us -> none  [shards(): table = jnp.concatenate([page_table] + rows, axis=0)]
    broadcast_in_dim x1 -> x0, local copies, waits for them, and re-layouts: 0.67 us -> none  [shards(): rows = [jnp.pad(row, spare)[None] for row in (cache_lengths, group_prompt)]]
    shift_left x0 -> x1, other arithmetic: none -> 0.66 us  [shards(): table = page_table | live << 16 | group_prompt[:, None] << 24]
    pallas_call x1, Pallas kernels: 7.25 us -> 6.71 us  [ridge_reads(): pl.pallas_call(functools.partial(read_kernel, heads, len(grams)), in_spec...]
  transfers between devices with their start and end apart: 14 -> 14, of which waited for: 4 -> 4; matrix products, arithmetic and copies ran while one was open for 3% -> 3% of each run, Pallas kernels for 45% -> 43%
where the time goes in v5:
time: 46.6 us; the launch traced here: 46.5 us
  Pallas kernels  21.6 us (46%)
  starting transfers between devices  16.7 us (36%)
  waiting for transfers between devices  6.34 us (14%)
  other arithmetic  1.42 us (3%)
    ppermute x14, starting transfers between devices, swap(): return lax.ppermute(block, axis, [(i, i ^ distance) for i in range(size)])  16.7 us
    pallas_call x1, Pallas kernels, page_sums(): pl.pallas_call(functools.partial(sums_kernel, heads, owners), in_specs=[p...  8.54 us
    pallas_call x1, Pallas kernels, ridge_reads(): pl.pallas_call(functools.partial(read_kernel, heads, len(grams)), in_spec...  6.71 us
    ppermute x14, waiting for transfers between devices, swap(): return lax.ppermute(block, axis, [(i, i ^ distance) for i in range(size)])  6.34 us
    pallas_call x1, Pallas kernels, token_vectors(): pl.pallas_call(functools.partial(token_kernel, heads), in_specs=[whole] *...  4.73 us
    pallas_call x1, Pallas kernels, output_rows(): pl.pallas_call(output_kernel, in_specs=[whole] * (2 + len(reads)), out_sp...  1.21 us
  transfers between devices with their start and end apart: 14, of which 4 were waited for; matrix products, arithmetic and copies ran while one was open for 3% of the time, Pallas kernels for 43%

profile of v5, /device:TPU:0, one launch (start us, length us, event | category | flops | bytes accessed | tf_op | source)
XLA Modules:
  0.0 46.5 jit_solution(14368860859270939954)
XLA Ops:
  0.0 2.9 %collective-permute-start.1 = (bf16[128,1024]{1,0:T(8,128)(2,1)}, bf16[128,1024]{1,0:T(8,128)(2,1)S(1)}, u32[]{:S(2)}, u32[]{:S(2)}) collective-permute-start(bf16[128,1024]{1,0:T(8,128)(2,1)} %tokens_ref.1), channel_id=1, source_target_pairs={{0,2},{1,3},{2,0},{3,1},{4,6},{5,7},{6,4},{7,5},{8,10},{9,11},{10,... | collective-permute-start | bytes 786440 | tf_op jit(solution)/shard_map/ppermute | solution.py:26
  2.9 0.0 collective-permute-start
  2.9 0.7 %broadcast_shift-left_fusion = s32[8]{0:T(128)S(1)} fusion(s32[8]{0:T(128)} %param.28), kind=kLoop, calls=%fused_computation.2 | loop fusion | flops 8 | bytes 64 | tf_op jit(solution)/shard_map/shift_left | solution.py:547
  3.6 0.8 %or_or_fusion.table_hbm = s32[8,64]{1,0:T(8,128)S(1)} fusion(s32[8,64]{1,0:T(8,128)} %param.26, s32[8]{0:T(128)S(1)} %broadcast_shift-left_fusion, s32[64]{0:T(128)S(1)} %iota_multiply_fusion, s32[8]{0:T(128)} %param.27), kind=kLoop, calls=%fused_computation | loop fusion | flops 2560 | bytes 4416 | tf_op jit(solution)/shard_map/or | solution.py:547
  4.4 0.0 copy-start.8
  4.4 0.0 copy-start.1
  4.4 0.0 copy-start.3
  4.4 0.0 copy-start.4
  4.4 0.0 copy-start.5
  4.4 0.0 copy-start.6
  4.4 8.5 %page_sums.1 = (bf16[4,256,128]{2,1,0:T(8,128)(2,1)S(1)}, bf16[4,256,128]{2,1,0:T(8,128)(2,1)S(1)}, bf16[4,256,128]{2,1,0:T(8,128)(2,1)S(1)}, bf16[4,256,128]{2,1,0:T(8,128)(2,1)}) custom-call(s32[8,64]{1,0:T(8,128)S(1)} %or_or_fusion.table_hbm, bf16[64,256,128]{2,1,0:T(8,128)(2,1)} %bitcast.8, bf16[64,256,128]{2,1,0:T(8,128)(2,1)} %bitcast.9, ...), custom_call_target="tpu_custom_call" | custom-call | flops 4294967296 | bytes 8388608 | tf_op jit(solution)/shard_map/page_sums/pallas_call | solution.py:176
  13.0 0.0 collective-permute-done.1.refs_0_
  13.0 0.6 %collective-permute-start.2 = (bf16[128,1024]{1,0:T(8,128)(2,1)S(1)}, bf16[128,1024]{1,0:T(8,128)(2,1)S(1)}, u32[]{:S(2)}, u32[]{:S(2)}) collective-permute-start(bf16[128,1024]{1,0:T(8,128)(2,1)S(1)} %hold.1.refs_2_), channel_id=1, source_target_pairs={{0,1},{1,0},{2,3},{3,2},{4,5},{5,4},{6,7},{7,6},{8,9},{9,8},{10,11... | collective-permute-start | bytes 786440 | tf_op jit(solution)/shard_map/ppermute | solution.py:26
  13.6 1.3 %collective-permute-start.7 = (bf16[4,256,128]{2,1,0:T(8,128)(2,1)S(1)}, bf16[4,256,128]{2,1,0:T(8,128)(2,1)S(1)}, u32[]{:S(2)}, u32[]{:S(2)}) collective-permute-start(bf16[4,256,128]{2,1,0:T(8,128)(2,1)S(1)} %get-tuple-element.39), channel_id=1, source_target_pairs={{0,4},{4,0},{8,12},{12,8},{16,20},{20,16},{24,28},{28,24},{1,5},{5... | collective-permute-start | bytes 786440 | tf_op jit(solution)/shard_map/ppermute | solution.py:26
  14.9 0.0 copy-done.8
  14.9 0.2 copy.18.refs_6_
  15.1 0.0 collective-permute-done.refs_1_
  15.1 0.0 collective-permute-done.2.refs_3_
  15.1 0.0 copy-done.1
  15.1 0.0 copy-done.3
  15.1 0.0 copy-done.4
  15.1 0.0 copy-done.5
  15.1 0.0 copy-done.6
  15.1 0.0 copy-start.2
  15.2 0.0 copy-start.7
  15.2 4.7 %token_vectors.1 = (bf16[4,256,128]{2,1,0:T(8,128)(2,1)S(1)}, bf16[2,128,512]{2,1,0:T(8,128)(2,1)S(1)}, bf16[2,512,128]{2,1,0:T(8,128)(2,1)S(1)}, bf16[2,128,512...) custom-call(bf16[128,1024]{1,0:T(8,128)(2,1)S(1)} %copy-done.1, ...), custom_call_target="tpu_custom_call", output_to_operand_aliasing={{0}: (10, {})} | custom-call | flops 805306368 | bytes 6815744 | tf_op jit(solution)/shard_map/token_vectors/pallas_call | solution.py:335
  19.9 1.0 %collective-permute-start.3 = (bf16[4,256,128]{2,1,0:T(8,128)(2,1)S(1)}, bf16[4,256,128]{2,1,0:T(8,128)(2,1)S(1)}, u32[]{:S(2)}, u32[]{:S(2)}) collective-permute-start(bf16[4,256,128]{2,1,0:T(8,128)(2,1)S(1)} %get-tuple-element.34), channel_id=1, source_target_pairs={{0,4},{4,0},{8,12},{12,8},{16,20},{20,16},{24,28},{28,24},{1,5},{5... | collective-permute-start | bytes 786440 | tf_op jit(solution)/shard_map/ppermute | solution.py:26
  20.9 0.9 %collective-permute-done.7.got_ref = bf16[4,256,128]{2,1,0:T(8,128)(2,1)S(1)} collective-permute-done((bf16[4,256,128]{2,1,0:T(8,128)(2,1)S(1)}, bf16[4,256,128]{2,1,0:T(8,128)(2,1)S(1)}, u32[]{:S(2)}, u32[]{:S(2)}) %collective-permute-start.7) | collective-permute-done | bytes 262176 | tf_op jit(solution)/shard_map/ppermute | solution.py:26
  21.9 0.1 halve_sums.3
  21.9 1.3 %collective-permute-start.8 = (bf16[256,128]{1,0:T(8,128)(2,1)S(1)}, bf16[256,128]{1,0:T(8,128)(2,1)S(1)}, u32[]{:S(2)}, u32[]{:S(2)}) collective-permute-start(bf16[256,128]{1,0:T(8,128)(2,1)S(1)} %get-tuple-element.41), channel_id=1, source_target_pairs={{0,8},{4,12},{8,0},{12,4},{16,24},{20,28},{24,16},{28,20},{1,9},{5... | collective-permute-start | bytes 196616 | tf_op jit(solution)/shard_map/ppermute | solution.py:26
  23.2 2.9 %collective-permute-start.9 = (bf16[256,128]{1,0:T(8,128)(2,1)S(1)}, bf16[256,128]{1,0:T(8,128)(2,1)S(1)}, u32[]{:S(2)}, u32[]{:S(2)}) collective-permute-start(bf16[256,128]{1,0:T(8,128)(2,1)S(1)} %get-tuple-element.42), channel_id=1, source_target_pairs={{0,16},{4,20},{8,24},{12,28},{16,0},{20,4},{24,8},{28,12},{1,17},{... | collective-permute-start | bytes 196616 | tf_op jit(solution)/shard_map/ppermute | solution.py:26
  26.2 0.2 collective-permute-start.10
  26.4 1.8 %collective-permute-done.3.got_ref = bf16[4,256,128]{2,1,0:T(8,128)(2,1)S(1)} collective-permute-done((bf16[4,256,128]{2,1,0:T(8,128)(2,1)S(1)}, bf16[4,256,128]{2,1,0:T(8,128)(2,1)S(1)}, u32[]{:S(2)}, u32[]{:S(2)}) %collective-permute-start.3) | collective-permute-done | bytes 262176 | tf_op jit(solution)/shard_map/ppermute | solution.py:26
  28.2 0.0 copy-done.2
  28.2 0.1 halve_sums.2
  28.2 1.6 %collective-permute-start.4 = (bf16[256,128]{1,0:T(8,128)(2,1)S(1)}, bf16[256,128]{1,0:T(8,128)(2,1)S(1)}, u32[]{:S(2)}, u32[]{:S(2)}) collective-permute-start(bf16[256,128]{1,0:T(8,128)(2,1)S(1)} %get-tuple-element.36), channel_id=1, source_target_pairs={{0,8},{4,12},{8,0},{12,4},{16,24},{20,28},{24,16},{28,20},{1,9},{5... | collective-permute-start | bytes 196616 | tf_op jit(solution)/shard_map/ppermute | solution.py:26
  29.8 2.7 %collective-permute-start.5 = (bf16[256,128]{1,0:T(8,128)(2,1)S(1)}, bf16[256,128]{1,0:T(8,128)(2,1)S(1)}, u32[]{:S(2)}, u32[]{:S(2)}) collective-permute-start(bf16[256,128]{1,0:T(8,128)(2,1)S(1)} %get-tuple-element.37), channel_id=1, source_target_pairs={{0,16},{4,20},{8,24},{12,28},{16,0},{20,4},{24,8},{28,12},{1,17},{... | collective-permute-start | bytes 196616 | tf_op jit(solution)/shard_map/ppermute | solution.py:26
  32.5 0.0 collective-permute-done.8.refs_1_
  32.5 0.2 collective-permute-start.6
  32.7 0.0 collective-permute-done.9.refs_2_
  32.7 0.0 collective-permute-done.10.refs_3_
  32.7 0.0 copy-done.7
  32.7 0.0 copy-start
  32.7 6.7 %ridge_reads.1 = (f32[512,256]{1,0:T(8,128)S(1)}, bf16[512,256]{1,0:T(8,128)(2,1)S(1)}) custom-call(f32[1,2]{1,0:T(1,128)S(1)} %bitcast.7, f32[256,128]{1,0:T(8,128)S(1)} %get-tuple-element.40.refs_0_, bf16[256,128]{1,0:T(8,128)(2,1)S(1)} %collective-permute-done.8.refs_1_, bf16[256,128]{1,0:T(8,128)(2,1)S(1)} %collective-permute-done.9.refs_2_, ...), custom_call_target="tpu_custom_call" | custom-call | flops 6442450944 | bytes 8388608 | tf_op jit(solution)/shard_map/ridge_reads/pallas_call | solution.py:438
  39.4 0.0 collective-permute-done.4.refs_1_
  39.4 0.0 collective-permute-done.5.refs_2_
  39.5 0.0 collective-permute-done.6.refs_3_
  39.5 0.3 cross_reads.1
  39.7 0.1 collective-permute-start.11
  39.8 0.6 %collective-permute-start.12 = (bf16[128,256]{1,0:T(8,128)(2,1)S(1)}, bf16[128,256]{1,0:T(8,128)(2,1)S(1)}, u32[]{:S(2)}, u32[]{:S(2)}) collective-permute-start(bf16[128,256]{1,0:T(8,128)(2,1)S(1)} %get-tuple-element.55), channel_id=1, source_target_pairs={{0,2},{1,3},{2,0},{3,1},{4,6},{5,7},{6,4},{7,5},{8,10},{9,11},{10,... | collective-permute-start | bytes 196616 | tf_op jit(solution)/shard_map/ppermute | solution.py:26
  40.4 1.3 %collective-permute-start.13 = (bf16[128,256]{1,0:T(8,128)(2,1)S(1)}, bf16[128,256]{1,0:T(8,128)(2,1)S(1)}, u32[]{:S(2)}, u32[]{:S(2)}) collective-permute-start(bf16[128,256]{1,0:T(8,128)(2,1)S(1)} %get-tuple-element.56), channel_id=1, source_target_pairs={{0,3},{1,2},{2,1},{3,0},{4,7},{5,6},{6,5},{7,4},{8,11},{9,10},{10,... | collective-permute-start | bytes 196616 | tf_op jit(solution)/shard_map/ppermute | solution.py:26
  41.7 0.0 collective-permute-done.11.refs_1_
  41.7 3.1 %collective-permute-done.12.refs_2_ = bf16[128,256]{1,0:T(8,128)(2,1)S(1)} collective-permute-done((bf16[128,256]{1,0:T(8,128)(2,1)S(1)}, bf16[128,256]{1,0:T(8,128)(2,1)S(1)}, u32[]{:S(2)}, u32[]{:S(2)}) %collective-permute-start.12) | collective-permute-done | bytes 65568 | tf_op jit(solution)/shard_map/ppermute | solution.py:26
  44.8 0.5 %collective-permute-done.13.refs_3_ = bf16[128,256]{1,0:T(8,128)(2,1)S(1)} collective-permute-done((bf16[128,256]{1,0:T(8,128)(2,1)S(1)}, bf16[128,256]{1,0:T(8,128)(2,1)S(1)}, u32[]{:S(2)}, u32[]{:S(2)}) %collective-permute-start.13) | collective-permute-done | bytes 65568 | tf_op jit(solution)/shard_map/ppermute | solution.py:26
  45.3 0.0 copy-done
  45.3 1.2 %output_rows.1 = bf16[128,1024]{1,0:T(8,128)(2,1)} custom-call(bf16[128,1024]{1,0:T(8,128)(2,1)S(1)} %copy-done.1, bf16[1024,1024]{1,0:T(8,128)(2,1)S(1)} %copy-done, bf16[128,256]{1,0:T(8,128)(2,1)S(1)} %get-tuple-element.53.refs_0_, bf16[128,256]{1,0:T(8,128)(2,1)S(1)} %collective-permute-done.11.refs_1_, ...), custom_call_target="tpu_custom_call" | custom-call | flops 268435456 | bytes 2883584 | tf_op jit(solution)/shard_map/output_rows/pallas_call | solution.py:505
  (2 shorter events, 0.0 us)
Async XLA Ops:
  0.0 13.0 %collective-permute-start.1 = (bf16[128,1024]{1,0:T(8,128)(2,1)}, bf16[128,1024]{1,0:T(8,128)(2,1)S(1)}, u32[]{:S(2)}, u32[]{:S(2)}) collective-permute-start(bf16[128,1024]{1,0:T(8,128)(2,1)} %tokens_ref.1), channel_id=1, source_target_pairs={{0,2},{1,3},{2,0},{3,1},{4,6},{5,7},{6,4},{7,5},{8,10},{9,11},{10,... | collective-permute-start | bytes 786440 | tf_op jit(solution)/shard_map/ppermute | solution.py:26
  2.9 12.1 %collective-permute-start = (bf16[128,1024]{1,0:T(8,128)(2,1)}, bf16[128,1024]{1,0:T(8,128)(2,1)S(1)}, u32[]{:S(2)}, u32[]{:S(2)}) collective-permute-start(bf16[128,1024]{1,0:T(8,128)(2,1)} %tokens_ref.1), channel_id=1, source_target_pairs={{0,1},{1,0},{2,3},{3,2},{4,5},{5,4},{6,7},{7,6},{8,9},{9,8},{10,11... | collective-permute-start | bytes 786440 | tf_op jit(solution)/shard_map/ppermute | solution.py:26
  4.4 10.5 %copy-start.8 = (bf16[1024,16]{0,1:T(8,128)(2,1)S(1)}, bf16[1024,16]{0,1:T(8,128)(2,1)}, u32[]{:S(2)}) copy-start(bf16[1024,16]{0,1:T(8,128)(2,1)} %param.18) | copy-start | bytes 98308
  4.4 10.7 %copy-start.1 = (bf16[128,1024]{1,0:T(8,128)(2,1)S(1)}, bf16[128,1024]{1,0:T(8,128)(2,1)}, u32[]{:S(2)}) copy-start(bf16[128,1024]{1,0:T(8,128)(2,1)} %tokens_ref.1) | copy-start | bytes 786436
  4.4 10.7 %copy-start.3 = (f32[4,3072]{1,0:T(4,128)S(1)}, f32[4,3072]{1,0:T(4,128)}, u32[]{:S(2)}) copy-start(f32[4,3072]{1,0:T(4,128)} %refs_7_.1) | copy-start | bytes 147460
  4.4 10.7 %copy-start.4 = (bf16[1,3,3072]{2,1,0:T(4,128)(2,1)S(1)}, bf16[1,3,3072]{2,1,0:T(4,128)(2,1)}, u32[]{:S(2)}) copy-start(bf16[1,3,3072]{2,1,0:T(4,128)(2,1)} %refs_8_.1) | copy-start | bytes 55300
  4.4 10.7 %copy-start.5 = (f32[1024]{0:T(1024)S(1)}, f32[1024]{0:T(1024)}, u32[]{:S(2)}) copy-start(f32[1024]{0:T(1024)} %param.16) | copy-start | bytes 12292
  4.4 10.7 %copy-start.6 = (f32[8]{0:T(128)S(1)}, f32[8]{0:T(128)}, u32[]{:S(2)}) copy-start(f32[8]{0:T(128)} %param.21) | copy-start | bytes 100
  13.0 2.1 %collective-permute-start.2 = (bf16[128,1024]{1,0:T(8,128)(2,1)S(1)}, bf16[128,1024]{1,0:T(8,128)(2,1)S(1)}, u32[]{:S(2)}, u32[]{:S(2)}) collective-permute-start(bf16[128,1024]{1,0:T(8,128)(2,1)S(1)} %hold.1.refs_2_), channel_id=1, source_target_pairs={{0,1},{1,0},{2,3},{3,2},{4,5},{5,4},{6,7},{7,6},{8,9},{9,8},{10,11... | collective-permute-start | bytes 786440 | tf_op jit(solution)/shard_map/ppermute | solution.py:26
  13.6 8.3 %collective-permute-start.7 = (bf16[4,256,128]{2,1,0:T(8,128)(2,1)S(1)}, bf16[4,256,128]{2,1,0:T(8,128)(2,1)S(1)}, u32[]{:S(2)}, u32[]{:S(2)}) collective-permute-start(bf16[4,256,128]{2,1,0:T(8,128)(2,1)S(1)} %get-tuple-element.39), channel_id=1, source_target_pairs={{0,4},{4,0},{8,12},{12,8},{16,20},{20,16},{24,28},{28,24},{1,5},{5... | collective-permute-start | bytes 786440 | tf_op jit(solution)/shard_map/ppermute | solution.py:26
  15.1 13.0 %copy-start.2 = (bf16[4,256,128]{2,1,0:T(8,128)(2,1)S(1)}, bf16[4,256,128]{2,1,0:T(8,128)(2,1)}, u32[]{:S(2)}) copy-start(bf16[4,256,128]{2,1,0:T(8,128)(2,1)} %get-tuple-element.31.keep_ref) | copy-start | bytes 786436
  15.2 17.5 %copy-start.7 = (f32[2]{0:T(128)S(1)}, f32[2]{0:T(128)}, u32[]{:S(2)}) copy-start(f32[2]{0:T(128)} %param.22) | copy-start | bytes 28
  19.9 8.3 %collective-permute-start.3 = (bf16[4,256,128]{2,1,0:T(8,128)(2,1)S(1)}, bf16[4,256,128]{2,1,0:T(8,128)(2,1)S(1)}, u32[]{:S(2)}, u32[]{:S(2)}) collective-permute-start(bf16[4,256,128]{2,1,0:T(8,128)(2,1)S(1)} %get-tuple-element.34), channel_id=1, source_target_pairs={{0,4},{4,0},{8,12},{12,8},{16,20},{20,16},{24,28},{28,24},{1,5},{5... | collective-permute-start | bytes 786440 | tf_op jit(solution)/shard_map/ppermute | solution.py:26
  21.9 10.6 %collective-permute-start.8 = (bf16[256,128]{1,0:T(8,128)(2,1)S(1)}, bf16[256,128]{1,0:T(8,128)(2,1)S(1)}, u32[]{:S(2)}, u32[]{:S(2)}) collective-permute-start(bf16[256,128]{1,0:T(8,128)(2,1)S(1)} %get-tuple-element.41), channel_id=1, source_target_pairs={{0,8},{4,12},{8,0},{12,4},{16,24},{20,28},{24,16},{28,20},{1,9},{5... | collective-permute-start | bytes 196616 | tf_op jit(solution)/shard_map/ppermute | solution.py:26
  23.2 9.4 %collective-permute-start.9 = (bf16[256,128]{1,0:T(8,128)(2,1)S(1)}, bf16[256,128]{1,0:T(8,128)(2,1)S(1)}, u32[]{:S(2)}, u32[]{:S(2)}) collective-permute-start(bf16[256,128]{1,0:T(8,128)(2,1)S(1)} %get-tuple-element.42), channel_id=1, source_target_pairs={{0,16},{4,20},{8,24},{12,28},{16,0},{20,4},{24,8},{28,12},{1,17},{... | collective-permute-start | bytes 196616 | tf_op jit(solution)/shard_map/ppermute | solution.py:26
  26.2 6.5 %collective-permute-start.10 = (bf16[256,128]{1,0:T(8,128)(2,1)S(1)}, bf16[256,128]{1,0:T(8,128)(2,1)S(1)}, u32[]{:S(2)}, u32[]{:S(2)}) collective-permute-start(bf16[256,128]{1,0:T(8,128)(2,1)S(1)} %get-tuple-element.43), channel_id=1, source_target_pairs={{0,24},{4,28},{8,16},{12,20},{16,8},{20,12},{24,0},{28,4},{1,25},{... | collective-permute-start | bytes 196616 | tf_op jit(solution)/shard_map/ppermute | solution.py:26
  28.2 11.2 %collective-permute-start.4 = (bf16[256,128]{1,0:T(8,128)(2,1)S(1)}, bf16[256,128]{1,0:T(8,128)(2,1)S(1)}, u32[]{:S(2)}, u32[]{:S(2)}) collective-permute-start(bf16[256,128]{1,0:T(8,128)(2,1)S(1)} %get-tuple-element.36), channel_id=1, source_target_pairs={{0,8},{4,12},{8,0},{12,4},{16,24},{20,28},{24,16},{28,20},{1,9},{5... | collective-permute-start | bytes 196616 | tf_op jit(solution)/shard_map/ppermute | solution.py:26
  29.8 9.7 %collective-permute-start.5 = (bf16[256,128]{1,0:T(8,128)(2,1)S(1)}, bf16[256,128]{1,0:T(8,128)(2,1)S(1)}, u32[]{:S(2)}, u32[]{:S(2)}) collective-permute-start(bf16[256,128]{1,0:T(8,128)(2,1)S(1)} %get-tuple-element.37), channel_id=1, source_target_pairs={{0,16},{4,20},{8,24},{12,28},{16,0},{20,4},{24,8},{28,12},{1,17},{... | collective-permute-start | bytes 196616 | tf_op jit(solution)/shard_map/ppermute | solution.py:26
  32.5 7.0 %collective-permute-start.6 = (bf16[256,128]{1,0:T(8,128)(2,1)S(1)}, bf16[256,128]{1,0:T(8,128)(2,1)S(1)}, u32[]{:S(2)}, u32[]{:S(2)}) collective-permute-start(bf16[256,128]{1,0:T(8,128)(2,1)S(1)} %get-tuple-element.38), channel_id=1, source_target_pairs={{0,24},{4,28},{8,16},{12,20},{16,8},{20,12},{24,0},{28,4},{1,25},{... | collective-permute-start | bytes 196616 | tf_op jit(solution)/shard_map/ppermute | solution.py:26
  32.7 12.6 %copy-start = (bf16[1024,1024]{1,0:T(8,128)(2,1)S(1)}, bf16[1024,1024]{1,0:T(8,128)(2,1)}, u32[]{:S(2)}) copy-start(bf16[1024,1024]{1,0:T(8,128)(2,1)} %w_ref.1) | copy-start | bytes 6291460
  39.7 1.9 %collective-permute-start.11 = (bf16[128,256]{1,0:T(8,128)(2,1)S(1)}, bf16[128,256]{1,0:T(8,128)(2,1)S(1)}, u32[]{:S(2)}, u32[]{:S(2)}) collective-permute-start(bf16[128,256]{1,0:T(8,128)(2,1)S(1)} %get-tuple-element.54), channel_id=1, source_target_pairs={{0,1},{1,0},{2,3},{3,2},{4,5},{5,4},{6,7},{7,6},{8,9},{9,8},{10,11... | collective-permute-start | bytes 196616 | tf_op jit(solution)/shard_map/ppermute | solution.py:26
  39.8 5.0 %collective-permute-start.12 = (bf16[128,256]{1,0:T(8,128)(2,1)S(1)}, bf16[128,256]{1,0:T(8,128)(2,1)S(1)}, u32[]{:S(2)}, u32[]{:S(2)}) collective-permute-start(bf16[128,256]{1,0:T(8,128)(2,1)S(1)} %get-tuple-element.55), channel_id=1, source_target_pairs={{0,2},{1,3},{2,0},{3,1},{4,6},{5,7},{6,4},{7,5},{8,10},{9,11},{10,... | collective-permute-start | bytes 196616 | tf_op jit(solution)/shard_map/ppermute | solution.py:26
  40.4 4.9 %collective-permute-start.13 = (bf16[128,256]{1,0:T(8,128)(2,1)S(1)}, bf16[128,256]{1,0:T(8,128)(2,1)S(1)}, u32[]{:S(2)}, u32[]{:S(2)}) collective-permute-start(bf16[128,256]{1,0:T(8,128)(2,1)S(1)} %get-tuple-element.56), channel_id=1, source_target_pairs={{0,3},{1,2},{2,1},{3,0},{4,7},{5,6},{6,5},{7,4},{8,11},{9,10},{10,... | collective-permute-start | bytes 196616 | tf_op jit(solution)/shard_map/ppermute | solution.py:26

commit v6 on v5

--- a/solution.py
+++ b/solution.py
@@ -62,8 +62,8 @@
     )
 
 
-def sums_kernel(heads, owners, table_hbm, keys_hbm, values_hbm, prompt_hbm,
-                send_gram, send_cross, keep_gram, keep_cross,
+def sums_kernel(heads, owners, table_hbm, keys_hbm, values_hbm, prompt_hbm, tokens_hbm,
+                send_gram, send_cross, keep_gram, keep_cross, tokens_ref,
                 acc_ref, keys_ref, values_ref, stored_ref, table_ref, list_ref,
                 key_sem, value_sem, small_sem):
     pool, rows = keys_hbm.shape[0], keys_hbm.shape[1]
@@ -71,8 +71,10 @@
     mine = lax.axis_index("grp")
     load_table = pltpu.make_async_copy(table_hbm, table_ref, small_sem.at[0])
     load_prompt = pltpu.make_async_copy(prompt_hbm, stored_ref, small_sem.at[1])
+    load_tokens = pltpu.make_async_copy(tokens_hbm, tokens_ref, small_sem.at[2])
     load_table.start()
     load_prompt.start()
+    load_tokens.start()
     acc_ref[...] = jnp.zeros_like(acc_ref)
     load_table.wait()
 
@@ -143,6 +145,7 @@
         return carry
 
     lax.fori_loop(0, turns, one_turn, 0)
+    load_tokens.wait()
     load_prompt.wait()
     stored = stored_ref.shape[0]
 
@@ -168,15 +171,15 @@
         keep_cross[pair] = acc_ref[here, :, HDIM:].astype(BF16)
 
 
-def page_sums(table, keys, values, prompt_state, owners):
+def page_sums(table, keys, values, prompt_state, tokens, owners):
     pool, rows, _ = keys.shape
     heads = prompt_state.shape[1]
     half = (owners // 2, heads * HDIM, HDIM)
     items = pool + 4
     return pl.pallas_call(
         functools.partial(sums_kernel, heads, owners),
-        in_specs=[pl.BlockSpec(memory_space=pl.ANY)] * 4,
-        out_specs=[pl.BlockSpec(memory_space=pltpu.VMEM)] * 4,
+        in_specs=[pl.BlockSpec(memory_space=pl.ANY)] * 5,
+        out_specs=[pl.BlockSpec(memory_space=pltpu.VMEM)] * 5,
         scratch_shapes=[
             pltpu.VMEM((owners + 1, heads * HDIM, 2 * HDIM), F32),
             pltpu.VMEM((items, rows, HDIM), BF16),
@@ -186,9 +189,10 @@
             pltpu.SMEM((items,), jnp.int32),
             pltpu.SemaphoreType.DMA((items,)),
             pltpu.SemaphoreType.DMA((items,)),
-            pltpu.SemaphoreType.DMA((2,)),
+            pltpu.SemaphoreType.DMA((3,)),
         ],
-        out_shape=[jax.ShapeDtypeStruct(half, BF16)] * 4,
+        out_shape=[jax.ShapeDtypeStruct(half, BF16)] * 4
+        + [jax.ShapeDtypeStruct(tokens.shape, BF16)],
         compiler_params=pltpu.CompilerParams(vmem_limit_bytes=PAGE_VMEM * 2**20),
         cost_estimate=pl.CostEstimate(
             flops=8 * pool * rows * heads * HDIM * HDIM,
@@ -196,23 +200,23 @@
             transcendentals=0,
         ),
         name="page_sums",
-    )(table, keys, values, prompt_state)
-
-
-def halve_kernel(keep_ref, got_ref, *outs):
-    for distance, out_ref in enumerate(outs):
+    )(table, keys, values, prompt_state, tokens)
+
+
+def halve_kernel(keep_ref, got_ref, *refs):
+    for distance, out_ref in enumerate(refs[-keep_ref.shape[0] :]):
         row = (lax.axis_index("grp") >> 1) ^ distance
         total = keep_ref[row].astype(F32) + got_ref[row].astype(F32)
         out_ref[...] = total.astype(out_ref.dtype)
 
 
-def halve_sums(keep, got):
+def halve_sums(keep, got, after=()):
     count, rows, cols = keep.shape
     outs = [jax.ShapeDtypeStruct((rows, cols), F32 if i == 0 else BF16) for i in range(count)]
     whole = pl.BlockSpec(memory_space=pltpu.VMEM)
     return pl.pallas_call(
         halve_kernel,
-        in_specs=[whole, whole],
+        in_specs=[whole] * (2 + len(after)),
         out_specs=[whole] * count,
         out_shape=outs,
         compiler_params=pltpu.CompilerParams(vmem_limit_bytes=32 * 2**20),
@@ -220,7 +224,7 @@
             flops=count * rows * cols, bytes_accessed=6 * count * rows * cols, transcendentals=0
         ),
         name="halve_sums",
-    )(keep, got)
+    )(keep, got, *after)
 
 
 def token_kernel(heads, *refs):
@@ -313,7 +317,7 @@
 
 
 def token_vectors(
-    decay_rate, blocks, norm_gain, w_qkv, w_gates, conv_weight, conv_state, held
+    decay_rate, blocks, norm_gain, w_qkv, w_gates, conv_weight, conv_state, after
 ):
     head_count = len(blocks)
     heads = HEADS // head_count
@@ -334,8 +338,8 @@
     ]
     return pl.pallas_call(
         functools.partial(token_kernel, heads),
-        in_specs=[whole] * head_count + [whole, anywhere] + [whole] * 4 + [anywhere],
-        out_specs=[anywhere] + [whole] * len(outs),
+        in_specs=[whole] * head_count + [whole, anywhere] + [whole] * 5,
+        out_specs=[whole] * len(outs),
         scratch_shapes=[
             pltpu.VMEM((8 + length, width), F32),
             pltpu.VMEM((length, HDIM), F32),
@@ -343,8 +347,7 @@
             pltpu.VMEM((model, width), BF16),
             pltpu.SemaphoreType.DMA,
         ],
-        out_shape=[jax.ShapeDtypeStruct(held.shape, held.dtype)] + outs,
-        input_output_aliases={head_count + 6: 0},
+        out_shape=outs,
         compiler_params=pltpu.CompilerParams(vmem_limit_bytes=TOKEN_VMEM * 2**20),
         cost_estimate=pl.CostEstimate(
             flops=2 * length * model * width,
@@ -360,7 +363,7 @@
         conv_weight,
         conv_state,
         decay_rate.reshape(1, HEADS),
-        held,
+        after,
     )
 
 
@@ -536,11 +539,6 @@
 ):
     head_count = lax.axis_size("head")
     owners = lax.axis_size("grp")
-    bits = [head_count >> i for i in range(1, head_count.bit_length())]
-    blocks = {0: tokens}
-    for bit in bits:
-        blocks[bit] = swap(tokens, "head", bit)
-
     pool, page, heads, _ = cache_keys.shape
     starts = jnp.arange(page_table.shape[1], dtype=jnp.int32) * PAGE
     live = jnp.clip(cache_lengths[:, None] - starts, 0, PAGE)
@@ -551,25 +549,29 @@
     def scattered(parts):
         return [parts[0]] + [swap(parts[i], "grp", 2 * i) for i in range(1, owners // 2)]
 
-    send_gram, send_cross, keep_gram, keep_cross = page_sums(
-        table, keys, values, prompt_state, owners
+    send_gram, send_cross, keep_gram, keep_cross, handed = page_sums(
+        table, keys, values, prompt_state, tokens, owners
     )
     got_gram = swap(send_gram, "grp", 1)
-    for bit in bits[1:]:
+
+    blocks = {0: handed}
+    bit = head_count // 2
+    while bit:
         for distance in list(blocks):
-            if distance and not distance & bit and distance ^ bit not in blocks:
-                blocks[distance] = hold(blocks[distance], keep_gram)
-                blocks[distance ^ bit] = swap(blocks[distance], "head", bit)
+            blocks[distance ^ bit] = swap(blocks[distance], "head", bit)
+        bit //= 2
     blocks = [blocks[i] for i in range(head_count)]
-    send_cross, *vectors = token_vectors(
-        decay_rate, blocks, norm_gain, w_qkv, w_gates, conv_weight, conv_state, send_cross
+
+    grams = halve_sums(keep_gram, got_gram)
+    got_cross = swap(hold(send_cross, grams[0]), "grp", 1)
+    vectors = token_vectors(
+        decay_rate, blocks, norm_gain, w_qkv, w_gates, conv_weight, conv_state, grams[0]
     )
-    grams = halve_sums(keep_gram, got_gram)
-    crosses = halve_sums(keep_cross, swap(send_cross, "grp", 1))
+    crosses = halve_sums(keep_cross, got_cross, vectors[-1:])
     base, solved = ridge_reads(ridge, scattered(grams), vectors, [crosses[0]])
     reads = cross_reads(scattered(crosses), base, solved, head_count)
     reads = [reads[0]] + [swap(reads[i], "head", i) for i in range(1, head_count)]
-    return output_rows(tokens, w_out, reads)
+    return output_rows(handed, w_out, reads)
 
 
 def solution(mesh):

time: 46.6 us -> 51 us (1.094)
  waiting for transfers between devices: 6.34 us -> 10.2 us
  local copies, waits for them, and re-layouts: 0.22 us -> 1.15 us
    ppermute x14, waiting for transfers between devices: 6.34 us -> 10.2 us  [swap(): return lax.ppermute(block, axis, [(i, i ^ distance) for i in range(size)])]
    unnamed x19, local copies, waits for them, and re-layouts: 0.22 us -> 1.15 us
  transfers between devices with their start and end apart: 14 -> 14, of which waited for: 4 -> 4; matrix products, arithmetic and copies ran while one was open for 3% -> 0% of each run, Pallas kernels for 43% -> 23%
where the time goes in v6:
time: 51 us; the launch traced here: 50.8 us
  Pallas kernels  21.5 us (42%)
  starting transfers between devices  16.4 us (32%)
  waiting for transfers between devices  10.2 us (20%)
  other arithmetic  1.42 us (3%)
  local copies, waits for them, and re-layouts  1.15 us (2%)
    ppermute x14, starting transfers between devices, swap(): return lax.ppermute(block, axis, [(i, i ^ distance) for i in range(size)])  16.4 us
    ppermute x14, waiting for transfers between devices, swap(): return lax.ppermute(block, axis, [(i, i ^ distance) for i in range(size)])  10.2 us
    pallas_call x1, Pallas kernels, page_sums(): pl.pallas_call(functools.partial(sums_kernel, heads, owners), in_specs=[p...  8.46 us
    pallas_call x1, Pallas kernels, ridge_reads(): pl.pallas_call(functools.partial(read_kernel, heads, len(grams)), in_spec...  6.74 us
    pallas_call x1, Pallas kernels, token_vectors(): pl.pallas_call(functools.partial(token_kernel, heads), in_specs=[whole] *...  4.73 us
    pallas_call x1, Pallas kernels, output_rows(): pl.pallas_call(output_kernel, in_specs=[whole] * (2 + len(reads)), out_sp...  1.18 us
    unnamed x19, local copies, waits for them, and re-layouts  1.15 us
  transfers between devices with their start and end apart: 14, of which 4 were waited for; matrix products, arithmetic and copies ran while one was open for 0% of the time, Pallas kernels for 23%

profile of v6, /device:TPU:0, one launch (start us, length us, event | category | flops | bytes accessed | tf_op | source)
XLA Modules:
  0.0 50.8 jit_solution(4657243512390822506)
XLA Ops:
  0.0 0.7 %broadcast_shift-left_fusion = s32[8]{0:T(128)S(1)} fusion(s32[8]{0:T(128)} %param.28), kind=kLoop, calls=%fused_computation.2 | loop fusion | flops 8 | bytes 64 | tf_op jit(solution)/shard_map/shift_left | solution.py:545
  0.7 0.8 %or_or_fusion.table_hbm = s32[8,64]{1,0:T(8,128)S(1)} fusion(s32[8,64]{1,0:T(8,128)} %param.26, s32[8]{0:T(128)S(1)} %broadcast_shift-left_fusion, s32[64]{0:T(128)S(1)} %iota_multiply_fusion, s32[8]{0:T(128)} %param.27), kind=kLoop, calls=%fused_computation | loop fusion | flops 2560 | bytes 4416 | tf_op jit(solution)/shard_map/or | solution.py:545
  1.4 0.0 copy-start.8
  1.4 0.0 copy-start.3
  1.4 0.0 copy-start.4
  1.4 0.0 copy-start.5
  1.5 0.0 copy-start.6
  1.5 8.5 %page_sums.1 = (bf16[4,256,128]{2,1,0:T(8,128)(2,1)S(1)}, bf16[4,256,128]{2,1,0:T(8,128)(2,1)S(1)}, bf16[4,256,128]{2,1,0:T(8,128)(2,1)S(1)}, bf16[4,256,128]{2,1,0:T(8,128)(2,1)}, bf16[128,1024]{1,0:T(8,128)(2,1)}) custom-call(s32[8,64]{1,0:T(8,128)S(1)} %or_or_fusion.table_hbm, bf16[64,256,128]{2,1,0:T(8,128)(2,1)} %bitcast.8, ...), custom_call_target="tpu_custom_call" | custom-call | flops 4294967296 | bytes 8388608 | tf_op jit(solution)/shard_map/page_sums/pallas_call | solution.py:179
  9.9 3.0 %collective-permute-start.3 = (bf16[128,1024]{1,0:T(8,128)(2,1)}, bf16[128,1024]{1,0:T(8,128)(2,1)S(1)}, u32[]{:S(2)}, u32[]{:S(2)}) collective-permute-start(bf16[128,1024]{1,0:T(8,128)(2,1)} %get-tuple-element.31.refs_0_.tokens_ref), channel_id=1, source_target_pairs={{0,2},{1,3},{2,0},{3,1},{4,6},{5,7},{6,4},{7,5},{8,10},{9,11},{10,... | collective-permute-start | bytes 786440 | tf_op jit(solution)/shard_map/ppermute | solution.py:26
  12.9 1.2 %collective-permute-start = (bf16[4,256,128]{2,1,0:T(8,128)(2,1)S(1)}, bf16[4,256,128]{2,1,0:T(8,128)(2,1)S(1)}, u32[]{:S(2)}, u32[]{:S(2)}) collective-permute-start(bf16[4,256,128]{2,1,0:T(8,128)(2,1)S(1)} %get-tuple-element.35), channel_id=1, source_target_pairs={{0,4},{4,0},{8,12},{12,8},{16,20},{20,16},{24,28},{28,24},{1,5},{5... | collective-permute-start | bytes 786440 | tf_op jit(solution)/shard_map/ppermute | solution.py:26
  14.2 0.0 collective-permute-start.2
  14.2 5.3 %collective-permute-done.3.refs_2_ = bf16[128,1024]{1,0:T(8,128)(2,1)S(1)} collective-permute-done((bf16[128,1024]{1,0:T(8,128)(2,1)}, bf16[128,1024]{1,0:T(8,128)(2,1)S(1)}, u32[]{:S(2)}, u32[]{:S(2)}) %collective-permute-start.3) | collective-permute-done | bytes 262176 | tf_op jit(solution)/shard_map/ppermute | solution.py:26
  19.5 0.0 collective-permute-start.4
  19.5 1.2 %collective-permute-done.got_ref = bf16[4,256,128]{2,1,0:T(8,128)(2,1)S(1)} collective-permute-done((bf16[4,256,128]{2,1,0:T(8,128)(2,1)S(1)}, bf16[4,256,128]{2,1,0:T(8,128)(2,1)S(1)}, u32[]{:S(2)}, u32[]{:S(2)}) %collective-permute-start) | collective-permute-done | bytes 262176 | tf_op jit(solution)/shard_map/ppermute | solution.py:26
  20.7 0.1 halve_sums.2
  20.8 0.0 copy-start.2
  20.8 1.3 %collective-permute-start.1 = (bf16[4,256,128]{2,1,0:T(8,128)(2,1)S(1)}, bf16[4,256,128]{2,1,0:T(8,128)(2,1)S(1)}, u32[]{:S(2)}, u32[]{:S(2)}) collective-permute-start(bf16[4,256,128]{2,1,0:T(8,128)(2,1)S(1)} %hold.1), channel_id=1, source_target_pairs={{0,4},{4,0},{8,12},{12,8},{16,20},{20,16},{24,28},{28,24},{1,5},{5... | collective-permute-start | bytes 786440 | tf_op jit(solution)/shard_map/ppermute | solution.py:26
  22.1 0.0 copy-done.8
  22.1 0.2 copy.17.refs_6_
  22.3 1.6 %collective-permute-start.8 = (bf16[256,128]{1,0:T(8,128)(2,1)S(1)}, bf16[256,128]{1,0:T(8,128)(2,1)S(1)}, u32[]{:S(2)}, u32[]{:S(2)}) collective-permute-start(bf16[256,128]{1,0:T(8,128)(2,1)S(1)} %get-tuple-element.42), channel_id=1, source_target_pairs={{0,8},{4,12},{8,0},{12,4},{16,24},{20,28},{24,16},{28,20},{1,9},{5... | collective-permute-start | bytes 196616 | tf_op jit(solution)/shard_map/ppermute | solution.py:26
  23.9 2.1 %collective-permute-start.9 = (bf16[256,128]{1,0:T(8,128)(2,1)S(1)}, bf16[256,128]{1,0:T(8,128)(2,1)S(1)}, u32[]{:S(2)}, u32[]{:S(2)}) collective-permute-start(bf16[256,128]{1,0:T(8,128)(2,1)S(1)} %get-tuple-element.43), channel_id=1, source_target_pairs={{0,16},{4,20},{8,24},{12,28},{16,0},{20,4},{24,8},{28,12},{1,17},{... | collective-permute-start | bytes 196616 | tf_op jit(solution)/shard_map/ppermute | solution.py:26
  26.0 0.0 collective-permute-done.2.refs_1_
  26.0 0.7 %collective-permute-start.10 = (bf16[256,128]{1,0:T(8,128)(2,1)S(1)}, bf16[256,128]{1,0:T(8,128)(2,1)S(1)}, u32[]{:S(2)}, u32[]{:S(2)}) collective-permute-start(bf16[256,128]{1,0:T(8,128)(2,1)S(1)} %get-tuple-element.44), channel_id=1, source_target_pairs={{0,24},{4,28},{8,16},{12,20},{16,8},{20,12},{24,0},{28,4},{1,25},{... | collective-permute-start | bytes 196616 | tf_op jit(solution)/shard_map/ppermute | solution.py:26
  26.7 0.0 collective-permute-done.4.refs_3_
  26.7 0.0 copy-done.3
  26.7 0.0 copy-done.4
  26.7 0.0 copy-done.5
  26.7 0.0 copy-done.6
  26.7 0.0 copy-start.1
  26.8 0.9 %copy-done.1 = bf16[128,1024]{1,0:T(8,128)(2,1)S(1)} copy-done((bf16[128,1024]{1,0:T(8,128)(2,1)S(1)}, bf16[128,1024]{1,0:T(8,128)(2,1)}, u32[]{:S(2)}) %copy-start.1) | copy-done | bytes 262168
  27.7 0.0 copy-start.7
  27.7 4.7 %token_vectors.1 = (bf16[2,128,512]{2,1,0:T(8,128)(2,1)S(1)}, bf16[2,512,128]{2,1,0:T(8,128)(2,1)S(1)}, bf16[2,128,512]{2,1,0:T(8,128)(2,1)S(1)}, bf16[2,128,512...) custom-call(bf16[128,1024]{1,0:T(8,128)(2,1)S(1)} %copy-done.1, ...), custom_call_target="tpu_custom_call" | custom-call | flops 805306368 | bytes 6815744 | tf_op jit(solution)/shard_map/token_vectors/pallas_call | solution.py:339
  32.4 0.0 collective-permute-done.1.got_ref
  32.4 0.0 copy-done.2
  32.5 0.1 halve_sums.3
  32.5 0.7 %collective-permute-start.5 = (bf16[256,128]{1,0:T(8,128)(2,1)S(1)}, bf16[256,128]{1,0:T(8,128)(2,1)S(1)}, u32[]{:S(2)}, u32[]{:S(2)}) collective-permute-start(bf16[256,128]{1,0:T(8,128)(2,1)S(1)} %get-tuple-element.39), channel_id=1, source_target_pairs={{0,8},{4,12},{8,0},{12,4},{16,24},{20,28},{24,16},{28,20},{1,9},{5... | collective-permute-start | bytes 196616 | tf_op jit(solution)/shard_map/ppermute | solution.py:26
  33.3 3.0 %collective-permute-start.6 = (bf16[256,128]{1,0:T(8,128)(2,1)S(1)}, bf16[256,128]{1,0:T(8,128)(2,1)S(1)}, u32[]{:S(2)}, u32[]{:S(2)}) collective-permute-start(bf16[256,128]{1,0:T(8,128)(2,1)S(1)} %get-tuple-element.40), channel_id=1, source_target_pairs={{0,16},{4,20},{8,24},{12,28},{16,0},{20,4},{24,8},{28,12},{1,17},{... | collective-permute-start | bytes 196616 | tf_op jit(solution)/shard_map/ppermute | solution.py:26
  36.3 0.0 collective-permute-done.8.refs_1_
  36.3 0.7 %collective-permute-start.7 = (bf16[256,128]{1,0:T(8,128)(2,1)S(1)}, bf16[256,128]{1,0:T(8,128)(2,1)S(1)}, u32[]{:S(2)}, u32[]{:S(2)}) collective-permute-start(bf16[256,128]{1,0:T(8,128)(2,1)S(1)} %get-tuple-element.41), channel_id=1, source_target_pairs={{0,24},{4,28},{8,16},{12,20},{16,8},{20,12},{24,0},{28,4},{1,25},{... | collective-permute-start | bytes 196616 | tf_op jit(solution)/shard_map/ppermute | solution.py:26
  37.0 0.0 collective-permute-done.9.refs_2_
  37.0 0.0 collective-permute-done.10.refs_3_
  37.0 0.0 copy-done.7
  37.0 0.0 copy-start
  37.0 6.7 %ridge_reads.1 = (f32[512,256]{1,0:T(8,128)S(1)}, bf16[512,256]{1,0:T(8,128)(2,1)S(1)}) custom-call(f32[1,2]{1,0:T(1,128)S(1)} %bitcast.7, f32[256,128]{1,0:T(8,128)S(1)} %get-tuple-element.36.refs_1_.refs_10_.refs_0_, bf16[256,128]{1,0:T(8,128)(2,1)S(1)} %collective-permute-done.8.refs_1_, bf16[256,128]{1,0:T(8,128)(2,1)S(1)} %collective-permute-done.9.refs_2_, ...), custom_call_target="tpu_custom_call" | custom-call | flops 6442450944 | bytes 8388608 | tf_op jit(solution)/shard_map/ridge_reads/pallas_call | solution.py:441
  43.8 0.0 collective-permute-done.5.refs_1_
  43.8 0.0 collective-permute-done.6.refs_2_
  43.8 0.0 collective-permute-done.7.refs_3_
  43.8 0.3 cross_reads.1
  44.1 0.1 collective-permute-start.11
  44.1 0.6 %collective-permute-start.12 = (bf16[128,256]{1,0:T(8,128)(2,1)S(1)}, bf16[128,256]{1,0:T(8,128)(2,1)S(1)}, u32[]{:S(2)}, u32[]{:S(2)}) collective-permute-start(bf16[128,256]{1,0:T(8,128)(2,1)S(1)} %get-tuple-element.55), channel_id=1, source_target_pairs={{0,2},{1,3},{2,0},{3,1},{4,6},{5,7},{6,4},{7,5},{8,10},{9,11},{10,... | collective-permute-start | bytes 196616 | tf_op jit(solution)/shard_map/ppermute | solution.py:26
  44.7 1.3 %collective-permute-start.13 = (bf16[128,256]{1,0:T(8,128)(2,1)S(1)}, bf16[128,256]{1,0:T(8,128)(2,1)S(1)}, u32[]{:S(2)}, u32[]{:S(2)}) collective-permute-start(bf16[128,256]{1,0:T(8,128)(2,1)S(1)} %get-tuple-element.56), channel_id=1, source_target_pairs={{0,3},{1,2},{2,1},{3,0},{4,7},{5,6},{6,5},{7,4},{8,11},{9,10},{10,... | collective-permute-start | bytes 196616 | tf_op jit(solution)/shard_map/ppermute | solution.py:26
  46.0 0.0 collective-permute-done.11.refs_1_
  46.0 3.1 %collective-permute-done.12.refs_2_ = bf16[128,256]{1,0:T(8,128)(2,1)S(1)} collective-permute-done((bf16[128,256]{1,0:T(8,128)(2,1)S(1)}, bf16[128,256]{1,0:T(8,128)(2,1)S(1)}, u32[]{:S(2)}, u32[]{:S(2)}) %collective-permute-start.12) | collective-permute-done | bytes 65568 | tf_op jit(solution)/shard_map/ppermute | solution.py:26
  49.1 0.5 collective-permute-done.13.refs_3_
  49.6 0.0 copy-done
  49.6 1.2 %output_rows.1 = bf16[128,1024]{1,0:T(8,128)(2,1)} custom-call(bf16[128,1024]{1,0:T(8,128)(2,1)S(1)} %copy-done.1, bf16[1024,1024]{1,0:T(8,128)(2,1)S(1)} %copy-done, bf16[128,256]{1,0:T(8,128)(2,1)S(1)} %get-tuple-element.53.refs_0_, bf16[128,256]{1,0:T(8,128)(2,1)S(1)} %collective-permute-done.11.refs_1_, ...), custom_call_target="tpu_custom_call" | custom-call | flops 268435456 | bytes 2883584 | tf_op jit(solution)/shard_map/output_rows/pallas_call | solution.py:508
  (2 shorter events, 0.0 us)
Async XLA Ops:
  1.4 20.7 %copy-start.8 = (bf16[1024,16]{0,1:T(8,128)(2,1)S(1)}, bf16[1024,16]{0,1:T(8,128)(2,1)}, u32[]{:S(2)}) copy-start(bf16[1024,16]{0,1:T(8,128)(2,1)} %param.18) | copy-start | bytes 98308
  1.4 25.3 %copy-start.3 = (f32[4,3072]{1,0:T(4,128)S(1)}, f32[4,3072]{1,0:T(4,128)}, u32[]{:S(2)}) copy-start(f32[4,3072]{1,0:T(4,128)} %refs_7_.1) | copy-start | bytes 147460
  1.4 25.3 %copy-start.4 = (bf16[1,3,3072]{2,1,0:T(4,128)(2,1)S(1)}, bf16[1,3,3072]{2,1,0:T(4,128)(2,1)}, u32[]{:S(2)}) copy-start(bf16[1,3,3072]{2,1,0:T(4,128)(2,1)} %refs_8_.1) | copy-start | bytes 55300
  1.4 25.3 %copy-start.5 = (f32[1024]{0:T(1024)S(1)}, f32[1024]{0:T(1024)}, u32[]{:S(2)}) copy-start(f32[1024]{0:T(1024)} %param.16) | copy-start | bytes 12292
  1.5 25.3 %copy-start.6 = (f32[8]{0:T(128)S(1)}, f32[8]{0:T(128)}, u32[]{:S(2)}) copy-start(f32[8]{0:T(128)} %param.21) | copy-start | bytes 100
  9.9 9.5 %collective-permute-start.3 = (bf16[128,1024]{1,0:T(8,128)(2,1)}, bf16[128,1024]{1,0:T(8,128)(2,1)S(1)}, u32[]{:S(2)}, u32[]{:S(2)}) collective-permute-start(bf16[128,1024]{1,0:T(8,128)(2,1)} %get-tuple-element.31.refs_0_.tokens_ref), channel_id=1, source_target_pairs={{0,2},{1,3},{2,0},{3,1},{4,6},{5,7},{6,4},{7,5},{8,10},{9,11},{10,... | collective-permute-start | bytes 786440 | tf_op jit(solution)/shard_map/ppermute | solution.py:26
  12.9 7.8 %collective-permute-start = (bf16[4,256,128]{2,1,0:T(8,128)(2,1)S(1)}, bf16[4,256,128]{2,1,0:T(8,128)(2,1)S(1)}, u32[]{:S(2)}, u32[]{:S(2)}) collective-permute-start(bf16[4,256,128]{2,1,0:T(8,128)(2,1)S(1)} %get-tuple-element.35), channel_id=1, source_target_pairs={{0,4},{4,0},{8,12},{12,8},{16,20},{20,16},{24,28},{28,24},{1,5},{5... | collective-permute-start | bytes 786440 | tf_op jit(solution)/shard_map/ppermute | solution.py:26
  14.2 11.8 %collective-permute-start.2 = (bf16[128,1024]{1,0:T(8,128)(2,1)}, bf16[128,1024]{1,0:T(8,128)(2,1)S(1)}, u32[]{:S(2)}, u32[]{:S(2)}) collective-permute-start(bf16[128,1024]{1,0:T(8,128)(2,1)} %get-tuple-element.31.refs_0_.tokens_ref), channel_id=1, source_target_pairs={{0,1},{1,0},{2,3},{3,2},{4,5},{5,4},{6,7},{7,6},{8,9},{9,8},{10,11... | collective-permute-start | bytes 786440 | tf_op jit(solution)/shard_map/ppermute | solution.py:26
  19.5 7.3 %collective-permute-start.4 = (bf16[128,1024]{1,0:T(8,128)(2,1)S(1)}, bf16[128,1024]{1,0:T(8,128)(2,1)S(1)}, u32[]{:S(2)}, u32[]{:S(2)}) collective-permute-start(bf16[128,1024]{1,0:T(8,128)(2,1)S(1)} %collective-permute-done.3.refs_2_), channel_id=1, source_target_pairs={{0,1},{1,0},{2,3},{3,2},{4,5},{5,4},{6,7},{7,6},{8,9},{9,8},{10,11... | collective-permute-start | bytes 786440 | tf_op jit(solution)/shard_map/ppermute | solution.py:26
  20.8 11.7 %copy-start.2 = (bf16[4,256,128]{2,1,0:T(8,128)(2,1)S(1)}, bf16[4,256,128]{2,1,0:T(8,128)(2,1)}, u32[]{:S(2)}) copy-start(bf16[4,256,128]{2,1,0:T(8,128)(2,1)} %get-tuple-element.32.keep_ref) | copy-start | bytes 786436
  20.8 11.6 %collective-permute-start.1 = (bf16[4,256,128]{2,1,0:T(8,128)(2,1)S(1)}, bf16[4,256,128]{2,1,0:T(8,128)(2,1)S(1)}, u32[]{:S(2)}, u32[]{:S(2)}) collective-permute-start(bf16[4,256,128]{2,1,0:T(8,128)(2,1)S(1)} %hold.1), channel_id=1, source_target_pairs={{0,4},{4,0},{8,12},{12,8},{16,20},{20,16},{24,28},{28,24},{1,5},{5... | collective-permute-start | bytes 786440 | tf_op jit(solution)/shard_map/ppermute | solution.py:26
  22.3 14.0 %collective-permute-start.8 = (bf16[256,128]{1,0:T(8,128)(2,1)S(1)}, bf16[256,128]{1,0:T(8,128)(2,1)S(1)}, u32[]{:S(2)}, u32[]{:S(2)}) collective-permute-start(bf16[256,128]{1,0:T(8,128)(2,1)S(1)} %get-tuple-element.42), channel_id=1, source_target_pairs={{0,8},{4,12},{8,0},{12,4},{16,24},{20,28},{24,16},{28,20},{1,9},{5... | collective-permute-start | bytes 196616 | tf_op jit(solution)/shard_map/ppermute | solution.py:26
  23.9 13.1 %collective-permute-start.9 = (bf16[256,128]{1,0:T(8,128)(2,1)S(1)}, bf16[256,128]{1,0:T(8,128)(2,1)S(1)}, u32[]{:S(2)}, u32[]{:S(2)}) collective-permute-start(bf16[256,128]{1,0:T(8,128)(2,1)S(1)} %get-tuple-element.43), channel_id=1, source_target_pairs={{0,16},{4,20},{8,24},{12,28},{16,0},{20,4},{24,8},{28,12},{1,17},{... | collective-permute-start | bytes 196616 | tf_op jit(solution)/shard_map/ppermute | solution.py:26
  26.0 11.0 %collective-permute-start.10 = (bf16[256,128]{1,0:T(8,128)(2,1)S(1)}, bf16[256,128]{1,0:T(8,128)(2,1)S(1)}, u32[]{:S(2)}, u32[]{:S(2)}) collective-permute-start(bf16[256,128]{1,0:T(8,128)(2,1)S(1)} %get-tuple-element.44), channel_id=1, source_target_pairs={{0,24},{4,28},{8,16},{12,20},{16,8},{20,12},{24,0},{28,4},{1,25},{... | collective-permute-start | bytes 196616 | tf_op jit(solution)/shard_map/ppermute | solution.py:26
  26.7 1.0 %copy-start.1 = (bf16[128,1024]{1,0:T(8,128)(2,1)S(1)}, bf16[128,1024]{1,0:T(8,128)(2,1)}, u32[]{:S(2)}) copy-start(bf16[128,1024]{1,0:T(8,128)(2,1)} %get-tuple-element.31.refs_0_.tokens_ref) | copy-start | bytes 786436
  27.7 9.3 %copy-start.7 = (f32[2]{0:T(128)S(1)}, f32[2]{0:T(128)}, u32[]{:S(2)}) copy-start(f32[2]{0:T(128)} %param.22) | copy-start | bytes 28
  32.5 11.2 %collective-permute-start.5 = (bf16[256,128]{1,0:T(8,128)(2,1)S(1)}, bf16[256,128]{1,0:T(8,128)(2,1)S(1)}, u32[]{:S(2)}, u32[]{:S(2)}) collective-permute-start(bf16[256,128]{1,0:T(8,128)(2,1)S(1)} %get-tuple-element.39), channel_id=1, source_target_pairs={{0,8},{4,12},{8,0},{12,4},{16,24},{20,28},{24,16},{28,20},{1,9},{5... | collective-permute-start | bytes 196616 | tf_op jit(solution)/shard_map/ppermute | solution.py:26
  33.3 10.5 %collective-permute-start.6 = (bf16[256,128]{1,0:T(8,128)(2,1)S(1)}, bf16[256,128]{1,0:T(8,128)(2,1)S(1)}, u32[]{:S(2)}, u32[]{:S(2)}) collective-permute-start(bf16[256,128]{1,0:T(8,128)(2,1)S(1)} %get-tuple-element.40), channel_id=1, source_target_pairs={{0,16},{4,20},{8,24},{12,28},{16,0},{20,4},{24,8},{28,12},{1,17},{... | collective-permute-start | bytes 196616 | tf_op jit(solution)/shard_map/ppermute | solution.py:26
  36.3 7.5 %collective-permute-start.7 = (bf16[256,128]{1,0:T(8,128)(2,1)S(1)}, bf16[256,128]{1,0:T(8,128)(2,1)S(1)}, u32[]{:S(2)}, u32[]{:S(2)}) collective-permute-start(bf16[256,128]{1,0:T(8,128)(2,1)S(1)} %get-tuple-element.41), channel_id=1, source_target_pairs={{0,24},{4,28},{8,16},{12,20},{16,8},{20,12},{24,0},{28,4},{1,25},{... | collective-permute-start | bytes 196616 | tf_op jit(solution)/shard_map/ppermute | solution.py:26
  37.0 12.6 %copy-start = (bf16[1024,1024]{1,0:T(8,128)(2,1)S(1)}, bf16[1024,1024]{1,0:T(8,128)(2,1)}, u32[]{:S(2)}) copy-start(bf16[1024,1024]{1,0:T(8,128)(2,1)} %w_ref.1) | copy-start | bytes 6291460
  44.1 1.9 %collective-permute-start.11 = (bf16[128,256]{1,0:T(8,128)(2,1)S(1)}, bf16[128,256]{1,0:T(8,128)(2,1)S(1)}, u32[]{:S(2)}, u32[]{:S(2)}) collective-permute-start(bf16[128,256]{1,0:T(8,128)(2,1)S(1)} %get-tuple-element.54), channel_id=1, source_target_pairs={{0,1},{1,0},{2,3},{3,2},{4,5},{5,4},{6,7},{7,6},{8,9},{9,8},{10,11... | collective-permute-start | bytes 196616 | tf_op jit(solution)/shard_map/ppermute | solution.py:26
  44.1 5.0 %collective-permute-start.12 = (bf16[128,256]{1,0:T(8,128)(2,1)S(1)}, bf16[128,256]{1,0:T(8,128)(2,1)S(1)}, u32[]{:S(2)}, u32[]{:S(2)}) collective-permute-start(bf16[128,256]{1,0:T(8,128)(2,1)S(1)} %get-tuple-element.55), channel_id=1, source_target_pairs={{0,2},{1,3},{2,0},{3,1},{4,6},{5,7},{6,4},{7,5},{8,10},{9,11},{10,... | collective-permute-start | bytes 196616 | tf_op jit(solution)/shard_map/ppermute | solution.py:26
  44.7 4.9 %collective-permute-start.13 = (bf16[128,256]{1,0:T(8,128)(2,1)S(1)}, bf16[128,256]{1,0:T(8,128)(2,1)S(1)}, u32[]{:S(2)}, u32[]{:S(2)}) collective-permute-start(bf16[128,256]{1,0:T(8,128)(2,1)S(1)} %get-tuple-element.56), channel_id=1, source_target_pairs={{0,3},{1,2},{2,1},{3,0},{4,7},{5,6},{6,5},{7,4},{8,11},{9,10},{10,... | collective-permute-start | bytes 196616 | tf_op jit(solution)/shard_map/ppermute | solution.py:26

commit v7 on v5

--- a/solution.py
+++ b/solution.py
@@ -62,19 +62,18 @@
     )
 
 
-def sums_kernel(heads, owners, table_hbm, keys_hbm, values_hbm, prompt_hbm,
+def sums_kernel(heads, owners, code_hbm, keys_hbm, values_hbm, prompt_hbm,
                 send_gram, send_cross, keep_gram, keep_cross,
-                acc_ref, keys_ref, values_ref, stored_ref, table_ref, list_ref,
+                acc_ref, keys_ref, values_ref, stored_ref, code_ref, pick_ref, list_ref,
                 key_sem, value_sem, small_sem):
     pool, rows = keys_hbm.shape[0], keys_hbm.shape[1]
-    slots = table_hbm.shape[1]
     mine = lax.axis_index("grp")
-    load_table = pltpu.make_async_copy(table_hbm, table_ref, small_sem.at[0])
+    load_code = pltpu.make_async_copy(code_hbm, code_ref, small_sem.at[0])
     load_prompt = pltpu.make_async_copy(prompt_hbm, stored_ref, small_sem.at[1])
-    load_table.start()
+    load_code.start()
     load_prompt.start()
     acc_ref[...] = jnp.zeros_like(acc_ref)
-    load_table.wait()
+    load_code.wait()
 
     def load(item):
         page = list_ref[item] & 0xFFFF
@@ -88,27 +87,19 @@
             copy.start()
         return carry
 
-    first = mine * pool
     wide = 8
-    count = jnp.int32(0)
-    for owner in range(owners):
-
-        def note(chunk, count):
-            for i in range(wide):
-                entry = table_ref[owner, chunk * wide + i]
-                page = (entry & 0xFFFF) - first
-                live = entry & 0xFF0000
-                list_ref[count] = (owner << 24) | live | (page & 0xFFFF)
-                inside = (page >= 0) & (page < pool) & (live > 0)
-                count = count + inside.astype(jnp.int32)
-            return count
-
-        chunks = jnp.int32(0)
-        for slot in range(0, slots, wide):
-            chunks = chunks + ((table_ref[owner, slot] & 0xFF0000) > 0).astype(jnp.int32)
-        before = count
-        count = lax.fori_loop(0, chunks, note, before)
-        lax.fori_loop(before, count, start, 0)
+
+    def note(chunk, count):
+        for i in range(wide):
+            page = chunk * wide + i
+            code = code_ref[page]
+            pick_ref[code >> 24] = code & 0xFFFF
+            list_ref[count] = (code & -65536) | page
+            count = count + ((code & 0xFF0000) > 0).astype(jnp.int32)
+        return count
+
+    count = lax.fori_loop(0, pool // wide, note, jnp.int32(0))
+    lax.fori_loop(0, count, start, 0)
 
     turn = 4
     turns = (count + (turn - 1)) >> 2
@@ -149,7 +140,7 @@
     def add_prompt(owner, carry):
         for slot in range(stored):
 
-            @pl.when((table_ref[owner, 0] >> 24) == mine * stored + slot)
+            @pl.when(pick_ref[owner] == mine * stored + slot)
             def _():
                 for head in range(heads):
                     at = slice(head * HDIM, (head + 1) * HDIM)
@@ -168,7 +159,7 @@
         keep_cross[pair] = acc_ref[here, :, HDIM:].astype(BF16)
 
 
-def page_sums(table, keys, values, prompt_state, owners):
+def page_sums(code, keys, values, prompt_state, owners):
     pool, rows, _ = keys.shape
     heads = prompt_state.shape[1]
     half = (owners // 2, heads * HDIM, HDIM)
@@ -182,7 +173,8 @@
             pltpu.VMEM((items, rows, HDIM), BF16),
             pltpu.VMEM((items, rows, HDIM), BF16),
             pltpu.VMEM(prompt_state.shape, F32),
-            pltpu.SMEM(table.shape, jnp.int32),
+            pltpu.SMEM(code.shape, jnp.int32),
+            pltpu.SMEM((owners,), jnp.int32),
             pltpu.SMEM((items,), jnp.int32),
             pltpu.SemaphoreType.DMA((items,)),
             pltpu.SemaphoreType.DMA((items,)),
@@ -196,7 +188,7 @@
             transcendentals=0,
         ),
         name="page_sums",
-    )(table, keys, values, prompt_state)
+    )(code, keys, values, prompt_state)
 
 
 def halve_kernel(keep_ref, got_ref, *outs):
@@ -414,7 +406,7 @@
             later.append(norm_next)
         return tuple(later)
 
-    lax.fori_loop(0, CG_STEPS, one_step, tuple(norms), unroll=2)
+    lax.fori_loop(0, CG_STEPS, one_step, tuple(norms), unroll=4)
     for head, pair in groups:
         cols = slice(head * HDIM, (head + 1) * HDIM)
         span = slice(pair * PAIR, (pair + 1) * PAIR)
@@ -542,17 +534,23 @@
         blocks[bit] = swap(tokens, "head", bit)
 
     pool, page, heads, _ = cache_keys.shape
-    starts = jnp.arange(page_table.shape[1], dtype=jnp.int32) * PAGE
-    live = jnp.clip(cache_lengths[:, None] - starts, 0, PAGE)
-    table = page_table | (live << 16) | (group_prompt[:, None] << 24)
+    slots = jnp.arange(page_table.shape[1], dtype=jnp.int32)
+    live = jnp.clip(cache_lengths[:, None] - slots * PAGE, 0, PAGE)
+    tag = (jnp.arange(owners, dtype=jnp.int32) << 24) | group_prompt
+    tag = tag[:, None] | (live << 16)
+    ids = lax.axis_index("grp").astype(jnp.int32) * pool + jnp.arange(pool, dtype=jnp.int32)
+    code = jnp.sum(
+        jnp.where(page_table[:, :, None] == ids, tag[:, :, None], 0), axis=(0, 1), dtype=jnp.int32
+    )
     keys = cache_keys.reshape(pool, page * heads, HDIM)
     values = cache_values.reshape(pool, page * heads, HDIM)
 
     def scattered(parts):
-        return [parts[0]] + [swap(parts[i], "grp", 2 * i) for i in range(1, owners // 2)]
+        sent = [swap(parts[i], "grp", 2 * i) for i in reversed(range(1, owners // 2))]
+        return [parts[0]] + sent
 
     send_gram, send_cross, keep_gram, keep_cross = page_sums(
-        table, keys, values, prompt_state, owners
+        code, keys, values, prompt_state, owners
     )
     got_gram = swap(send_gram, "grp", 1)
     for bit in bits[1:]:
@@ -568,7 +566,8 @@
     crosses = halve_sums(keep_cross, swap(send_cross, "grp", 1))
     base, solved = ridge_reads(ridge, scattered(grams), vectors, [crosses[0]])
     reads = cross_reads(scattered(crosses), base, solved, head_count)
-    reads = [reads[0]] + [swap(reads[i], "head", i) for i in range(1, head_count)]
+    sent = {i: swap(reads[i], "head", i) for i in reversed(range(1, head_count))}
+    reads = [reads[0]] + [sent[i] for i in range(1, head_count)]
     return output_rows(tokens, w_out, reads)
 
 

time: 46.6 us -> 46.4 us (level)
  Pallas kernels: 21.6 us -> 19.9 us
  other arithmetic: 1.42 us -> 2.3 us
  starting transfers between devices: 16.7 us -> 17.4 us
    pallas_call x1, Pallas kernels: 8.54 us -> 7.09 us  [page_sums(): pl.pallas_call(functools.partial(sums_kernel, heads, owners), in_specs=[p...]
    reduce_sum x0 -> x1, other arithmetic: none -> 0.9 us  [shards(): jnp.sum(jnp.where(page_table[:, :, None] == ids, tag[:, :, None], 0), axi...]
    ppermute x14, starting transfers between devices: 16.7 us -> 17.4 us  [swap(): return lax.ppermute(block, axis, [(i, i ^ distance) for i in range(size)])]
    shift_left x1 -> x0, other arithmetic: 0.66 us -> none  [shards(): table = page_table | live << 16 | group_prompt[:, None] << 24]
    or x1 -> x2, other arithmetic: 0.76 us -> 1.39 us  [the longest x1 0.73 us: shards(): tag = tag[:, None] | live << 16]
  transfers between devices with their start and end apart: 14 -> 14, of which waited for: 4 -> 4; matrix products, arithmetic and copies ran while one was open for 3% -> 5% of each run, Pallas kernels for 43% -> 40%
where the time goes in v7:
time: 46.4 us; the launch traced here: 46.2 us
  Pallas kernels  19.9 us (43%)
  starting transfers between devices  17.4 us (37%)
  waiting for transfers between devices  6.09 us (13%)
  other arithmetic  2.3 us (5%)
    ppermute x14, starting transfers between devices, swap(): return lax.ppermute(block, axis, [(i, i ^ distance) for i in range(size)])  17.4 us
    pallas_call x1, Pallas kernels, page_sums(): pl.pallas_call(functools.partial(sums_kernel, heads, owners), in_specs=[p...  7.09 us
    pallas_call x1, Pallas kernels, ridge_reads(): pl.pallas_call(functools.partial(read_kernel, heads, len(grams)), in_spec...  6.46 us
    ppermute x14, waiting for transfers between devices, swap(): return lax.ppermute(block, axis, [(i, i ^ distance) for i in range(size)])  6.09 us
    pallas_call x1, Pallas kernels, token_vectors(): pl.pallas_call(functools.partial(token_kernel, heads), in_specs=[whole] *...  4.73 us
    pallas_call x1, Pallas kernels, output_rows(): pl.pallas_call(output_kernel, in_specs=[whole] * (2 + len(reads)), out_sp...  1.21 us
  transfers between devices with their start and end apart: 14, of which 4 were waited for; matrix products, arithmetic and copies ran while one was open for 5% of the time, Pallas kernels for 40%

profile of v7, /device:TPU:0, one launch (start us, length us, event | category | flops | bytes accessed | tf_op | source)
XLA Modules:
  0.0 46.2 jit_solution(3098954230220447681)
XLA Ops:
  0.0 2.9 %collective-permute-start.1 = (bf16[128,1024]{1,0:T(8,128)(2,1)}, bf16[128,1024]{1,0:T(8,128)(2,1)S(1)}, u32[]{:S(2)}, u32[]{:S(2)}) collective-permute-start(bf16[128,1024]{1,0:T(8,128)(2,1)} %tokens_ref.1), channel_id=1, source_target_pairs={{0,2},{1,3},{2,0},{3,1},{4,6},{5,7},{6,4},{7,5},{8,10},{9,11},{10,... | collective-permute-start | bytes 786440 | tf_op jit(solution)/shard_map/ppermute | solution.py:26
  2.9 0.0 collective-permute-start
  3.0 0.7 %shift-left_or_fusion.1 = s32[8]{0:T(128)S(1)} fusion(s32[8]{0:T(128)} %param.28), kind=kLoop, calls=%fused_computation.3 | loop fusion | flops 16 | bytes 64 | tf_op jit(solution)/shard_map/or | solution.py:539
  3.6 0.7 %shift-left_or_fusion = s32[8,64]{1,0:T(8,128)S(1)} fusion(s32[64]{0:T(128)S(1)} %iota_multiply_fusion, s32[8]{0:T(128)} %param.27, s32[8]{0:T(128)S(1)} %shift-left_or_fusion.1), kind=kLoop, calls=%fused_computation.1 | loop fusion | flops 2048 | bytes 2368 | tf_op jit(solution)/shard_map/or | solution.py:540
  4.3 0.9 %select_reduce_fusion.code_hbm = s32[64]{0:T(128)S(1)} fusion(s32[8,64]{1,0:T(8,128)S(1)} %shift-left_or_fusion, s32[64]{0:T(128)S(1)} %iota_add_fusion, s32[8,64]{1,0:T(8,128)} %param.26), kind=kLoop, calls=%fused_computation | loop fusion | flops 98240 | bytes 4608 | tf_op jit(solution)/shard_map/reduce_sum | solution.py:542
  5.2 0.0 copy-start.8
  5.3 0.0 copy-start.1
  5.3 0.0 copy-start.3
  5.3 0.0 copy-start.4
  5.3 0.0 copy-start.5
  5.3 0.0 copy-start.6
  5.3 7.1 %page_sums.1 = (bf16[4,256,128]{2,1,0:T(8,128)(2,1)S(1)}, bf16[4,256,128]{2,1,0:T(8,128)(2,1)S(1)}, bf16[4,256,128]{2,1,0:T(8,128)(2,1)S(1)}, bf16[4,256,128]{2,1,0:T(8,128)(2,1)}) custom-call(s32[64]{0:T(128)S(1)} %select_reduce_fusion.code_hbm, bf16[64,256,128]{2,1,0:T(8,128)(2,1)} %bitcast.8, bf16[64,256,128]{2,1,0:T(8,128)(2,1)} %bitcast.9, ...), custom_call_target="tpu_custom_call" | custom-call | flops 4294967296 | bytes 8388608 | tf_op jit(solution)/shard_map/page_sums/pallas_call | solution.py:167
  12.4 0.0 collective-permute-done.1.refs_0_
  12.4 0.6 %collective-permute-start.2 = (bf16[128,1024]{1,0:T(8,128)(2,1)S(1)}, bf16[128,1024]{1,0:T(8,128)(2,1)S(1)}, u32[]{:S(2)}, u32[]{:S(2)}) collective-permute-start(bf16[128,1024]{1,0:T(8,128)(2,1)S(1)} %hold.1.refs_2_), channel_id=1, source_target_pairs={{0,1},{1,0},{2,3},{3,2},{4,5},{5,4},{6,7},{7,6},{8,9},{9,8},{10,11... | collective-permute-start | bytes 786440 | tf_op jit(solution)/shard_map/ppermute | solution.py:26
  13.0 1.3 %collective-permute-start.7 = (bf16[4,256,128]{2,1,0:T(8,128)(2,1)S(1)}, bf16[4,256,128]{2,1,0:T(8,128)(2,1)S(1)}, u32[]{:S(2)}, u32[]{:S(2)}) collective-permute-start(bf16[4,256,128]{2,1,0:T(8,128)(2,1)S(1)} %get-tuple-element.39), channel_id=1, source_target_pairs={{0,4},{4,0},{8,12},{12,8},{16,20},{20,16},{24,28},{28,24},{1,5},{5... | collective-permute-start | bytes 786440 | tf_op jit(solution)/shard_map/ppermute | solution.py:26
  14.3 0.0 copy-done.8
  14.3 0.2 copy.19.refs_6_
  14.5 0.0 collective-permute-done.refs_1_
  14.5 0.0 collective-permute-done.2.refs_3_
  14.5 0.0 copy-done.1
  14.5 0.0 copy-done.3
  14.5 0.0 copy-done.4
  14.6 0.0 copy-done.5
  14.6 0.0 copy-done.6
  14.6 0.0 copy-start.2
  14.6 0.0 copy-start.7
  14.6 4.7 %token_vectors.1 = (bf16[4,256,128]{2,1,0:T(8,128)(2,1)S(1)}, bf16[2,128,512]{2,1,0:T(8,128)(2,1)S(1)}, bf16[2,512,128]{2,1,0:T(8,128)(2,1)S(1)}, bf16[2,128,512...) custom-call(bf16[128,1024]{1,0:T(8,128)(2,1)S(1)} %copy-done.1, ...), custom_call_target="tpu_custom_call", output_to_operand_aliasing={{0}: (10, {})} | custom-call | flops 805306368 | bytes 6815744 | tf_op jit(solution)/shard_map/token_vectors/pallas_call | solution.py:327
  19.3 1.0 %collective-permute-start.3 = (bf16[4,256,128]{2,1,0:T(8,128)(2,1)S(1)}, bf16[4,256,128]{2,1,0:T(8,128)(2,1)S(1)}, u32[]{:S(2)}, u32[]{:S(2)}) collective-permute-start(bf16[4,256,128]{2,1,0:T(8,128)(2,1)S(1)} %get-tuple-element.34), channel_id=1, source_target_pairs={{0,4},{4,0},{8,12},{12,8},{16,20},{20,16},{24,28},{28,24},{1,5},{5... | collective-permute-start | bytes 786440 | tf_op jit(solution)/shard_map/ppermute | solution.py:26
  20.4 0.9 %collective-permute-done.7.got_ref = bf16[4,256,128]{2,1,0:T(8,128)(2,1)S(1)} collective-permute-done((bf16[4,256,128]{2,1,0:T(8,128)(2,1)S(1)}, bf16[4,256,128]{2,1,0:T(8,128)(2,1)S(1)}, u32[]{:S(2)}, u32[]{:S(2)}) %collective-permute-start.7) | collective-permute-done | bytes 262176 | tf_op jit(solution)/shard_map/ppermute | solution.py:26
  21.3 0.1 halve_sums.3
  21.4 4.1 %collective-permute-start.8 = (bf16[256,128]{1,0:T(8,128)(2,1)S(1)}, bf16[256,128]{1,0:T(8,128)(2,1)S(1)}, u32[]{:S(2)}, u32[]{:S(2)}) collective-permute-start(bf16[256,128]{1,0:T(8,128)(2,1)S(1)} %get-tuple-element.41), channel_id=1, source_target_pairs={{0,24},{4,28},{8,16},{12,20},{16,8},{20,12},{24,0},{28,4},{1,25},{... | collective-permute-start | bytes 196616 | tf_op jit(solution)/shard_map/ppermute | solution.py:26
  25.4 0.0 collective-permute-start.9
  25.4 0.6 %collective-permute-start.10 = (bf16[256,128]{1,0:T(8,128)(2,1)S(1)}, bf16[256,128]{1,0:T(8,128)(2,1)S(1)}, u32[]{:S(2)}, u32[]{:S(2)}) collective-permute-start(bf16[256,128]{1,0:T(8,128)(2,1)S(1)} %get-tuple-element.43), channel_id=1, source_target_pairs={{0,8},{4,12},{8,0},{12,4},{16,24},{20,28},{24,16},{28,20},{1,9},{5... | collective-permute-start | bytes 196616 | tf_op jit(solution)/shard_map/ppermute | solution.py:26
  26.1 1.5 %collective-permute-done.3.got_ref = bf16[4,256,128]{2,1,0:T(8,128)(2,1)S(1)} collective-permute-done((bf16[4,256,128]{2,1,0:T(8,128)(2,1)S(1)}, bf16[4,256,128]{2,1,0:T(8,128)(2,1)S(1)}, u32[]{:S(2)}, u32[]{:S(2)}) %collective-permute-start.3) | collective-permute-done | bytes 262176 | tf_op jit(solution)/shard_map/ppermute | solution.py:26
  27.6 0.0 copy-done.2
  27.6 0.1 halve_sums.2
  27.7 4.3 %collective-permute-start.4 = (bf16[256,128]{1,0:T(8,128)(2,1)S(1)}, bf16[256,128]{1,0:T(8,128)(2,1)S(1)}, u32[]{:S(2)}, u32[]{:S(2)}) collective-permute-start(bf16[256,128]{1,0:T(8,128)(2,1)S(1)} %get-tuple-element.36), channel_id=1, source_target_pairs={{0,24},{4,28},{8,16},{12,20},{16,8},{20,12},{24,0},{28,4},{1,25},{... | collective-permute-start | bytes 196616 | tf_op jit(solution)/shard_map/ppermute | solution.py:26
  32.0 0.0 collective-permute-start.5
  32.0 0.0 collective-permute-done.8.refs_1_
  32.0 0.6 %collective-permute-start.6 = (bf16[256,128]{1,0:T(8,128)(2,1)S(1)}, bf16[256,128]{1,0:T(8,128)(2,1)S(1)}, u32[]{:S(2)}, u32[]{:S(2)}) collective-permute-start(bf16[256,128]{1,0:T(8,128)(2,1)S(1)} %get-tuple-element.38), channel_id=1, source_target_pairs={{0,8},{4,12},{8,0},{12,4},{16,24},{20,28},{24,16},{28,20},{1,9},{5... | collective-permute-start | bytes 196616 | tf_op jit(solution)/shard_map/ppermute | solution.py:26
  32.6 0.0 collective-permute-done.9.refs_2_
  32.6 0.0 collective-permute-done.10.refs_3_
  32.6 0.0 copy-done.7
  32.6 0.0 copy-start
  32.6 6.5 %ridge_reads.1 = (f32[512,256]{1,0:T(8,128)S(1)}, bf16[512,256]{1,0:T(8,128)(2,1)S(1)}) custom-call(f32[1,2]{1,0:T(1,128)S(1)} %bitcast.7, f32[256,128]{1,0:T(8,128)S(1)} %get-tuple-element.40.refs_0_, bf16[256,128]{1,0:T(8,128)(2,1)S(1)} %collective-permute-done.8.refs_1_, bf16[256,128]{1,0:T(8,128)(2,1)S(1)} %collective-permute-done.9.refs_2_, ...), custom_call_target="tpu_custom_call" | custom-call | flops 6442450944 | bytes 8388608 | tf_op jit(solution)/shard_map/ridge_reads/pallas_call | solution.py:430
  39.1 0.0 collective-permute-done.4.refs_1_
  39.1 0.0 collective-permute-done.5.refs_2_
  39.1 0.0 collective-permute-done.6.refs_3_
  39.1 0.3 cross_reads.1
  39.4 0.1 collective-permute-start.11
  39.5 0.6 %collective-permute-start.12 = (bf16[128,256]{1,0:T(8,128)(2,1)S(1)}, bf16[128,256]{1,0:T(8,128)(2,1)S(1)}, u32[]{:S(2)}, u32[]{:S(2)}) collective-permute-start(bf16[128,256]{1,0:T(8,128)(2,1)S(1)} %get-tuple-element.55), channel_id=1, source_target_pairs={{0,2},{1,3},{2,0},{3,1},{4,6},{5,7},{6,4},{7,5},{8,10},{9,11},{10,... | collective-permute-start | bytes 196616 | tf_op jit(solution)/shard_map/ppermute | solution.py:26
  40.1 1.3 %collective-permute-start.13 = (bf16[128,256]{1,0:T(8,128)(2,1)S(1)}, bf16[128,256]{1,0:T(8,128)(2,1)S(1)}, u32[]{:S(2)}, u32[]{:S(2)}) collective-permute-start(bf16[128,256]{1,0:T(8,128)(2,1)S(1)} %get-tuple-element.56), channel_id=1, source_target_pairs={{0,3},{1,2},{2,1},{3,0},{4,7},{5,6},{6,5},{7,4},{8,11},{9,10},{10,... | collective-permute-start | bytes 196616 | tf_op jit(solution)/shard_map/ppermute | solution.py:26
  41.4 0.0 collective-permute-done.11.refs_1_
  41.4 3.1 %collective-permute-done.12.refs_2_ = bf16[128,256]{1,0:T(8,128)(2,1)S(1)} collective-permute-done((bf16[128,256]{1,0:T(8,128)(2,1)S(1)}, bf16[128,256]{1,0:T(8,128)(2,1)S(1)}, u32[]{:S(2)}, u32[]{:S(2)}) %collective-permute-start.12) | collective-permute-done | bytes 65568 | tf_op jit(solution)/shard_map/ppermute | solution.py:26
  44.5 0.5 %collective-permute-done.13.refs_3_ = bf16[128,256]{1,0:T(8,128)(2,1)S(1)} collective-permute-done((bf16[128,256]{1,0:T(8,128)(2,1)S(1)}, bf16[128,256]{1,0:T(8,128)(2,1)S(1)}, u32[]{:S(2)}, u32[]{:S(2)}) %collective-permute-start.13) | collective-permute-done | bytes 65568 | tf_op jit(solution)/shard_map/ppermute | solution.py:26
  45.0 0.0 copy-done
  45.0 1.2 %output_rows.1 = bf16[128,1024]{1,0:T(8,128)(2,1)} custom-call(bf16[128,1024]{1,0:T(8,128)(2,1)S(1)} %copy-done.1, bf16[1024,1024]{1,0:T(8,128)(2,1)S(1)} %copy-done, bf16[128,256]{1,0:T(8,128)(2,1)S(1)} %get-tuple-element.53.refs_0_, bf16[128,256]{1,0:T(8,128)(2,1)S(1)} %collective-permute-done.11.refs_1_, ...), custom_call_target="tpu_custom_call" | custom-call | flops 268435456 | bytes 2883584 | tf_op jit(solution)/shard_map/output_rows/pallas_call | solution.py:497
  (3 shorter events, 0.0 us)
Async XLA Ops:
  0.0 12.4 %collective-permute-start.1 = (bf16[128,1024]{1,0:T(8,128)(2,1)}, bf16[128,1024]{1,0:T(8,128)(2,1)S(1)}, u32[]{:S(2)}, u32[]{:S(2)}) collective-permute-start(bf16[128,1024]{1,0:T(8,128)(2,1)} %tokens_ref.1), channel_id=1, source_target_pairs={{0,2},{1,3},{2,0},{3,1},{4,6},{5,7},{6,4},{7,5},{8,10},{9,11},{10,... | collective-permute-start | bytes 786440 | tf_op jit(solution)/shard_map/ppermute | solution.py:26
  2.9 11.6 %collective-permute-start = (bf16[128,1024]{1,0:T(8,128)(2,1)}, bf16[128,1024]{1,0:T(8,128)(2,1)S(1)}, u32[]{:S(2)}, u32[]{:S(2)}) collective-permute-start(bf16[128,1024]{1,0:T(8,128)(2,1)} %tokens_ref.1), channel_id=1, source_target_pairs={{0,1},{1,0},{2,3},{3,2},{4,5},{5,4},{6,7},{7,6},{8,9},{9,8},{10,11... | collective-permute-start | bytes 786440 | tf_op jit(solution)/shard_map/ppermute | solution.py:26
  5.2 9.1 %copy-start.8 = (bf16[1024,16]{0,1:T(8,128)(2,1)S(1)}, bf16[1024,16]{0,1:T(8,128)(2,1)}, u32[]{:S(2)}) copy-start(bf16[1024,16]{0,1:T(8,128)(2,1)} %param.18) | copy-start | bytes 98308
  5.3 9.3 %copy-start.1 = (bf16[128,1024]{1,0:T(8,128)(2,1)S(1)}, bf16[128,1024]{1,0:T(8,128)(2,1)}, u32[]{:S(2)}) copy-start(bf16[128,1024]{1,0:T(8,128)(2,1)} %tokens_ref.1) | copy-start | bytes 786436
  5.3 9.3 %copy-start.3 = (f32[4,3072]{1,0:T(4,128)S(1)}, f32[4,3072]{1,0:T(4,128)}, u32[]{:S(2)}) copy-start(f32[4,3072]{1,0:T(4,128)} %refs_7_.1) | copy-start | bytes 147460
  5.3 9.3 %copy-start.4 = (bf16[1,3,3072]{2,1,0:T(4,128)(2,1)S(1)}, bf16[1,3,3072]{2,1,0:T(4,128)(2,1)}, u32[]{:S(2)}) copy-start(bf16[1,3,3072]{2,1,0:T(4,128)(2,1)} %refs_8_.1) | copy-start | bytes 55300
  5.3 9.3 %copy-start.5 = (f32[1024]{0:T(1024)S(1)}, f32[1024]{0:T(1024)}, u32[]{:S(2)}) copy-start(f32[1024]{0:T(1024)} %param.16) | copy-start | bytes 12292
  5.3 9.3 %copy-start.6 = (f32[8]{0:T(128)S(1)}, f32[8]{0:T(128)}, u32[]{:S(2)}) copy-start(f32[8]{0:T(128)} %param.21) | copy-start | bytes 100
  12.4 2.1 %collective-permute-start.2 = (bf16[128,1024]{1,0:T(8,128)(2,1)S(1)}, bf16[128,1024]{1,0:T(8,128)(2,1)S(1)}, u32[]{:S(2)}, u32[]{:S(2)}) collective-permute-start(bf16[128,1024]{1,0:T(8,128)(2,1)S(1)} %hold.1.refs_2_), channel_id=1, source_target_pairs={{0,1},{1,0},{2,3},{3,2},{4,5},{5,4},{6,7},{7,6},{8,9},{9,8},{10,11... | collective-permute-start | bytes 786440 | tf_op jit(solution)/shard_map/ppermute | solution.py:26
  13.0 8.3 %collective-permute-start.7 = (bf16[4,256,128]{2,1,0:T(8,128)(2,1)S(1)}, bf16[4,256,128]{2,1,0:T(8,128)(2,1)S(1)}, u32[]{:S(2)}, u32[]{:S(2)}) collective-permute-start(bf16[4,256,128]{2,1,0:T(8,128)(2,1)S(1)} %get-tuple-element.39), channel_id=1, source_target_pairs={{0,4},{4,0},{8,12},{12,8},{16,20},{20,16},{24,28},{28,24},{1,5},{5... | collective-permute-start | bytes 786440 | tf_op jit(solution)/shard_map/ppermute | solution.py:26
  14.6 13.0 %copy-start.2 = (bf16[4,256,128]{2,1,0:T(8,128)(2,1)S(1)}, bf16[4,256,128]{2,1,0:T(8,128)(2,1)}, u32[]{:S(2)}) copy-start(bf16[4,256,128]{2,1,0:T(8,128)(2,1)} %get-tuple-element.31.keep_ref) | copy-start | bytes 786436
  14.6 18.0 %copy-start.7 = (f32[2]{0:T(128)S(1)}, f32[2]{0:T(128)}, u32[]{:S(2)}) copy-start(f32[2]{0:T(128)} %param.22) | copy-start | bytes 28
  19.3 8.3 %collective-permute-start.3 = (bf16[4,256,128]{2,1,0:T(8,128)(2,1)S(1)}, bf16[4,256,128]{2,1,0:T(8,128)(2,1)S(1)}, u32[]{:S(2)}, u32[]{:S(2)}) collective-permute-start(bf16[4,256,128]{2,1,0:T(8,128)(2,1)S(1)} %get-tuple-element.34), channel_id=1, source_target_pairs={{0,4},{4,0},{8,12},{12,8},{16,20},{20,16},{24,28},{28,24},{1,5},{5... | collective-permute-start | bytes 786440 | tf_op jit(solution)/shard_map/ppermute | solution.py:26
  21.4 10.6 %collective-permute-start.8 = (bf16[256,128]{1,0:T(8,128)(2,1)S(1)}, bf16[256,128]{1,0:T(8,128)(2,1)S(1)}, u32[]{:S(2)}, u32[]{:S(2)}) collective-permute-start(bf16[256,128]{1,0:T(8,128)(2,1)S(1)} %get-tuple-element.41), channel_id=1, source_target_pairs={{0,24},{4,28},{8,16},{12,20},{16,8},{20,12},{24,0},{28,4},{1,25},{... | collective-permute-start | bytes 196616 | tf_op jit(solution)/shard_map/ppermute | solution.py:26
  25.4 7.2 %collective-permute-start.9 = (bf16[256,128]{1,0:T(8,128)(2,1)S(1)}, bf16[256,128]{1,0:T(8,128)(2,1)S(1)}, u32[]{:S(2)}, u32[]{:S(2)}) collective-permute-start(bf16[256,128]{1,0:T(8,128)(2,1)S(1)} %get-tuple-element.42), channel_id=1, source_target_pairs={{0,16},{4,20},{8,24},{12,28},{16,0},{20,4},{24,8},{28,12},{1,17},{... | collective-permute-start | bytes 196616 | tf_op jit(solution)/shard_map/ppermute | solution.py:26
  25.4 7.2 %collective-permute-start.10 = (bf16[256,128]{1,0:T(8,128)(2,1)S(1)}, bf16[256,128]{1,0:T(8,128)(2,1)S(1)}, u32[]{:S(2)}, u32[]{:S(2)}) collective-permute-start(bf16[256,128]{1,0:T(8,128)(2,1)S(1)} %get-tuple-element.43), channel_id=1, source_target_pairs={{0,8},{4,12},{8,0},{12,4},{16,24},{20,28},{24,16},{28,20},{1,9},{5... | collective-permute-start | bytes 196616 | tf_op jit(solution)/shard_map/ppermute | solution.py:26
  27.7 11.4 %collective-permute-start.4 = (bf16[256,128]{1,0:T(8,128)(2,1)S(1)}, bf16[256,128]{1,0:T(8,128)(2,1)S(1)}, u32[]{:S(2)}, u32[]{:S(2)}) collective-permute-start(bf16[256,128]{1,0:T(8,128)(2,1)S(1)} %get-tuple-element.36), channel_id=1, source_target_pairs={{0,24},{4,28},{8,16},{12,20},{16,8},{20,12},{24,0},{28,4},{1,25},{... | collective-permute-start | bytes 196616 | tf_op jit(solution)/shard_map/ppermute | solution.py:26
  32.0 7.2 %collective-permute-start.5 = (bf16[256,128]{1,0:T(8,128)(2,1)S(1)}, bf16[256,128]{1,0:T(8,128)(2,1)S(1)}, u32[]{:S(2)}, u32[]{:S(2)}) collective-permute-start(bf16[256,128]{1,0:T(8,128)(2,1)S(1)} %get-tuple-element.37), channel_id=1, source_target_pairs={{0,16},{4,20},{8,24},{12,28},{16,0},{20,4},{24,8},{28,12},{1,17},{... | collective-permute-start | bytes 196616 | tf_op jit(solution)/shard_map/ppermute | solution.py:26
  32.0 7.2 %collective-permute-start.6 = (bf16[256,128]{1,0:T(8,128)(2,1)S(1)}, bf16[256,128]{1,0:T(8,128)(2,1)S(1)}, u32[]{:S(2)}, u32[]{:S(2)}) collective-permute-start(bf16[256,128]{1,0:T(8,128)(2,1)S(1)} %get-tuple-element.38), channel_id=1, source_target_pairs={{0,8},{4,12},{8,0},{12,4},{16,24},{20,28},{24,16},{28,20},{1,9},{5... | collective-permute-start | bytes 196616 | tf_op jit(solution)/shard_map/ppermute | solution.py:26
  32.6 12.3 %copy-start = (bf16[1024,1024]{1,0:T(8,128)(2,1)S(1)}, bf16[1024,1024]{1,0:T(8,128)(2,1)}, u32[]{:S(2)}) copy-start(bf16[1024,1024]{1,0:T(8,128)(2,1)} %w_ref.1) | copy-start | bytes 6291460
  39.4 1.9 %collective-permute-start.11 = (bf16[128,256]{1,0:T(8,128)(2,1)S(1)}, bf16[128,256]{1,0:T(8,128)(2,1)S(1)}, u32[]{:S(2)}, u32[]{:S(2)}) collective-permute-start(bf16[128,256]{1,0:T(8,128)(2,1)S(1)} %get-tuple-element.54), channel_id=1, source_target_pairs={{0,1},{1,0},{2,3},{3,2},{4,5},{5,4},{6,7},{7,6},{8,9},{9,8},{10,11... | collective-permute-start | bytes 196616 | tf_op jit(solution)/shard_map/ppermute | solution.py:26
  39.5 5.0 %collective-permute-start.12 = (bf16[128,256]{1,0:T(8,128)(2,1)S(1)}, bf16[128,256]{1,0:T(8,128)(2,1)S(1)}, u32[]{:S(2)}, u32[]{:S(2)}) collective-permute-start(bf16[128,256]{1,0:T(8,128)(2,1)S(1)} %get-tuple-element.55), channel_id=1, source_target_pairs={{0,2},{1,3},{2,0},{3,1},{4,6},{5,7},{6,4},{7,5},{8,10},{9,11},{10,... | collective-permute-start | bytes 196616 | tf_op jit(solution)/shard_map/ppermute | solution.py:26
  40.1 4.9 %collective-permute-start.13 = (bf16[128,256]{1,0:T(8,128)(2,1)S(1)}, bf16[128,256]{1,0:T(8,128)(2,1)S(1)}, u32[]{:S(2)}, u32[]{:S(2)}) collective-permute-start(bf16[128,256]{1,0:T(8,128)(2,1)S(1)} %get-tuple-element.56), channel_id=1, source_target_pairs={{0,3},{1,2},{2,1},{3,0},{4,7},{5,6},{6,5},{7,4},{8,11},{9,10},{10,... | collective-permute-start | bytes 196616 | tf_op jit(solution)/shard_map/ppermute | solution.py:26

commit v8 on v7

--- a/solution.py
+++ b/solution.py
@@ -62,18 +62,21 @@
     )
 
 
-def sums_kernel(heads, owners, code_hbm, keys_hbm, values_hbm, prompt_hbm,
+def sums_kernel(heads, owners, slot_bits, code_hbm, pack_hbm, keys_hbm, values_hbm, prompt_hbm,
                 send_gram, send_cross, keep_gram, keep_cross,
-                acc_ref, keys_ref, values_ref, stored_ref, code_ref, pick_ref, list_ref,
+                acc_ref, keys_ref, values_ref, stored_ref, code_ref, pack_ref, list_ref,
                 key_sem, value_sem, small_sem):
     pool, rows = keys_hbm.shape[0], keys_hbm.shape[1]
     mine = lax.axis_index("grp")
     load_code = pltpu.make_async_copy(code_hbm, code_ref, small_sem.at[0])
     load_prompt = pltpu.make_async_copy(prompt_hbm, stored_ref, small_sem.at[1])
+    load_pack = pltpu.make_async_copy(pack_hbm, pack_ref, small_sem.at[2])
     load_code.start()
+    load_pack.start()
     load_prompt.start()
     acc_ref[...] = jnp.zeros_like(acc_ref)
     load_code.wait()
+    load_pack.wait()
 
     def load(item):
         page = list_ref[item] & 0xFFFF
@@ -93,9 +96,11 @@
         for i in range(wide):
             page = chunk * wide + i
             code = code_ref[page]
-            pick_ref[code >> 24] = code & 0xFFFF
-            list_ref[count] = (code & -65536) | page
-            count = count + ((code & 0xFF0000) > 0).astype(jnp.int32)
+            owner = code >> slot_bits
+            length = pack_ref[owner] & 0xFFFF
+            live = length - ((code & ((1 << slot_bits) - 1)) * PAGE)
+            list_ref[count] = (owner << 24) | (jnp.minimum(live, PAGE) << 16) | page
+            count = count + (live > 0).astype(jnp.int32)
         return count
 
     count = lax.fori_loop(0, pool // wide, note, jnp.int32(0))
@@ -140,7 +145,7 @@
     def add_prompt(owner, carry):
         for slot in range(stored):
 
-            @pl.when(pick_ref[owner] == mine * stored + slot)
+            @pl.when((pack_ref[owner] >> 16) == mine * stored + slot)
             def _():
                 for head in range(heads):
                     at = slice(head * HDIM, (head + 1) * HDIM)
@@ -159,14 +164,14 @@
         keep_cross[pair] = acc_ref[here, :, HDIM:].astype(BF16)
 
 
-def page_sums(code, keys, values, prompt_state, owners):
+def page_sums(code, pack, slot_bits, keys, values, prompt_state, owners):
     pool, rows, _ = keys.shape
     heads = prompt_state.shape[1]
     half = (owners // 2, heads * HDIM, HDIM)
     items = pool + 4
     return pl.pallas_call(
-        functools.partial(sums_kernel, heads, owners),
-        in_specs=[pl.BlockSpec(memory_space=pl.ANY)] * 4,
+        functools.partial(sums_kernel, heads, owners, slot_bits),
+        in_specs=[pl.BlockSpec(memory_space=pl.ANY)] * 5,
         out_specs=[pl.BlockSpec(memory_space=pltpu.VMEM)] * 4,
         scratch_shapes=[
             pltpu.VMEM((owners + 1, heads * HDIM, 2 * HDIM), F32),
@@ -174,11 +179,11 @@
             pltpu.VMEM((items, rows, HDIM), BF16),
             pltpu.VMEM(prompt_state.shape, F32),
             pltpu.SMEM(code.shape, jnp.int32),
-            pltpu.SMEM((owners,), jnp.int32),
+            pltpu.SMEM(pack.shape, jnp.int32),
             pltpu.SMEM((items,), jnp.int32),
             pltpu.SemaphoreType.DMA((items,)),
             pltpu.SemaphoreType.DMA((items,)),
-            pltpu.SemaphoreType.DMA((2,)),
+            pltpu.SemaphoreType.DMA((3,)),
         ],
         out_shape=[jax.ShapeDtypeStruct(half, BF16)] * 4,
         compiler_params=pltpu.CompilerParams(vmem_limit_bytes=PAGE_VMEM * 2**20),
@@ -188,7 +193,7 @@
             transcendentals=0,
         ),
         name="page_sums",
-    )(code, keys, values, prompt_state)
+    )(code, pack, keys, values, prompt_state)
 
 
 def halve_kernel(keep_ref, got_ref, *outs):
@@ -481,32 +486,32 @@
     )(*crosses, base, solved)
 
 
-def output_kernel(tokens_ref, w_ref, *refs):
+def output_kernel(distances, start_ref, w_ref, *refs):
     out_ref = refs[-1]
     me = lax.axis_index("head")
-    total = tokens_ref[...].astype(F32)
-    for distance, part in enumerate(refs[:-1]):
+    total = start_ref[...].astype(F32)
+    for distance, part in zip(distances, refs[:-1]):
         width = part.shape[1]
         first = pl.multiple_of((me ^ distance) * width, width)
         total = total + dot(part[...], w_ref[pl.ds(first, width), :])
-    out_ref[...] = total.astype(BF16)
-
-
-def output_rows(tokens, w_out, reads):
+    out_ref[...] = total.astype(out_ref.dtype)
+
+
+def output_rows(start, w_out, parts, distances, dtype):
     whole = pl.BlockSpec(memory_space=pltpu.VMEM)
     return pl.pallas_call(
-        output_kernel,
-        in_specs=[whole] * (2 + len(reads)),
+        functools.partial(output_kernel, distances),
+        in_specs=[whole] * (2 + len(parts)),
         out_specs=whole,
-        out_shape=jax.ShapeDtypeStruct(tokens.shape, BF16),
+        out_shape=jax.ShapeDtypeStruct(start.shape, dtype),
         compiler_params=pltpu.CompilerParams(vmem_limit_bytes=24 * 2**20),
         cost_estimate=pl.CostEstimate(
-            flops=2 * tokens.shape[0] * w_out.shape[0] * w_out.shape[1],
-            bytes_accessed=2 * w_out.size + 6 * tokens.size,
+            flops=2 * start.shape[0] * parts[0].shape[1] * len(parts) * w_out.shape[1],
+            bytes_accessed=2 * w_out.size + 6 * start.size,
             transcendentals=0,
         ),
         name="output_rows",
-    )(tokens, w_out, *reads)
+    )(start, w_out, *parts)
 
 
 def shards(
@@ -534,10 +539,11 @@
         blocks[bit] = swap(tokens, "head", bit)
 
     pool, page, heads, _ = cache_keys.shape
-    slots = jnp.arange(page_table.shape[1], dtype=jnp.int32)
-    live = jnp.clip(cache_lengths[:, None] - slots * PAGE, 0, PAGE)
-    tag = (jnp.arange(owners, dtype=jnp.int32) << 24) | group_prompt
-    tag = tag[:, None] | (live << 16)
+    slots = page_table.shape[1]
+    slot_bits = slots.bit_length() - 1
+    assert slots == 1 << slot_bits
+    tag = jnp.arange(owners * slots, dtype=jnp.int32).reshape(owners, slots)
+    pack = cache_lengths | (group_prompt << 16)
     ids = lax.axis_index("grp").astype(jnp.int32) * pool + jnp.arange(pool, dtype=jnp.int32)
     code = jnp.sum(
         jnp.where(page_table[:, :, None] == ids, tag[:, :, None], 0), axis=(0, 1), dtype=jnp.int32
@@ -550,7 +556,7 @@
         return [parts[0]] + sent
 
     send_gram, send_cross, keep_gram, keep_cross = page_sums(
-        code, keys, values, prompt_state, owners
+        code, pack, slot_bits, keys, values, prompt_state, owners
     )
     got_gram = swap(send_gram, "grp", 1)
     for bit in bits[1:]:
@@ -566,9 +572,9 @@
     crosses = halve_sums(keep_cross, swap(send_cross, "grp", 1))
     base, solved = ridge_reads(ridge, scattered(grams), vectors, [crosses[0]])
     reads = cross_reads(scattered(crosses), base, solved, head_count)
-    sent = {i: swap(reads[i], "head", i) for i in reversed(range(1, head_count))}
-    reads = [reads[0]] + [sent[i] for i in range(1, head_count)]
-    return output_rows(tokens, w_out, reads)
+    parts = [reads[0]] + [swap(reads[i], "head", i) for i in range(1, head_count)]
+    total = output_rows(tokens, w_out, parts[:2], (0, 1), F32)
+    return output_rows(total, w_out, parts[2:], tuple(range(2, head_count)), BF16)
 
 
 def solution(mesh):

time: 46.4 us -> 45.4 us (0.978)
  other arithmetic: 2.3 us -> 1.59 us
    or x2 -> x1, other arithmetic: 1.39 us -> 0.68 us  [shards(): pack = cache_lengths | group_prompt << 16]
    pallas_call x2 -> x3, Pallas kernels: 8.3 us -> 8.37 us  [the longest x1 7.02 us: page_sums(): pl.pallas_call(functools.partial(sums_kernel, heads, owners, slot_bits),...]
  transfers between devices with their start and end apart: 14 -> 14, of which waited for: 4 -> 4; matrix products, arithmetic and copies ran while one was open for 5% -> 4% of each run, Pallas kernels for 40% -> 41%
where the time goes in v8:
time: 45.4 us; the launch traced here: 45.1 us
  Pallas kernels  20 us (44%)
  starting transfers between devices  17.2 us (38%)
  waiting for transfers between devices  5.82 us (13%)
  other arithmetic  1.59 us (4%)
    ppermute x14, starting transfers between devices, swap(): return lax.ppermute(block, axis, [(i, i ^ distance) for i in range(size)])  17.2 us
    pallas_call x1, Pallas kernels, page_sums(): pl.pallas_call(functools.partial(sums_kernel, heads, owners, slot_bits),...  7.02 us
    pallas_call x1, Pallas kernels, ridge_reads(): pl.pallas_call(functools.partial(read_kernel, heads, len(grams)), in_spec...  6.46 us
    ppermute x14, waiting for transfers between devices, swap(): return lax.ppermute(block, axis, [(i, i ^ distance) for i in range(size)])  5.82 us
    pallas_call x1, Pallas kernels, token_vectors(): pl.pallas_call(functools.partial(token_kernel, heads), in_specs=[whole] *...  4.73 us
    pallas_call x2, Pallas kernels, output_rows(): pl.pallas_call(functools.partial(output_kernel, distances), in_specs=[who...  1.35 us
  transfers between devices with their start and end apart: 14, of which 4 were waited for; matrix products, arithmetic and copies ran while one was open for 4% of the time, Pallas kernels for 41%

profile of v8, /device:TPU:0, one launch (start us, length us, event | category | flops | bytes accessed | tf_op | source)
XLA Modules:
  0.0 45.1 jit_solution(13540928665226914634)
XLA Ops:
  0.0 2.9 %collective-permute-start.1 = (bf16[128,1024]{1,0:T(8,128)(2,1)}, bf16[128,1024]{1,0:T(8,128)(2,1)S(1)}, u32[]{:S(2)}, u32[]{:S(2)}) collective-permute-start(bf16[128,1024]{1,0:T(8,128)(2,1)} %start_ref.1), channel_id=1, source_target_pairs={{0,2},{1,3},{2,0},{3,1},{4,6},{5,7},{6,4},{7,5},{8,10},{9,11},{10,... | collective-permute-start | bytes 786440 | tf_op jit(solution)/shard_map/ppermute | solution.py:26
  2.9 0.0 collective-permute-start
  3.0 0.7 %shift-left_or_fusion.pack_hbm = s32[8]{0:T(128)S(1)} fusion(s32[8]{0:T(128)} %param.27, s32[8]{0:T(128)} %param.28), kind=kLoop, calls=%fused_computation.2 | loop fusion | flops 16 | bytes 96 | tf_op jit(solution)/shard_map/or | solution.py:546
  3.6 0.9 %select_reduce_fusion.code_hbm = s32[64]{0:T(128)S(1)} fusion(s32[8,64]{1,0:T(8,128)S(1)} %multiply_add_fusion, s32[64]{0:T(128)S(1)} %iota_add_fusion, s32[8,64]{1,0:T(8,128)} %param.26), kind=kLoop, calls=%fused_computation | loop fusion | flops 98240 | bytes 4608 | tf_op jit(solution)/shard_map/reduce_sum | solution.py:548
  4.5 0.0 copy-start.8
  4.5 0.0 copy-start.1
  4.6 0.0 copy-start.3
  4.6 0.0 copy-start.4
  4.6 0.0 copy-start.5
  4.6 0.0 copy-start.6
  4.6 7.0 %page_sums.1 = (bf16[4,256,128]{2,1,0:T(8,128)(2,1)S(1)}, bf16[4,256,128]{2,1,0:T(8,128)(2,1)S(1)}, bf16[4,256,128]{2,1,0:T(8,128)(2,1)S(1)}, bf16[4,256,128]{2,1,0:T(8,128)(2,1)}) custom-call(s32[64]{0:T(128)S(1)} %select_reduce_fusion.code_hbm, s32[8]{0:T(128)S(1)} %shift-left_or_fusion.pack_hbm, bf16[64,256,128]{2,1,0:T(8,128)(2,1)} %bitcast.8, ...), custom_call_target="tpu_custom_call" | custom-call | flops 4294967296 | bytes 8388608 | tf_op jit(solution)/shard_map/page_sums/pallas_call | solution.py:172
  11.6 0.0 collective-permute-done.1.refs_0_
  11.7 0.6 %collective-permute-start.2 = (bf16[128,1024]{1,0:T(8,128)(2,1)S(1)}, bf16[128,1024]{1,0:T(8,128)(2,1)S(1)}, u32[]{:S(2)}, u32[]{:S(2)}) collective-permute-start(bf16[128,1024]{1,0:T(8,128)(2,1)S(1)} %hold.1.refs_2_), channel_id=1, source_target_pairs={{0,1},{1,0},{2,3},{3,2},{4,5},{5,4},{6,7},{7,6},{8,9},{9,8},{10,11... | collective-permute-start | bytes 786440 | tf_op jit(solution)/shard_map/ppermute | solution.py:26
  12.2 1.9 %collective-permute-start.7 = (bf16[4,256,128]{2,1,0:T(8,128)(2,1)S(1)}, bf16[4,256,128]{2,1,0:T(8,128)(2,1)S(1)}, u32[]{:S(2)}, u32[]{:S(2)}) collective-permute-start(bf16[4,256,128]{2,1,0:T(8,128)(2,1)S(1)} %get-tuple-element.39), channel_id=1, source_target_pairs={{0,4},{4,0},{8,12},{12,8},{16,20},{20,16},{24,28},{28,24},{1,5},{5... | collective-permute-start | bytes 786440 | tf_op jit(solution)/shard_map/ppermute | solution.py:26
  14.1 0.0 copy-done.8
  14.1 0.2 copy.19.refs_6_
  14.3 0.0 collective-permute-done.refs_1_
  14.3 0.0 collective-permute-done.2.refs_3_
  14.3 0.0 copy-done.1
  14.3 0.0 copy-done.3
  14.3 0.0 copy-done.4
  14.3 0.0 copy-done.5
  14.3 0.0 copy-done.6
  14.3 0.0 copy-start.2
  14.4 0.0 copy-start.7
  14.4 4.7 %token_vectors.1 = (bf16[4,256,128]{2,1,0:T(8,128)(2,1)S(1)}, bf16[2,128,512]{2,1,0:T(8,128)(2,1)S(1)}, bf16[2,512,128]{2,1,0:T(8,128)(2,1)S(1)}, bf16[2,128,512...) custom-call(bf16[128,1024]{1,0:T(8,128)(2,1)S(1)} %copy-done.1, ...), custom_call_target="tpu_custom_call", output_to_operand_aliasing={{0}: (10, {})} | custom-call | flops 805306368 | bytes 6815744 | tf_op jit(solution)/shard_map/token_vectors/pallas_call | solution.py:332
  19.1 1.0 %collective-permute-start.3 = (bf16[4,256,128]{2,1,0:T(8,128)(2,1)S(1)}, bf16[4,256,128]{2,1,0:T(8,128)(2,1)S(1)}, u32[]{:S(2)}, u32[]{:S(2)}) collective-permute-start(bf16[4,256,128]{2,1,0:T(8,128)(2,1)S(1)} %get-tuple-element.34), channel_id=1, source_target_pairs={{0,4},{4,0},{8,12},{12,8},{16,20},{20,16},{24,28},{28,24},{1,5},{5... | collective-permute-start | bytes 786440 | tf_op jit(solution)/shard_map/ppermute | solution.py:26
  20.1 0.5 %collective-permute-done.7.got_ref = bf16[4,256,128]{2,1,0:T(8,128)(2,1)S(1)} collective-permute-done((bf16[4,256,128]{2,1,0:T(8,128)(2,1)S(1)}, bf16[4,256,128]{2,1,0:T(8,128)(2,1)S(1)}, u32[]{:S(2)}, u32[]{:S(2)}) %collective-permute-start.7) | collective-permute-done | bytes 262176 | tf_op jit(solution)/shard_map/ppermute | solution.py:26
  20.7 0.1 halve_sums.3
  20.7 3.5 %collective-permute-start.8 = (bf16[256,128]{1,0:T(8,128)(2,1)S(1)}, bf16[256,128]{1,0:T(8,128)(2,1)S(1)}, u32[]{:S(2)}, u32[]{:S(2)}) collective-permute-start(bf16[256,128]{1,0:T(8,128)(2,1)S(1)} %get-tuple-element.41), channel_id=1, source_target_pairs={{0,24},{4,28},{8,16},{12,20},{16,8},{20,12},{24,0},{28,4},{1,25},{... | collective-permute-start | bytes 196616 | tf_op jit(solution)/shard_map/ppermute | solution.py:26
  24.2 0.0 collective-permute-start.9
  24.2 0.9 %collective-permute-start.10 = (bf16[256,128]{1,0:T(8,128)(2,1)S(1)}, bf16[256,128]{1,0:T(8,128)(2,1)S(1)}, u32[]{:S(2)}, u32[]{:S(2)}) collective-permute-start(bf16[256,128]{1,0:T(8,128)(2,1)S(1)} %get-tuple-element.43), channel_id=1, source_target_pairs={{0,8},{4,12},{8,0},{12,4},{16,24},{20,28},{24,16},{28,20},{1,9},{5... | collective-permute-start | bytes 196616 | tf_op jit(solution)/shard_map/ppermute | solution.py:26
  25.2 2.0 %collective-permute-done.3.got_ref = bf16[4,256,128]{2,1,0:T(8,128)(2,1)S(1)} collective-permute-done((bf16[4,256,128]{2,1,0:T(8,128)(2,1)S(1)}, bf16[4,256,128]{2,1,0:T(8,128)(2,1)S(1)}, u32[]{:S(2)}, u32[]{:S(2)}) %collective-permute-start.3) | collective-permute-done | bytes 262176 | tf_op jit(solution)/shard_map/ppermute | solution.py:26
  27.2 0.0 copy-done.2
  27.2 0.1 halve_sums.2
  27.3 3.5 %collective-permute-start.4 = (bf16[256,128]{1,0:T(8,128)(2,1)S(1)}, bf16[256,128]{1,0:T(8,128)(2,1)S(1)}, u32[]{:S(2)}, u32[]{:S(2)}) collective-permute-start(bf16[256,128]{1,0:T(8,128)(2,1)S(1)} %get-tuple-element.36), channel_id=1, source_target_pairs={{0,24},{4,28},{8,16},{12,20},{16,8},{20,12},{24,0},{28,4},{1,25},{... | collective-permute-start | bytes 196616 | tf_op jit(solution)/shard_map/ppermute | solution.py:26
  30.8 0.0 collective-permute-start.5
  30.8 0.0 collective-permute-done.8.refs_1_
  30.8 1.0 %collective-permute-start.6 = (bf16[256,128]{1,0:T(8,128)(2,1)S(1)}, bf16[256,128]{1,0:T(8,128)(2,1)S(1)}, u32[]{:S(2)}, u32[]{:S(2)}) collective-permute-start(bf16[256,128]{1,0:T(8,128)(2,1)S(1)} %get-tuple-element.38), channel_id=1, source_target_pairs={{0,8},{4,12},{8,0},{12,4},{16,24},{20,28},{24,16},{28,20},{1,9},{5... | collective-permute-start | bytes 196616 | tf_op jit(solution)/shard_map/ppermute | solution.py:26
  31.7 0.0 collective-permute-done.9.refs_2_
  31.7 0.0 collective-permute-done.10.refs_3_
  31.7 0.0 copy-done.7
  31.7 0.0 copy-start
  31.7 6.5 %ridge_reads.1 = (f32[512,256]{1,0:T(8,128)S(1)}, bf16[512,256]{1,0:T(8,128)(2,1)S(1)}) custom-call(f32[1,2]{1,0:T(1,128)S(1)} %bitcast.7, f32[256,128]{1,0:T(8,128)S(1)} %get-tuple-element.40.refs_0_, bf16[256,128]{1,0:T(8,128)(2,1)S(1)} %collective-permute-done.8.refs_1_, bf16[256,128]{1,0:T(8,128)(2,1)S(1)} %collective-permute-done.9.refs_2_, ...), custom_call_target="tpu_custom_call" | custom-call | flops 6442450944 | bytes 8388608 | tf_op jit(solution)/shard_map/ridge_reads/pallas_call | solution.py:435
  38.2 0.0 collective-permute-done.4.refs_1_
  38.2 0.0 collective-permute-done.5.refs_2_
  38.2 0.0 collective-permute-done.6.refs_3_
  38.2 0.3 cross_reads.1
  38.5 0.1 collective-permute-start.11
  38.6 0.6 %collective-permute-start.12 = (bf16[128,256]{1,0:T(8,128)(2,1)S(1)}, bf16[128,256]{1,0:T(8,128)(2,1)S(1)}, u32[]{:S(2)}, u32[]{:S(2)}) collective-permute-start(bf16[128,256]{1,0:T(8,128)(2,1)S(1)} %get-tuple-element.55), channel_id=1, source_target_pairs={{0,2},{1,3},{2,0},{3,1},{4,6},{5,7},{6,4},{7,5},{8,10},{9,11},{10,... | collective-permute-start | bytes 196616 | tf_op jit(solution)/shard_map/ppermute | solution.py:26
  39.2 1.3 %collective-permute-start.13 = (bf16[128,256]{1,0:T(8,128)(2,1)S(1)}, bf16[128,256]{1,0:T(8,128)(2,1)S(1)}, u32[]{:S(2)}, u32[]{:S(2)}) collective-permute-start(bf16[128,256]{1,0:T(8,128)(2,1)S(1)} %get-tuple-element.56), channel_id=1, source_target_pairs={{0,3},{1,2},{2,1},{3,0},{4,7},{5,6},{6,5},{7,4},{8,11},{9,10},{10,... | collective-permute-start | bytes 196616 | tf_op jit(solution)/shard_map/ppermute | solution.py:26
  40.5 0.0 collective-permute-done.11.refs_1_
  40.5 0.0 copy-done
  40.5 0.3 output_rows.2.start_ref
  40.8 2.8 %collective-permute-done.12.refs_0_ = bf16[128,256]{1,0:T(8,128)(2,1)S(1)} collective-permute-done((bf16[128,256]{1,0:T(8,128)(2,1)S(1)}, bf16[128,256]{1,0:T(8,128)(2,1)S(1)}, u32[]{:S(2)}, u32[]{:S(2)}) %collective-permute-start.12) | collective-permute-done | bytes 65568 | tf_op jit(solution)/shard_map/ppermute | solution.py:26
  43.6 0.5 %collective-permute-done.13.refs_1_ = bf16[128,256]{1,0:T(8,128)(2,1)S(1)} collective-permute-done((bf16[128,256]{1,0:T(8,128)(2,1)S(1)}, bf16[128,256]{1,0:T(8,128)(2,1)S(1)}, u32[]{:S(2)}, u32[]{:S(2)}) %collective-permute-start.13) | collective-permute-done | bytes 65568 | tf_op jit(solution)/shard_map/ppermute | solution.py:26
  44.1 1.0 %output_rows.3 = bf16[128,1024]{1,0:T(8,128)(2,1)} custom-call(f32[128,1024]{1,0:T(8,128)S(1)} %output_rows.2.start_ref, bf16[1024,1024]{1,0:T(8,128)(2,1)S(1)} %copy-done, bf16[128,256]{1,0:T(8,128)(2,1)S(1)} %collective-permute-done.12.refs_0_, bf16[128,256]{1,0:T(8,128)(2,1)S(1)} %collective-permute-done.13.refs_1_), custom_call_target="tpu_custom_call" | custom-call | flops 134217728 | bytes 2883584 | tf_op jit(solution)/shard_map/output_rows/pallas_call | solution.py:502
  (3 shorter events, 0.0 us)
Async XLA Ops:
  0.0 11.6 %collective-permute-start.1 = (bf16[128,1024]{1,0:T(8,128)(2,1)}, bf16[128,1024]{1,0:T(8,128)(2,1)S(1)}, u32[]{:S(2)}, u32[]{:S(2)}) collective-permute-start(bf16[128,1024]{1,0:T(8,128)(2,1)} %start_ref.1), channel_id=1, source_target_pairs={{0,2},{1,3},{2,0},{3,1},{4,6},{5,7},{6,4},{7,5},{8,10},{9,11},{10,... | collective-permute-start | bytes 786440 | tf_op jit(solution)/shard_map/ppermute | solution.py:26
  2.9 11.3 %collective-permute-start = (bf16[128,1024]{1,0:T(8,128)(2,1)}, bf16[128,1024]{1,0:T(8,128)(2,1)S(1)}, u32[]{:S(2)}, u32[]{:S(2)}) collective-permute-start(bf16[128,1024]{1,0:T(8,128)(2,1)} %start_ref.1), channel_id=1, source_target_pairs={{0,1},{1,0},{2,3},{3,2},{4,5},{5,4},{6,7},{7,6},{8,9},{9,8},{10,11... | collective-permute-start | bytes 786440 | tf_op jit(solution)/shard_map/ppermute | solution.py:26
  4.5 9.6 %copy-start.8 = (bf16[1024,16]{0,1:T(8,128)(2,1)S(1)}, bf16[1024,16]{0,1:T(8,128)(2,1)}, u32[]{:S(2)}) copy-start(bf16[1024,16]{0,1:T(8,128)(2,1)} %param.18) | copy-start | bytes 98308
  4.5 9.8 %copy-start.1 = (bf16[128,1024]{1,0:T(8,128)(2,1)S(1)}, bf16[128,1024]{1,0:T(8,128)(2,1)}, u32[]{:S(2)}) copy-start(bf16[128,1024]{1,0:T(8,128)(2,1)} %start_ref.1) | copy-start | bytes 786436
  4.6 9.8 %copy-start.3 = (f32[4,3072]{1,0:T(4,128)S(1)}, f32[4,3072]{1,0:T(4,128)}, u32[]{:S(2)}) copy-start(f32[4,3072]{1,0:T(4,128)} %refs_7_.1) | copy-start | bytes 147460
  4.6 9.8 %copy-start.4 = (bf16[1,3,3072]{2,1,0:T(4,128)(2,1)S(1)}, bf16[1,3,3072]{2,1,0:T(4,128)(2,1)}, u32[]{:S(2)}) copy-start(bf16[1,3,3072]{2,1,0:T(4,128)(2,1)} %refs_8_.1) | copy-start | bytes 55300
  4.6 9.8 %copy-start.5 = (f32[1024]{0:T(1024)S(1)}, f32[1024]{0:T(1024)}, u32[]{:S(2)}) copy-start(f32[1024]{0:T(1024)} %param.16) | copy-start | bytes 12292
  4.6 9.8 %copy-start.6 = (f32[8]{0:T(128)S(1)}, f32[8]{0:T(128)}, u32[]{:S(2)}) copy-start(f32[8]{0:T(128)} %param.21) | copy-start | bytes 100
  11.7 2.6 %collective-permute-start.2 = (bf16[128,1024]{1,0:T(8,128)(2,1)S(1)}, bf16[128,1024]{1,0:T(8,128)(2,1)S(1)}, u32[]{:S(2)}, u32[]{:S(2)}) collective-permute-start(bf16[128,1024]{1,0:T(8,128)(2,1)S(1)} %hold.1.refs_2_), channel_id=1, source_target_pairs={{0,1},{1,0},{2,3},{3,2},{4,5},{5,4},{6,7},{7,6},{8,9},{9,8},{10,11... | collective-permute-start | bytes 786440 | tf_op jit(solution)/shard_map/ppermute | solution.py:26
  12.2 8.4 %collective-permute-start.7 = (bf16[4,256,128]{2,1,0:T(8,128)(2,1)S(1)}, bf16[4,256,128]{2,1,0:T(8,128)(2,1)S(1)}, u32[]{:S(2)}, u32[]{:S(2)}) collective-permute-start(bf16[4,256,128]{2,1,0:T(8,128)(2,1)S(1)} %get-tuple-element.39), channel_id=1, source_target_pairs={{0,4},{4,0},{8,12},{12,8},{16,20},{20,16},{24,28},{28,24},{1,5},{5... | collective-permute-start | bytes 786440 | tf_op jit(solution)/shard_map/ppermute | solution.py:26
  14.3 12.8 %copy-start.2 = (bf16[4,256,128]{2,1,0:T(8,128)(2,1)S(1)}, bf16[4,256,128]{2,1,0:T(8,128)(2,1)}, u32[]{:S(2)}) copy-start(bf16[4,256,128]{2,1,0:T(8,128)(2,1)} %get-tuple-element.31.keep_ref) | copy-start | bytes 786436
  14.4 17.4 %copy-start.7 = (f32[2]{0:T(128)S(1)}, f32[2]{0:T(128)}, u32[]{:S(2)}) copy-start(f32[2]{0:T(128)} %param.22) | copy-start | bytes 28
  19.1 8.1 %collective-permute-start.3 = (bf16[4,256,128]{2,1,0:T(8,128)(2,1)S(1)}, bf16[4,256,128]{2,1,0:T(8,128)(2,1)S(1)}, u32[]{:S(2)}, u32[]{:S(2)}) collective-permute-start(bf16[4,256,128]{2,1,0:T(8,128)(2,1)S(1)} %get-tuple-element.34), channel_id=1, source_target_pairs={{0,4},{4,0},{8,12},{12,8},{16,20},{20,16},{24,28},{28,24},{1,5},{5... | collective-permute-start | bytes 786440 | tf_op jit(solution)/shard_map/ppermute | solution.py:26
  20.7 10.0 %collective-permute-start.8 = (bf16[256,128]{1,0:T(8,128)(2,1)S(1)}, bf16[256,128]{1,0:T(8,128)(2,1)S(1)}, u32[]{:S(2)}, u32[]{:S(2)}) collective-permute-start(bf16[256,128]{1,0:T(8,128)(2,1)S(1)} %get-tuple-element.41), channel_id=1, source_target_pairs={{0,24},{4,28},{8,16},{12,20},{16,8},{20,12},{24,0},{28,4},{1,25},{... | collective-permute-start | bytes 196616 | tf_op jit(solution)/shard_map/ppermute | solution.py:26
  24.2 7.5 %collective-permute-start.9 = (bf16[256,128]{1,0:T(8,128)(2,1)S(1)}, bf16[256,128]{1,0:T(8,128)(2,1)S(1)}, u32[]{:S(2)}, u32[]{:S(2)}) collective-permute-start(bf16[256,128]{1,0:T(8,128)(2,1)S(1)} %get-tuple-element.42), channel_id=1, source_target_pairs={{0,16},{4,20},{8,24},{12,28},{16,0},{20,4},{24,8},{28,12},{1,17},{... | collective-permute-start | bytes 196616 | tf_op jit(solution)/shard_map/ppermute | solution.py:26
  24.2 7.5 %collective-permute-start.10 = (bf16[256,128]{1,0:T(8,128)(2,1)S(1)}, bf16[256,128]{1,0:T(8,128)(2,1)S(1)}, u32[]{:S(2)}, u32[]{:S(2)}) collective-permute-start(bf16[256,128]{1,0:T(8,128)(2,1)S(1)} %get-tuple-element.43), channel_id=1, source_target_pairs={{0,8},{4,12},{8,0},{12,4},{16,24},{20,28},{24,16},{28,20},{1,9},{5... | collective-permute-start | bytes 196616 | tf_op jit(solution)/shard_map/ppermute | solution.py:26
  27.3 11.0 %collective-permute-start.4 = (bf16[256,128]{1,0:T(8,128)(2,1)S(1)}, bf16[256,128]{1,0:T(8,128)(2,1)S(1)}, u32[]{:S(2)}, u32[]{:S(2)}) collective-permute-start(bf16[256,128]{1,0:T(8,128)(2,1)S(1)} %get-tuple-element.36), channel_id=1, source_target_pairs={{0,24},{4,28},{8,16},{12,20},{16,8},{20,12},{24,0},{28,4},{1,25},{... | collective-permute-start | bytes 196616 | tf_op jit(solution)/shard_map/ppermute | solution.py:26
  30.8 7.5 %collective-permute-start.5 = (bf16[256,128]{1,0:T(8,128)(2,1)S(1)}, bf16[256,128]{1,0:T(8,128)(2,1)S(1)}, u32[]{:S(2)}, u32[]{:S(2)}) collective-permute-start(bf16[256,128]{1,0:T(8,128)(2,1)S(1)} %get-tuple-element.37), channel_id=1, source_target_pairs={{0,16},{4,20},{8,24},{12,28},{16,0},{20,4},{24,8},{28,12},{1,17},{... | collective-permute-start | bytes 196616 | tf_op jit(solution)/shard_map/ppermute | solution.py:26
  30.8 7.5 %collective-permute-start.6 = (bf16[256,128]{1,0:T(8,128)(2,1)S(1)}, bf16[256,128]{1,0:T(8,128)(2,1)S(1)}, u32[]{:S(2)}, u32[]{:S(2)}) collective-permute-start(bf16[256,128]{1,0:T(8,128)(2,1)S(1)} %get-tuple-element.38), channel_id=1, source_target_pairs={{0,8},{4,12},{8,0},{12,4},{16,24},{20,28},{24,16},{28,20},{1,9},{5... | collective-permute-start | bytes 196616 | tf_op jit(solution)/shard_map/ppermute | solution.py:26
  31.7 8.7 %copy-start = (bf16[1024,1024]{1,0:T(8,128)(2,1)S(1)}, bf16[1024,1024]{1,0:T(8,128)(2,1)}, u32[]{:S(2)}) copy-start(bf16[1024,1024]{1,0:T(8,128)(2,1)} %w_ref.3) | copy-start | bytes 6291460
  38.5 1.9 %collective-permute-start.11 = (bf16[128,256]{1,0:T(8,128)(2,1)S(1)}, bf16[128,256]{1,0:T(8,128)(2,1)S(1)}, u32[]{:S(2)}, u32[]{:S(2)}) collective-permute-start(bf16[128,256]{1,0:T(8,128)(2,1)S(1)} %get-tuple-element.54), channel_id=1, source_target_pairs={{0,1},{1,0},{2,3},{3,2},{4,5},{5,4},{6,7},{7,6},{8,9},{9,8},{10,11... | collective-permute-start | bytes 196616 | tf_op jit(solution)/shard_map/ppermute | solution.py:26
  38.6 5.0 %collective-permute-start.12 = (bf16[128,256]{1,0:T(8,128)(2,1)S(1)}, bf16[128,256]{1,0:T(8,128)(2,1)S(1)}, u32[]{:S(2)}, u32[]{:S(2)}) collective-permute-start(bf16[128,256]{1,0:T(8,128)(2,1)S(1)} %get-tuple-element.55), channel_id=1, source_target_pairs={{0,2},{1,3},{2,0},{3,1},{4,6},{5,7},{6,4},{7,5},{8,10},{9,11},{10,... | collective-permute-start | bytes 196616 | tf_op jit(solution)/shard_map/ppermute | solution.py:26
  39.2 4.9 %collective-permute-start.13 = (bf16[128,256]{1,0:T(8,128)(2,1)S(1)}, bf16[128,256]{1,0:T(8,128)(2,1)S(1)}, u32[]{:S(2)}, u32[]{:S(2)}) collective-permute-start(bf16[128,256]{1,0:T(8,128)(2,1)S(1)} %get-tuple-element.56), channel_id=1, source_target_pairs={{0,3},{1,2},{2,1},{3,0},{4,7},{5,6},{6,5},{7,4},{8,11},{9,10},{10,... | collective-permute-start | bytes 196616 | tf_op jit(solution)/shard_map/ppermute | solution.py:26

commit v9 on v8

--- a/solution.py
+++ b/solution.py
@@ -15,6 +15,7 @@
 CHUNK = 128
 PAIR = 2 * CHUNK
 EPS_NORM = 1e-06
+BASE = 8
 PAGE_VMEM = 53
 TOKEN_VMEM = 48
 F32 = jnp.float32
@@ -220,11 +221,10 @@
     )(keep, got)
 
 
-def token_kernel(heads, *refs):
+def project_kernel(heads, *refs):
     head_count = HEADS // heads
     blocks = refs[:head_count]
-    (gain_ref, w_hbm, wg_ref, taps_all, state_ref, rate_ref) = refs[head_count : head_count + 6]
-    (q_ref, k_ref, kt_ref, vt_ref, weight_ref, prefix_ref, rows_ref) = refs[-12:-5]
+    (gain_ref, w_hbm, wg_ref, state_ref) = refs[head_count : head_count + 4]
     ext_ref, gate_ref, normed_ref, w_ref, w_sem = refs[-5:]
     me = lax.axis_index("head")
     tok_rows = blocks[0].shape[0]
@@ -232,11 +232,8 @@
     columns = pl.ds(pl.multiple_of(me * width, HDIM), width)
     load = pltpu.make_async_copy(w_hbm.at[:, columns], w_ref, w_sem)
     load.start()
-    length = tok_rows * head_count
-    chunks = length // CHUNK
-    base = 8
-    taps_ref = taps_all[:, columns]
-    ext_ref[base - (CONV - 1) : base, :] = state_ref[0, :, columns].astype(F32)
+    chunks = tok_rows * head_count // CHUNK
+    ext_ref[BASE - (CONV - 1) : BASE, :] = state_ref[0, :, columns].astype(F32)
     gate_ref[...] = jnp.zeros_like(gate_ref)
     for distance, block in enumerate(blocks):
         first = pl.multiple_of((me ^ distance) * tok_rows, tok_rows)
@@ -249,7 +246,51 @@
     for c in range(chunks):
         rows = slice(c * CHUNK, (c + 1) * CHUNK)
         mixed = dot(normed_ref[rows, :], w_ref[...]).astype(BF16)
-        ext_ref[base + c * CHUNK : base + (c + 1) * CHUNK, :] = mixed.astype(F32)
+        ext_ref[BASE + c * CHUNK : BASE + (c + 1) * CHUNK, :] = mixed.astype(F32)
+
+
+def project(blocks, norm_gain, w_qkv, w_gates, conv_state, held):
+    head_count = len(blocks)
+    heads = HEADS // head_count
+    width = heads * 3 * HDIM
+    tok_rows, model = blocks[0].shape
+    length = head_count * tok_rows
+    whole = pl.BlockSpec(memory_space=pltpu.VMEM)
+    anywhere = pl.BlockSpec(memory_space=pl.ANY)
+    return pl.pallas_call(
+        functools.partial(project_kernel, heads),
+        in_specs=[whole] * head_count + [whole, anywhere] + [whole] * 2 + [anywhere],
+        out_specs=[anywhere, whole, whole],
+        scratch_shapes=[
+            pltpu.VMEM((length, model), BF16),
+            pltpu.VMEM((model, width), BF16),
+            pltpu.SemaphoreType.DMA,
+        ],
+        out_shape=[
+            jax.ShapeDtypeStruct(held.shape, held.dtype),
+            jax.ShapeDtypeStruct((BASE + length, width), F32),
+            jax.ShapeDtypeStruct((length, HDIM), F32),
+        ],
+        input_output_aliases={head_count + 4: 0},
+        compiler_params=pltpu.CompilerParams(vmem_limit_bytes=TOKEN_VMEM * 2**20),
+        cost_estimate=pl.CostEstimate(
+            flops=2 * length * model * width,
+            bytes_accessed=2 * model * (length + width) + 4 * length * width,
+            transcendentals=0,
+        ),
+        name="project",
+    )(*blocks, norm_gain.reshape(1, model), w_qkv, w_gates, conv_state, held)
+
+
+def token_kernel(heads, *refs):
+    ext_ref, gate_ref, taps_all, rate_ref = refs[:4]
+    (q_ref, k_ref, kt_ref, vt_ref, weight_ref, prefix_ref, rows_ref) = refs[4:]
+    me = lax.axis_index("head")
+    width = ext_ref.shape[1]
+    taps_ref = taps_all[:, pl.ds(pl.multiple_of(me * width, HDIM), width)]
+    base = BASE
+    length = gate_ref.shape[0]
+    chunks = length // CHUNK
 
     shift = lax.rem(HDIM - 2 * heads * me, HDIM)
     logits = pltpu.roll(gate_ref[...], shift, 1)
@@ -309,17 +350,11 @@
                 so_far = so_far + whole
 
 
-def token_vectors(
-    decay_rate, blocks, norm_gain, w_qkv, w_gates, conv_weight, conv_state, held
-):
-    head_count = len(blocks)
-    heads = HEADS // head_count
-    width = heads * 3 * HDIM
-    tok_rows, model = blocks[0].shape
-    length = head_count * tok_rows
+def token_vectors(ext, gates, conv_weight, decay_rate):
+    length = gates.shape[0]
+    heads = ext.shape[1] // (3 * HDIM)
     chunks = length // CHUNK
     whole = pl.BlockSpec(memory_space=pltpu.VMEM)
-    anywhere = pl.BlockSpec(memory_space=pl.ANY)
     outs = [
         jax.ShapeDtypeStruct((heads, HDIM, length), BF16),
         jax.ShapeDtypeStruct((heads, length, HDIM), BF16),
@@ -331,34 +366,15 @@
     ]
     return pl.pallas_call(
         functools.partial(token_kernel, heads),
-        in_specs=[whole] * head_count + [whole, anywhere] + [whole] * 4 + [anywhere],
-        out_specs=[anywhere] + [whole] * len(outs),
-        scratch_shapes=[
-            pltpu.VMEM((8 + length, width), F32),
-            pltpu.VMEM((length, HDIM), F32),
-            pltpu.VMEM((length, model), BF16),
-            pltpu.VMEM((model, width), BF16),
-            pltpu.SemaphoreType.DMA,
-        ],
-        out_shape=[jax.ShapeDtypeStruct(held.shape, held.dtype)] + outs,
-        input_output_aliases={head_count + 6: 0},
-        compiler_params=pltpu.CompilerParams(vmem_limit_bytes=TOKEN_VMEM * 2**20),
+        in_specs=[whole] * 4,
+        out_specs=[whole] * len(outs),
+        out_shape=outs,
+        compiler_params=pltpu.CompilerParams(vmem_limit_bytes=32 * 2**20),
         cost_estimate=pl.CostEstimate(
-            flops=2 * length * model * width,
-            bytes_accessed=2 * model * (length + width) + 4 * 2**20,
-            transcendentals=length * width,
+            flops=64 * ext.size, bytes_accessed=4 * ext.size, transcendentals=ext.size
         ),
         name="token_vectors",
-    )(
-        *blocks,
-        norm_gain.reshape(1, model),
-        w_qkv,
-        w_gates,
-        conv_weight,
-        conv_state,
-        decay_rate.reshape(1, HEADS),
-        held,
-    )
+    )(ext, gates, conv_weight, decay_rate.reshape(1, HEADS))
 
 
 def read_kernel(heads, terms, ridge_ref, *refs):
@@ -565,16 +581,17 @@
                 blocks[distance] = hold(blocks[distance], keep_gram)
                 blocks[distance ^ bit] = swap(blocks[distance], "head", bit)
     blocks = [blocks[i] for i in range(head_count)]
-    send_cross, *vectors = token_vectors(
-        decay_rate, blocks, norm_gain, w_qkv, w_gates, conv_weight, conv_state, send_cross
-    )
+    send_cross, ext, gates = project(blocks, norm_gain, w_qkv, w_gates, conv_state, send_cross)
+    got_cross = swap(send_cross, "grp", 1)
+    vectors = token_vectors(ext, gates, conv_weight, decay_rate)
     grams = halve_sums(keep_gram, got_gram)
-    crosses = halve_sums(keep_cross, swap(send_cross, "grp", 1))
+    crosses = halve_sums(keep_cross, got_cross)
     base, solved = ridge_reads(ridge, scattered(grams), vectors, [crosses[0]])
     reads = cross_reads(scattered(crosses), base, solved, head_count)
-    parts = [reads[0]] + [swap(reads[i], "head", i) for i in range(1, head_count)]
-    total = output_rows(tokens, w_out, parts[:2], (0, 1), F32)
-    return output_rows(total, w_out, parts[2:], tuple(range(2, head_count)), BF16)
+    far = tuple(reversed(range(1, head_count)))
+    parts = [swap(reads[i], "head", i) for i in far]
+    total = output_rows(tokens, w_out, reads[:1], (0,), F32)
+    return output_rows(total, w_out, parts, far, BF16)
 
 
 def solution(mesh):

time: 45.4 us -> 46.7 us (1.029)
  Pallas kernels: 20 us -> 21.6 us
  waiting for transfers between devices: 5.82 us -> 7.1 us
  starting transfers between devices: 17.2 us -> 16.1 us
    pallas_call x0 -> x1, Pallas kernels: none -> 2.96 us  [project(): pl.pallas_call(functools.partial(project_kernel, heads), in_specs=[whole]...]
    pallas_call x1, Pallas kernels: 4.73 us -> 2.49 us  [token_vectors(): pl.pallas_call(functools.partial(token_kernel, heads), in_specs=[whole] *...]
    ppermute x14, waiting for transfers between devices: 5.82 us -> 7.1 us  [swap(): return lax.ppermute(block, axis, [(i, i ^ distance) for i in range(size)])]
    ppermute x14, starting transfers between devices: 17.2 us -> 16.1 us  [swap(): return lax.ppermute(block, axis, [(i, i ^ distance) for i in range(size)])]
    pallas_call x1, Pallas kernels: 7.02 us -> 8.01 us  [page_sums(): pl.pallas_call(functools.partial(sums_kernel, heads, owners, slot_bits),...]
  transfers between devices with their start and end apart: 14 -> 14, of which waited for: 4 -> 4; matrix products, arithmetic and copies ran while one was open for 4% -> 4% of each run, Pallas kernels for 41% -> 43%
where the time goes in v9:
time: 46.7 us; the launch traced here: 46.8 us
  Pallas kernels  21.6 us (46%)
  starting transfers between devices  16.1 us (34%)
  waiting for transfers between devices  7.1 us (15%)
  other arithmetic  1.59 us (3%)
    ppermute x14, starting transfers between devices, swap(): return lax.ppermute(block, axis, [(i, i ^ distance) for i in range(size)])  16.1 us
    pallas_call x1, Pallas kernels, page_sums(): pl.pallas_call(functools.partial(sums_kernel, heads, owners, slot_bits),...  8.01 us
    ppermute x14, waiting for transfers between devices, swap(): return lax.ppermute(block, axis, [(i, i ^ distance) for i in range(size)])  7.1 us
    pallas_call x1, Pallas kernels, ridge_reads(): pl.pallas_call(functools.partial(read_kernel, heads, len(grams)), in_spec...  6.4 us
    pallas_call x1, Pallas kernels, project(): pl.pallas_call(functools.partial(project_kernel, heads), in_specs=[whole]...  2.96 us
    pallas_call x1, Pallas kernels, token_vectors(): pl.pallas_call(functools.partial(token_kernel, heads), in_specs=[whole] *...  2.49 us
    pallas_call x2, Pallas kernels, output_rows(): pl.pallas_call(functools.partial(output_kernel, distances), in_specs=[who...  1.33 us
  transfers between devices with their start and end apart: 14, of which 4 were waited for; matrix products, arithmetic and copies ran while one was open for 4% of the time, Pallas kernels for 43%

profile of v9, /device:TPU:0, one launch (start us, length us, event | category | flops | bytes accessed | tf_op | source)
XLA Modules:
  0.0 46.8 jit_solution(7163830536741771946)
XLA Ops:
  0.0 2.9 %collective-permute-start.1 = (bf16[128,1024]{1,0:T(8,128)(2,1)}, bf16[128,1024]{1,0:T(8,128)(2,1)S(1)}, u32[]{:S(2)}, u32[]{:S(2)}) collective-permute-start(bf16[128,1024]{1,0:T(8,128)(2,1)} %start_ref.1), channel_id=1, source_target_pairs={{0,2},{1,3},{2,0},{3,1},{4,6},{5,7},{6,4},{7,5},{8,10},{9,11},{10,... | collective-permute-start | bytes 786440 | tf_op jit(solution)/shard_map/ppermute | solution.py:27
  2.9 0.0 collective-permute-start
  3.0 0.7 %shift-left_or_fusion.pack_hbm = s32[8]{0:T(128)S(1)} fusion(s32[8]{0:T(128)} %param.27, s32[8]{0:T(128)} %param.28), kind=kLoop, calls=%fused_computation.2 | loop fusion | flops 16 | bytes 96 | tf_op jit(solution)/shard_map/or | solution.py:562
  3.6 0.9 %select_reduce_fusion.code_hbm = s32[64]{0:T(128)S(1)} fusion(s32[8,64]{1,0:T(8,128)S(1)} %multiply_add_fusion, s32[64]{0:T(128)S(1)} %iota_add_fusion, s32[8,64]{1,0:T(8,128)} %param.26), kind=kLoop, calls=%fused_computation | loop fusion | flops 98240 | bytes 4608 | tf_op jit(solution)/shard_map/reduce_sum | solution.py:564
  4.5 0.0 copy-start.8
  4.5 0.0 copy-start.1
  4.6 0.0 copy-start.4
  4.6 0.0 copy-start.5
  4.6 8.0 %page_sums.1 = (bf16[4,256,128]{2,1,0:T(8,128)(2,1)S(1)}, bf16[4,256,128]{2,1,0:T(8,128)(2,1)S(1)}, bf16[4,256,128]{2,1,0:T(8,128)(2,1)S(1)}, bf16[4,256,128]{2,1,0:T(8,128)(2,1)}) custom-call(s32[64]{0:T(128)S(1)} %select_reduce_fusion.code_hbm, s32[8]{0:T(128)S(1)} %shift-left_or_fusion.pack_hbm, bf16[64,256,128]{2,1,0:T(8,128)(2,1)} %bitcast.8, ...), custom_call_target="tpu_custom_call" | custom-call | flops 4294967296 | bytes 8388608 | tf_op jit(solution)/shard_map/page_sums/pallas_call | solution.py:173
  12.6 0.0 collective-permute-done.1.refs_0_
  12.6 0.6 %collective-permute-start.2 = (bf16[128,1024]{1,0:T(8,128)(2,1)S(1)}, bf16[128,1024]{1,0:T(8,128)(2,1)S(1)}, u32[]{:S(2)}, u32[]{:S(2)}) collective-permute-start(bf16[128,1024]{1,0:T(8,128)(2,1)S(1)} %hold.1.refs_2_), channel_id=1, source_target_pairs={{0,1},{1,0},{2,3},{3,2},{4,5},{5,4},{6,7},{7,6},{8,9},{9,8},{10,11... | collective-permute-start | bytes 786440 | tf_op jit(solution)/shard_map/ppermute | solution.py:27
  13.2 0.6 %collective-permute-start.7 = (bf16[4,256,128]{2,1,0:T(8,128)(2,1)S(1)}, bf16[4,256,128]{2,1,0:T(8,128)(2,1)S(1)}, u32[]{:S(2)}, u32[]{:S(2)}) collective-permute-start(bf16[4,256,128]{2,1,0:T(8,128)(2,1)S(1)} %get-tuple-element.41), channel_id=1, source_target_pairs={{0,4},{4,0},{8,12},{12,8},{16,20},{20,16},{24,28},{28,24},{1,5},{5... | collective-permute-start | bytes 786440 | tf_op jit(solution)/shard_map/ppermute | solution.py:27
  13.8 0.0 copy-done.8
  13.8 0.2 copy.19.refs_6_
  14.0 0.0 collective-permute-done.refs_1_
  14.0 0.4 collective-permute-done.2.refs_3_
  14.3 0.0 copy-done.1
  14.4 0.0 copy-done.4
  14.4 0.0 copy-done.5
  14.4 0.0 copy-start.3
  14.4 0.0 copy-start.6
  14.4 0.0 copy-start.2
  14.4 0.0 copy-start.7
  14.4 3.0 %project.1 = (bf16[4,256,128]{2,1,0:T(8,128)(2,1)S(1)}, f32[520,768]{1,0:T(8,128)S(1)}, f32[512,128]{1,0:T(8,128)S(1)}) custom-call(bf16[128,1024]{1,0:T(8,128)(2,1)S(1)} %copy-done.1, bf16[128,1024]{1,0:T(8,128)(2,1)S(1)} %collective-permute-done.refs_1_, bf16[128,1024]{1,0:T(8,128)(2,1)S(1)} %hold.1.refs_2_, ...), custom_call_target="tpu_custom_call", output_to_operand_aliasing={{0}: (8, {})} | custom-call | flops 805306368 | bytes 4194304 | tf_op jit(solution)/shard_map/project/pallas_call | solution.py:260
  17.4 1.2 %collective-permute-start.3 = (bf16[4,256,128]{2,1,0:T(8,128)(2,1)S(1)}, bf16[4,256,128]{2,1,0:T(8,128)(2,1)S(1)}, u32[]{:S(2)}, u32[]{:S(2)}) collective-permute-start(bf16[4,256,128]{2,1,0:T(8,128)(2,1)S(1)} %get-tuple-element.36), channel_id=1, source_target_pairs={{0,4},{4,0},{8,12},{12,8},{16,20},{20,16},{24,28},{28,24},{1,5},{5... | collective-permute-start | bytes 786440 | tf_op jit(solution)/shard_map/ppermute | solution.py:27
  18.5 3.8 %collective-permute-done.7.got_ref = bf16[4,256,128]{2,1,0:T(8,128)(2,1)S(1)} collective-permute-done((bf16[4,256,128]{2,1,0:T(8,128)(2,1)S(1)}, bf16[4,256,128]{2,1,0:T(8,128)(2,1)S(1)}, u32[]{:S(2)}, u32[]{:S(2)}) %collective-permute-start.7) | collective-permute-done | bytes 262176 | tf_op jit(solution)/shard_map/ppermute | solution.py:27
  22.3 0.1 halve_sums.3
  22.4 2.8 %collective-permute-start.8 = (bf16[256,128]{1,0:T(8,128)(2,1)S(1)}, bf16[256,128]{1,0:T(8,128)(2,1)S(1)}, u32[]{:S(2)}, u32[]{:S(2)}) collective-permute-start(bf16[256,128]{1,0:T(8,128)(2,1)S(1)} %get-tuple-element.43), channel_id=1, source_target_pairs={{0,24},{4,28},{8,16},{12,20},{16,8},{20,12},{24,0},{28,4},{1,25},{... | collective-permute-start | bytes 196616 | tf_op jit(solution)/shard_map/ppermute | solution.py:27
  25.2 0.0 collective-permute-start.9
  25.2 1.7 %collective-permute-start.10 = (bf16[256,128]{1,0:T(8,128)(2,1)S(1)}, bf16[256,128]{1,0:T(8,128)(2,1)S(1)}, u32[]{:S(2)}, u32[]{:S(2)}) collective-permute-start(bf16[256,128]{1,0:T(8,128)(2,1)S(1)} %get-tuple-element.45), channel_id=1, source_target_pairs={{0,8},{4,12},{8,0},{12,4},{16,24},{20,28},{24,16},{28,20},{1,9},{5... | collective-permute-start | bytes 196616 | tf_op jit(solution)/shard_map/ppermute | solution.py:27
  26.9 0.0 copy-done.3
  26.9 0.0 copy-done.6
  26.9 2.5 %token_vectors.1 = (bf16[2,128,512]{2,1,0:T(8,128)(2,1)S(1)}, bf16[2,512,128]{2,1,0:T(8,128)(2,1)S(1)}, bf16[2,128,512]{2,1,0:T(8,128)(2,1)S(1)}, bf16[2,128,512...) custom-call(f32[520,768]{1,0:T(8,128)S(1)} %get-tuple-element.46.ref, ...), custom_call_target="tpu_custom_call" | custom-call | flops 25559040 | bytes 1597440 | tf_op jit(solution)/shard_map/token_vectors/pallas_call | solution.py:367
  29.4 0.0 collective-permute-done.3.got_ref
  29.4 0.0 copy-done.2
  29.4 0.1 halve_sums.2
  29.5 2.8 %collective-permute-start.4 = (bf16[256,128]{1,0:T(8,128)(2,1)S(1)}, bf16[256,128]{1,0:T(8,128)(2,1)S(1)}, u32[]{:S(2)}, u32[]{:S(2)}) collective-permute-start(bf16[256,128]{1,0:T(8,128)(2,1)S(1)} %get-tuple-element.38), channel_id=1, source_target_pairs={{0,24},{4,28},{8,16},{12,20},{16,8},{20,12},{24,0},{28,4},{1,25},{... | collective-permute-start | bytes 196616 | tf_op jit(solution)/shard_map/ppermute | solution.py:27
  32.2 0.0 collective-permute-start.5
  32.2 0.0 collective-permute-done.8.refs_1_
  32.2 1.7 %collective-permute-start.6 = (bf16[256,128]{1,0:T(8,128)(2,1)S(1)}, bf16[256,128]{1,0:T(8,128)(2,1)S(1)}, u32[]{:S(2)}, u32[]{:S(2)}) collective-permute-start(bf16[256,128]{1,0:T(8,128)(2,1)S(1)} %get-tuple-element.40), channel_id=1, source_target_pairs={{0,8},{4,12},{8,0},{12,4},{16,24},{20,28},{24,16},{28,20},{1,9},{5... | collective-permute-start | bytes 196616 | tf_op jit(solution)/shard_map/ppermute | solution.py:27
  33.9 0.0 collective-permute-done.9.refs_2_
  33.9 0.0 collective-permute-done.10.refs_3_
  33.9 0.0 copy-done.7
  33.9 0.0 copy-start
  34.0 6.4 %ridge_reads.1 = (f32[512,256]{1,0:T(8,128)S(1)}, bf16[512,256]{1,0:T(8,128)(2,1)S(1)}) custom-call(f32[1,2]{1,0:T(1,128)S(1)} %bitcast.7, f32[256,128]{1,0:T(8,128)S(1)} %get-tuple-element.42.refs_0_, bf16[256,128]{1,0:T(8,128)(2,1)S(1)} %collective-permute-done.8.refs_1_, bf16[256,128]{1,0:T(8,128)(2,1)S(1)} %collective-permute-done.9.refs_2_, ...), custom_call_target="tpu_custom_call" | custom-call | flops 6442450944 | bytes 8388608 | tf_op jit(solution)/shard_map/ridge_reads/pallas_call | solution.py:451
  40.4 0.0 collective-permute-done.4.refs_1_
  40.4 0.0 collective-permute-done.5.refs_2_
  40.4 0.0 collective-permute-done.6.refs_3_
  40.4 0.3 cross_reads.1
  40.7 0.1 collective-permute-start.11
  40.7 0.1 collective-permute-start.12
  40.8 1.8 %collective-permute-start.13 = (bf16[128,256]{1,0:T(8,128)(2,1)S(1)}, bf16[128,256]{1,0:T(8,128)(2,1)S(1)}, u32[]{:S(2)}, u32[]{:S(2)}) collective-permute-start(bf16[128,256]{1,0:T(8,128)(2,1)S(1)} %get-tuple-element.60), channel_id=1, source_target_pairs={{0,1},{1,0},{2,3},{3,2},{4,5},{5,4},{6,7},{7,6},{8,9},{9,8},{10,11... | collective-permute-start | bytes 196616 | tf_op jit(solution)/shard_map/ppermute | solution.py:27
  42.6 0.0 copy-done
  42.6 0.2 output_rows.2.start_ref
  42.8 1.7 %collective-permute-done.11.refs_0_ = bf16[128,256]{1,0:T(8,128)(2,1)S(1)} collective-permute-done((bf16[128,256]{1,0:T(8,128)(2,1)S(1)}, bf16[128,256]{1,0:T(8,128)(2,1)S(1)}, u32[]{:S(2)}, u32[]{:S(2)}) %collective-permute-start.11) | collective-permute-done | bytes 65568 | tf_op jit(solution)/shard_map/ppermute | solution.py:27
  44.5 1.2 %collective-permute-done.12.refs_1_ = bf16[128,256]{1,0:T(8,128)(2,1)S(1)} collective-permute-done((bf16[128,256]{1,0:T(8,128)(2,1)S(1)}, bf16[128,256]{1,0:T(8,128)(2,1)S(1)}, u32[]{:S(2)}, u32[]{:S(2)}) %collective-permute-start.12) | collective-permute-done | bytes 65568 | tf_op jit(solution)/shard_map/ppermute | solution.py:27
  45.7 0.0 collective-permute-done.13.refs_2_
  45.7 1.1 %output_rows.3 = bf16[128,1024]{1,0:T(8,128)(2,1)} custom-call(f32[128,1024]{1,0:T(8,128)S(1)} %output_rows.2.start_ref, bf16[1024,1024]{1,0:T(8,128)(2,1)S(1)} %copy-done, bf16[128,256]{1,0:T(8,128)(2,1)S(1)} %collective-permute-done.11.refs_0_, bf16[128,256]{1,0:T(8,128)(2,1)S(1)} %collective-permute-done.12.refs_1_, ...), custom_call_target="tpu_custom_call" | custom-call | flops 201326592 | bytes 2883584 | tf_op jit(solution)/shard_map/output_rows/pallas_call | solution.py:518
  (3 shorter events, 0.0 us)
Async XLA Ops:
  0.0 12.6 %collective-permute-start.1 = (bf16[128,1024]{1,0:T(8,128)(2,1)}, bf16[128,1024]{1,0:T(8,128)(2,1)S(1)}, u32[]{:S(2)}, u32[]{:S(2)}) collective-permute-start(bf16[128,1024]{1,0:T(8,128)(2,1)} %start_ref.1), channel_id=1, source_target_pairs={{0,2},{1,3},{2,0},{3,1},{4,6},{5,7},{6,4},{7,5},{8,10},{9,11},{10,... | collective-permute-start | bytes 786440 | tf_op jit(solution)/shard_map/ppermute | solution.py:27
  2.9 11.0 %collective-permute-start = (bf16[128,1024]{1,0:T(8,128)(2,1)}, bf16[128,1024]{1,0:T(8,128)(2,1)S(1)}, u32[]{:S(2)}, u32[]{:S(2)}) collective-permute-start(bf16[128,1024]{1,0:T(8,128)(2,1)} %start_ref.1), channel_id=1, source_target_pairs={{0,1},{1,0},{2,3},{3,2},{4,5},{5,4},{6,7},{7,6},{8,9},{9,8},{10,11... | collective-permute-start | bytes 786440 | tf_op jit(solution)/shard_map/ppermute | solution.py:27
  4.5 9.3 %copy-start.8 = (bf16[1024,16]{0,1:T(8,128)(2,1)S(1)}, bf16[1024,16]{0,1:T(8,128)(2,1)}, u32[]{:S(2)}) copy-start(bf16[1024,16]{0,1:T(8,128)(2,1)} %param.18) | copy-start | bytes 98308
  4.5 9.8 %copy-start.1 = (bf16[128,1024]{1,0:T(8,128)(2,1)S(1)}, bf16[128,1024]{1,0:T(8,128)(2,1)}, u32[]{:S(2)}) copy-start(bf16[128,1024]{1,0:T(8,128)(2,1)} %start_ref.1) | copy-start | bytes 786436
  4.6 9.8 %copy-start.4 = (bf16[1,3,3072]{2,1,0:T(4,128)(2,1)S(1)}, bf16[1,3,3072]{2,1,0:T(4,128)(2,1)}, u32[]{:S(2)}) copy-start(bf16[1,3,3072]{2,1,0:T(4,128)(2,1)} %refs_7_.1) | copy-start | bytes 55300
  4.6 9.8 %copy-start.5 = (f32[1024]{0:T(1024)S(1)}, f32[1024]{0:T(1024)}, u32[]{:S(2)}) copy-start(f32[1024]{0:T(1024)} %param.16) | copy-start | bytes 12292
  12.6 1.7 %collective-permute-start.2 = (bf16[128,1024]{1,0:T(8,128)(2,1)S(1)}, bf16[128,1024]{1,0:T(8,128)(2,1)S(1)}, u32[]{:S(2)}, u32[]{:S(2)}) collective-permute-start(bf16[128,1024]{1,0:T(8,128)(2,1)S(1)} %hold.1.refs_2_), channel_id=1, source_target_pairs={{0,1},{1,0},{2,3},{3,2},{4,5},{5,4},{6,7},{7,6},{8,9},{9,8},{10,11... | collective-permute-start | bytes 786440 | tf_op jit(solution)/shard_map/ppermute | solution.py:27
  13.2 9.2 %collective-permute-start.7 = (bf16[4,256,128]{2,1,0:T(8,128)(2,1)S(1)}, bf16[4,256,128]{2,1,0:T(8,128)(2,1)S(1)}, u32[]{:S(2)}, u32[]{:S(2)}) collective-permute-start(bf16[4,256,128]{2,1,0:T(8,128)(2,1)S(1)} %get-tuple-element.41), channel_id=1, source_target_pairs={{0,4},{4,0},{8,12},{12,8},{16,20},{20,16},{24,28},{28,24},{1,5},{5... | collective-permute-start | bytes 786440 | tf_op jit(solution)/shard_map/ppermute | solution.py:27
  14.4 12.5 %copy-start.3 = (f32[4,3072]{1,0:T(4,128)S(1)}, f32[4,3072]{1,0:T(4,128)}, u32[]{:S(2)}) copy-start(f32[4,3072]{1,0:T(4,128)} %refs_2_.1) | copy-start | bytes 147460
  14.4 12.5 %copy-start.6 = (f32[8]{0:T(128)S(1)}, f32[8]{0:T(128)}, u32[]{:S(2)}) copy-start(f32[8]{0:T(128)} %param.21) | copy-start | bytes 100
  14.4 15.0 %copy-start.2 = (bf16[4,256,128]{2,1,0:T(8,128)(2,1)S(1)}, bf16[4,256,128]{2,1,0:T(8,128)(2,1)}, u32[]{:S(2)}) copy-start(bf16[4,256,128]{2,1,0:T(8,128)(2,1)} %get-tuple-element.33.keep_ref) | copy-start | bytes 786436
  14.4 19.5 %copy-start.7 = (f32[2]{0:T(128)S(1)}, f32[2]{0:T(128)}, u32[]{:S(2)}) copy-start(f32[2]{0:T(128)} %param.22) | copy-start | bytes 28
  17.4 12.0 %collective-permute-start.3 = (bf16[4,256,128]{2,1,0:T(8,128)(2,1)S(1)}, bf16[4,256,128]{2,1,0:T(8,128)(2,1)S(1)}, u32[]{:S(2)}, u32[]{:S(2)}) collective-permute-start(bf16[4,256,128]{2,1,0:T(8,128)(2,1)S(1)} %get-tuple-element.36), channel_id=1, source_target_pairs={{0,4},{4,0},{8,12},{12,8},{16,20},{20,16},{24,28},{28,24},{1,5},{5... | collective-permute-start | bytes 786440 | tf_op jit(solution)/shard_map/ppermute | solution.py:27
  22.4 9.8 %collective-permute-start.8 = (bf16[256,128]{1,0:T(8,128)(2,1)S(1)}, bf16[256,128]{1,0:T(8,128)(2,1)S(1)}, u32[]{:S(2)}, u32[]{:S(2)}) collective-permute-start(bf16[256,128]{1,0:T(8,128)(2,1)S(1)} %get-tuple-element.43), channel_id=1, source_target_pairs={{0,24},{4,28},{8,16},{12,20},{16,8},{20,12},{24,0},{28,4},{1,25},{... | collective-permute-start | bytes 196616 | tf_op jit(solution)/shard_map/ppermute | solution.py:27
  25.2 8.8 %collective-permute-start.9 = (bf16[256,128]{1,0:T(8,128)(2,1)S(1)}, bf16[256,128]{1,0:T(8,128)(2,1)S(1)}, u32[]{:S(2)}, u32[]{:S(2)}) collective-permute-start(bf16[256,128]{1,0:T(8,128)(2,1)S(1)} %get-tuple-element.44), channel_id=1, source_target_pairs={{0,16},{4,20},{8,24},{12,28},{16,0},{20,4},{24,8},{28,12},{1,17},{... | collective-permute-start | bytes 196616 | tf_op jit(solution)/shard_map/ppermute | solution.py:27
  25.2 8.8 %collective-permute-start.10 = (bf16[256,128]{1,0:T(8,128)(2,1)S(1)}, bf16[256,128]{1,0:T(8,128)(2,1)S(1)}, u32[]{:S(2)}, u32[]{:S(2)}) collective-permute-start(bf16[256,128]{1,0:T(8,128)(2,1)S(1)} %get-tuple-element.45), channel_id=1, source_target_pairs={{0,8},{4,12},{8,0},{12,4},{16,24},{20,28},{24,16},{28,20},{1,9},{5... | collective-permute-start | bytes 196616 | tf_op jit(solution)/shard_map/ppermute | solution.py:27
  29.5 10.9 %collective-permute-start.4 = (bf16[256,128]{1,0:T(8,128)(2,1)S(1)}, bf16[256,128]{1,0:T(8,128)(2,1)S(1)}, u32[]{:S(2)}, u32[]{:S(2)}) collective-permute-start(bf16[256,128]{1,0:T(8,128)(2,1)S(1)} %get-tuple-element.38), channel_id=1, source_target_pairs={{0,24},{4,28},{8,16},{12,20},{16,8},{20,12},{24,0},{28,4},{1,25},{... | collective-permute-start | bytes 196616 | tf_op jit(solution)/shard_map/ppermute | solution.py:27
  32.2 8.1 %collective-permute-start.5 = (bf16[256,128]{1,0:T(8,128)(2,1)S(1)}, bf16[256,128]{1,0:T(8,128)(2,1)S(1)}, u32[]{:S(2)}, u32[]{:S(2)}) collective-permute-start(bf16[256,128]{1,0:T(8,128)(2,1)S(1)} %get-tuple-element.39), channel_id=1, source_target_pairs={{0,16},{4,20},{8,24},{12,28},{16,0},{20,4},{24,8},{28,12},{1,17},{... | collective-permute-start | bytes 196616 | tf_op jit(solution)/shard_map/ppermute | solution.py:27
  32.2 8.1 %collective-permute-start.6 = (bf16[256,128]{1,0:T(8,128)(2,1)S(1)}, bf16[256,128]{1,0:T(8,128)(2,1)S(1)}, u32[]{:S(2)}, u32[]{:S(2)}) collective-permute-start(bf16[256,128]{1,0:T(8,128)(2,1)S(1)} %get-tuple-element.40), channel_id=1, source_target_pairs={{0,8},{4,12},{8,0},{12,4},{16,24},{20,28},{24,16},{28,20},{1,9},{5... | collective-permute-start | bytes 196616 | tf_op jit(solution)/shard_map/ppermute | solution.py:27
  33.9 8.7 %copy-start = (bf16[1024,1024]{1,0:T(8,128)(2,1)S(1)}, bf16[1024,1024]{1,0:T(8,128)(2,1)}, u32[]{:S(2)}) copy-start(bf16[1024,1024]{1,0:T(8,128)(2,1)} %w_ref.3) | copy-start | bytes 6291460
  40.7 3.8 %collective-permute-start.11 = (bf16[128,256]{1,0:T(8,128)(2,1)S(1)}, bf16[128,256]{1,0:T(8,128)(2,1)S(1)}, u32[]{:S(2)}, u32[]{:S(2)}) collective-permute-start(bf16[128,256]{1,0:T(8,128)(2,1)S(1)} %get-tuple-element.58), channel_id=1, source_target_pairs={{0,3},{1,2},{2,1},{3,0},{4,7},{5,6},{6,5},{7,4},{8,11},{9,10},{10,... | collective-permute-start | bytes 196616 | tf_op jit(solution)/shard_map/ppermute | solution.py:27
  40.7 5.0 %collective-permute-start.12 = (bf16[128,256]{1,0:T(8,128)(2,1)S(1)}, bf16[128,256]{1,0:T(8,128)(2,1)S(1)}, u32[]{:S(2)}, u32[]{:S(2)}) collective-permute-start(bf16[128,256]{1,0:T(8,128)(2,1)S(1)} %get-tuple-element.59), channel_id=1, source_target_pairs={{0,2},{1,3},{2,0},{3,1},{4,6},{5,7},{6,4},{7,5},{8,10},{9,11},{10,... | collective-permute-start | bytes 196616 | tf_op jit(solution)/shard_map/ppermute | solution.py:27
  40.8 4.9 %collective-permute-start.13 = (bf16[128,256]{1,0:T(8,128)(2,1)S(1)}, bf16[128,256]{1,0:T(8,128)(2,1)S(1)}, u32[]{:S(2)}, u32[]{:S(2)}) collective-permute-start(bf16[128,256]{1,0:T(8,128)(2,1)S(1)} %get-tuple-element.60), channel_id=1, source_target_pairs={{0,1},{1,0},{2,3},{3,2},{4,5},{5,4},{6,7},{7,6},{8,9},{9,8},{10,11... | collective-permute-start | bytes 196616 | tf_op jit(solution)/shard_map/ppermute | solution.py:27

commit v10 on v9

--- a/solution.py
+++ b/solution.py
@@ -197,20 +197,20 @@
     )(code, pack, keys, values, prompt_state)
 
 
-def halve_kernel(keep_ref, got_ref, *outs):
-    for distance, out_ref in enumerate(outs):
+def halve_kernel(keep_ref, got_ref, *refs):
+    for distance, out_ref in enumerate(refs[-keep_ref.shape[0] :]):
         row = (lax.axis_index("grp") >> 1) ^ distance
         total = keep_ref[row].astype(F32) + got_ref[row].astype(F32)
         out_ref[...] = total.astype(out_ref.dtype)
 
 
-def halve_sums(keep, got):
+def halve_sums(keep, got, after=()):
     count, rows, cols = keep.shape
     outs = [jax.ShapeDtypeStruct((rows, cols), F32 if i == 0 else BF16) for i in range(count)]
     whole = pl.BlockSpec(memory_space=pltpu.VMEM)
     return pl.pallas_call(
         halve_kernel,
-        in_specs=[whole, whole],
+        in_specs=[whole] * (2 + len(after)),
         out_specs=[whole] * count,
         out_shape=outs,
         compiler_params=pltpu.CompilerParams(vmem_limit_bytes=32 * 2**20),
@@ -218,7 +218,7 @@
             flops=count * rows * cols, bytes_accessed=6 * count * rows * cols, transcendentals=0
         ),
         name="halve_sums",
-    )(keep, got)
+    )(keep, got, *after)
 
 
 def project_kernel(heads, *refs):
@@ -584,7 +584,7 @@
     send_cross, ext, gates = project(blocks, norm_gain, w_qkv, w_gates, conv_state, send_cross)
     got_cross = swap(send_cross, "grp", 1)
     vectors = token_vectors(ext, gates, conv_weight, decay_rate)
-    grams = halve_sums(keep_gram, got_gram)
+    grams = halve_sums(keep_gram, got_gram, vectors[-1:])
     crosses = halve_sums(keep_cross, got_cross)
     base, solved = ridge_reads(ridge, scattered(grams), vectors, [crosses[0]])
     reads = cross_reads(scattered(crosses), base, solved, head_count)

time: 46.7 us -> 46 us (0.985); the launches traced: 46.8 us -> 45.4 us
  waiting for transfers between devices: 7.1 us -> 5.4 us
  starting transfers between devices: 16.1 us -> 17.4 us
  Pallas kernels: 21.6 us -> 20.6 us
    ppermute x14, waiting for transfers between devices: 7.1 us -> 5.4 us  [swap(): return lax.ppermute(block, axis, [(i, i ^ distance) for i in range(size)])]
    ppermute x14, starting transfers between devices: 16.1 us -> 17.4 us  [swap(): return lax.ppermute(block, axis, [(i, i ^ distance) for i in range(size)])]
    pallas_call x1, Pallas kernels: 8.01 us -> 7.01 us  [page_sums(): pl.pallas_call(functools.partial(sums_kernel, heads, owners, slot_bits),...]
  transfers between devices with their start and end apart: 14 -> 14, of which waited for: 4 -> 4; matrix products, arithmetic and copies ran while one was open for 4% -> 4% of each run, Pallas kernels for 43% -> 42%
where the time goes in v10:
time: 46 us; the launch traced here: 45.4 us
  Pallas kernels  20.6 us (45%)
  starting transfers between devices  17.4 us (38%)
  waiting for transfers between devices  5.4 us (12%)
  other arithmetic  1.59 us (3%)
    ppermute x14, starting transfers between devices, swap(): return lax.ppermute(block, axis, [(i, i ^ distance) for i in range(size)])  17.4 us
    pallas_call x1, Pallas kernels, page_sums(): pl.pallas_call(functools.partial(sums_kernel, heads, owners, slot_bits),...  7.01 us
    pallas_call x1, Pallas kernels, ridge_reads(): pl.pallas_call(functools.partial(read_kernel, heads, len(grams)), in_spec...  6.4 us
    ppermute x14, waiting for transfers between devices, swap(): return lax.ppermute(block, axis, [(i, i ^ distance) for i in range(size)])  5.4 us
    pallas_call x1, Pallas kernels, project(): pl.pallas_call(functools.partial(project_kernel, heads), in_specs=[whole]...  2.96 us
    pallas_call x1, Pallas kernels, token_vectors(): pl.pallas_call(functools.partial(token_kernel, heads), in_specs=[whole] *...  2.49 us
    pallas_call x2, Pallas kernels, output_rows(): pl.pallas_call(functools.partial(output_kernel, distances), in_specs=[who...  1.33 us
  transfers between devices with their start and end apart: 14, of which 4 were waited for; matrix products, arithmetic and copies ran while one was open for 4% of the time, Pallas kernels for 42%

profile of v10, /device:TPU:0, one launch (start us, length us, event | category | flops | bytes accessed | tf_op | source)
XLA Modules:
  0.0 45.4 jit_solution(4966840622435538644)
XLA Ops:
  0.0 2.9 %collective-permute-start.1 = (bf16[128,1024]{1,0:T(8,128)(2,1)}, bf16[128,1024]{1,0:T(8,128)(2,1)S(1)}, u32[]{:S(2)}, u32[]{:S(2)}) collective-permute-start(bf16[128,1024]{1,0:T(8,128)(2,1)} %start_ref.1), channel_id=1, source_target_pairs={{0,2},{1,3},{2,0},{3,1},{4,6},{5,7},{6,4},{7,5},{8,10},{9,11},{10,... | collective-permute-start | bytes 786440 | tf_op jit(solution)/shard_map/ppermute | solution.py:27
  2.9 0.0 collective-permute-start
  3.0 0.7 %shift-left_or_fusion.pack_hbm = s32[8]{0:T(128)S(1)} fusion(s32[8]{0:T(128)} %param.27, s32[8]{0:T(128)} %param.28), kind=kLoop, calls=%fused_computation.2 | loop fusion | flops 16 | bytes 96 | tf_op jit(solution)/shard_map/or | solution.py:562
  3.6 0.9 %select_reduce_fusion.code_hbm = s32[64]{0:T(128)S(1)} fusion(s32[8,64]{1,0:T(8,128)S(1)} %multiply_add_fusion, s32[64]{0:T(128)S(1)} %iota_add_fusion, s32[8,64]{1,0:T(8,128)} %param.26), kind=kLoop, calls=%fused_computation | loop fusion | flops 98240 | bytes 4608 | tf_op jit(solution)/shard_map/reduce_sum | solution.py:564
  4.5 0.0 copy-start.8
  4.5 0.0 copy-start.1
  4.6 0.0 copy-start.4
  4.6 0.0 copy-start.5
  4.6 7.0 %page_sums.1 = (bf16[4,256,128]{2,1,0:T(8,128)(2,1)S(1)}, bf16[4,256,128]{2,1,0:T(8,128)(2,1)S(1)}, bf16[4,256,128]{2,1,0:T(8,128)(2,1)S(1)}, bf16[4,256,128]{2,1,0:T(8,128)(2,1)}) custom-call(s32[64]{0:T(128)S(1)} %select_reduce_fusion.code_hbm, s32[8]{0:T(128)S(1)} %shift-left_or_fusion.pack_hbm, bf16[64,256,128]{2,1,0:T(8,128)(2,1)} %bitcast.8, ...), custom_call_target="tpu_custom_call" | custom-call | flops 4294967296 | bytes 8388608 | tf_op jit(solution)/shard_map/page_sums/pallas_call | solution.py:173
  11.6 0.0 collective-permute-done.1.refs_0_
  11.6 0.0 copy-start.3
  11.6 0.0 copy-start.6
  11.6 0.6 %collective-permute-start.2 = (bf16[128,1024]{1,0:T(8,128)(2,1)S(1)}, bf16[128,1024]{1,0:T(8,128)(2,1)S(1)}, u32[]{:S(2)}, u32[]{:S(2)}) collective-permute-start(bf16[128,1024]{1,0:T(8,128)(2,1)S(1)} %hold.1.refs_2_), channel_id=1, source_target_pairs={{0,1},{1,0},{2,3},{3,2},{4,5},{5,4},{6,7},{7,6},{8,9},{9,8},{10,11... | collective-permute-start | bytes 786440 | tf_op jit(solution)/shard_map/ppermute | solution.py:27
  12.2 1.5 %collective-permute-start.7 = (bf16[4,256,128]{2,1,0:T(8,128)(2,1)S(1)}, bf16[4,256,128]{2,1,0:T(8,128)(2,1)S(1)}, u32[]{:S(2)}, u32[]{:S(2)}) collective-permute-start(bf16[4,256,128]{2,1,0:T(8,128)(2,1)S(1)} %get-tuple-element.41), channel_id=1, source_target_pairs={{0,4},{4,0},{8,12},{12,8},{16,20},{20,16},{24,28},{28,24},{1,5},{5... | collective-permute-start | bytes 786440 | tf_op jit(solution)/shard_map/ppermute | solution.py:27
  13.7 0.0 copy-done.8
  13.7 0.2 copy.19.refs_6_
  13.9 0.0 collective-permute-done.refs_1_
  13.9 0.0 collective-permute-done.2.refs_3_
  13.9 0.0 copy-done.1
  13.9 0.0 copy-done.4
  13.9 0.0 copy-done.5
  14.0 0.0 copy-start.2
  14.0 0.0 copy-start.7
  14.0 3.0 %project.1 = (bf16[4,256,128]{2,1,0:T(8,128)(2,1)S(1)}, f32[520,768]{1,0:T(8,128)S(1)}, f32[512,128]{1,0:T(8,128)S(1)}) custom-call(bf16[128,1024]{1,0:T(8,128)(2,1)S(1)} %copy-done.1, bf16[128,1024]{1,0:T(8,128)(2,1)S(1)} %collective-permute-done.refs_1_, bf16[128,1024]{1,0:T(8,128)(2,1)S(1)} %hold.1.refs_2_, ...), custom_call_target="tpu_custom_call", output_to_operand_aliasing={{0}: (8, {})} | custom-call | flops 805306368 | bytes 4194304 | tf_op jit(solution)/shard_map/project/pallas_call | solution.py:260
  16.9 1.0 %collective-permute-start.3 = (bf16[4,256,128]{2,1,0:T(8,128)(2,1)S(1)}, bf16[4,256,128]{2,1,0:T(8,128)(2,1)S(1)}, u32[]{:S(2)}, u32[]{:S(2)}) collective-permute-start(bf16[4,256,128]{2,1,0:T(8,128)(2,1)S(1)} %get-tuple-element.36), channel_id=1, source_target_pairs={{0,4},{4,0},{8,12},{12,8},{16,20},{20,16},{24,28},{28,24},{1,5},{5... | collective-permute-start | bytes 786440 | tf_op jit(solution)/shard_map/ppermute | solution.py:27
  18.0 0.0 copy-done.3
  18.0 0.0 copy-done.6
  18.0 2.5 %token_vectors.1 = (bf16[2,128,512]{2,1,0:T(8,128)(2,1)S(1)}, bf16[2,512,128]{2,1,0:T(8,128)(2,1)S(1)}, bf16[2,128,512]{2,1,0:T(8,128)(2,1)S(1)}, bf16[2,128,512...) custom-call(f32[520,768]{1,0:T(8,128)S(1)} %get-tuple-element.42.ref, ...), custom_call_target="tpu_custom_call" | custom-call | flops 25559040 | bytes 1597440 | tf_op jit(solution)/shard_map/token_vectors/pallas_call | solution.py:367
  20.5 0.9 %collective-permute-done.7.got_ref = bf16[4,256,128]{2,1,0:T(8,128)(2,1)S(1)} collective-permute-done((bf16[4,256,128]{2,1,0:T(8,128)(2,1)S(1)}, bf16[4,256,128]{2,1,0:T(8,128)(2,1)S(1)}, u32[]{:S(2)}, u32[]{:S(2)}) %collective-permute-start.7) | collective-permute-done | bytes 262176 | tf_op jit(solution)/shard_map/ppermute | solution.py:27
  21.4 0.1 halve_sums.3
  21.4 4.1 %collective-permute-start.8 = (bf16[256,128]{1,0:T(8,128)(2,1)S(1)}, bf16[256,128]{1,0:T(8,128)(2,1)S(1)}, u32[]{:S(2)}, u32[]{:S(2)}) collective-permute-start(bf16[256,128]{1,0:T(8,128)(2,1)S(1)} %get-tuple-element.46), channel_id=1, source_target_pairs={{0,24},{4,28},{8,16},{12,20},{16,8},{20,12},{24,0},{28,4},{1,25},{... | collective-permute-start | bytes 196616 | tf_op jit(solution)/shard_map/ppermute | solution.py:27
  25.6 0.0 collective-permute-start.9
  25.6 0.6 %collective-permute-start.10 = (bf16[256,128]{1,0:T(8,128)(2,1)S(1)}, bf16[256,128]{1,0:T(8,128)(2,1)S(1)}, u32[]{:S(2)}, u32[]{:S(2)}) collective-permute-start(bf16[256,128]{1,0:T(8,128)(2,1)S(1)} %get-tuple-element.48), channel_id=1, source_target_pairs={{0,8},{4,12},{8,0},{12,4},{16,24},{20,28},{24,16},{28,20},{1,9},{5... | collective-permute-start | bytes 196616 | tf_op jit(solution)/shard_map/ppermute | solution.py:27
  26.2 0.0 collective-permute-done.3.got_ref
  26.2 0.0 copy-done.2
  26.2 0.1 halve_sums.2
  26.3 4.0 %collective-permute-start.4 = (bf16[256,128]{1,0:T(8,128)(2,1)S(1)}, bf16[256,128]{1,0:T(8,128)(2,1)S(1)}, u32[]{:S(2)}, u32[]{:S(2)}) collective-permute-start(bf16[256,128]{1,0:T(8,128)(2,1)S(1)} %get-tuple-element.38), channel_id=1, source_target_pairs={{0,24},{4,28},{8,16},{12,20},{16,8},{20,12},{24,0},{28,4},{1,25},{... | collective-permute-start | bytes 196616 | tf_op jit(solution)/shard_map/ppermute | solution.py:27
  30.3 0.0 collective-permute-start.5
  30.3 0.0 collective-permute-done.8.refs_1_
  30.3 0.6 %collective-permute-start.6 = (bf16[256,128]{1,0:T(8,128)(2,1)S(1)}, bf16[256,128]{1,0:T(8,128)(2,1)S(1)}, u32[]{:S(2)}, u32[]{:S(2)}) collective-permute-start(bf16[256,128]{1,0:T(8,128)(2,1)S(1)} %get-tuple-element.40), channel_id=1, source_target_pairs={{0,8},{4,12},{8,0},{12,4},{16,24},{20,28},{24,16},{28,20},{1,9},{5... | collective-permute-start | bytes 196616 | tf_op jit(solution)/shard_map/ppermute | solution.py:27
  31.0 1.6 %collective-permute-done.9.refs_2_ = bf16[256,128]{1,0:T(8,128)(2,1)S(1)} collective-permute-done((bf16[256,128]{1,0:T(8,128)(2,1)S(1)}, bf16[256,128]{1,0:T(8,128)(2,1)S(1)}, u32[]{:S(2)}, u32[]{:S(2)}) %collective-permute-start.9) | collective-permute-done | bytes 65568 | tf_op jit(solution)/shard_map/ppermute | solution.py:27
  32.6 0.0 collective-permute-done.10.refs_3_
  32.6 0.0 copy-done.7
  32.6 0.0 copy-start
  32.6 6.4 %ridge_reads.1 = (f32[512,256]{1,0:T(8,128)S(1)}, bf16[512,256]{1,0:T(8,128)(2,1)S(1)}) custom-call(f32[1,2]{1,0:T(1,128)S(1)} %bitcast.7, f32[256,128]{1,0:T(8,128)S(1)} %get-tuple-element.45.refs_0_, bf16[256,128]{1,0:T(8,128)(2,1)S(1)} %collective-permute-done.8.refs_1_, bf16[256,128]{1,0:T(8,128)(2,1)S(1)} %collective-permute-done.9.refs_2_, ...), custom_call_target="tpu_custom_call" | custom-call | flops 6442450944 | bytes 8388608 | tf_op jit(solution)/shard_map/ridge_reads/pallas_call | solution.py:451
  39.0 0.0 collective-permute-done.4.refs_1_
  39.0 0.0 collective-permute-done.5.refs_2_
  39.0 0.0 collective-permute-done.6.refs_3_
  39.0 0.3 cross_reads.1
  39.3 0.1 collective-permute-start.11
  39.4 0.6 %collective-permute-start.12 = (bf16[128,256]{1,0:T(8,128)(2,1)S(1)}, bf16[128,256]{1,0:T(8,128)(2,1)S(1)}, u32[]{:S(2)}, u32[]{:S(2)}) collective-permute-start(bf16[128,256]{1,0:T(8,128)(2,1)S(1)} %get-tuple-element.59), channel_id=1, source_target_pairs={{0,2},{1,3},{2,0},{3,1},{4,6},{5,7},{6,4},{7,5},{8,10},{9,11},{10,... | collective-permute-start | bytes 196616 | tf_op jit(solution)/shard_map/ppermute | solution.py:27
  40.0 1.2 %collective-permute-start.13 = (bf16[128,256]{1,0:T(8,128)(2,1)S(1)}, bf16[128,256]{1,0:T(8,128)(2,1)S(1)}, u32[]{:S(2)}, u32[]{:S(2)}) collective-permute-start(bf16[128,256]{1,0:T(8,128)(2,1)S(1)} %get-tuple-element.60), channel_id=1, source_target_pairs={{0,1},{1,0},{2,3},{3,2},{4,5},{5,4},{6,7},{7,6},{8,9},{9,8},{10,11... | collective-permute-start | bytes 196616 | tf_op jit(solution)/shard_map/ppermute | solution.py:27
  41.2 0.0 copy-done
  41.2 0.2 output_rows.2.start_ref
  41.5 1.7 %collective-permute-done.11.refs_0_ = bf16[128,256]{1,0:T(8,128)(2,1)S(1)} collective-permute-done((bf16[128,256]{1,0:T(8,128)(2,1)S(1)}, bf16[128,256]{1,0:T(8,128)(2,1)S(1)}, u32[]{:S(2)}, u32[]{:S(2)}) %collective-permute-start.11) | collective-permute-done | bytes 65568 | tf_op jit(solution)/shard_map/ppermute | solution.py:27
  43.1 1.2 %collective-permute-done.12.refs_1_ = bf16[128,256]{1,0:T(8,128)(2,1)S(1)} collective-permute-done((bf16[128,256]{1,0:T(8,128)(2,1)S(1)}, bf16[128,256]{1,0:T(8,128)(2,1)S(1)}, u32[]{:S(2)}, u32[]{:S(2)}) %collective-permute-start.12) | collective-permute-done | bytes 65568 | tf_op jit(solution)/shard_map/ppermute | solution.py:27
  44.3 0.0 collective-permute-done.13.refs_2_
  44.3 1.1 %output_rows.3 = bf16[128,1024]{1,0:T(8,128)(2,1)} custom-call(f32[128,1024]{1,0:T(8,128)S(1)} %output_rows.2.start_ref, bf16[1024,1024]{1,0:T(8,128)(2,1)S(1)} %copy-done, bf16[128,256]{1,0:T(8,128)(2,1)S(1)} %collective-permute-done.11.refs_0_, bf16[128,256]{1,0:T(8,128)(2,1)S(1)} %collective-permute-done.12.refs_1_, ...), custom_call_target="tpu_custom_call" | custom-call | flops 201326592 | bytes 2883584 | tf_op jit(solution)/shard_map/output_rows/pallas_call | solution.py:518
  (3 shorter events, 0.0 us)
Async XLA Ops:
  0.0 11.6 %collective-permute-start.1 = (bf16[128,1024]{1,0:T(8,128)(2,1)}, bf16[128,1024]{1,0:T(8,128)(2,1)S(1)}, u32[]{:S(2)}, u32[]{:S(2)}) collective-permute-start(bf16[128,1024]{1,0:T(8,128)(2,1)} %start_ref.1), channel_id=1, source_target_pairs={{0,2},{1,3},{2,0},{3,1},{4,6},{5,7},{6,4},{7,5},{8,10},{9,11},{10,... | collective-permute-start | bytes 786440 | tf_op jit(solution)/shard_map/ppermute | solution.py:27
  2.9 11.0 %collective-permute-start = (bf16[128,1024]{1,0:T(8,128)(2,1)}, bf16[128,1024]{1,0:T(8,128)(2,1)S(1)}, u32[]{:S(2)}, u32[]{:S(2)}) collective-permute-start(bf16[128,1024]{1,0:T(8,128)(2,1)} %start_ref.1), channel_id=1, source_target_pairs={{0,1},{1,0},{2,3},{3,2},{4,5},{5,4},{6,7},{7,6},{8,9},{9,8},{10,11... | collective-permute-start | bytes 786440 | tf_op jit(solution)/shard_map/ppermute | solution.py:27
  4.5 9.2 %copy-start.8 = (bf16[1024,16]{0,1:T(8,128)(2,1)S(1)}, bf16[1024,16]{0,1:T(8,128)(2,1)}, u32[]{:S(2)}) copy-start(bf16[1024,16]{0,1:T(8,128)(2,1)} %param.18) | copy-start | bytes 98308
  4.5 9.4 %copy-start.1 = (bf16[128,1024]{1,0:T(8,128)(2,1)S(1)}, bf16[128,1024]{1,0:T(8,128)(2,1)}, u32[]{:S(2)}) copy-start(bf16[128,1024]{1,0:T(8,128)(2,1)} %start_ref.1) | copy-start | bytes 786436
  4.6 9.4 %copy-start.4 = (bf16[1,3,3072]{2,1,0:T(4,128)(2,1)S(1)}, bf16[1,3,3072]{2,1,0:T(4,128)(2,1)}, u32[]{:S(2)}) copy-start(bf16[1,3,3072]{2,1,0:T(4,128)(2,1)} %refs_7_.1) | copy-start | bytes 55300
  4.6 9.4 %copy-start.5 = (f32[1024]{0:T(1024)S(1)}, f32[1024]{0:T(1024)}, u32[]{:S(2)}) copy-start(f32[1024]{0:T(1024)} %param.16) | copy-start | bytes 12292
  11.6 6.4 %copy-start.3 = (f32[4,3072]{1,0:T(4,128)S(1)}, f32[4,3072]{1,0:T(4,128)}, u32[]{:S(2)}) copy-start(f32[4,3072]{1,0:T(4,128)} %refs_2_.1) | copy-start | bytes 147460
  11.6 6.4 %copy-start.6 = (f32[8]{0:T(128)S(1)}, f32[8]{0:T(128)}, u32[]{:S(2)}) copy-start(f32[8]{0:T(128)} %param.21) | copy-start | bytes 100
  11.6 2.3 %collective-permute-start.2 = (bf16[128,1024]{1,0:T(8,128)(2,1)S(1)}, bf16[128,1024]{1,0:T(8,128)(2,1)S(1)}, u32[]{:S(2)}, u32[]{:S(2)}) collective-permute-start(bf16[128,1024]{1,0:T(8,128)(2,1)S(1)} %hold.1.refs_2_), channel_id=1, source_target_pairs={{0,1},{1,0},{2,3},{3,2},{4,5},{5,4},{6,7},{7,6},{8,9},{9,8},{10,11... | collective-permute-start | bytes 786440 | tf_op jit(solution)/shard_map/ppermute | solution.py:27
  12.2 9.2 %collective-permute-start.7 = (bf16[4,256,128]{2,1,0:T(8,128)(2,1)S(1)}, bf16[4,256,128]{2,1,0:T(8,128)(2,1)S(1)}, u32[]{:S(2)}, u32[]{:S(2)}) collective-permute-start(bf16[4,256,128]{2,1,0:T(8,128)(2,1)S(1)} %get-tuple-element.41), channel_id=1, source_target_pairs={{0,4},{4,0},{8,12},{12,8},{16,20},{20,16},{24,28},{28,24},{1,5},{5... | collective-permute-start | bytes 786440 | tf_op jit(solution)/shard_map/ppermute | solution.py:27
  14.0 12.2 %copy-start.2 = (bf16[4,256,128]{2,1,0:T(8,128)(2,1)S(1)}, bf16[4,256,128]{2,1,0:T(8,128)(2,1)}, u32[]{:S(2)}) copy-start(bf16[4,256,128]{2,1,0:T(8,128)(2,1)} %get-tuple-element.33.keep_ref) | copy-start | bytes 786436
  14.0 18.6 %copy-start.7 = (f32[2]{0:T(128)S(1)}, f32[2]{0:T(128)}, u32[]{:S(2)}) copy-start(f32[2]{0:T(128)} %param.22) | copy-start | bytes 28
  16.9 9.3 %collective-permute-start.3 = (bf16[4,256,128]{2,1,0:T(8,128)(2,1)S(1)}, bf16[4,256,128]{2,1,0:T(8,128)(2,1)S(1)}, u32[]{:S(2)}, u32[]{:S(2)}) collective-permute-start(bf16[4,256,128]{2,1,0:T(8,128)(2,1)S(1)} %get-tuple-element.36), channel_id=1, source_target_pairs={{0,4},{4,0},{8,12},{12,8},{16,20},{20,16},{24,28},{28,24},{1,5},{5... | collective-permute-start | bytes 786440 | tf_op jit(solution)/shard_map/ppermute | solution.py:27
  21.4 8.9 %collective-permute-start.8 = (bf16[256,128]{1,0:T(8,128)(2,1)S(1)}, bf16[256,128]{1,0:T(8,128)(2,1)S(1)}, u32[]{:S(2)}, u32[]{:S(2)}) collective-permute-start(bf16[256,128]{1,0:T(8,128)(2,1)S(1)} %get-tuple-element.46), channel_id=1, source_target_pairs={{0,24},{4,28},{8,16},{12,20},{16,8},{20,12},{24,0},{28,4},{1,25},{... | collective-permute-start | bytes 196616 | tf_op jit(solution)/shard_map/ppermute | solution.py:27
  25.6 7.0 %collective-permute-start.9 = (bf16[256,128]{1,0:T(8,128)(2,1)S(1)}, bf16[256,128]{1,0:T(8,128)(2,1)S(1)}, u32[]{:S(2)}, u32[]{:S(2)}) collective-permute-start(bf16[256,128]{1,0:T(8,128)(2,1)S(1)} %get-tuple-element.47), channel_id=1, source_target_pairs={{0,16},{4,20},{8,24},{12,28},{16,0},{20,4},{24,8},{28,12},{1,17},{... | collective-permute-start | bytes 196616 | tf_op jit(solution)/shard_map/ppermute | solution.py:27
  25.6 7.0 %collective-permute-start.10 = (bf16[256,128]{1,0:T(8,128)(2,1)S(1)}, bf16[256,128]{1,0:T(8,128)(2,1)S(1)}, u32[]{:S(2)}, u32[]{:S(2)}) collective-permute-start(bf16[256,128]{1,0:T(8,128)(2,1)S(1)} %get-tuple-element.48), channel_id=1, source_target_pairs={{0,8},{4,12},{8,0},{12,4},{16,24},{20,28},{24,16},{28,20},{1,9},{5... | collective-permute-start | bytes 196616 | tf_op jit(solution)/shard_map/ppermute | solution.py:27
  26.3 12.7 %collective-permute-start.4 = (bf16[256,128]{1,0:T(8,128)(2,1)S(1)}, bf16[256,128]{1,0:T(8,128)(2,1)S(1)}, u32[]{:S(2)}, u32[]{:S(2)}) collective-permute-start(bf16[256,128]{1,0:T(8,128)(2,1)S(1)} %get-tuple-element.38), channel_id=1, source_target_pairs={{0,24},{4,28},{8,16},{12,20},{16,8},{20,12},{24,0},{28,4},{1,25},{... | collective-permute-start | bytes 196616 | tf_op jit(solution)/shard_map/ppermute | solution.py:27
  30.3 8.7 %collective-permute-start.5 = (bf16[256,128]{1,0:T(8,128)(2,1)S(1)}, bf16[256,128]{1,0:T(8,128)(2,1)S(1)}, u32[]{:S(2)}, u32[]{:S(2)}) collective-permute-start(bf16[256,128]{1,0:T(8,128)(2,1)S(1)} %get-tuple-element.39), channel_id=1, source_target_pairs={{0,16},{4,20},{8,24},{12,28},{16,0},{20,4},{24,8},{28,12},{1,17},{... | collective-permute-start | bytes 196616 | tf_op jit(solution)/shard_map/ppermute | solution.py:27
  30.3 8.7 %collective-permute-start.6 = (bf16[256,128]{1,0:T(8,128)(2,1)S(1)}, bf16[256,128]{1,0:T(8,128)(2,1)S(1)}, u32[]{:S(2)}, u32[]{:S(2)}) collective-permute-start(bf16[256,128]{1,0:T(8,128)(2,1)S(1)} %get-tuple-element.40), channel_id=1, source_target_pairs={{0,8},{4,12},{8,0},{12,4},{16,24},{20,28},{24,16},{28,20},{1,9},{5... | collective-permute-start | bytes 196616 | tf_op jit(solution)/shard_map/ppermute | solution.py:27
  32.6 8.6 %copy-start = (bf16[1024,1024]{1,0:T(8,128)(2,1)S(1)}, bf16[1024,1024]{1,0:T(8,128)(2,1)}, u32[]{:S(2)}) copy-start(bf16[1024,1024]{1,0:T(8,128)(2,1)} %w_ref.3) | copy-start | bytes 6291460
  39.3 3.8 %collective-permute-start.11 = (bf16[128,256]{1,0:T(8,128)(2,1)S(1)}, bf16[128,256]{1,0:T(8,128)(2,1)S(1)}, u32[]{:S(2)}, u32[]{:S(2)}) collective-permute-start(bf16[128,256]{1,0:T(8,128)(2,1)S(1)} %get-tuple-element.58), channel_id=1, source_target_pairs={{0,3},{1,2},{2,1},{3,0},{4,7},{5,6},{6,5},{7,4},{8,11},{9,10},{10,... | collective-permute-start | bytes 196616 | tf_op jit(solution)/shard_map/ppermute | solution.py:27
  39.4 5.0 %collective-permute-start.12 = (bf16[128,256]{1,0:T(8,128)(2,1)S(1)}, bf16[128,256]{1,0:T(8,128)(2,1)S(1)}, u32[]{:S(2)}, u32[]{:S(2)}) collective-permute-start(bf16[128,256]{1,0:T(8,128)(2,1)S(1)} %get-tuple-element.59), channel_id=1, source_target_pairs={{0,2},{1,3},{2,0},{3,1},{4,6},{5,7},{6,4},{7,5},{8,10},{9,11},{10,... | collective-permute-start | bytes 196616 | tf_op jit(solution)/shard_map/ppermute | solution.py:27
  40.0 4.4 %collective-permute-start.13 = (bf16[128,256]{1,0:T(8,128)(2,1)S(1)}, bf16[128,256]{1,0:T(8,128)(2,1)S(1)}, u32[]{:S(2)}, u32[]{:S(2)}) collective-permute-start(bf16[128,256]{1,0:T(8,128)(2,1)S(1)} %get-tuple-element.60), channel_id=1, source_target_pairs={{0,1},{1,0},{2,3},{3,2},{4,5},{5,4},{6,7},{7,6},{8,9},{9,8},{10,11... | collective-permute-start | bytes 196616 | tf_op jit(solution)/shard_map/ppermute | solution.py:27

commit v11 on v10

--- a/solution.py
+++ b/solution.py
@@ -63,21 +63,24 @@
     )
 
 
-def sums_kernel(heads, owners, slot_bits, code_hbm, pack_hbm, keys_hbm, values_hbm, prompt_hbm,
+def sums_kernel(heads, owners, slot_bits, code_hbm, length_hbm, pick_hbm, keys_hbm, values_hbm, prompt_hbm,
                 send_gram, send_cross, keep_gram, keep_cross,
-                acc_ref, keys_ref, values_ref, stored_ref, code_ref, pack_ref, list_ref,
+                acc_ref, keys_ref, values_ref, stored_ref, code_ref, length_ref, pick_ref, hit_ref, list_ref,
                 key_sem, value_sem, small_sem):
     pool, rows = keys_hbm.shape[0], keys_hbm.shape[1]
     mine = lax.axis_index("grp")
     load_code = pltpu.make_async_copy(code_hbm, code_ref, small_sem.at[0])
     load_prompt = pltpu.make_async_copy(prompt_hbm, stored_ref, small_sem.at[1])
-    load_pack = pltpu.make_async_copy(pack_hbm, pack_ref, small_sem.at[2])
+    load_length = pltpu.make_async_copy(length_hbm, length_ref, small_sem.at[2])
+    load_pick = pltpu.make_async_copy(pick_hbm, pick_ref, small_sem.at[3])
     load_code.start()
-    load_pack.start()
+    load_length.start()
+    load_pick.start()
     load_prompt.start()
     acc_ref[...] = jnp.zeros_like(acc_ref)
     load_code.wait()
-    load_pack.wait()
+    load_length.wait()
+    load_pick.wait()
 
     def load(item):
         page = list_ref[item] & 0xFFFF
@@ -98,8 +101,8 @@
             page = chunk * wide + i
             code = code_ref[page]
             owner = code >> slot_bits
-            length = pack_ref[owner] & 0xFFFF
-            live = length - ((code & ((1 << slot_bits) - 1)) * PAGE)
+            hit_ref[owner] = pick_ref[page]
+            live = length_ref[page] - ((code & ((1 << slot_bits) - 1)) * PAGE)
             list_ref[count] = (owner << 24) | (jnp.minimum(live, PAGE) << 16) | page
             count = count + (live > 0).astype(jnp.int32)
         return count
@@ -146,7 +149,7 @@
     def add_prompt(owner, carry):
         for slot in range(stored):
 
-            @pl.when((pack_ref[owner] >> 16) == mine * stored + slot)
+            @pl.when(hit_ref[owner] == mine * stored + slot)
             def _():
                 for head in range(heads):
                     at = slice(head * HDIM, (head + 1) * HDIM)
@@ -165,26 +168,28 @@
         keep_cross[pair] = acc_ref[here, :, HDIM:].astype(BF16)
 
 
-def page_sums(code, pack, slot_bits, keys, values, prompt_state, owners):
+def page_sums(maps, slot_bits, keys, values, prompt_state, owners):
     pool, rows, _ = keys.shape
     heads = prompt_state.shape[1]
     half = (owners // 2, heads * HDIM, HDIM)
     items = pool + 4
     return pl.pallas_call(
         functools.partial(sums_kernel, heads, owners, slot_bits),
-        in_specs=[pl.BlockSpec(memory_space=pl.ANY)] * 5,
+        in_specs=[pl.BlockSpec(memory_space=pl.ANY)] * 6,
         out_specs=[pl.BlockSpec(memory_space=pltpu.VMEM)] * 4,
         scratch_shapes=[
             pltpu.VMEM((owners + 1, heads * HDIM, 2 * HDIM), F32),
             pltpu.VMEM((items, rows, HDIM), BF16),
             pltpu.VMEM((items, rows, HDIM), BF16),
             pltpu.VMEM(prompt_state.shape, F32),
-            pltpu.SMEM(code.shape, jnp.int32),
-            pltpu.SMEM(pack.shape, jnp.int32),
+            pltpu.SMEM((pool,), jnp.int32),
+            pltpu.SMEM((pool,), jnp.int32),
+            pltpu.SMEM((pool,), jnp.int32),
+            pltpu.SMEM((owners,), jnp.int32),
             pltpu.SMEM((items,), jnp.int32),
             pltpu.SemaphoreType.DMA((items,)),
             pltpu.SemaphoreType.DMA((items,)),
-            pltpu.SemaphoreType.DMA((3,)),
+            pltpu.SemaphoreType.DMA((4,)),
         ],
         out_shape=[jax.ShapeDtypeStruct(half, BF16)] * 4,
         compiler_params=pltpu.CompilerParams(vmem_limit_bytes=PAGE_VMEM * 2**20),
@@ -194,7 +199,7 @@
             transcendentals=0,
         ),
         name="page_sums",
-    )(code, pack, keys, values, prompt_state)
+    )(*maps, keys, values, prompt_state)
 
 
 def halve_kernel(keep_ref, got_ref, *refs):
@@ -558,12 +563,13 @@
     slots = page_table.shape[1]
     slot_bits = slots.bit_length() - 1
     assert slots == 1 << slot_bits
-    tag = jnp.arange(owners * slots, dtype=jnp.int32).reshape(owners, slots)
-    pack = cache_lengths | (group_prompt << 16)
+    tag = jnp.arange(owners * slots, dtype=jnp.int32).reshape(owners, slots, 1)
     ids = lax.axis_index("grp").astype(jnp.int32) * pool + jnp.arange(pool, dtype=jnp.int32)
-    code = jnp.sum(
-        jnp.where(page_table[:, :, None] == ids, tag[:, :, None], 0), axis=(0, 1), dtype=jnp.int32
-    )
+    match = page_table[:, :, None] == ids
+    maps = [
+        jnp.sum(jnp.where(match, what, 0), axis=(0, 1), dtype=jnp.int32)
+        for what in (tag, cache_lengths[:, None, None], group_prompt[:, None, None])
+    ]
     keys = cache_keys.reshape(pool, page * heads, HDIM)
     values = cache_values.reshape(pool, page * heads, HDIM)
 
@@ -572,7 +578,7 @@
         return [parts[0]] + sent
 
     send_gram, send_cross, keep_gram, keep_cross = page_sums(
-        code, pack, slot_bits, keys, values, prompt_state, owners
+        maps, slot_bits, keys, values, prompt_state, owners
     )
     got_gram = swap(send_gram, "grp", 1)
     for bit in bits[1:]:

time: 46 us -> 44.8 us (0.974)
  other arithmetic: 1.59 us -> 0.93 us
  waiting for transfers between devices: 5.4 us -> 4.89 us
    or x1 -> x0, other arithmetic: 0.68 us -> none  [shards(): pack = cache_lengths | group_prompt << 16]
    ppermute x14, waiting for transfers between devices: 5.4 us -> 4.89 us  [swap(): return lax.ppermute(block, axis, [(i, i ^ distance) for i in range(size)])]
  transfers between devices with their start and end apart: 14 -> 14, of which waited for: 4 -> 4; matrix products, arithmetic and copies ran while one was open for 4% -> 2% of each run, Pallas kernels for 42% -> 43%
where the time goes in v11:
time: 44.8 us; the launch traced here: 44.5 us
  Pallas kernels  20.7 us (46%)
  starting transfers between devices  17.6 us (39%)
  waiting for transfers between devices  4.89 us (11%)
  other arithmetic  0.93 us (2%)
    ppermute x14, starting transfers between devices, swap(): return lax.ppermute(block, axis, [(i, i ^ distance) for i in range(size)])  17.6 us
    pallas_call x1, Pallas kernels, page_sums(): pl.pallas_call(functools.partial(sums_kernel, heads, owners, slot_bits),...  7.07 us
    pallas_call x1, Pallas kernels, ridge_reads(): pl.pallas_call(functools.partial(read_kernel, heads, len(grams)), in_spec...  6.41 us
    ppermute x14, waiting for transfers between devices, swap(): return lax.ppermute(block, axis, [(i, i ^ distance) for i in range(size)])  4.89 us
    pallas_call x1, Pallas kernels, project(): pl.pallas_call(functools.partial(project_kernel, heads), in_specs=[whole]...  2.96 us
    pallas_call x1, Pallas kernels, token_vectors(): pl.pallas_call(functools.partial(token_kernel, heads), in_specs=[whole] *...  2.49 us
    pallas_call x2, Pallas kernels, output_rows(): pl.pallas_call(functools.partial(output_kernel, distances), in_specs=[who...  1.33 us
    reduce_sum x1, other arithmetic, shards(): jnp.sum(jnp.where(match, what, 0), axis=(0, 1), dtype=jnp.int32)  0.92 us
  transfers between devices with their start and end apart: 14, of which 4 were waited for; matrix products, arithmetic and copies ran while one was open for 2% of the time, Pallas kernels for 43%

profile of v11, /device:TPU:0, one launch (start us, length us, event | category | flops | bytes accessed | tf_op | source)
XLA Modules:
  0.0 44.5 jit_solution(9124333651383815075)
XLA Ops:
  0.0 2.9 %collective-permute-start.1 = (bf16[128,1024]{1,0:T(8,128)(2,1)}, bf16[128,1024]{1,0:T(8,128)(2,1)S(1)}, u32[]{:S(2)}, u32[]{:S(2)}) collective-permute-start(bf16[128,1024]{1,0:T(8,128)(2,1)} %start_ref.1), channel_id=1, source_target_pairs={{0,2},{1,3},{2,0},{3,1},{4,6},{5,7},{6,4},{7,5},{8,10},{9,11},{10,... | collective-permute-start | bytes 786440 | tf_op jit(solution)/shard_map/ppermute | solution.py:27
  2.9 0.0 collective-permute-start
  3.0 0.9 %fusion.2 = (s32[64]{0:T(128)S(1)}, s32[64]{0:T(128)S(1)}, s32[64]{0:T(128)S(1)}) fusion(s32[8]{0:T(128)} %param.28, s32[64]{0:T(128)S(1)} %iota_add_fusion, s32[8,64]{1,0:T(8,128)} %param.26, s32[8]{0:T(128)} %param.27, s32[8,64]{1,0:T(8,128)S(1)} %multiply_add_fusion), kind=kLoop, calls=%fused_computation.5 | loop fusion | flops 229184 | bytes 5184 | tf_op jit(solution)/shard_map/reduce_sum | solution.py:570
  3.9 0.0 copy-start.8
  3.9 0.0 copy-start.1
  3.9 0.0 copy-start.4
  3.9 0.0 copy-start.5
  3.9 7.1 %page_sums.1 = (bf16[4,256,128]{2,1,0:T(8,128)(2,1)S(1)}, bf16[4,256,128]{2,1,0:T(8,128)(2,1)S(1)}, bf16[4,256,128]{2,1,0:T(8,128)(2,1)S(1)}, bf16[4,256,128]{2,1,0:T(8,128)(2,1)}) custom-call(s32[64]{0:T(128)S(1)} %get-tuple-element.63.code_hbm, s32[64]{0:T(128)S(1)} %get-tuple-element.62.length_hbm, s32[64]{0:T(128)S(1)} %get-tuple-element.61.pick_hbm, ...), custom_call_target="tpu_custom_call" | custom-call | flops 4294967296 | bytes 8388608 | tf_op jit(solution)/shard_map/page_sums/pallas_call | solution.py:176
  11.0 0.0 collective-permute-done.1.refs_0_
  11.0 0.0 copy-start.3
  11.0 0.0 copy-start.6
  11.0 0.6 %collective-permute-start.2 = (bf16[128,1024]{1,0:T(8,128)(2,1)S(1)}, bf16[128,1024]{1,0:T(8,128)(2,1)S(1)}, u32[]{:S(2)}, u32[]{:S(2)}) collective-permute-start(bf16[128,1024]{1,0:T(8,128)(2,1)S(1)} %hold.1.refs_2_), channel_id=1, source_target_pairs={{0,1},{1,0},{2,3},{3,2},{4,5},{5,4},{6,7},{7,6},{8,9},{9,8},{10,11... | collective-permute-start | bytes 786440 | tf_op jit(solution)/shard_map/ppermute | solution.py:27
  11.6 1.6 %collective-permute-start.7 = (bf16[4,256,128]{2,1,0:T(8,128)(2,1)S(1)}, bf16[4,256,128]{2,1,0:T(8,128)(2,1)S(1)}, u32[]{:S(2)}, u32[]{:S(2)}) collective-permute-start(bf16[4,256,128]{2,1,0:T(8,128)(2,1)S(1)} %get-tuple-element.41), channel_id=1, source_target_pairs={{0,4},{4,0},{8,12},{12,8},{16,20},{20,16},{24,28},{28,24},{1,5},{5... | collective-permute-start | bytes 786440 | tf_op jit(solution)/shard_map/ppermute | solution.py:27
  13.2 0.0 copy-done.8
  13.2 0.2 copy.19.refs_6_
  13.4 0.0 collective-permute-done.refs_1_
  13.4 0.0 collective-permute-done.2.refs_3_
  13.4 0.0 copy-done.1
  13.4 0.0 copy-done.4
  13.5 0.0 copy-done.5
  13.5 0.0 copy-start.2
  13.5 0.0 copy-start.7
  13.5 3.0 %project.1 = (bf16[4,256,128]{2,1,0:T(8,128)(2,1)S(1)}, f32[520,768]{1,0:T(8,128)S(1)}, f32[512,128]{1,0:T(8,128)S(1)}) custom-call(bf16[128,1024]{1,0:T(8,128)(2,1)S(1)} %copy-done.1, bf16[128,1024]{1,0:T(8,128)(2,1)S(1)} %collective-permute-done.refs_1_, bf16[128,1024]{1,0:T(8,128)(2,1)S(1)} %hold.1.refs_2_, ...), custom_call_target="tpu_custom_call", output_to_operand_aliasing={{0}: (8, {})} | custom-call | flops 805306368 | bytes 4194304 | tf_op jit(solution)/shard_map/project/pallas_call | solution.py:265
  16.5 1.0 %collective-permute-start.3 = (bf16[4,256,128]{2,1,0:T(8,128)(2,1)S(1)}, bf16[4,256,128]{2,1,0:T(8,128)(2,1)S(1)}, u32[]{:S(2)}, u32[]{:S(2)}) collective-permute-start(bf16[4,256,128]{2,1,0:T(8,128)(2,1)S(1)} %get-tuple-element.36), channel_id=1, source_target_pairs={{0,4},{4,0},{8,12},{12,8},{16,20},{20,16},{24,28},{28,24},{1,5},{5... | collective-permute-start | bytes 786440 | tf_op jit(solution)/shard_map/ppermute | solution.py:27
  17.5 0.0 copy-done.3
  17.5 0.0 copy-done.6
  17.5 2.5 %token_vectors.1 = (bf16[2,128,512]{2,1,0:T(8,128)(2,1)S(1)}, bf16[2,512,128]{2,1,0:T(8,128)(2,1)S(1)}, bf16[2,128,512]{2,1,0:T(8,128)(2,1)S(1)}, bf16[2,128,512...) custom-call(f32[520,768]{1,0:T(8,128)S(1)} %get-tuple-element.42.ref, ...), custom_call_target="tpu_custom_call" | custom-call | flops 25559040 | bytes 1597440 | tf_op jit(solution)/shard_map/token_vectors/pallas_call | solution.py:372
  20.0 0.8 %collective-permute-done.7.got_ref = bf16[4,256,128]{2,1,0:T(8,128)(2,1)S(1)} collective-permute-done((bf16[4,256,128]{2,1,0:T(8,128)(2,1)S(1)}, bf16[4,256,128]{2,1,0:T(8,128)(2,1)S(1)}, u32[]{:S(2)}, u32[]{:S(2)}) %collective-permute-start.7) | collective-permute-done | bytes 262176 | tf_op jit(solution)/shard_map/ppermute | solution.py:27
  20.8 0.1 halve_sums.3
  20.8 4.2 %collective-permute-start.8 = (bf16[256,128]{1,0:T(8,128)(2,1)S(1)}, bf16[256,128]{1,0:T(8,128)(2,1)S(1)}, u32[]{:S(2)}, u32[]{:S(2)}) collective-permute-start(bf16[256,128]{1,0:T(8,128)(2,1)S(1)} %get-tuple-element.46), channel_id=1, source_target_pairs={{0,24},{4,28},{8,16},{12,20},{16,8},{20,12},{24,0},{28,4},{1,25},{... | collective-permute-start | bytes 196616 | tf_op jit(solution)/shard_map/ppermute | solution.py:27
  25.1 0.0 collective-permute-start.9
  25.1 0.6 %collective-permute-start.10 = (bf16[256,128]{1,0:T(8,128)(2,1)S(1)}, bf16[256,128]{1,0:T(8,128)(2,1)S(1)}, u32[]{:S(2)}, u32[]{:S(2)}) collective-permute-start(bf16[256,128]{1,0:T(8,128)(2,1)S(1)} %get-tuple-element.48), channel_id=1, source_target_pairs={{0,8},{4,12},{8,0},{12,4},{16,24},{20,28},{24,16},{28,20},{1,9},{5... | collective-permute-start | bytes 196616 | tf_op jit(solution)/shard_map/ppermute | solution.py:27
  25.7 0.0 collective-permute-done.3.got_ref
  25.7 0.0 copy-done.2
  25.7 0.1 halve_sums.2
  25.8 4.0 %collective-permute-start.4 = (bf16[256,128]{1,0:T(8,128)(2,1)S(1)}, bf16[256,128]{1,0:T(8,128)(2,1)S(1)}, u32[]{:S(2)}, u32[]{:S(2)}) collective-permute-start(bf16[256,128]{1,0:T(8,128)(2,1)S(1)} %get-tuple-element.38), channel_id=1, source_target_pairs={{0,24},{4,28},{8,16},{12,20},{16,8},{20,12},{24,0},{28,4},{1,25},{... | collective-permute-start | bytes 196616 | tf_op jit(solution)/shard_map/ppermute | solution.py:27
  29.8 0.0 collective-permute-start.5
  29.8 0.0 collective-permute-done.8.refs_1_
  29.8 0.6 %collective-permute-start.6 = (bf16[256,128]{1,0:T(8,128)(2,1)S(1)}, bf16[256,128]{1,0:T(8,128)(2,1)S(1)}, u32[]{:S(2)}, u32[]{:S(2)}) collective-permute-start(bf16[256,128]{1,0:T(8,128)(2,1)S(1)} %get-tuple-element.40), channel_id=1, source_target_pairs={{0,8},{4,12},{8,0},{12,4},{16,24},{20,28},{24,16},{28,20},{1,9},{5... | collective-permute-start | bytes 196616 | tf_op jit(solution)/shard_map/ppermute | solution.py:27
  30.5 1.2 %collective-permute-done.9.refs_2_ = bf16[256,128]{1,0:T(8,128)(2,1)S(1)} collective-permute-done((bf16[256,128]{1,0:T(8,128)(2,1)S(1)}, bf16[256,128]{1,0:T(8,128)(2,1)S(1)}, u32[]{:S(2)}, u32[]{:S(2)}) %collective-permute-start.9) | collective-permute-done | bytes 65568 | tf_op jit(solution)/shard_map/ppermute | solution.py:27
  31.6 0.0 collective-permute-done.10.refs_3_
  31.6 0.0 copy-done.7
  31.6 0.0 copy-start
  31.6 6.4 %ridge_reads.1 = (f32[512,256]{1,0:T(8,128)S(1)}, bf16[512,256]{1,0:T(8,128)(2,1)S(1)}) custom-call(f32[1,2]{1,0:T(1,128)S(1)} %bitcast.7, f32[256,128]{1,0:T(8,128)S(1)} %get-tuple-element.45.refs_0_, bf16[256,128]{1,0:T(8,128)(2,1)S(1)} %collective-permute-done.8.refs_1_, bf16[256,128]{1,0:T(8,128)(2,1)S(1)} %collective-permute-done.9.refs_2_, ...), custom_call_target="tpu_custom_call" | custom-call | flops 6442450944 | bytes 8388608 | tf_op jit(solution)/shard_map/ridge_reads/pallas_call | solution.py:456
  38.1 0.0 collective-permute-done.4.refs_1_
  38.1 0.0 collective-permute-done.5.refs_2_
  38.1 0.0 collective-permute-done.6.refs_3_
  38.1 0.3 cross_reads.1
  38.4 0.1 collective-permute-start.11
  38.4 0.6 %collective-permute-start.12 = (bf16[128,256]{1,0:T(8,128)(2,1)S(1)}, bf16[128,256]{1,0:T(8,128)(2,1)S(1)}, u32[]{:S(2)}, u32[]{:S(2)}) collective-permute-start(bf16[128,256]{1,0:T(8,128)(2,1)S(1)} %get-tuple-element.59), channel_id=1, source_target_pairs={{0,2},{1,3},{2,0},{3,1},{4,6},{5,7},{6,4},{7,5},{8,10},{9,11},{10,... | collective-permute-start | bytes 196616 | tf_op jit(solution)/shard_map/ppermute | solution.py:27
  39.0 1.3 %collective-permute-start.13 = (bf16[128,256]{1,0:T(8,128)(2,1)S(1)}, bf16[128,256]{1,0:T(8,128)(2,1)S(1)}, u32[]{:S(2)}, u32[]{:S(2)}) collective-permute-start(bf16[128,256]{1,0:T(8,128)(2,1)S(1)} %get-tuple-element.60), channel_id=1, source_target_pairs={{0,1},{1,0},{2,3},{3,2},{4,5},{5,4},{6,7},{7,6},{8,9},{9,8},{10,11... | collective-permute-start | bytes 196616 | tf_op jit(solution)/shard_map/ppermute | solution.py:27
  40.3 0.0 copy-done
  40.3 0.2 output_rows.2.start_ref
  40.5 1.7 %collective-permute-done.11.refs_0_ = bf16[128,256]{1,0:T(8,128)(2,1)S(1)} collective-permute-done((bf16[128,256]{1,0:T(8,128)(2,1)S(1)}, bf16[128,256]{1,0:T(8,128)(2,1)S(1)}, u32[]{:S(2)}, u32[]{:S(2)}) %collective-permute-start.11) | collective-permute-done | bytes 65568 | tf_op jit(solution)/shard_map/ppermute | solution.py:27
  42.2 1.2 %collective-permute-done.12.refs_1_ = bf16[128,256]{1,0:T(8,128)(2,1)S(1)} collective-permute-done((bf16[128,256]{1,0:T(8,128)(2,1)S(1)}, bf16[128,256]{1,0:T(8,128)(2,1)S(1)}, u32[]{:S(2)}, u32[]{:S(2)}) %collective-permute-start.12) | collective-permute-done | bytes 65568 | tf_op jit(solution)/shard_map/ppermute | solution.py:27
  43.4 0.0 collective-permute-done.13.refs_2_
  43.4 1.1 %output_rows.3 = bf16[128,1024]{1,0:T(8,128)(2,1)} custom-call(f32[128,1024]{1,0:T(8,128)S(1)} %output_rows.2.start_ref, bf16[1024,1024]{1,0:T(8,128)(2,1)S(1)} %copy-done, bf16[128,256]{1,0:T(8,128)(2,1)S(1)} %collective-permute-done.11.refs_0_, bf16[128,256]{1,0:T(8,128)(2,1)S(1)} %collective-permute-done.12.refs_1_, ...), custom_call_target="tpu_custom_call" | custom-call | flops 201326592 | bytes 2883584 | tf_op jit(solution)/shard_map/output_rows/pallas_call | solution.py:523
  (3 shorter events, 0.0 us)
Async XLA Ops:
  0.0 11.0 %collective-permute-start.1 = (bf16[128,1024]{1,0:T(8,128)(2,1)}, bf16[128,1024]{1,0:T(8,128)(2,1)S(1)}, u32[]{:S(2)}, u32[]{:S(2)}) collective-permute-start(bf16[128,1024]{1,0:T(8,128)(2,1)} %start_ref.1), channel_id=1, source_target_pairs={{0,2},{1,3},{2,0},{3,1},{4,6},{5,7},{6,4},{7,5},{8,10},{9,11},{10,... | collective-permute-start | bytes 786440 | tf_op jit(solution)/shard_map/ppermute | solution.py:27
  2.9 10.5 %collective-permute-start = (bf16[128,1024]{1,0:T(8,128)(2,1)}, bf16[128,1024]{1,0:T(8,128)(2,1)S(1)}, u32[]{:S(2)}, u32[]{:S(2)}) collective-permute-start(bf16[128,1024]{1,0:T(8,128)(2,1)} %start_ref.1), channel_id=1, source_target_pairs={{0,1},{1,0},{2,3},{3,2},{4,5},{5,4},{6,7},{7,6},{8,9},{9,8},{10,11... | collective-permute-start | bytes 786440 | tf_op jit(solution)/shard_map/ppermute | solution.py:27
  3.9 9.4 %copy-start.8 = (bf16[1024,16]{0,1:T(8,128)(2,1)S(1)}, bf16[1024,16]{0,1:T(8,128)(2,1)}, u32[]{:S(2)}) copy-start(bf16[1024,16]{0,1:T(8,128)(2,1)} %param.18) | copy-start | bytes 98308
  3.9 9.5 %copy-start.1 = (bf16[128,1024]{1,0:T(8,128)(2,1)S(1)}, bf16[128,1024]{1,0:T(8,128)(2,1)}, u32[]{:S(2)}) copy-start(bf16[128,1024]{1,0:T(8,128)(2,1)} %start_ref.1) | copy-start | bytes 786436
  3.9 9.5 %copy-start.4 = (bf16[1,3,3072]{2,1,0:T(4,128)(2,1)S(1)}, bf16[1,3,3072]{2,1,0:T(4,128)(2,1)}, u32[]{:S(2)}) copy-start(bf16[1,3,3072]{2,1,0:T(4,128)(2,1)} %refs_7_.1) | copy-start | bytes 55300
  3.9 9.5 %copy-start.5 = (f32[1024]{0:T(1024)S(1)}, f32[1024]{0:T(1024)}, u32[]{:S(2)}) copy-start(f32[1024]{0:T(1024)} %param.16) | copy-start | bytes 12292
  11.0 6.5 %copy-start.3 = (f32[4,3072]{1,0:T(4,128)S(1)}, f32[4,3072]{1,0:T(4,128)}, u32[]{:S(2)}) copy-start(f32[4,3072]{1,0:T(4,128)} %refs_2_.1) | copy-start | bytes 147460
  11.0 6.5 %copy-start.6 = (f32[8]{0:T(128)S(1)}, f32[8]{0:T(128)}, u32[]{:S(2)}) copy-start(f32[8]{0:T(128)} %param.21) | copy-start | bytes 100
  11.0 2.4 %collective-permute-start.2 = (bf16[128,1024]{1,0:T(8,128)(2,1)S(1)}, bf16[128,1024]{1,0:T(8,128)(2,1)S(1)}, u32[]{:S(2)}, u32[]{:S(2)}) collective-permute-start(bf16[128,1024]{1,0:T(8,128)(2,1)S(1)} %hold.1.refs_2_), channel_id=1, source_target_pairs={{0,1},{1,0},{2,3},{3,2},{4,5},{5,4},{6,7},{7,6},{8,9},{9,8},{10,11... | collective-permute-start | bytes 786440 | tf_op jit(solution)/shard_map/ppermute | solution.py:27
  11.6 9.2 %collective-permute-start.7 = (bf16[4,256,128]{2,1,0:T(8,128)(2,1)S(1)}, bf16[4,256,128]{2,1,0:T(8,128)(2,1)S(1)}, u32[]{:S(2)}, u32[]{:S(2)}) collective-permute-start(bf16[4,256,128]{2,1,0:T(8,128)(2,1)S(1)} %get-tuple-element.41), channel_id=1, source_target_pairs={{0,4},{4,0},{8,12},{12,8},{16,20},{20,16},{24,28},{28,24},{1,5},{5... | collective-permute-start | bytes 786440 | tf_op jit(solution)/shard_map/ppermute | solution.py:27
  13.5 12.2 %copy-start.2 = (bf16[4,256,128]{2,1,0:T(8,128)(2,1)S(1)}, bf16[4,256,128]{2,1,0:T(8,128)(2,1)}, u32[]{:S(2)}) copy-start(bf16[4,256,128]{2,1,0:T(8,128)(2,1)} %get-tuple-element.33.keep_ref) | copy-start | bytes 786436
  13.5 18.2 %copy-start.7 = (f32[2]{0:T(128)S(1)}, f32[2]{0:T(128)}, u32[]{:S(2)}) copy-start(f32[2]{0:T(128)} %param.22) | copy-start | bytes 28
  16.5 9.3 %collective-permute-start.3 = (bf16[4,256,128]{2,1,0:T(8,128)(2,1)S(1)}, bf16[4,256,128]{2,1,0:T(8,128)(2,1)S(1)}, u32[]{:S(2)}, u32[]{:S(2)}) collective-permute-start(bf16[4,256,128]{2,1,0:T(8,128)(2,1)S(1)} %get-tuple-element.36), channel_id=1, source_target_pairs={{0,4},{4,0},{8,12},{12,8},{16,20},{20,16},{24,28},{28,24},{1,5},{5... | collective-permute-start | bytes 786440 | tf_op jit(solution)/shard_map/ppermute | solution.py:27
  20.8 9.0 %collective-permute-start.8 = (bf16[256,128]{1,0:T(8,128)(2,1)S(1)}, bf16[256,128]{1,0:T(8,128)(2,1)S(1)}, u32[]{:S(2)}, u32[]{:S(2)}) collective-permute-start(bf16[256,128]{1,0:T(8,128)(2,1)S(1)} %get-tuple-element.46), channel_id=1, source_target_pairs={{0,24},{4,28},{8,16},{12,20},{16,8},{20,12},{24,0},{28,4},{1,25},{... | collective-permute-start | bytes 196616 | tf_op jit(solution)/shard_map/ppermute | solution.py:27
  25.1 6.6 %collective-permute-start.9 = (bf16[256,128]{1,0:T(8,128)(2,1)S(1)}, bf16[256,128]{1,0:T(8,128)(2,1)S(1)}, u32[]{:S(2)}, u32[]{:S(2)}) collective-permute-start(bf16[256,128]{1,0:T(8,128)(2,1)S(1)} %get-tuple-element.47), channel_id=1, source_target_pairs={{0,16},{4,20},{8,24},{12,28},{16,0},{20,4},{24,8},{28,12},{1,17},{... | collective-permute-start | bytes 196616 | tf_op jit(solution)/shard_map/ppermute | solution.py:27
  25.1 6.6 %collective-permute-start.10 = (bf16[256,128]{1,0:T(8,128)(2,1)S(1)}, bf16[256,128]{1,0:T(8,128)(2,1)S(1)}, u32[]{:S(2)}, u32[]{:S(2)}) collective-permute-start(bf16[256,128]{1,0:T(8,128)(2,1)S(1)} %get-tuple-element.48), channel_id=1, source_target_pairs={{0,8},{4,12},{8,0},{12,4},{16,24},{20,28},{24,16},{28,20},{1,9},{5... | collective-permute-start | bytes 196616 | tf_op jit(solution)/shard_map/ppermute | solution.py:27
  25.8 12.3 %collective-permute-start.4 = (bf16[256,128]{1,0:T(8,128)(2,1)S(1)}, bf16[256,128]{1,0:T(8,128)(2,1)S(1)}, u32[]{:S(2)}, u32[]{:S(2)}) collective-permute-start(bf16[256,128]{1,0:T(8,128)(2,1)S(1)} %get-tuple-element.38), channel_id=1, source_target_pairs={{0,24},{4,28},{8,16},{12,20},{16,8},{20,12},{24,0},{28,4},{1,25},{... | collective-permute-start | bytes 196616 | tf_op jit(solution)/shard_map/ppermute | solution.py:27
  29.8 8.3 %collective-permute-start.5 = (bf16[256,128]{1,0:T(8,128)(2,1)S(1)}, bf16[256,128]{1,0:T(8,128)(2,1)S(1)}, u32[]{:S(2)}, u32[]{:S(2)}) collective-permute-start(bf16[256,128]{1,0:T(8,128)(2,1)S(1)} %get-tuple-element.39), channel_id=1, source_target_pairs={{0,16},{4,20},{8,24},{12,28},{16,0},{20,4},{24,8},{28,12},{1,17},{... | collective-permute-start | bytes 196616 | tf_op jit(solution)/shard_map/ppermute | solution.py:27
  29.8 8.3 %collective-permute-start.6 = (bf16[256,128]{1,0:T(8,128)(2,1)S(1)}, bf16[256,128]{1,0:T(8,128)(2,1)S(1)}, u32[]{:S(2)}, u32[]{:S(2)}) collective-permute-start(bf16[256,128]{1,0:T(8,128)(2,1)S(1)} %get-tuple-element.40), channel_id=1, source_target_pairs={{0,8},{4,12},{8,0},{12,4},{16,24},{20,28},{24,16},{28,20},{1,9},{5... | collective-permute-start | bytes 196616 | tf_op jit(solution)/shard_map/ppermute | solution.py:27
  31.6 8.7 %copy-start = (bf16[1024,1024]{1,0:T(8,128)(2,1)S(1)}, bf16[1024,1024]{1,0:T(8,128)(2,1)}, u32[]{:S(2)}) copy-start(bf16[1024,1024]{1,0:T(8,128)(2,1)} %w_ref.3) | copy-start | bytes 6291460
  38.4 3.8 %collective-permute-start.11 = (bf16[128,256]{1,0:T(8,128)(2,1)S(1)}, bf16[128,256]{1,0:T(8,128)(2,1)S(1)}, u32[]{:S(2)}, u32[]{:S(2)}) collective-permute-start(bf16[128,256]{1,0:T(8,128)(2,1)S(1)} %get-tuple-element.58), channel_id=1, source_target_pairs={{0,3},{1,2},{2,1},{3,0},{4,7},{5,6},{6,5},{7,4},{8,11},{9,10},{10,... | collective-permute-start | bytes 196616 | tf_op jit(solution)/shard_map/ppermute | solution.py:27
  38.4 5.0 %collective-permute-start.12 = (bf16[128,256]{1,0:T(8,128)(2,1)S(1)}, bf16[128,256]{1,0:T(8,128)(2,1)S(1)}, u32[]{:S(2)}, u32[]{:S(2)}) collective-permute-start(bf16[128,256]{1,0:T(8,128)(2,1)S(1)} %get-tuple-element.59), channel_id=1, source_target_pairs={{0,2},{1,3},{2,0},{3,1},{4,6},{5,7},{6,4},{7,5},{8,10},{9,11},{10,... | collective-permute-start | bytes 196616 | tf_op jit(solution)/shard_map/ppermute | solution.py:27
  39.0 4.4 %collective-permute-start.13 = (bf16[128,256]{1,0:T(8,128)(2,1)S(1)}, bf16[128,256]{1,0:T(8,128)(2,1)S(1)}, u32[]{:S(2)}, u32[]{:S(2)}) collective-permute-start(bf16[128,256]{1,0:T(8,128)(2,1)S(1)} %get-tuple-element.60), channel_id=1, source_target_pairs={{0,1},{1,0},{2,3},{3,2},{4,5},{5,4},{6,7},{7,6},{8,9},{9,8},{10,11... | collective-permute-start | bytes 196616 | tf_op jit(solution)/shard_map/ppermute | solution.py:27

commit v12 on v8

--- a/solution.py
+++ b/solution.py
@@ -62,21 +62,24 @@
     )
 
 
-def sums_kernel(heads, owners, slot_bits, code_hbm, pack_hbm, keys_hbm, values_hbm, prompt_hbm,
+def sums_kernel(heads, owners, slot_bits, code_hbm, length_hbm, pick_hbm, keys_hbm, values_hbm, prompt_hbm,
                 send_gram, send_cross, keep_gram, keep_cross,
-                acc_ref, keys_ref, values_ref, stored_ref, code_ref, pack_ref, list_ref,
+                acc_ref, keys_ref, values_ref, stored_ref, code_ref, length_ref, pick_ref, hit_ref, list_ref,
                 key_sem, value_sem, small_sem):
     pool, rows = keys_hbm.shape[0], keys_hbm.shape[1]
     mine = lax.axis_index("grp")
     load_code = pltpu.make_async_copy(code_hbm, code_ref, small_sem.at[0])
     load_prompt = pltpu.make_async_copy(prompt_hbm, stored_ref, small_sem.at[1])
-    load_pack = pltpu.make_async_copy(pack_hbm, pack_ref, small_sem.at[2])
+    load_length = pltpu.make_async_copy(length_hbm, length_ref, small_sem.at[2])
+    load_pick = pltpu.make_async_copy(pick_hbm, pick_ref, small_sem.at[3])
     load_code.start()
-    load_pack.start()
+    load_length.start()
+    load_pick.start()
     load_prompt.start()
     acc_ref[...] = jnp.zeros_like(acc_ref)
     load_code.wait()
-    load_pack.wait()
+    load_length.wait()
+    load_pick.wait()
 
     def load(item):
         page = list_ref[item] & 0xFFFF
@@ -97,8 +100,8 @@
             page = chunk * wide + i
             code = code_ref[page]
             owner = code >> slot_bits
-            length = pack_ref[owner] & 0xFFFF
-            live = length - ((code & ((1 << slot_bits) - 1)) * PAGE)
+            hit_ref[owner] = pick_ref[page]
+            live = length_ref[page] - ((code & ((1 << slot_bits) - 1)) * PAGE)
             list_ref[count] = (owner << 24) | (jnp.minimum(live, PAGE) << 16) | page
             count = count + (live > 0).astype(jnp.int32)
         return count
@@ -145,7 +148,7 @@
     def add_prompt(owner, carry):
         for slot in range(stored):
 
-            @pl.when((pack_ref[owner] >> 16) == mine * stored + slot)
+            @pl.when(hit_ref[owner] == mine * stored + slot)
             def _():
                 for head in range(heads):
                     at = slice(head * HDIM, (head + 1) * HDIM)
@@ -164,26 +167,28 @@
         keep_cross[pair] = acc_ref[here, :, HDIM:].astype(BF16)
 
 
-def page_sums(code, pack, slot_bits, keys, values, prompt_state, owners):
+def page_sums(maps, slot_bits, keys, values, prompt_state, owners):
     pool, rows, _ = keys.shape
     heads = prompt_state.shape[1]
     half = (owners // 2, heads * HDIM, HDIM)
     items = pool + 4
     return pl.pallas_call(
         functools.partial(sums_kernel, heads, owners, slot_bits),
-        in_specs=[pl.BlockSpec(memory_space=pl.ANY)] * 5,
+        in_specs=[pl.BlockSpec(memory_space=pl.ANY)] * 6,
         out_specs=[pl.BlockSpec(memory_space=pltpu.VMEM)] * 4,
         scratch_shapes=[
             pltpu.VMEM((owners + 1, heads * HDIM, 2 * HDIM), F32),
             pltpu.VMEM((items, rows, HDIM), BF16),
             pltpu.VMEM((items, rows, HDIM), BF16),
             pltpu.VMEM(prompt_state.shape, F32),
-            pltpu.SMEM(code.shape, jnp.int32),
-            pltpu.SMEM(pack.shape, jnp.int32),
+            pltpu.SMEM((pool,), jnp.int32),
+            pltpu.SMEM((pool,), jnp.int32),
+            pltpu.SMEM((pool,), jnp.int32),
+            pltpu.SMEM((owners,), jnp.int32),
             pltpu.SMEM((items,), jnp.int32),
             pltpu.SemaphoreType.DMA((items,)),
             pltpu.SemaphoreType.DMA((items,)),
-            pltpu.SemaphoreType.DMA((3,)),
+            pltpu.SemaphoreType.DMA((4,)),
         ],
         out_shape=[jax.ShapeDtypeStruct(half, BF16)] * 4,
         compiler_params=pltpu.CompilerParams(vmem_limit_bytes=PAGE_VMEM * 2**20),
@@ -193,7 +198,7 @@
             transcendentals=0,
         ),
         name="page_sums",
-    )(code, pack, keys, values, prompt_state)
+    )(*maps, keys, values, prompt_state)
 
 
 def halve_kernel(keep_ref, got_ref, *outs):
@@ -542,12 +547,13 @@
     slots = page_table.shape[1]
     slot_bits = slots.bit_length() - 1
     assert slots == 1 << slot_bits
-    tag = jnp.arange(owners * slots, dtype=jnp.int32).reshape(owners, slots)
-    pack = cache_lengths | (group_prompt << 16)
+    tag = jnp.arange(owners * slots, dtype=jnp.int32).reshape(owners, slots, 1)
     ids = lax.axis_index("grp").astype(jnp.int32) * pool + jnp.arange(pool, dtype=jnp.int32)
-    code = jnp.sum(
-        jnp.where(page_table[:, :, None] == ids, tag[:, :, None], 0), axis=(0, 1), dtype=jnp.int32
-    )
+    match = page_table[:, :, None] == ids
+    maps = [
+        jnp.sum(jnp.where(match, what, 0), axis=(0, 1), dtype=jnp.int32)
+        for what in (tag, cache_lengths[:, None, None], group_prompt[:, None, None])
+    ]
     keys = cache_keys.reshape(pool, page * heads, HDIM)
     values = cache_values.reshape(pool, page * heads, HDIM)
 
@@ -556,7 +562,7 @@
         return [parts[0]] + sent
 
     send_gram, send_cross, keep_gram, keep_cross = page_sums(
-        code, pack, slot_bits, keys, values, prompt_state, owners
+        maps, slot_bits, keys, values, prompt_state, owners
     )
     got_gram = swap(send_gram, "grp", 1)
     for bit in bits[1:]:
@@ -572,9 +578,10 @@
     crosses = halve_sums(keep_cross, swap(send_cross, "grp", 1))
     base, solved = ridge_reads(ridge, scattered(grams), vectors, [crosses[0]])
     reads = cross_reads(scattered(crosses), base, solved, head_count)
-    parts = [reads[0]] + [swap(reads[i], "head", i) for i in range(1, head_count)]
-    total = output_rows(tokens, w_out, parts[:2], (0, 1), F32)
-    return output_rows(total, w_out, parts[2:], tuple(range(2, head_count)), BF16)
+    far = tuple(reversed(range(1, head_count)))
+    parts = [swap(reads[i], "head", i) for i in far]
+    total = output_rows(tokens, w_out, reads[:1], (0,), F32)
+    return output_rows(total, w_out, parts, far, BF16)
 
 
 def solution(mesh):

time: 45.4 us -> 44.4 us (0.978)
  other arithmetic: 1.59 us -> 0.93 us
    or x1 -> x0, other arithmetic: 0.68 us -> none  [shards(): pack = cache_lengths | group_prompt << 16]
  transfers between devices with their start and end apart: 14 -> 14, of which waited for: 4 -> 4; matrix products, arithmetic and copies ran while one was open for 4% -> 2% of each run, Pallas kernels for 41% -> 42%
where the time goes in v12:
time: 44.4 us; the launch traced here: 44.2 us
  Pallas kernels  20.1 us (45%)
  starting transfers between devices  17.3 us (39%)
  waiting for transfers between devices  5.45 us (12%)
  other arithmetic  0.93 us (2%)
    ppermute x14, starting transfers between devices, swap(): return lax.ppermute(block, axis, [(i, i ^ distance) for i in range(size)])  17.3 us
    pallas_call x1, Pallas kernels, page_sums(): pl.pallas_call(functools.partial(sums_kernel, heads, owners, slot_bits),...  7.15 us
    pallas_call x1, Pallas kernels, ridge_reads(): pl.pallas_call(functools.partial(read_kernel, heads, len(grams)), in_spec...  6.46 us
    ppermute x14, waiting for transfers between devices, swap(): return lax.ppermute(block, axis, [(i, i ^ distance) for i in range(size)])  5.45 us
    pallas_call x1, Pallas kernels, token_vectors(): pl.pallas_call(functools.partial(token_kernel, heads), in_specs=[whole] *...  4.73 us
    pallas_call x2, Pallas kernels, output_rows(): pl.pallas_call(functools.partial(output_kernel, distances), in_specs=[who...  1.33 us
    reduce_sum x1, other arithmetic, shards(): jnp.sum(jnp.where(match, what, 0), axis=(0, 1), dtype=jnp.int32)  0.92 us
  transfers between devices with their start and end apart: 14, of which 4 were waited for; matrix products, arithmetic and copies ran while one was open for 2% of the time, Pallas kernels for 42%

profile of v12, /device:TPU:0, one launch (start us, length us, event | category | flops | bytes accessed | tf_op | source)
XLA Modules:
  0.0 44.2 jit_solution(173432638091212113)
XLA Ops:
  0.0 2.9 %collective-permute-start.1 = (bf16[128,1024]{1,0:T(8,128)(2,1)}, bf16[128,1024]{1,0:T(8,128)(2,1)S(1)}, u32[]{:S(2)}, u32[]{:S(2)}) collective-permute-start(bf16[128,1024]{1,0:T(8,128)(2,1)} %start_ref.1), channel_id=1, source_target_pairs={{0,2},{1,3},{2,0},{3,1},{4,6},{5,7},{6,4},{7,5},{8,10},{9,11},{10,... | collective-permute-start | bytes 786440 | tf_op jit(solution)/shard_map/ppermute | solution.py:26
  2.9 0.0 collective-permute-start
  3.0 0.9 %fusion.2 = (s32[64]{0:T(128)S(1)}, s32[64]{0:T(128)S(1)}, s32[64]{0:T(128)S(1)}) fusion(s32[8]{0:T(128)} %param.28, s32[64]{0:T(128)S(1)} %iota_add_fusion, s32[8,64]{1,0:T(8,128)} %param.26, s32[8]{0:T(128)} %param.27, s32[8,64]{1,0:T(8,128)S(1)} %multiply_add_fusion), kind=kLoop, calls=%fused_computation.5 | loop fusion | flops 229184 | bytes 5184 | tf_op jit(solution)/shard_map/reduce_sum | solution.py:554
  3.9 0.0 copy-start.8
  3.9 0.0 copy-start.1
  3.9 0.0 copy-start.3
  3.9 0.0 copy-start.4
  3.9 0.0 copy-start.5
  3.9 0.0 copy-start.6
  3.9 7.1 %page_sums.1 = (bf16[4,256,128]{2,1,0:T(8,128)(2,1)S(1)}, bf16[4,256,128]{2,1,0:T(8,128)(2,1)S(1)}, bf16[4,256,128]{2,1,0:T(8,128)(2,1)S(1)}, bf16[4,256,128]{2,1,0:T(8,128)(2,1)}) custom-call(s32[64]{0:T(128)S(1)} %get-tuple-element.59.code_hbm, s32[64]{0:T(128)S(1)} %get-tuple-element.58.length_hbm, s32[64]{0:T(128)S(1)} %get-tuple-element.57.pick_hbm, ...), custom_call_target="tpu_custom_call" | custom-call | flops 4294967296 | bytes 8388608 | tf_op jit(solution)/shard_map/page_sums/pallas_call | solution.py:175
  11.1 0.0 collective-permute-done.1.refs_0_
  11.1 0.6 %collective-permute-start.2 = (bf16[128,1024]{1,0:T(8,128)(2,1)S(1)}, bf16[128,1024]{1,0:T(8,128)(2,1)S(1)}, u32[]{:S(2)}, u32[]{:S(2)}) collective-permute-start(bf16[128,1024]{1,0:T(8,128)(2,1)S(1)} %hold.1.refs_2_), channel_id=1, source_target_pairs={{0,1},{1,0},{2,3},{3,2},{4,5},{5,4},{6,7},{7,6},{8,9},{9,8},{10,11... | collective-permute-start | bytes 786440 | tf_op jit(solution)/shard_map/ppermute | solution.py:26
  11.7 2.0 %collective-permute-start.7 = (bf16[4,256,128]{2,1,0:T(8,128)(2,1)S(1)}, bf16[4,256,128]{2,1,0:T(8,128)(2,1)S(1)}, u32[]{:S(2)}, u32[]{:S(2)}) collective-permute-start(bf16[4,256,128]{2,1,0:T(8,128)(2,1)S(1)} %get-tuple-element.39), channel_id=1, source_target_pairs={{0,4},{4,0},{8,12},{12,8},{16,20},{20,16},{24,28},{28,24},{1,5},{5... | collective-permute-start | bytes 786440 | tf_op jit(solution)/shard_map/ppermute | solution.py:26
  13.7 0.0 copy-done.8
  13.7 0.2 copy.19.refs_6_
  13.8 0.0 collective-permute-done.refs_1_
  13.8 0.0 collective-permute-done.2.refs_3_
  13.9 0.0 copy-done.1
  13.9 0.0 copy-done.3
  13.9 0.0 copy-done.4
  13.9 0.0 copy-done.5
  13.9 0.0 copy-done.6
  13.9 0.0 copy-start.2
  13.9 0.0 copy-start.7
  13.9 4.7 %token_vectors.1 = (bf16[4,256,128]{2,1,0:T(8,128)(2,1)S(1)}, bf16[2,128,512]{2,1,0:T(8,128)(2,1)S(1)}, bf16[2,512,128]{2,1,0:T(8,128)(2,1)S(1)}, bf16[2,128,512...) custom-call(bf16[128,1024]{1,0:T(8,128)(2,1)S(1)} %copy-done.1, ...), custom_call_target="tpu_custom_call", output_to_operand_aliasing={{0}: (10, {})} | custom-call | flops 805306368 | bytes 6815744 | tf_op jit(solution)/shard_map/token_vectors/pallas_call | solution.py:337
  18.7 1.0 %collective-permute-start.3 = (bf16[4,256,128]{2,1,0:T(8,128)(2,1)S(1)}, bf16[4,256,128]{2,1,0:T(8,128)(2,1)S(1)}, u32[]{:S(2)}, u32[]{:S(2)}) collective-permute-start(bf16[4,256,128]{2,1,0:T(8,128)(2,1)S(1)} %get-tuple-element.34), channel_id=1, source_target_pairs={{0,4},{4,0},{8,12},{12,8},{16,20},{20,16},{24,28},{28,24},{1,5},{5... | collective-permute-start | bytes 786440 | tf_op jit(solution)/shard_map/ppermute | solution.py:26
  19.7 0.5 %collective-permute-done.7.got_ref = bf16[4,256,128]{2,1,0:T(8,128)(2,1)S(1)} collective-permute-done((bf16[4,256,128]{2,1,0:T(8,128)(2,1)S(1)}, bf16[4,256,128]{2,1,0:T(8,128)(2,1)S(1)}, u32[]{:S(2)}, u32[]{:S(2)}) %collective-permute-start.7) | collective-permute-done | bytes 262176 | tf_op jit(solution)/shard_map/ppermute | solution.py:26
  20.2 0.1 halve_sums.3
  20.3 3.4 %collective-permute-start.8 = (bf16[256,128]{1,0:T(8,128)(2,1)S(1)}, bf16[256,128]{1,0:T(8,128)(2,1)S(1)}, u32[]{:S(2)}, u32[]{:S(2)}) collective-permute-start(bf16[256,128]{1,0:T(8,128)(2,1)S(1)} %get-tuple-element.41), channel_id=1, source_target_pairs={{0,24},{4,28},{8,16},{12,20},{16,8},{20,12},{24,0},{28,4},{1,25},{... | collective-permute-start | bytes 196616 | tf_op jit(solution)/shard_map/ppermute | solution.py:26
  23.7 0.0 collective-permute-start.9
  23.7 1.0 %collective-permute-start.10 = (bf16[256,128]{1,0:T(8,128)(2,1)S(1)}, bf16[256,128]{1,0:T(8,128)(2,1)S(1)}, u32[]{:S(2)}, u32[]{:S(2)}) collective-permute-start(bf16[256,128]{1,0:T(8,128)(2,1)S(1)} %get-tuple-element.43), channel_id=1, source_target_pairs={{0,8},{4,12},{8,0},{12,4},{16,24},{20,28},{24,16},{28,20},{1,9},{5... | collective-permute-start | bytes 196616 | tf_op jit(solution)/shard_map/ppermute | solution.py:26
  24.7 2.0 %collective-permute-done.3.got_ref = bf16[4,256,128]{2,1,0:T(8,128)(2,1)S(1)} collective-permute-done((bf16[4,256,128]{2,1,0:T(8,128)(2,1)S(1)}, bf16[4,256,128]{2,1,0:T(8,128)(2,1)S(1)}, u32[]{:S(2)}, u32[]{:S(2)}) %collective-permute-start.3) | collective-permute-done | bytes 262176 | tf_op jit(solution)/shard_map/ppermute | solution.py:26
  26.7 0.0 copy-done.2
  26.7 0.1 halve_sums.2
  26.8 3.2 %collective-permute-start.4 = (bf16[256,128]{1,0:T(8,128)(2,1)S(1)}, bf16[256,128]{1,0:T(8,128)(2,1)S(1)}, u32[]{:S(2)}, u32[]{:S(2)}) collective-permute-start(bf16[256,128]{1,0:T(8,128)(2,1)S(1)} %get-tuple-element.36), channel_id=1, source_target_pairs={{0,24},{4,28},{8,16},{12,20},{16,8},{20,12},{24,0},{28,4},{1,25},{... | collective-permute-start | bytes 196616 | tf_op jit(solution)/shard_map/ppermute | solution.py:26
  30.0 0.0 collective-permute-start.5
  30.0 0.0 collective-permute-done.8.refs_1_
  30.0 1.2 %collective-permute-start.6 = (bf16[256,128]{1,0:T(8,128)(2,1)S(1)}, bf16[256,128]{1,0:T(8,128)(2,1)S(1)}, u32[]{:S(2)}, u32[]{:S(2)}) collective-permute-start(bf16[256,128]{1,0:T(8,128)(2,1)S(1)} %get-tuple-element.38), channel_id=1, source_target_pairs={{0,8},{4,12},{8,0},{12,4},{16,24},{20,28},{24,16},{28,20},{1,9},{5... | collective-permute-start | bytes 196616 | tf_op jit(solution)/shard_map/ppermute | solution.py:26
  31.3 0.0 collective-permute-done.9.refs_2_
  31.3 0.0 collective-permute-done.10.refs_3_
  31.3 0.0 copy-done.7
  31.3 0.0 copy-start
  31.3 6.5 %ridge_reads.1 = (f32[512,256]{1,0:T(8,128)S(1)}, bf16[512,256]{1,0:T(8,128)(2,1)S(1)}) custom-call(f32[1,2]{1,0:T(1,128)S(1)} %bitcast.7, f32[256,128]{1,0:T(8,128)S(1)} %get-tuple-element.40.refs_0_, bf16[256,128]{1,0:T(8,128)(2,1)S(1)} %collective-permute-done.8.refs_1_, bf16[256,128]{1,0:T(8,128)(2,1)S(1)} %collective-permute-done.9.refs_2_, ...), custom_call_target="tpu_custom_call" | custom-call | flops 6442450944 | bytes 8388608 | tf_op jit(solution)/shard_map/ridge_reads/pallas_call | solution.py:440
  37.8 0.0 collective-permute-done.4.refs_1_
  37.8 0.0 collective-permute-done.5.refs_2_
  37.8 0.0 collective-permute-done.6.refs_3_
  37.8 0.3 cross_reads.1
  38.1 0.1 collective-permute-start.11
  38.1 0.6 %collective-permute-start.12 = (bf16[128,256]{1,0:T(8,128)(2,1)S(1)}, bf16[128,256]{1,0:T(8,128)(2,1)S(1)}, u32[]{:S(2)}, u32[]{:S(2)}) collective-permute-start(bf16[128,256]{1,0:T(8,128)(2,1)S(1)} %get-tuple-element.55), channel_id=1, source_target_pairs={{0,2},{1,3},{2,0},{3,1},{4,6},{5,7},{6,4},{7,5},{8,10},{9,11},{10,... | collective-permute-start | bytes 196616 | tf_op jit(solution)/shard_map/ppermute | solution.py:26
  38.8 1.2 %collective-permute-start.13 = (bf16[128,256]{1,0:T(8,128)(2,1)S(1)}, bf16[128,256]{1,0:T(8,128)(2,1)S(1)}, u32[]{:S(2)}, u32[]{:S(2)}) collective-permute-start(bf16[128,256]{1,0:T(8,128)(2,1)S(1)} %get-tuple-element.56), channel_id=1, source_target_pairs={{0,1},{1,0},{2,3},{3,2},{4,5},{5,4},{6,7},{7,6},{8,9},{9,8},{10,11... | collective-permute-start | bytes 196616 | tf_op jit(solution)/shard_map/ppermute | solution.py:26
  40.0 0.0 copy-done
  40.0 0.2 output_rows.2.start_ref
  40.2 1.7 %collective-permute-done.11.refs_0_ = bf16[128,256]{1,0:T(8,128)(2,1)S(1)} collective-permute-done((bf16[128,256]{1,0:T(8,128)(2,1)S(1)}, bf16[128,256]{1,0:T(8,128)(2,1)S(1)}, u32[]{:S(2)}, u32[]{:S(2)}) %collective-permute-start.11) | collective-permute-done | bytes 65568 | tf_op jit(solution)/shard_map/ppermute | solution.py:26
  41.9 1.2 %collective-permute-done.12.refs_1_ = bf16[128,256]{1,0:T(8,128)(2,1)S(1)} collective-permute-done((bf16[128,256]{1,0:T(8,128)(2,1)S(1)}, bf16[128,256]{1,0:T(8,128)(2,1)S(1)}, u32[]{:S(2)}, u32[]{:S(2)}) %collective-permute-start.12) | collective-permute-done | bytes 65568 | tf_op jit(solution)/shard_map/ppermute | solution.py:26
  43.1 0.0 collective-permute-done.13.refs_2_
  43.1 1.1 %output_rows.3 = bf16[128,1024]{1,0:T(8,128)(2,1)} custom-call(f32[128,1024]{1,0:T(8,128)S(1)} %output_rows.2.start_ref, bf16[1024,1024]{1,0:T(8,128)(2,1)S(1)} %copy-done, bf16[128,256]{1,0:T(8,128)(2,1)S(1)} %collective-permute-done.11.refs_0_, bf16[128,256]{1,0:T(8,128)(2,1)S(1)} %collective-permute-done.12.refs_1_, ...), custom_call_target="tpu_custom_call" | custom-call | flops 201326592 | bytes 2883584 | tf_op jit(solution)/shard_map/output_rows/pallas_call | solution.py:507
  (3 shorter events, 0.0 us)
Async XLA Ops:
  0.0 11.1 %collective-permute-start.1 = (bf16[128,1024]{1,0:T(8,128)(2,1)}, bf16[128,1024]{1,0:T(8,128)(2,1)S(1)}, u32[]{:S(2)}, u32[]{:S(2)}) collective-permute-start(bf16[128,1024]{1,0:T(8,128)(2,1)} %start_ref.1), channel_id=1, source_target_pairs={{0,2},{1,3},{2,0},{3,1},{4,6},{5,7},{6,4},{7,5},{8,10},{9,11},{10,... | collective-permute-start | bytes 786440 | tf_op jit(solution)/shard_map/ppermute | solution.py:26
  2.9 10.9 %collective-permute-start = (bf16[128,1024]{1,0:T(8,128)(2,1)}, bf16[128,1024]{1,0:T(8,128)(2,1)S(1)}, u32[]{:S(2)}, u32[]{:S(2)}) collective-permute-start(bf16[128,1024]{1,0:T(8,128)(2,1)} %start_ref.1), channel_id=1, source_target_pairs={{0,1},{1,0},{2,3},{3,2},{4,5},{5,4},{6,7},{7,6},{8,9},{9,8},{10,11... | collective-permute-start | bytes 786440 | tf_op jit(solution)/shard_map/ppermute | solution.py:26
  3.9 9.8 %copy-start.8 = (bf16[1024,16]{0,1:T(8,128)(2,1)S(1)}, bf16[1024,16]{0,1:T(8,128)(2,1)}, u32[]{:S(2)}) copy-start(bf16[1024,16]{0,1:T(8,128)(2,1)} %param.18) | copy-start | bytes 98308
  3.9 10.0 %copy-start.1 = (bf16[128,1024]{1,0:T(8,128)(2,1)S(1)}, bf16[128,1024]{1,0:T(8,128)(2,1)}, u32[]{:S(2)}) copy-start(bf16[128,1024]{1,0:T(8,128)(2,1)} %start_ref.1) | copy-start | bytes 786436
  3.9 10.0 %copy-start.3 = (f32[4,3072]{1,0:T(4,128)S(1)}, f32[4,3072]{1,0:T(4,128)}, u32[]{:S(2)}) copy-start(f32[4,3072]{1,0:T(4,128)} %refs_7_.1) | copy-start | bytes 147460
  3.9 10.0 %copy-start.4 = (bf16[1,3,3072]{2,1,0:T(4,128)(2,1)S(1)}, bf16[1,3,3072]{2,1,0:T(4,128)(2,1)}, u32[]{:S(2)}) copy-start(bf16[1,3,3072]{2,1,0:T(4,128)(2,1)} %refs_8_.1) | copy-start | bytes 55300
  3.9 10.0 %copy-start.5 = (f32[1024]{0:T(1024)S(1)}, f32[1024]{0:T(1024)}, u32[]{:S(2)}) copy-start(f32[1024]{0:T(1024)} %param.16) | copy-start | bytes 12292
  3.9 10.0 %copy-start.6 = (f32[8]{0:T(128)S(1)}, f32[8]{0:T(128)}, u32[]{:S(2)}) copy-start(f32[8]{0:T(128)} %param.21) | copy-start | bytes 100
  11.1 2.7 %collective-permute-start.2 = (bf16[128,1024]{1,0:T(8,128)(2,1)S(1)}, bf16[128,1024]{1,0:T(8,128)(2,1)S(1)}, u32[]{:S(2)}, u32[]{:S(2)}) collective-permute-start(bf16[128,1024]{1,0:T(8,128)(2,1)S(1)} %hold.1.refs_2_), channel_id=1, source_target_pairs={{0,1},{1,0},{2,3},{3,2},{4,5},{5,4},{6,7},{7,6},{8,9},{9,8},{10,11... | collective-permute-start | bytes 786440 | tf_op jit(solution)/shard_map/ppermute | solution.py:26
  11.7 8.5 %collective-permute-start.7 = (bf16[4,256,128]{2,1,0:T(8,128)(2,1)S(1)}, bf16[4,256,128]{2,1,0:T(8,128)(2,1)S(1)}, u32[]{:S(2)}, u32[]{:S(2)}) collective-permute-start(bf16[4,256,128]{2,1,0:T(8,128)(2,1)S(1)} %get-tuple-element.39), channel_id=1, source_target_pairs={{0,4},{4,0},{8,12},{12,8},{16,20},{20,16},{24,28},{28,24},{1,5},{5... | collective-permute-start | bytes 786440 | tf_op jit(solution)/shard_map/ppermute | solution.py:26
  13.9 12.8 %copy-start.2 = (bf16[4,256,128]{2,1,0:T(8,128)(2,1)S(1)}, bf16[4,256,128]{2,1,0:T(8,128)(2,1)}, u32[]{:S(2)}) copy-start(bf16[4,256,128]{2,1,0:T(8,128)(2,1)} %get-tuple-element.31.keep_ref) | copy-start | bytes 786436
  13.9 17.4 %copy-start.7 = (f32[2]{0:T(128)S(1)}, f32[2]{0:T(128)}, u32[]{:S(2)}) copy-start(f32[2]{0:T(128)} %param.22) | copy-start | bytes 28
  18.7 8.1 %collective-permute-start.3 = (bf16[4,256,128]{2,1,0:T(8,128)(2,1)S(1)}, bf16[4,256,128]{2,1,0:T(8,128)(2,1)S(1)}, u32[]{:S(2)}, u32[]{:S(2)}) collective-permute-start(bf16[4,256,128]{2,1,0:T(8,128)(2,1)S(1)} %get-tuple-element.34), channel_id=1, source_target_pairs={{0,4},{4,0},{8,12},{12,8},{16,20},{20,16},{24,28},{28,24},{1,5},{5... | collective-permute-start | bytes 786440 | tf_op jit(solution)/shard_map/ppermute | solution.py:26
  20.3 9.8 %collective-permute-start.8 = (bf16[256,128]{1,0:T(8,128)(2,1)S(1)}, bf16[256,128]{1,0:T(8,128)(2,1)S(1)}, u32[]{:S(2)}, u32[]{:S(2)}) collective-permute-start(bf16[256,128]{1,0:T(8,128)(2,1)S(1)} %get-tuple-element.41), channel_id=1, source_target_pairs={{0,24},{4,28},{8,16},{12,20},{16,8},{20,12},{24,0},{28,4},{1,25},{... | collective-permute-start | bytes 196616 | tf_op jit(solution)/shard_map/ppermute | solution.py:26
  23.7 7.6 %collective-permute-start.9 = (bf16[256,128]{1,0:T(8,128)(2,1)S(1)}, bf16[256,128]{1,0:T(8,128)(2,1)S(1)}, u32[]{:S(2)}, u32[]{:S(2)}) collective-permute-start(bf16[256,128]{1,0:T(8,128)(2,1)S(1)} %get-tuple-element.42), channel_id=1, source_target_pairs={{0,16},{4,20},{8,24},{12,28},{16,0},{20,4},{24,8},{28,12},{1,17},{... | collective-permute-start | bytes 196616 | tf_op jit(solution)/shard_map/ppermute | solution.py:26
  23.7 7.6 %collective-permute-start.10 = (bf16[256,128]{1,0:T(8,128)(2,1)S(1)}, bf16[256,128]{1,0:T(8,128)(2,1)S(1)}, u32[]{:S(2)}, u32[]{:S(2)}) collective-permute-start(bf16[256,128]{1,0:T(8,128)(2,1)S(1)} %get-tuple-element.43), channel_id=1, source_target_pairs={{0,8},{4,12},{8,0},{12,4},{16,24},{20,28},{24,16},{28,20},{1,9},{5... | collective-permute-start | bytes 196616 | tf_op jit(solution)/shard_map/ppermute | solution.py:26
  26.8 11.0 %collective-permute-start.4 = (bf16[256,128]{1,0:T(8,128)(2,1)S(1)}, bf16[256,128]{1,0:T(8,128)(2,1)S(1)}, u32[]{:S(2)}, u32[]{:S(2)}) collective-permute-start(bf16[256,128]{1,0:T(8,128)(2,1)S(1)} %get-tuple-element.36), channel_id=1, source_target_pairs={{0,24},{4,28},{8,16},{12,20},{16,8},{20,12},{24,0},{28,4},{1,25},{... | collective-permute-start | bytes 196616 | tf_op jit(solution)/shard_map/ppermute | solution.py:26
  30.0 7.7 %collective-permute-start.5 = (bf16[256,128]{1,0:T(8,128)(2,1)S(1)}, bf16[256,128]{1,0:T(8,128)(2,1)S(1)}, u32[]{:S(2)}, u32[]{:S(2)}) collective-permute-start(bf16[256,128]{1,0:T(8,128)(2,1)S(1)} %get-tuple-element.37), channel_id=1, source_target_pairs={{0,16},{4,20},{8,24},{12,28},{16,0},{20,4},{24,8},{28,12},{1,17},{... | collective-permute-start | bytes 196616 | tf_op jit(solution)/shard_map/ppermute | solution.py:26
  30.0 7.8 %collective-permute-start.6 = (bf16[256,128]{1,0:T(8,128)(2,1)S(1)}, bf16[256,128]{1,0:T(8,128)(2,1)S(1)}, u32[]{:S(2)}, u32[]{:S(2)}) collective-permute-start(bf16[256,128]{1,0:T(8,128)(2,1)S(1)} %get-tuple-element.38), channel_id=1, source_target_pairs={{0,8},{4,12},{8,0},{12,4},{16,24},{20,28},{24,16},{28,20},{1,9},{5... | collective-permute-start | bytes 196616 | tf_op jit(solution)/shard_map/ppermute | solution.py:26
  31.3 8.7 %copy-start = (bf16[1024,1024]{1,0:T(8,128)(2,1)S(1)}, bf16[1024,1024]{1,0:T(8,128)(2,1)}, u32[]{:S(2)}) copy-start(bf16[1024,1024]{1,0:T(8,128)(2,1)} %w_ref.3) | copy-start | bytes 6291460
  38.1 3.8 %collective-permute-start.11 = (bf16[128,256]{1,0:T(8,128)(2,1)S(1)}, bf16[128,256]{1,0:T(8,128)(2,1)S(1)}, u32[]{:S(2)}, u32[]{:S(2)}) collective-permute-start(bf16[128,256]{1,0:T(8,128)(2,1)S(1)} %get-tuple-element.54), channel_id=1, source_target_pairs={{0,3},{1,2},{2,1},{3,0},{4,7},{5,6},{6,5},{7,4},{8,11},{9,10},{10,... | collective-permute-start | bytes 196616 | tf_op jit(solution)/shard_map/ppermute | solution.py:26
  38.1 5.0 %collective-permute-start.12 = (bf16[128,256]{1,0:T(8,128)(2,1)S(1)}, bf16[128,256]{1,0:T(8,128)(2,1)S(1)}, u32[]{:S(2)}, u32[]{:S(2)}) collective-permute-start(bf16[128,256]{1,0:T(8,128)(2,1)S(1)} %get-tuple-element.55), channel_id=1, source_target_pairs={{0,2},{1,3},{2,0},{3,1},{4,6},{5,7},{6,4},{7,5},{8,10},{9,11},{10,... | collective-permute-start | bytes 196616 | tf_op jit(solution)/shard_map/ppermute | solution.py:26
  38.8 4.4 %collective-permute-start.13 = (bf16[128,256]{1,0:T(8,128)(2,1)S(1)}, bf16[128,256]{1,0:T(8,128)(2,1)S(1)}, u32[]{:S(2)}, u32[]{:S(2)}) collective-permute-start(bf16[128,256]{1,0:T(8,128)(2,1)S(1)} %get-tuple-element.56), channel_id=1, source_target_pairs={{0,1},{1,0},{2,3},{3,2},{4,5},{5,4},{6,7},{7,6},{8,9},{9,8},{10,11... | collective-permute-start | bytes 196616 | tf_op jit(solution)/shard_map/ppermute | solution.py:26
